TPU v7x, 128 devices: a whole 4x4x4 slice. The times are simulated.
128 devices in a mesh: dp: 4 (over x_hi, core), head: 4 (over y), ctx: 8 (over x_lo, z).
Axes of the slice: x: 4 (x_hi: 2, x_lo: 2; x = x_hi * 2 + x_lo), y: 4, z: 4, core: 2. Of those that a mesh axis runs over, the one named last changes fastest.
Arguments:
- hidden_in: bfloat16 [4, 2048, 12288], P('dp', 'ctx'), may hold values from -6 to 6
- queries: bfloat16 [4, 2048, 6144], P('dp', 'ctx', 'head')
- rotary_key_rows: bfloat16 [4, 2048, 512], P('dp', 'ctx', 'head'), may hold values from -4.5 to 4.5
- value_projection: bfloat16 [12288, 512], P(('dp', 'ctx'), 'head'), may hold values from -0.0546875 to 0.0546875
- output_gradient: bfloat16 [4, 2048, 6144], P('dp', 'ctx', 'head'), may hold values from -1.5 to 1.5
- attended: bfloat16 [4, 2048, 6144], P('dp', 'ctx', 'head'), may hold values from -6 to 6
- doc_ids: int32 [4, 2048], P('dp'), may hold values from 0 to 5, never falling along the last dimension, each value on 1 to 1024 neighbouring positions
- block_place: int32 [4, 16], P('dp'), may hold values from 0 to 15, each once within a row
Outputs:
- query_gradient_rows: bfloat16 [4, 2048, 6144], P('dp', 'ctx', 'head')
- key_gradient_rows: bfloat16 [4, 2048, 512], P('dp', 'ctx', 'head')
- input_grad: bfloat16 [4, 2048, 12288], P('dp', 'ctx', 'head')
- weight_grad: float32 [12288, 512], P(('dp', 'ctx'), 'head')
Inputs may be any that keep to these rules, and one draw needn't show every extreme that they name: `doc_ids`: along each sequence the document numbers never fall; no document holds more than 1024 positions and one holds exactly that many. `block_place`: each row names every place 0 to 15 once.
All inputs are finite; a program needn't handle non-finite values.
Results may differ from a plain program's by a relative error of at most 0.02.
Values may be sent and summed in bfloat16 or wider, within the bound.
No kernel may reach another device: no remote copies, remote signals or barrier semaphores. Data moves between devices by JAX's collectives and lax.ppermute only.
A program may use at most 128 MiB of HBM per device.

v0:
```python
import jax
import jax.numpy as jnp
from jax import lax
from jax.experimental import pallas as pl
from jax.experimental.pallas import tpu as pltpu
from jax.sharding import PartitionSpec as P

HEAD_SIZE = 128
QUERY_PER_KEY = 12
PAIRS = QUERY_PER_KEY // 2
BLOCK = 128
WINDOW = 9
SPAN = WINDOW * BLOCK
SLAB = 384
QUARTER = 3072
MASKED = -1e30
LOG2E = 1.4426950408889634
SCALING = float(HEAD_SIZE) ** (-0.5)
f32 = jnp.float32
bf16 = jnp.bfloat16


def place_of(index):
    dp, ctx = divmod(index, 8)
    x_hi, core = divmod(dp, 2)
    x_lo, z = divmod(ctx, 4)
    return x_hi * 2 + x_lo, z, core


def index_of(x, z, core):
    x_hi, x_lo = divmod(x % 4, 2)
    return (x_hi * 2 + core) * 8 + x_lo * 4 + z % 4


def moved(value, where):
    pairs = [(i, index_of(*where(*place_of(i)))) for i in range(32)]
    return lax.ppermute(value, ("dp", "ctx"), pairs)


def core_swap(value):
    return moved(value, lambda x, z, c: (x, z, 1 - c))


def x_swap(value):
    return moved(value, lambda x, z, c: (x ^ 1, z, c))


def z_step(value, by):
    return moved(value, lambda x, z, c: (x, z + by, c))


def first_step(value, by):
    return moved(value, lambda x, z, c: (x, z + by, c) if c == 0 else (x + by, z, c))


def second_step(value, by):
    return moved(value, lambda x, z, c: (x + by, z, c) if c == 0 else (x, z + by, c))


def nt(a, b):
    return lax.dot_general(a, b, (((1,), (1,)), ((), ())), preferred_element_type=f32)


def nn(a, b):
    return lax.dot_general(a, b, (((1,), (0,)), ((), ())), preferred_element_type=f32)


def tn(a, b):
    return lax.dot_general(a, b, (((0,), (0,)), ((), ())), preferred_element_type=f32)


def row_terms_kernel(grad_ref, saved_ref, out_ref):
    for a in range(2):
        rows = slice(a * BLOCK, (a + 1) * BLOCK)
        for h in range(QUERY_PER_KEY):
            cols = slice(h * HEAD_SIZE, (h + 1) * HEAD_SIZE)
            product = grad_ref[rows, cols].astype(f32) * saved_ref[rows, cols].astype(f32)
            at = a * QUERY_PER_KEY + h
            out_ref[at : at + 1, :] = jnp.sum(product.T, axis=0, keepdims=True)


def pick_kernel(table_ref, in_ref, out_ref):
    out_ref[...] = in_ref[...]


def fill_bias(place, doc_ref, bias_ref):
    docs = doc_ref[...]
    own = doc_ref[pl.ds(place, 1), :]
    start = jnp.zeros((1, BLOCK), f32)
    for d in range(1, 6):
        held = jnp.sum(jnp.where(docs == d - 1, 1.0, 0.0), axis=(0, 1), keepdims=True)
        start = start + jnp.where(own >= d, held, 0.0)
    start = start.astype(jnp.int32)
    query = place * BLOCK + lax.broadcasted_iota(jnp.int32, (1, BLOCK), 1)
    key = (place - (WINDOW - 1)) * BLOCK + lax.broadcasted_iota(jnp.int32, (SPAN, 1), 0)
    bias_ref[...] = jnp.where((key >= start) & (key <= query), 0.0, MASKED)


def fill_window(table_ref, place, parts, win_ref):
    for j in range(WINDOW):
        block = table_ref[jnp.maximum(place - (WINDOW - 1) + j, 0)]
        win_ref[j * BLOCK : (j + 1) * BLOCK, :] = parts[pl.ds(pl.multiple_of(block * BLOCK, BLOCK), BLOCK), :]


def join(parts, all_ref):
    rows = parts[0].shape[0]
    for i, part in enumerate(parts):
        all_ref[i * rows : (i + 1) * rows, :] = part[...]


def stacked(ref, a, pair):
    rows = slice(a * BLOCK, (a + 1) * BLOCK)
    one = ref[rows, pair * 256 : pair * 256 + 128]
    two = ref[rows, pair * 256 + 128 : pair * 256 + 256]
    return jnp.concatenate([one, two], axis=0)


def beside(ref, a, pair):
    at = a * QUERY_PER_KEY + 2 * pair
    return jnp.concatenate([ref[at : at + 1, :], ref[at + 1 : at + 2, :]], axis=1)


def add_window(table_ref, place, win_ref, sum_ref):
    for j in range(WINDOW):
        block = table_ref[jnp.maximum(place - (WINDOW - 1) + j, 0)]
        at = pl.ds(pl.multiple_of(block * BLOCK, BLOCK), BLOCK)
        sum_ref[at, :] += win_ref[j * BLOCK : (j + 1) * BLOCK, :]


def value_side_kernel(
    table_ref, doc_ref, q_ref, g_ref, k0, k1, k2, k3,
    total_ref, o0, o1, o2, o3,
    all_ref, win_ref, bias_ref, score_ref, raised_ref, scaled_ref, acc_ref, sum_ref,
):
    join((k0, k1, k2, k3), all_ref)
    sum_ref[...] = jnp.zeros_like(sum_ref)
    for a in range(2):
        place = table_ref[16 + a]
        fill_bias(place, doc_ref, bias_ref)
        fill_window(table_ref, place, all_ref, win_ref)
        for pair in range(PAIRS):
            cols = slice(pair * 256, (pair + 1) * 256)
            products = nt(win_ref[...], stacked(q_ref, a, pair))
            highest = None
            for j in range(WINDOW):
                keys = slice(j * BLOCK, (j + 1) * BLOCK)
                bias = jnp.concatenate([bias_ref[keys, :]] * 2, axis=1)
                scores = products[keys] * (SCALING * LOG2E) + bias
                score_ref[keys, :] = scores
                highest = scores if highest is None else jnp.maximum(highest, scores)
            highest = jnp.max(highest, axis=0, keepdims=True)
            total = None
            for j in range(WINDOW):
                keys = slice(j * BLOCK, (j + 1) * BLOCK)
                raised = jnp.exp2(score_ref[keys, :] - highest)
                total = raised if total is None else total + raised
                raised_ref[keys, cols] = raised.astype(bf16)
            total = jnp.sum(total, axis=0, keepdims=True)
            log_total = highest + jnp.log2(total)
            share = 1.0 / total
            for half in range(2):
                h = 2 * pair + half
                lanes = slice(half * BLOCK, (half + 1) * BLOCK)
                at = a * QUERY_PER_KEY + h
                total_ref[at : at + 1, :] = log_total[:, lanes]
                factor = jnp.broadcast_to(share[:, lanes], (BLOCK, BLOCK)).T
                grads = g_ref[a * BLOCK : (a + 1) * BLOCK, h * HEAD_SIZE : (h + 1) * HEAD_SIZE]
                scaled_ref[h * BLOCK : (h + 1) * BLOCK, :] = (grads.astype(f32) * factor).astype(bf16)
        acc_ref[...] = nn(raised_ref[...], scaled_ref[...])
        add_window(table_ref, place, acc_ref, sum_ref)
    o0[...] = sum_ref[0:512, :]
    for i, out in enumerate((o1, o2, o3)):
        out[...] = sum_ref[512 * (i + 1) : 512 * (i + 2), :].astype(bf16)


def key_side_kernel(
    table_ref, doc_ref, q_ref, g_ref, total_ref, term_ref, k0, k1, k2, k3, v0, v1, v2, v3,
    dq_ref, o0, o1, o2, o3,
    allk_ref, allv_ref, wink_ref, winv_ref, bias_ref, ds_ref, qs_ref, acc_ref, sum_ref,
):
    join((k0, k1, k2, k3), allk_ref)
    join((v0, v1, v2, v3), allv_ref)
    sum_ref[...] = jnp.zeros_like(sum_ref)
    for a in range(2):
        place = table_ref[16 + a]
        fill_bias(place, doc_ref, bias_ref)
        fill_window(table_ref, place, allk_ref, wink_ref)
        fill_window(table_ref, place, allv_ref, winv_ref)
        for pair in range(PAIRS):
            cols = slice(pair * 256, (pair + 1) * 256)
            query = stacked(q_ref, a, pair)
            qs_ref[cols, :] = query
            products = nt(wink_ref[...], query)
            dprobs = nt(winv_ref[...], stacked(g_ref, a, pair))
            log_total = beside(total_ref, a, pair)
            terms = beside(term_ref, a, pair)
            for j in range(WINDOW):
                keys = slice(j * BLOCK, (j + 1) * BLOCK)
                bias = jnp.concatenate([bias_ref[keys, :]] * 2, axis=1)
                probs = jnp.exp2(products[keys] * (SCALING * LOG2E) + bias - log_total)
                ds_ref[keys, cols] = (probs * (dprobs[keys] - terms)).astype(bf16)
        dquery = tn(wink_ref[...], ds_ref[...]) * SCALING
        for h in range(QUERY_PER_KEY):
            dq_ref[a * BLOCK : (a + 1) * BLOCK, h * HEAD_SIZE : (h + 1) * HEAD_SIZE] = (
                dquery[:, h * BLOCK : (h + 1) * BLOCK].T.astype(bf16)
            )
        acc_ref[...] = nn(ds_ref[...], qs_ref[...])
        add_window(table_ref, place, acc_ref, sum_ref)
    o0[...] = sum_ref[0:512, :] * SCALING
    for i, out in enumerate((o1, o2, o3)):
        out[...] = (sum_ref[512 * (i + 1) : 512 * (i + 2), :] * SCALING).astype(bf16)


def own_half_copies(table_ref, hidden, half_ref, sems):
    return [
        pltpu.make_async_copy(
            hidden.at[:, pl.ds(pl.multiple_of(table_ref[16 + p] * QUARTER, BLOCK), QUARTER)],
            half_ref.at[:, p * QUARTER : (p + 1) * QUARTER],
            sems.at[p],
        )
        for p in range(2)
    ]


def project_kernel(table_ref, hidden, hb, w0, w1, w2, w3, oa, ob, lower, upper, ha_ref, all_ref, sems):
    copies = own_half_copies(table_ref, hidden, ha_ref, sems)
    for copy in copies:
        copy.start()
    for r, w in enumerate((w0, w1, w2, w3)):
        for i in range(4):
            at = pl.multiple_of(table_ref[r * 4 + i] * SLAB, BLOCK)
            all_ref[pl.ds(at, SLAB), :] = w[i * SLAB : (i + 1) * SLAB, :]
    lower[...] = all_ref[:QUARTER, :]
    upper[...] = all_ref[QUARTER:, :]
    ob[...] = nn(hb[...], all_ref[...])
    for copy in copies:
        copy.wait()
    oa[...] = nn(ha_ref[...], all_ref[...])


def weight_kernel(table_ref, hidden, hb, va, vb, o0, o1, o2, o3, ha_ref, sems):
    copies = own_half_copies(table_ref, hidden, ha_ref, sems)
    for copy in copies:
        copy.start()
    one, two = va[...].T, vb[...].T
    for copy in copies:
        copy.wait()
    for r, out in enumerate((o0, o1, o2, o3)):
        for i in range(4):
            cols = pl.ds(pl.multiple_of(table_ref[r * 4 + i] * SLAB, BLOCK), SLAB)
            block = nn(one, ha_ref[:, cols]) + nn(two, hb[:, cols])
            out[:, i * SLAB : (i + 1) * SLAB] = block.astype(out.dtype)


def input_kernel(table_ref, g0, g1, g2, g3, *refs):
    mine, other, out, rows_ref, sems = refs[:4], refs[4:8], refs[8], refs[9], refs[10]
    for choice, pieces in ((1, mine), (0, other)):

        @pl.when(table_ref[18] == choice)
        def _(pieces=pieces):
            copies = [
                pltpu.make_async_copy(p, rows_ref.at[:, d * BLOCK : (d + 1) * BLOCK], sems.at[d])
                for d, p in enumerate(pieces)
            ]
            for copy in copies:
                copy.start()
            for copy in copies:
                copy.wait()

    grads = jnp.concatenate([g0[...], g1[...], g2[...], g3[...]], axis=1)
    for part in range(4):
        cols = slice(part * 768, (part + 1) * 768)
        out[:, cols] = nt(grads, rows_ref[cols, :]).astype(bf16)


SMEM = pl.BlockSpec(memory_space=pltpu.SMEM)
VMEM = pl.BlockSpec(memory_space=pltpu.VMEM)


def call(kernel, outs, ins, scratch=(), flops=0, moved_bytes=0, exps=0, smem=1, anys=(), limit=40):
    any_spec = pl.BlockSpec(memory_space=pl.ANY)
    specs = [SMEM] * smem + [any_spec if i in anys else VMEM for i in range(smem, len(ins))]
    return pl.pallas_call(
        kernel,
        out_shape=tuple(jax.ShapeDtypeStruct(s, d) for s, d in outs),
        in_specs=specs,
        out_specs=tuple(VMEM for _ in outs),
        scratch_shapes=[s if not isinstance(s, tuple) else pltpu.VMEM(*s) for s in scratch],
        compiler_params=pltpu.CompilerParams(vmem_limit_bytes=limit * 1024 * 1024),
        cost_estimate=pl.CostEstimate(flops=flops, bytes_accessed=moved_bytes, transcendentals=exps),
    )(*ins)


def gathered(value):
    both = jnp.concatenate([value, x_swap(value)], axis=0)
    return (both, z_step(both, -1), z_step(both, -2), z_step(both, -3))


def summed(own, one, two, three):
    rows = own.shape[0] // 2
    total = (
        own
        + z_step(one, 1).astype(f32)
        + z_step(two, 2).astype(f32)
        + z_step(three, 3).astype(f32)
    )
    return total[:rows] + x_swap(total[rows:].astype(bf16)).astype(f32)


def local(
    hidden_in,
    queries,
    rotary_key_rows,
    value_projection,
    output_gradient,
    attended,
    doc_ids,
    block_place,
):
    dp = lax.axis_index("dp")
    ctx = lax.axis_index("ctx")
    x_hi, core = dp // 2, dp % 2
    x_lo, z = ctx // 4, ctx % 4
    x = x_hi * 2 + x_lo
    rows = queries.shape[1]
    grad_scale = float(rows * 32) ** (-0.5)
    query, grad, saved = queries[0], output_gradient[0], attended[0]
    docs = doc_ids[0].reshape(16, BLOCK)
    placing = block_place[0]

    stored = jnp.arange(16, dtype=jnp.int32)
    owner = stored // 2
    lies = ((owner % 4 - z) % 4) * 4 + ((owner // 4 + x_lo) % 2) * 2 + stored % 2
    at_place = jnp.sum(jnp.where(placing[None, :] == stored[:, None], lies[None, :], 0), axis=1)
    mine = jnp.sum(jnp.where(stored[None, :] == (2 * ctx + jnp.arange(2))[:, None], placing[None, :], 0), axis=1)
    table = jnp.concatenate([at_place, mine])

    head = lax.axis_index("head")

    def quarters_of(core):
        lead = ((head + (head % 2 != core)) % 4) // 2
        return jnp.stack([2 * lead + core, 2 * (1 - lead) + core]), lead

    own_quarters, lead = quarters_of(core)
    other_quarters, _ = quarters_of(1 - core)

    outer, inner = jnp.arange(16, dtype=jnp.int32) // 4, jnp.arange(16, dtype=jnp.int32) % 4
    slab_x = (x + jnp.where(core == 0, outer, inner)) % 4
    slab_z = (z + jnp.where(core == 0, inner, outer)) % 4
    slabs = ((slab_x // 2 + lead) % 2) * 8 + (slab_x % 2) * 4 + slab_z
    has_rows = (head % 2 == core).astype(jnp.int32)
    slabs = jnp.concatenate([slabs, own_quarters, has_rows[None]]).astype(jnp.int32)

    keys = gathered(rotary_key_rows[0])

    first = jnp.concatenate(
        [value_projection] + [first_step(value_projection, -i) for i in (1, 2, 3)], axis=0
    )
    weights = (first,) + tuple(second_step(first, -i) for i in (1, 2, 3))

    hidden = hidden_in[0]
    picked = pl.pallas_call(
        pick_kernel,
        grid_spec=pltpu.PrefetchScalarGridSpec(
            num_scalar_prefetch=1,
            grid=(4,),
            in_specs=[pl.BlockSpec((rows, QUARTER // 2), lambda i, t: (0, t[i // 2] * 2 + i % 2))],
            out_specs=pl.BlockSpec((rows, QUARTER // 2), lambda i, t: (0, i)),
        ),
        out_shape=jax.ShapeDtypeStruct((rows, 2 * QUARTER), bf16),
        cost_estimate=pl.CostEstimate(flops=0, bytes_accessed=6 << 20, transcendentals=0),
    )(other_quarters.astype(jnp.int32), hidden)
    hb = core_swap(picked)

    (terms,) = call(row_terms_kernel, [((24, 128), f32)], [grad, saved], smem=0, moved_bytes=1 << 21)

    window = ((SPAN, HEAD_SIZE), bf16)
    whole = ((2048, HEAD_SIZE), bf16)
    bias = ((SPAN, BLOCK), f32)
    square = ((SPAN, 1536), bf16)
    stack = ((1536, HEAD_SIZE), bf16)
    sums = [((SPAN, HEAD_SIZE), f32), ((2048, HEAD_SIZE), f32)]
    parts_out = [((512, HEAD_SIZE), f32)] + [((512, HEAD_SIZE), bf16)] * 3
    dots = 2 * 12 * 256 * SPAN * HEAD_SIZE
    totals, *value_parts = call(
        value_side_kernel,
        [((24, 128), f32)] + parts_out,
        [table, docs, query, grad, *keys],
        scratch=[whole, window, bias, ((SPAN, 256), f32), square, stack] + sums,
        flops=4 * dots, moved_bytes=4 << 20, exps=12 * 256 * SPAN,
    )
    value_grads = summed(*value_parts).astype(bf16)
    sibling_grads = core_swap(value_grads)

    half = ((rows, 2 * QUARTER), bf16)
    sems = pltpu.SemaphoreType.DMA((4,))
    part_a, part_b, lower, upper = call(
        project_kernel,
        [((rows, HEAD_SIZE), f32)] * 2 + [((QUARTER, HEAD_SIZE), bf16)] * 2,
        [slabs, hidden, hb, *weights],
        scratch=[half, ((2 * QUARTER, HEAD_SIZE), bf16), sems], anys=(1,),
        flops=2 * 512 * 6144 * 128, moved_bytes=10 << 20,
    )
    values = gathered((part_a + core_swap(part_b)).astype(bf16))

    def along_y(value, by):
        pairs = []
        for s in range(4):
            for dp_at in range(4):
                if (s + by) % 2 == dp_at % 2:
                    pairs.append((dp_at * 4 + s, dp_at * 4 + (s + by) % 4))
        return lax.ppermute(value, ("dp", "head"), pairs)

    own_rows = [lower, along_y(lower, 1), along_y(upper, 2), along_y(upper, 3)]
    swapped_rows = [core_swap(r) for r in own_rows]

    w_parts = call(
        weight_kernel,
        [((HEAD_SIZE, 1536), f32)] + [((HEAD_SIZE, 1536), bf16)] * 3,
        [slabs, hidden, hb, value_grads, sibling_grads],
        scratch=[half, sems], anys=(1,),
        flops=2 * 512 * 6144 * 128, moved_bytes=8 << 20,
    )
    w_sum = w_parts[0]
    for i in (1, 2, 3):
        w_sum = w_sum + second_step(w_parts[i], i).astype(f32)
    w_total = w_sum[:, :SLAB]
    for i in (1, 2, 3):
        w_total = w_total + first_step(w_sum[:, i * SLAB : (i + 1) * SLAB].astype(bf16), i).astype(f32)
    weight_grad = (w_total * grad_scale).T

    every = [value_grads] + [
        lax.ppermute(value_grads, "head", [(s, (s + i) % 4) for s in range(4)]) for i in (1, 2, 3)
    ]
    (input_grad,) = call(
        input_kernel,
        [((rows, QUARTER), bf16)],
        [slabs, *every, *own_rows, *swapped_rows],
        scratch=[((QUARTER, 512), bf16), sems], anys=tuple(range(5, 13)),
        flops=2 * 256 * 512 * 3072, moved_bytes=5 << 20,
    )

    dquery, *key_parts = call(
        key_side_kernel,
        [((rows, 1536), bf16)] + parts_out,
        [table, docs, query, grad, totals, terms, *keys, *values],
        scratch=[whole, whole, window, window, bias, square, stack] + sums,
        flops=8 * dots, moved_bytes=6 << 20, exps=12 * 256 * SPAN,
    )
    key_grads = summed(*key_parts).astype(bf16)
    return dquery[None], key_grads[None], input_grad[None], weight_grad


def solution(mesh):
    in_specs = (
        P("dp", "ctx", None),
        P("dp", "ctx", "head"),
        P("dp", "ctx", "head"),
        P(("dp", "ctx"), "head"),
        P("dp", "ctx", "head"),
        P("dp", "ctx", "head"),
        P("dp", None),
        P("dp", None),
    )
    out_specs = (
        P("dp", "ctx", "head"),
        P("dp", "ctx", "head"),
        P("dp", "ctx", "head"),
        P(("dp", "ctx"), "head"),
    )
    return jax.shard_map(local, mesh=mesh, in_specs=in_specs, out_specs=out_specs, check_vma=False)
```

profile of v0, /device:TPU:0, one launch (start us, length us, event | category | flops | bytes accessed | tf_op | source)
XLA Modules:
  0.0 128.4 jit_solution(6626786054619198230)
XLA Ops:
  0.7 0.6 pad_add_fusion.2.table_ref
  1.3 5.1 %shard_map.113 = bf16[256,6144]{1,0:T(8,128)(2,1)} custom-call(s32[2]{0:T(128)} %pad_add_fusion.2.table_ref, bf16[256,12288]{1,0:T(8,128)(2,1)} %bitcast.18), custom_call_target="tpu_custom_call" | custom-call | bytes 6291456 | tf_op jit(solution)/shard_map/pallas_call | solution.py:362
  6.4 4.1 %collective-permute-start.5 = (bf16[384,128]{1,0:T(8,128)(2,1)}, bf16[384,128]{1,0:T(8,128)(2,1)}, u32[]{:S(2)}, u32[]{:S(2)}) collective-permute-start(bf16[384,128]{1,0:T(8,128)(2,1)} %param.11), channel_id=1, source_target_pairs={{0,3},{1,0},{2,1},{3,2},{4,7},{5,4},{6,5},{7,6},{32,100},{33,101},... | collective-permute-start | bytes 294920 | tf_op jit(solution)/shard_map/ppermute | solution.py:37
  10.5 1.3 collective-permute-start.7
  11.7 1.5 %collective-permute-start = (bf16[256,128]{1,0:T(8,128)(2,1)}, bf16[256,128]{1,0:T(8,128)(2,1)}, u32[]{:S(2)}, u32[]{:S(2)}) collective-permute-start(bf16[256,128]{1,0:T(8,128)(2,1)} %bitcast.4), channel_id=1, source_target_pairs={{0,4},{1,5},{2,6},{3,7},{4,0},{5,1},{6,2},{7,3},{32,36},{33,37},{3... | collective-permute-start | bytes 196616 | tf_op jit(solution)/shard_map/ppermute | solution.py:37
  13.6 0.9 constant_dynamic-update-slice_fusion.3
  14.6 1.8 %collective-permute-done = bf16[256,128]{1,0:T(8,128)(2,1)} collective-permute-done((bf16[256,128]{1,0:T(8,128)(2,1)}, bf16[256,128]{1,0:T(8,128)(2,1)}, u32[]{:S(2)}, u32[]{:S(2)}) %collective-permute-start) | collective-permute-done | bytes 65568 | tf_op jit(solution)/shard_map/ppermute | solution.py:37
  16.3 1.5 %pad_maximum_fusion.k0 = bf16[512,128]{1,0:T(8,128)(2,1)} fusion(bf16[256,128]{1,0:T(8,128)(2,1)} %collective-permute-done, bf16[256,128]{1,0:T(8,128)(2,1)} %bitcast.4), kind=kLoop, calls=%fused_computation.14 | loop fusion | flops 262144 | bytes 262144 | tf_op jit(solution)/shard_map/concatenate | solution.py:295
  17.9 2.6 %collective-permute-start.1 = (bf16[512,128]{1,0:T(8,128)(2,1)}, bf16[512,128]{1,0:T(8,128)(2,1)S(1)}, u32[]{:S(2)}, u32[]{:S(2)}) collective-permute-start(bf16[512,128]{1,0:T(8,128)(2,1)} %pad_maximum_fusion.k0), channel_id=1, source_target_pairs={{0,3},{1,0},{2,1},{3,2},{4,7},{5,4},{6,5},{7,6},{32,35},{33,32},{3... | collective-permute-start | bytes 393224 | tf_op jit(solution)/shard_map/ppermute | solution.py:37
  20.5 1.7 %collective-permute-start.2 = (bf16[512,128]{1,0:T(8,128)(2,1)}, bf16[512,128]{1,0:T(8,128)(2,1)}, u32[]{:S(2)}, u32[]{:S(2)}) collective-permute-start(bf16[512,128]{1,0:T(8,128)(2,1)} %pad_maximum_fusion.k0), channel_id=1, source_target_pairs={{0,2},{1,3},{2,0},{3,1},{4,6},{5,7},{6,4},{7,5},{32,34},{33,35},{3... | collective-permute-start | bytes 393224 | tf_op jit(solution)/shard_map/ppermute | solution.py:37
  22.2 0.9 constant_dynamic-update-slice_fusion.2
  23.2 0.9 constant_dynamic-update-slice_fusion.1
  24.1 0.9 constant_dynamic-update-slice_fusion.w0
  25.0 1.6 %collective-permute-start.10 = (bf16[1536,128]{1,0:T(8,128)(2,1)S(1)}, bf16[1536,128]{1,0:T(8,128)(2,1)}, u32[]{:S(2)}, u32[]{:S(2)}) collective-permute-start(bf16[1536,128]{1,0:T(8,128)(2,1)S(1)} %constant_dynamic-update-slice_fusion.w0), channel_id=1, source_target_pairs={{0,4},{1,5},{2,6},{3,7},{4,64},{5,65},{6,66},{7,67},{32,33},{33,34... | collective-permute-start | bytes 1179656 | tf_op jit(solution)/shard_map/ppermute | solution.py:37
  26.6 0.7 copy-done.5
  27.3 2.9 %collective-permute-start.8 = (bf16[1536,128]{1,0:T(8,128)(2,1)S(1)}, bf16[1536,128]{1,0:T(8,128)(2,1)}, u32[]{:S(2)}, u32[]{:S(2)}) collective-permute-start(bf16[1536,128]{1,0:T(8,128)(2,1)S(1)} %constant_dynamic-update-slice_fusion.w0), channel_id=1, source_target_pairs={{0,68},{1,69},{2,70},{3,71},{4,0},{5,1},{6,2},{7,3},{32,35},{33,32... | collective-permute-start | bytes 1179656 | tf_op jit(solution)/shard_map/ppermute | solution.py:37
  30.2 0.6 fusion.9
  30.8 0.8 collective-permute-start.9
  31.6 1.3 copy-done.1
  32.9 1.3 %copy-done.3 = bf16[1,256,1536]{2,1,0:T(8,128)(2,1)S(1)} copy-done((bf16[1,256,1536]{2,1,0:T(8,128)(2,1)S(1)}, bf16[1,256,1536]{2,1,0:T(8,128)(2,1)}, u32[]{:S(2)}) %copy-start.3) | copy-done | bytes 786456
  34.2 0.9 copy-done.6
  35.1 7.3 %shard_map.111 = (f32[24,128]{1,0:T(8,128)S(1)}, f32[512,128]{1,0:T(8,128)S(1)}, bf16[512,128]{1,0:T(8,128)(2,1)S(1)}, bf16[512,128]{1,0:T(8,128)(2,1)S(1)}, bf16[512,128]{1,0:T(8,128)(2,1)S(1)}) custom-call(s32[18]{0:T(128)S(1)} %pad_add_fusion.table_ref, s32[16,128]{1,0:T(8,128)S(1)} %bitcast.29, bf16[256,1536]{1,0:T(8,128)(2,1)S(1)} %bitcast.27, ...), custom_call_target="tpu_custom_call" | custom-call | flops 3623878656 | bytes 4194304 | tf_op jit(solution)/shard_map/pallas_call | solution.py:283
  42.4 1.0 collective-permute-start.20
  43.4 4.1 %collective-permute-start.21 = (bf16[512,128]{1,0:T(8,128)(2,1)S(1)}, bf16[512,128]{1,0:T(8,128)(2,1)S(1)}, u32[]{:S(2)}, u32[]{:S(2)}) collective-permute-start(bf16[512,128]{1,0:T(8,128)(2,1)S(1)} %get-tuple-element.32), channel_id=1, source_target_pairs={{0,2},{1,3},{2,0},{3,1},{4,6},{5,7},{6,4},{7,5},{32,34},{33,35},{3... | collective-permute-start | bytes 393224 | tf_op jit(solution)/shard_map/ppermute | solution.py:37
  47.7 3.7 %shard_map.114 = (f32[256,128]{1,0:T(8,128)S(1)}, f32[256,128]{1,0:T(8,128)S(1)}, bf16[3072,128]{1,0:T(8,128)(2,1)}, bf16[3072,128]{1,0:T(8,128)(2,1)S(1)}) custom-call(s32[19]{0:T(128)S(1)} %pad_add_fusion.1.table_ref, bf16[256,12288]{1,0:T(8,128)(2,1)S(1)} %bitcast.21, bf16[256,6144]{1,0:T(8,128)(2,1)S(1)} %collective-permute-done.4.hb, ...), custom_call_target="tpu_custom_call" | custom-call | flops 805306368 | bytes 10485760 | tf_op jit(solution)/shard_map/pallas_call | solution.py:283
  51.9 0.6 collective-permute-done.22
  52.6 0.9 collective-permute-start.23
  53.5 1.3 %collective-permute-start.12 = (bf16[256,128]{1,0:T(8,128)(2,1)S(1)}, bf16[256,128]{1,0:T(8,128)(2,1)S(1)}, u32[]{:S(2)}, u32[]{:S(2)}) collective-permute-start(bf16[256,128]{1,0:T(8,128)(2,1)S(1)} %add_convert_fusion), channel_id=1, source_target_pairs={{0,4},{1,5},{2,6},{3,7},{4,0},{5,1},{6,2},{7,3},{32,36},{33,37},{3... | collective-permute-start | bytes 196616 | tf_op jit(solution)/shard_map/ppermute | solution.py:37
  54.8 2.2 %collective-permute-done.23 = bf16[256,128]{1,0:T(8,128)(2,1)S(1)} collective-permute-done((bf16[256,128]{1,0:T(8,128)(2,1)S(1)}, bf16[256,128]{1,0:T(8,128)(2,1)S(1)}, u32[]{:S(2)}, u32[]{:S(2)}) %collective-permute-start.23) | collective-permute-done | bytes 65568 | tf_op jit(solution)/shard_map/ppermute | solution.py:37
  57.2 0.7 collective-permute-done.12
  57.9 3.2 %collective-permute-start.13 = (bf16[512,128]{1,0:T(8,128)(2,1)S(1)}, bf16[512,128]{1,0:T(8,128)(2,1)S(1)}, u32[]{:S(2)}, u32[]{:S(2)}) collective-permute-start(bf16[512,128]{1,0:T(8,128)(2,1)S(1)} %pad_maximum_fusion.1.v0), channel_id=1, source_target_pairs={{0,3},{1,0},{2,1},{3,2},{4,7},{5,4},{6,5},{7,6},{32,35},{33,32},{3... | collective-permute-start | bytes 393224 | tf_op jit(solution)/shard_map/ppermute | solution.py:37
  61.1 0.7 collective-permute-start.14
  61.8 0.5 collective-permute-start.15
  62.3 0.5 shard_map.112.term_ref
  62.8 1.6 %collective-permute-start.24 = (bf16[256,128]{1,0:T(8,128)(2,1)S(1)}, bf16[256,128]{1,0:T(8,128)(2,1)S(1)}, u32[]{:S(2)}, u32[]{:S(2)}) collective-permute-start(bf16[256,128]{1,0:T(8,128)(2,1)S(1)} %fusion.4.g0.va), channel_id=1, source_target_pairs={{0,8},{8,16},{16,24},{24,0},{1,9},{9,17},{17,25},{25,1},{2,10},{10... | collective-permute-start | bytes 196616 | tf_op jit(solution)/shard_map/ppermute | solution.py:433
  64.4 2.9 %collective-permute-start.25 = (bf16[256,128]{1,0:T(8,128)(2,1)S(1)}, bf16[256,128]{1,0:T(8,128)(2,1)S(1)}, u32[]{:S(2)}, u32[]{:S(2)}) collective-permute-start(bf16[256,128]{1,0:T(8,128)(2,1)S(1)} %fusion.4.g0.va), channel_id=1, source_target_pairs={{0,16},{8,24},{16,0},{24,8},{1,17},{9,25},{17,1},{25,9},{2,18},{10... | collective-permute-start | bytes 196616 | tf_op jit(solution)/shard_map/ppermute | solution.py:433
  67.3 2.2 %shard_map.117 = (f32[128,1536]{1,0:T(8,128)S(1)}, bf16[128,1536]{1,0:T(8,128)(2,1)S(1)}, bf16[128,1536]{1,0:T(8,128)(2,1)S(1)}, bf16[128,1536]{1,0:T(8,128)(2,1)S(1)}) custom-call(s32[19]{0:T(128)S(1)} %pad_add_fusion.1.table_ref, bf16[256,12288]{1,0:T(8,128)(2,1)S(1)} %bitcast.22, bf16[256,6144]{1,0:T(8,128)(2,1)S(1)} %collective-permute-done.4.hb, ...), custom_call_target="tpu_custom_call" | custom-call | flops 805306368 | bytes 8388608 | tf_op jit(solution)/shard_map/pallas_call | solution.py:283
  69.5 1.0 collective-permute-start.35
  70.5 2.6 %collective-permute-start.36 = (bf16[128,1536]{1,0:T(8,128)(2,1)S(1)}, bf16[128,1536]{1,0:T(8,128)(2,1)S(1)}, u32[]{:S(2)}, u32[]{:S(2)}) collective-permute-start(bf16[128,1536]{1,0:T(8,128)(2,1)S(1)} %get-tuple-element.38), channel_id=1, source_target_pairs={{0,64},{1,65},{2,66},{3,67},{4,68},{5,69},{6,70},{7,71},{32,34},{3... | collective-permute-start | bytes 1179656 | tf_op jit(solution)/shard_map/ppermute | solution.py:37
  73.1 1.5 %collective-permute-start.37 = (bf16[128,1536]{1,0:T(8,128)(2,1)S(1)}, bf16[128,1536]{1,0:T(8,128)(2,1)S(1)}, u32[]{:S(2)}, u32[]{:S(2)}) collective-permute-start(bf16[128,1536]{1,0:T(8,128)(2,1)S(1)} %get-tuple-element.39), channel_id=1, source_target_pairs={{0,68},{1,69},{2,70},{3,71},{4,0},{5,1},{6,2},{7,3},{32,35},{33,32... | collective-permute-start | bytes 1179656 | tf_op jit(solution)/shard_map/ppermute | solution.py:37
  74.6 8.9 %shard_map.115 = (bf16[256,1536]{1,0:T(8,128)(2,1)}, f32[512,128]{1,0:T(8,128)S(1)}, bf16[512,128]{1,0:T(8,128)(2,1)S(1)}, bf16[512,128]{1,0:T(8,128)(2,1)S(1)}, bf16[512,128]{1,0:T(8,128)(2,1)S(1)}) custom-call(s32[18]{0:T(128)S(1)} %pad_add_fusion.table_ref, s32[16,128]{1,0:T(8,128)S(1)} %bitcast.30, bf16[256,1536]{1,0:T(8,128)(2,1)S(1)} %bitcast.28, ...), custom_call_target="tpu_custom_call" | custom-call | flops 7247757312 | bytes 6291456 | tf_op jit(solution)/shard_map/pallas_call | solution.py:283
  83.6 3.3 %collective-permute-start.28 = (bf16[3072,128]{1,0:T(8,128)(2,1)S(1)}, bf16[3072,128]{1,0:T(8,128)(2,1)S(1)}, u32[]{:S(2)}, u32[]{:S(2)}) collective-permute-start(bf16[3072,128]{1,0:T(8,128)(2,1)S(1)} %get-tuple-element.35), channel_id=1, source_target_pairs={{0,16},{64,80},{40,56},{104,120},{16,0},{80,64},{56,40},{120,104},... | collective-permute-start | bytes 2359304 | tf_op jit(solution)/shard_map/ppermute | solution.py:412
  86.9 1.3 %collective-permute-start.29 = (bf16[3072,128]{1,0:T(8,128)(2,1)S(1)}, bf16[3072,128]{1,0:T(8,128)(2,1)S(1)}, u32[]{:S(2)}, u32[]{:S(2)}) collective-permute-start(bf16[3072,128]{1,0:T(8,128)(2,1)S(1)} %get-tuple-element.35), channel_id=1, source_target_pairs={{32,56},{96,120},{8,0},{72,64},{48,40},{112,104},{24,16},{88,80},{... | collective-permute-start | bytes 2359304 | tf_op jit(solution)/shard_map/ppermute | solution.py:412
  88.2 1.3 %collective-permute-start.27 = (bf16[3072,128]{1,0:T(8,128)(2,1)}, bf16[3072,128]{1,0:T(8,128)(2,1)S(1)}, u32[]{:S(2)}, u32[]{:S(2)}) collective-permute-start(bf16[3072,128]{1,0:T(8,128)(2,1)} %get-tuple-element.34.refs_0_), channel_id=1, source_target_pairs={{32,40},{96,104},{8,16},{72,80},{48,56},{112,120},{24,0},{88,64},{... | collective-permute-start | bytes 2359304 | tf_op jit(solution)/shard_map/ppermute | solution.py:412
  89.5 1.8 %collective-permute-start.16 = (bf16[512,128]{1,0:T(8,128)(2,1)S(1)}, bf16[512,128]{1,0:T(8,128)(2,1)S(1)}, u32[]{:S(2)}, u32[]{:S(2)}) collective-permute-start(bf16[512,128]{1,0:T(8,128)(2,1)S(1)} %get-tuple-element.27), channel_id=1, source_target_pairs={{0,1},{1,2},{2,3},{3,0},{4,5},{5,6},{6,7},{7,4},{32,33},{33,34},{3... | collective-permute-start | bytes 393224 | tf_op jit(solution)/shard_map/ppermute | solution.py:37
  91.5 2.1 %collective-permute-start.17 = (bf16[512,128]{1,0:T(8,128)(2,1)S(1)}, bf16[512,128]{1,0:T(8,128)(2,1)S(1)}, u32[]{:S(2)}, u32[]{:S(2)}) collective-permute-start(bf16[512,128]{1,0:T(8,128)(2,1)S(1)} %get-tuple-element.28), channel_id=1, source_target_pairs={{0,2},{1,3},{2,0},{3,1},{4,6},{5,7},{6,4},{7,5},{32,34},{33,35},{3... | collective-permute-start | bytes 393224 | tf_op jit(solution)/shard_map/ppermute | solution.py:37
  93.7 2.7 %collective-permute-done.16 = bf16[512,128]{1,0:T(8,128)(2,1)S(1)} collective-permute-done((bf16[512,128]{1,0:T(8,128)(2,1)S(1)}, bf16[512,128]{1,0:T(8,128)(2,1)S(1)}, u32[]{:S(2)}, u32[]{:S(2)}) %collective-permute-start.16) | collective-permute-done | bytes 131104 | tf_op jit(solution)/shard_map/ppermute | solution.py:37
  96.4 0.6 collective-permute-start.18
  97.0 1.1 collective-permute-done.17
  98.1 0.7 collective-permute-start.38
  98.8 2.6 %collective-permute-done.18 = bf16[512,128]{1,0:T(8,128)(2,1)S(1)} collective-permute-done((bf16[512,128]{1,0:T(8,128)(2,1)S(1)}, bf16[512,128]{1,0:T(8,128)(2,1)S(1)}, u32[]{:S(2)}, u32[]{:S(2)}) %collective-permute-start.18) | collective-permute-done | bytes 131104 | tf_op jit(solution)/shard_map/ppermute | solution.py:37
  101.4 1.4 %collective-permute-start.39 = (bf16[128,384]{1,0:T(8,128)(2,1)S(1)}, bf16[128,384]{1,0:T(8,128)(2,1)S(1)}, u32[]{:S(2)}, u32[]{:S(2)}) collective-permute-start(bf16[128,384]{1,0:T(8,128)(2,1)S(1)} %get-tuple-element.52), channel_id=1, source_target_pairs={{0,2},{1,3},{2,0},{3,1},{4,6},{5,7},{6,4},{7,5},{32,96},{33,97},{3... | collective-permute-start | bytes 294920 | tf_op jit(solution)/shard_map/ppermute | solution.py:37
  102.7 1.2 collective-permute-done.38
  103.9 5.4 %collective-permute-done.27.refs_1_ = bf16[3072,128]{1,0:T(8,128)(2,1)S(1)} collective-permute-done((bf16[3072,128]{1,0:T(8,128)(2,1)}, bf16[3072,128]{1,0:T(8,128)(2,1)S(1)}, u32[]{:S(2)}, u32[]{:S(2)}) %collective-permute-start.27) | collective-permute-done | bytes 786464 | tf_op jit(solution)/shard_map/ppermute | solution.py:412
  109.4 0.5 collective-permute-start.32
  110.0 3.2 %collective-permute-start.40 = (bf16[128,384]{1,0:T(8,128)(2,1)S(1)}, bf16[128,384]{1,0:T(8,128)(2,1)S(1)}, u32[]{:S(2)}, u32[]{:S(2)}) collective-permute-start(bf16[128,384]{1,0:T(8,128)(2,1)S(1)} %get-tuple-element.51), channel_id=1, source_target_pairs={{0,3},{1,0},{2,1},{3,2},{4,7},{5,4},{6,5},{7,6},{32,100},{33,101},... | collective-permute-start | bytes 294920 | tf_op jit(solution)/shard_map/ppermute | solution.py:37
  113.1 0.8 convert_add_fusion.2
  113.9 1.5 %slice.65 = bf16[256,128]{1,0:T(8,128)(2,1)} slice(f32[512,128]{1,0:T(8,128)} %convert_add_fusion.2), slice={[256:512], [0:128]} | slice | bytes 131072 | tf_op jit(solution)/shard_map/slice | solution.py:307
  115.4 0.6 collective-permute-start.19
  116.0 0.8 copy.13
  116.9 3.2 %collective-permute-done.19 = bf16[256,128]{1,0:T(8,128)(2,1)} collective-permute-done((bf16[256,128]{1,0:T(8,128)(2,1)}, bf16[256,128]{1,0:T(8,128)(2,1)}, u32[]{:S(2)}, u32[]{:S(2)}) %collective-permute-start.19) | collective-permute-done | bytes 65568 | tf_op jit(solution)/shard_map/ppermute | solution.py:37
  120.2 1.6 %fusion.6 = bf16[1,256,128]{2,1,0:T(8,128)(2,1)} fusion(bf16[256,128]{1,0:T(8,128)(2,1)} %collective-permute-done.19, f32[512,128]{1,0:T(8,128)} %convert_add_fusion.2), kind=kLoop, calls=%fused_computation.17 | loop fusion | flops 98304 | bytes 262144 | tf_op jit(solution)/shard_map/broadcast_in_dim | solution.py:451
  121.8 2.5 %collective-permute-done.26.g3 = bf16[256,128]{1,0:T(8,128)(2,1)S(1)} collective-permute-done((bf16[256,128]{1,0:T(8,128)(2,1)S(1)}, bf16[256,128]{1,0:T(8,128)(2,1)S(1)}, u32[]{:S(2)}, u32[]{:S(2)}) %collective-permute-start.26) | collective-permute-done | bytes 65568 | tf_op jit(solution)/shard_map/ppermute | solution.py:433
  124.3 3.9 %shard_map.116 = bf16[256,3072]{1,0:T(8,128)(2,1)} custom-call(s32[19]{0:T(128)S(1)} %pad_add_fusion.1.table_ref, bf16[256,128]{1,0:T(8,128)(2,1)S(1)} %fusion.4.g0.va, bf16[256,128]{1,0:T(8,128)(2,1)S(1)} %collective-permute-done.24.g1, bf16[256,128]{1,0:T(8,128)(2,1)S(1)} %collective-permute-done.25.g2, bf16[256,128]{1,0:T(8,128)(2,1)S(1)} %collective-permute-done.26.g3, ...), custom_call_target="tpu_custom_call" | custom-call | flops 805306368 | bytes 5242880 | tf_op jit(solution)/shard_map/pallas_call | solution.py:283
  (75 shorter events, 2.0 us)
Async XLA Ops:
  1.3 12.0 %copy-start.9 = (s32[1,16]{1,0:T(1,128)S(1)}, s32[1,16]{1,0:T(1,128)}, u32[]{:S(2)}) copy-start(s32[1,16]{1,0:T(1,128)} %param.15) | copy-start | bytes 196
  1.3 30.3 %copy-start.7 = (s32[1,2048]{1,0:T(1,128)S(1)}, s32[1,2048]{1,0:T(1,128)}, u32[]{:S(2)}) copy-start(s32[1,2048]{1,0:T(1,128)} %param.14) | copy-start | bytes 24580
  6.4 41.3 %collective-permute-start.4 = (bf16[256,6144]{1,0:T(8,128)(2,1)}, bf16[256,6144]{1,0:T(8,128)(2,1)S(1)}, u32[]{:S(2)}, u32[]{:S(2)}) collective-permute-start(bf16[256,6144]{1,0:T(8,128)(2,1)} %shard_map.113), channel_id=1, source_target_pairs={{0,32},{1,33},{2,34},{3,35},{4,36},{5,37},{6,38},{7,39},{32,0},{33... | collective-permute-start | bytes 9437192 | tf_op jit(solution)/shard_map/ppermute | solution.py:37
  6.4 14.1 %collective-permute-start.5 = (bf16[384,128]{1,0:T(8,128)(2,1)}, bf16[384,128]{1,0:T(8,128)(2,1)}, u32[]{:S(2)}, u32[]{:S(2)}) collective-permute-start(bf16[384,128]{1,0:T(8,128)(2,1)} %param.11), channel_id=1, source_target_pairs={{0,3},{1,0},{2,1},{3,2},{4,7},{5,4},{6,5},{7,6},{32,100},{33,101},... | collective-permute-start | bytes 294920 | tf_op jit(solution)/shard_map/ppermute | solution.py:37
  10.5 12.6 %collective-permute-start.6 = (bf16[384,128]{1,0:T(8,128)(2,1)}, bf16[384,128]{1,0:T(8,128)(2,1)}, u32[]{:S(2)}, u32[]{:S(2)}) collective-permute-start(bf16[384,128]{1,0:T(8,128)(2,1)} %param.11), channel_id=1, source_target_pairs={{0,2},{1,3},{2,0},{3,1},{4,6},{5,7},{6,4},{7,5},{32,96},{33,97},{3... | collective-permute-start | bytes 294920 | tf_op jit(solution)/shard_map/ppermute | solution.py:37
  10.5 13.6 %collective-permute-start.7 = (bf16[384,128]{1,0:T(8,128)(2,1)}, bf16[384,128]{1,0:T(8,128)(2,1)}, u32[]{:S(2)}, u32[]{:S(2)}) collective-permute-start(bf16[384,128]{1,0:T(8,128)(2,1)} %param.11), channel_id=1, source_target_pairs={{0,1},{1,2},{2,3},{3,0},{4,5},{5,6},{6,7},{7,4},{32,36},{33,37},{3... | collective-permute-start | bytes 294920 | tf_op jit(solution)/shard_map/ppermute | solution.py:37
  11.7 4.6 %collective-permute-start = (bf16[256,128]{1,0:T(8,128)(2,1)}, bf16[256,128]{1,0:T(8,128)(2,1)}, u32[]{:S(2)}, u32[]{:S(2)}) collective-permute-start(bf16[256,128]{1,0:T(8,128)(2,1)} %bitcast.4), channel_id=1, source_target_pairs={{0,4},{1,5},{2,6},{3,7},{4,0},{5,1},{6,2},{7,3},{32,36},{33,37},{3... | collective-permute-start | bytes 196616 | tf_op jit(solution)/shard_map/ppermute | solution.py:37
  17.9 8.8 %collective-permute-start.1 = (bf16[512,128]{1,0:T(8,128)(2,1)}, bf16[512,128]{1,0:T(8,128)(2,1)S(1)}, u32[]{:S(2)}, u32[]{:S(2)}) collective-permute-start(bf16[512,128]{1,0:T(8,128)(2,1)} %pad_maximum_fusion.k0), channel_id=1, source_target_pairs={{0,3},{1,0},{2,1},{3,2},{4,7},{5,4},{6,5},{7,6},{32,35},{33,32},{3... | collective-permute-start | bytes 393224 | tf_op jit(solution)/shard_map/ppermute | solution.py:37
  20.5 10.3 %collective-permute-start.2 = (bf16[512,128]{1,0:T(8,128)(2,1)}, bf16[512,128]{1,0:T(8,128)(2,1)}, u32[]{:S(2)}, u32[]{:S(2)}) collective-permute-start(bf16[512,128]{1,0:T(8,128)(2,1)} %pad_maximum_fusion.k0), channel_id=1, source_target_pairs={{0,2},{1,3},{2,0},{3,1},{4,6},{5,7},{6,4},{7,5},{32,34},{33,35},{3... | collective-permute-start | bytes 393224 | tf_op jit(solution)/shard_map/ppermute | solution.py:37
  23.1 8.5 %collective-permute-start.3 = (bf16[512,128]{1,0:T(8,128)(2,1)}, bf16[512,128]{1,0:T(8,128)(2,1)}, u32[]{:S(2)}, u32[]{:S(2)}) collective-permute-start(bf16[512,128]{1,0:T(8,128)(2,1)} %pad_maximum_fusion.k0), channel_id=1, source_target_pairs={{0,1},{1,2},{2,3},{3,0},{4,5},{5,6},{6,7},{7,4},{32,33},{33,34},{3... | collective-permute-start | bytes 393224 | tf_op jit(solution)/shard_map/ppermute | solution.py:37
  25.0 18.4 %collective-permute-start.10 = (bf16[1536,128]{1,0:T(8,128)(2,1)S(1)}, bf16[1536,128]{1,0:T(8,128)(2,1)}, u32[]{:S(2)}, u32[]{:S(2)}) collective-permute-start(bf16[1536,128]{1,0:T(8,128)(2,1)S(1)} %constant_dynamic-update-slice_fusion.w0), channel_id=1, source_target_pairs={{0,4},{1,5},{2,6},{3,7},{4,64},{5,65},{6,66},{7,67},{32,33},{33,34... | collective-permute-start | bytes 1179656 | tf_op jit(solution)/shard_map/ppermute | solution.py:37
  26.6 0.7 copy-start.5
  27.3 20.3 %collective-permute-start.8 = (bf16[1536,128]{1,0:T(8,128)(2,1)S(1)}, bf16[1536,128]{1,0:T(8,128)(2,1)}, u32[]{:S(2)}, u32[]{:S(2)}) collective-permute-start(bf16[1536,128]{1,0:T(8,128)(2,1)S(1)} %constant_dynamic-update-slice_fusion.w0), channel_id=1, source_target_pairs={{0,68},{1,69},{2,70},{3,71},{4,0},{5,1},{6,2},{7,3},{32,35},{33,32... | collective-permute-start | bytes 1179656 | tf_op jit(solution)/shard_map/ppermute | solution.py:37
  30.8 16.9 %collective-permute-start.9 = (bf16[1536,128]{1,0:T(8,128)(2,1)S(1)}, bf16[1536,128]{1,0:T(8,128)(2,1)S(1)}, u32[]{:S(2)}, u32[]{:S(2)}) collective-permute-start(bf16[1536,128]{1,0:T(8,128)(2,1)S(1)} %constant_dynamic-update-slice_fusion.w0), channel_id=1, source_target_pairs={{0,64},{1,65},{2,66},{3,67},{4,68},{5,69},{6,70},{7,71},{32,34},{3... | collective-permute-start | bytes 1179656 | tf_op jit(solution)/shard_map/ppermute | solution.py:37
  31.6 16.1 %slice-start = ((s8[6291456]{0:T(1024)(128)(4,1)}), s8[4194304]{0:T(1024)(128)(4,1)S(1)}, s32[]{:S(2)}) async-start(s8[6291456]{0:T(1024)(128)(4,1)} %bitcast.19), calls=%async_computation | async-start | bytes 8388608
  31.6 1.3 %copy-start.1 = (bf16[1,256,1536]{2,1,0:T(8,128)(2,1)S(1)}, bf16[1,256,1536]{2,1,0:T(8,128)(2,1)}, u32[]{:S(2)}) copy-start(bf16[1,256,1536]{2,1,0:T(8,128)(2,1)} %param.12) | copy-start | bytes 2359300
  32.9 1.3 %copy-start.3 = (bf16[1,256,1536]{2,1,0:T(8,128)(2,1)S(1)}, bf16[1,256,1536]{2,1,0:T(8,128)(2,1)}, u32[]{:S(2)}) copy-start(bf16[1,256,1536]{2,1,0:T(8,128)(2,1)} %param.9) | copy-start | bytes 2359300
  34.2 0.9 copy-start.6
  35.1 12.4 %copy-start.8 = (s32[16]{0:T(128)S(1)}, s32[16]{0:T(128)}, u32[]{:S(2)}) copy-start(s32[16]{0:T(128)} %fusion.9) | copy-start | bytes 196
  35.1 12.5 %slice-start.1 = ((s8[6291456]{0:T(1024)(128)(4,1)}), s8[2097152]{0:T(1024)(128)(4,1)S(1)}, s32[]{:S(2)}) async-start(s8[6291456]{0:T(1024)(128)(4,1)} %bitcast.19), calls=%async_computation.1 | async-start | bytes 4194304
  42.4 9.1 %collective-permute-start.20 = (bf16[512,128]{1,0:T(8,128)(2,1)S(1)}, bf16[512,128]{1,0:T(8,128)(2,1)S(1)}, u32[]{:S(2)}, u32[]{:S(2)}) collective-permute-start(bf16[512,128]{1,0:T(8,128)(2,1)S(1)} %get-tuple-element.31), channel_id=1, source_target_pairs={{0,1},{1,2},{2,3},{3,0},{4,5},{5,6},{6,7},{7,4},{32,33},{33,34},{3... | collective-permute-start | bytes 393224 | tf_op jit(solution)/shard_map/ppermute | solution.py:37
  43.4 8.4 %collective-permute-start.21 = (bf16[512,128]{1,0:T(8,128)(2,1)S(1)}, bf16[512,128]{1,0:T(8,128)(2,1)S(1)}, u32[]{:S(2)}, u32[]{:S(2)}) collective-permute-start(bf16[512,128]{1,0:T(8,128)(2,1)S(1)} %get-tuple-element.32), channel_id=1, source_target_pairs={{0,2},{1,3},{2,0},{3,1},{4,6},{5,7},{6,4},{7,5},{32,34},{33,35},{3... | collective-permute-start | bytes 393224 | tf_op jit(solution)/shard_map/ppermute | solution.py:37
  47.5 5.0 %collective-permute-start.22 = (bf16[512,128]{1,0:T(8,128)(2,1)S(1)}, bf16[512,128]{1,0:T(8,128)(2,1)S(1)}, u32[]{:S(2)}, u32[]{:S(2)}) collective-permute-start(bf16[512,128]{1,0:T(8,128)(2,1)S(1)} %get-tuple-element.33), channel_id=1, source_target_pairs={{0,3},{1,0},{2,1},{3,2},{4,7},{5,4},{6,5},{7,6},{32,35},{33,32},{3... | collective-permute-start | bytes 393224 | tf_op jit(solution)/shard_map/ppermute | solution.py:37
  47.6 14.7 %copy-start = (bf16[1,256,1536]{2,1,0:T(8,128)(2,1)S(1)}, bf16[1,256,1536]{2,1,0:T(8,128)(2,1)}, u32[]{:S(2)}) copy-start(bf16[1,256,1536]{2,1,0:T(8,128)(2,1)} %param.13) | copy-start | bytes 2359300
  47.6 14.7 %copy-start.2 = (bf16[1,256,1536]{2,1,0:T(8,128)(2,1)S(1)}, bf16[1,256,1536]{2,1,0:T(8,128)(2,1)}, u32[]{:S(2)}) copy-start(bf16[1,256,1536]{2,1,0:T(8,128)(2,1)} %param.12) | copy-start | bytes 2359300
  51.4 2.1 %collective-permute-start.11 = (f32[256,128]{1,0:T(8,128)S(1)}, f32[256,128]{1,0:T(8,128)S(1)}, u32[]{:S(2)}, u32[]{:S(2)}) collective-permute-start(f32[256,128]{1,0:T(8,128)S(1)} %get-tuple-element.24), channel_id=1, source_target_pairs={{0,32},{1,33},{2,34},{3,35},{4,36},{5,37},{6,38},{7,39},{32,0},{33... | collective-permute-start | bytes 393224 | tf_op jit(solution)/shard_map/ppermute | solution.py:37
  52.6 4.5 %collective-permute-start.23 = (bf16[256,128]{1,0:T(8,128)(2,1)S(1)}, bf16[256,128]{1,0:T(8,128)(2,1)S(1)}, u32[]{:S(2)}, u32[]{:S(2)}) collective-permute-start(bf16[256,128]{1,0:T(8,128)(2,1)S(1)} %slice.64), channel_id=1, source_target_pairs={{0,4},{1,5},{2,6},{3,7},{4,0},{5,1},{6,2},{7,3},{32,36},{33,37},{3... | collective-permute-start | bytes 196616 | tf_op jit(solution)/shard_map/ppermute | solution.py:37
  53.5 4.3 %collective-permute-start.12 = (bf16[256,128]{1,0:T(8,128)(2,1)S(1)}, bf16[256,128]{1,0:T(8,128)(2,1)S(1)}, u32[]{:S(2)}, u32[]{:S(2)}) collective-permute-start(bf16[256,128]{1,0:T(8,128)(2,1)S(1)} %add_convert_fusion), channel_id=1, source_target_pairs={{0,4},{1,5},{2,6},{3,7},{4,0},{5,1},{6,2},{7,3},{32,36},{33,37},{3... | collective-permute-start | bytes 196616 | tf_op jit(solution)/shard_map/ppermute | solution.py:37
  57.1 7.3 %collective-permute-start.34 = (bf16[256,128]{1,0:T(8,128)(2,1)S(1)}, bf16[256,128]{1,0:T(8,128)(2,1)S(1)}, u32[]{:S(2)}, u32[]{:S(2)}) collective-permute-start(bf16[256,128]{1,0:T(8,128)(2,1)S(1)} %fusion.4.g0.va), channel_id=1, source_target_pairs={{0,32},{1,33},{2,34},{3,35},{4,36},{5,37},{6,38},{7,39},{32,0},{33... | collective-permute-start | bytes 196616 | tf_op jit(solution)/shard_map/ppermute | solution.py:37
  57.9 11.6 %collective-permute-start.13 = (bf16[512,128]{1,0:T(8,128)(2,1)S(1)}, bf16[512,128]{1,0:T(8,128)(2,1)S(1)}, u32[]{:S(2)}, u32[]{:S(2)}) collective-permute-start(bf16[512,128]{1,0:T(8,128)(2,1)S(1)} %pad_maximum_fusion.1.v0), channel_id=1, source_target_pairs={{0,3},{1,0},{2,1},{3,2},{4,7},{5,4},{6,5},{7,6},{32,35},{33,32},{3... | collective-permute-start | bytes 393224 | tf_op jit(solution)/shard_map/ppermute | solution.py:37
  61.1 9.4 %collective-permute-start.14 = (bf16[512,128]{1,0:T(8,128)(2,1)S(1)}, bf16[512,128]{1,0:T(8,128)(2,1)S(1)}, u32[]{:S(2)}, u32[]{:S(2)}) collective-permute-start(bf16[512,128]{1,0:T(8,128)(2,1)S(1)} %pad_maximum_fusion.1.v0), channel_id=1, source_target_pairs={{0,2},{1,3},{2,0},{3,1},{4,6},{5,7},{6,4},{7,5},{32,34},{33,35},{3... | collective-permute-start | bytes 393224 | tf_op jit(solution)/shard_map/ppermute | solution.py:37
  61.8 11.4 %collective-permute-start.15 = (bf16[512,128]{1,0:T(8,128)(2,1)S(1)}, bf16[512,128]{1,0:T(8,128)(2,1)S(1)}, u32[]{:S(2)}, u32[]{:S(2)}) collective-permute-start(bf16[512,128]{1,0:T(8,128)(2,1)S(1)} %pad_maximum_fusion.1.v0), channel_id=1, source_target_pairs={{0,1},{1,2},{2,3},{3,0},{4,5},{5,6},{6,7},{7,4},{32,33},{33,34},{3... | collective-permute-start | bytes 393224 | tf_op jit(solution)/shard_map/ppermute | solution.py:37
  62.8 11.8 %copy-start.4 = (bf16[1,256,1536]{2,1,0:T(8,128)(2,1)S(1)}, bf16[1,256,1536]{2,1,0:T(8,128)(2,1)}, u32[]{:S(2)}) copy-start(bf16[1,256,1536]{2,1,0:T(8,128)(2,1)} %param.9) | copy-start | bytes 2359300
  62.8 20.8 %collective-permute-start.24 = (bf16[256,128]{1,0:T(8,128)(2,1)S(1)}, bf16[256,128]{1,0:T(8,128)(2,1)S(1)}, u32[]{:S(2)}, u32[]{:S(2)}) collective-permute-start(bf16[256,128]{1,0:T(8,128)(2,1)S(1)} %fusion.4.g0.va), channel_id=1, source_target_pairs={{0,8},{8,16},{16,24},{24,0},{1,9},{9,17},{17,25},{25,1},{2,10},{10... | collective-permute-start | bytes 196616 | tf_op jit(solution)/shard_map/ppermute | solution.py:433
  64.4 27.1 %collective-permute-start.25 = (bf16[256,128]{1,0:T(8,128)(2,1)S(1)}, bf16[256,128]{1,0:T(8,128)(2,1)S(1)}, u32[]{:S(2)}, u32[]{:S(2)}) collective-permute-start(bf16[256,128]{1,0:T(8,128)(2,1)S(1)} %fusion.4.g0.va), channel_id=1, source_target_pairs={{0,16},{8,24},{16,0},{24,8},{1,17},{9,25},{17,1},{25,9},{2,18},{10... | collective-permute-start | bytes 196616 | tf_op jit(solution)/shard_map/ppermute | solution.py:433
  69.5 17.3 %collective-permute-start.35 = (bf16[128,1536]{1,0:T(8,128)(2,1)S(1)}, bf16[128,1536]{1,0:T(8,128)(2,1)S(1)}, u32[]{:S(2)}, u32[]{:S(2)}) collective-permute-start(bf16[128,1536]{1,0:T(8,128)(2,1)S(1)} %get-tuple-element.37), channel_id=1, source_target_pairs={{0,4},{1,5},{2,6},{3,7},{4,64},{5,65},{6,66},{7,67},{32,33},{33,34... | collective-permute-start | bytes 1179656 | tf_op jit(solution)/shard_map/ppermute | solution.py:37
  70.5 17.6 %collective-permute-start.36 = (bf16[128,1536]{1,0:T(8,128)(2,1)S(1)}, bf16[128,1536]{1,0:T(8,128)(2,1)S(1)}, u32[]{:S(2)}, u32[]{:S(2)}) collective-permute-start(bf16[128,1536]{1,0:T(8,128)(2,1)S(1)} %get-tuple-element.38), channel_id=1, source_target_pairs={{0,64},{1,65},{2,66},{3,67},{4,68},{5,69},{6,70},{7,71},{32,34},{3... | collective-permute-start | bytes 1179656 | tf_op jit(solution)/shard_map/ppermute | solution.py:37
  73.1 16.4 %collective-permute-start.37 = (bf16[128,1536]{1,0:T(8,128)(2,1)S(1)}, bf16[128,1536]{1,0:T(8,128)(2,1)S(1)}, u32[]{:S(2)}, u32[]{:S(2)}) collective-permute-start(bf16[128,1536]{1,0:T(8,128)(2,1)S(1)} %get-tuple-element.39), channel_id=1, source_target_pairs={{0,68},{1,69},{2,70},{3,71},{4,0},{5,1},{6,2},{7,3},{32,35},{33,32... | collective-permute-start | bytes 1179656 | tf_op jit(solution)/shard_map/ppermute | solution.py:37
  83.6 25.8 %collective-permute-start.28 = (bf16[3072,128]{1,0:T(8,128)(2,1)S(1)}, bf16[3072,128]{1,0:T(8,128)(2,1)S(1)}, u32[]{:S(2)}, u32[]{:S(2)}) collective-permute-start(bf16[3072,128]{1,0:T(8,128)(2,1)S(1)} %get-tuple-element.35), channel_id=1, source_target_pairs={{0,16},{64,80},{40,56},{104,120},{16,0},{80,64},{56,40},{120,104},... | collective-permute-start | bytes 2359304 | tf_op jit(solution)/shard_map/ppermute | solution.py:412
  86.9 23.0 %collective-permute-start.29 = (bf16[3072,128]{1,0:T(8,128)(2,1)S(1)}, bf16[3072,128]{1,0:T(8,128)(2,1)S(1)}, u32[]{:S(2)}, u32[]{:S(2)}) collective-permute-start(bf16[3072,128]{1,0:T(8,128)(2,1)S(1)} %get-tuple-element.35), channel_id=1, source_target_pairs={{32,56},{96,120},{8,0},{72,64},{48,40},{112,104},{24,16},{88,80},{... | collective-permute-start | bytes 2359304 | tf_op jit(solution)/shard_map/ppermute | solution.py:412
  88.2 21.2 %collective-permute-start.27 = (bf16[3072,128]{1,0:T(8,128)(2,1)}, bf16[3072,128]{1,0:T(8,128)(2,1)S(1)}, u32[]{:S(2)}, u32[]{:S(2)}) collective-permute-start(bf16[3072,128]{1,0:T(8,128)(2,1)} %get-tuple-element.34.refs_0_), channel_id=1, source_target_pairs={{32,40},{96,104},{8,16},{72,80},{48,56},{112,120},{24,0},{88,64},{... | collective-permute-start | bytes 2359304 | tf_op jit(solution)/shard_map/ppermute | solution.py:412
  89.5 6.9 %collective-permute-start.16 = (bf16[512,128]{1,0:T(8,128)(2,1)S(1)}, bf16[512,128]{1,0:T(8,128)(2,1)S(1)}, u32[]{:S(2)}, u32[]{:S(2)}) collective-permute-start(bf16[512,128]{1,0:T(8,128)(2,1)S(1)} %get-tuple-element.27), channel_id=1, source_target_pairs={{0,1},{1,2},{2,3},{3,0},{4,5},{5,6},{6,7},{7,4},{32,33},{33,34},{3... | collective-permute-start | bytes 393224 | tf_op jit(solution)/shard_map/ppermute | solution.py:37
  91.5 6.6 %collective-permute-start.17 = (bf16[512,128]{1,0:T(8,128)(2,1)S(1)}, bf16[512,128]{1,0:T(8,128)(2,1)S(1)}, u32[]{:S(2)}, u32[]{:S(2)}) collective-permute-start(bf16[512,128]{1,0:T(8,128)(2,1)S(1)} %get-tuple-element.28), channel_id=1, source_target_pairs={{0,2},{1,3},{2,0},{3,1},{4,6},{5,7},{6,4},{7,5},{32,34},{33,35},{3... | collective-permute-start | bytes 393224 | tf_op jit(solution)/shard_map/ppermute | solution.py:37
  96.4 5.0 %collective-permute-start.18 = (bf16[512,128]{1,0:T(8,128)(2,1)S(1)}, bf16[512,128]{1,0:T(8,128)(2,1)S(1)}, u32[]{:S(2)}, u32[]{:S(2)}) collective-permute-start(bf16[512,128]{1,0:T(8,128)(2,1)S(1)} %get-tuple-element.29), channel_id=1, source_target_pairs={{0,3},{1,0},{2,1},{3,2},{4,7},{5,4},{6,5},{7,6},{32,35},{33,32},{3... | collective-permute-start | bytes 393224 | tf_op jit(solution)/shard_map/ppermute | solution.py:37
  98.1 5.8 %collective-permute-start.38 = (bf16[128,384]{1,0:T(8,128)(2,1)S(1)}, bf16[128,384]{1,0:T(8,128)(2,1)S(1)}, u32[]{:S(2)}, u32[]{:S(2)}) collective-permute-start(bf16[128,384]{1,0:T(8,128)(2,1)S(1)} %get-tuple-element.50), channel_id=1, source_target_pairs={{0,1},{1,2},{2,3},{3,0},{4,5},{5,6},{6,7},{7,4},{32,36},{33,37},{3... | collective-permute-start | bytes 294920 | tf_op jit(solution)/shard_map/ppermute | solution.py:37
  101.4 8.6 %collective-permute-start.39 = (bf16[128,384]{1,0:T(8,128)(2,1)S(1)}, bf16[128,384]{1,0:T(8,128)(2,1)S(1)}, u32[]{:S(2)}, u32[]{:S(2)}) collective-permute-start(bf16[128,384]{1,0:T(8,128)(2,1)S(1)} %get-tuple-element.52), channel_id=1, source_target_pairs={{0,2},{1,3},{2,0},{3,1},{4,6},{5,7},{6,4},{7,5},{32,96},{33,97},{3... | collective-permute-start | bytes 294920 | tf_op jit(solution)/shard_map/ppermute | solution.py:37
  103.9 20.4 %collective-permute-start.30 = (bf16[3072,128]{1,0:T(8,128)(2,1)}, bf16[3072,128]{1,0:T(8,128)(2,1)S(1)}, u32[]{:S(2)}, u32[]{:S(2)}) collective-permute-start(bf16[3072,128]{1,0:T(8,128)(2,1)} %get-tuple-element.34.refs_0_), channel_id=1, source_target_pairs={{0,32},{1,33},{2,34},{3,35},{4,36},{5,37},{6,38},{7,39},{32,0},{33... | collective-permute-start | bytes 2359304 | tf_op jit(solution)/shard_map/ppermute | solution.py:37
  109.4 14.9 %collective-permute-start.31 = (bf16[3072,128]{1,0:T(8,128)(2,1)S(1)}, bf16[3072,128]{1,0:T(8,128)(2,1)}, u32[]{:S(2)}, u32[]{:S(2)}) collective-permute-start(bf16[3072,128]{1,0:T(8,128)(2,1)S(1)} %collective-permute-done.27.refs_1_), channel_id=1, source_target_pairs={{0,32},{1,33},{2,34},{3,35},{4,36},{5,37},{6,38},{7,39},{32,0},{33... | collective-permute-start | bytes 2359304 | tf_op jit(solution)/shard_map/ppermute | solution.py:37
  109.4 14.9 %collective-permute-start.32 = (bf16[3072,128]{1,0:T(8,128)(2,1)S(1)}, bf16[3072,128]{1,0:T(8,128)(2,1)}, u32[]{:S(2)}, u32[]{:S(2)}) collective-permute-start(bf16[3072,128]{1,0:T(8,128)(2,1)S(1)} %collective-permute-done.28.refs_2_), channel_id=1, source_target_pairs={{0,32},{1,33},{2,34},{3,35},{4,36},{5,37},{6,38},{7,39},{32,0},{33... | collective-permute-start | bytes 2359304 | tf_op jit(solution)/shard_map/ppermute | solution.py:37
  109.9 14.4 %collective-permute-start.33 = (bf16[3072,128]{1,0:T(8,128)(2,1)S(1)}, bf16[3072,128]{1,0:T(8,128)(2,1)}, u32[]{:S(2)}, u32[]{:S(2)}) collective-permute-start(bf16[3072,128]{1,0:T(8,128)(2,1)S(1)} %collective-permute-done.29.refs_3_), channel_id=1, source_target_pairs={{0,32},{1,33},{2,34},{3,35},{4,36},{5,37},{6,38},{7,39},{32,0},{33... | collective-permute-start | bytes 2359304 | tf_op jit(solution)/shard_map/ppermute | solution.py:37
  110.0 5.5 %collective-permute-start.40 = (bf16[128,384]{1,0:T(8,128)(2,1)S(1)}, bf16[128,384]{1,0:T(8,128)(2,1)S(1)}, u32[]{:S(2)}, u32[]{:S(2)}) collective-permute-start(bf16[128,384]{1,0:T(8,128)(2,1)S(1)} %get-tuple-element.51), channel_id=1, source_target_pairs={{0,3},{1,0},{2,1},{3,2},{4,7},{5,4},{6,5},{7,6},{32,100},{33,101},... | collective-permute-start | bytes 294920 | tf_op jit(solution)/shard_map/ppermute | solution.py:37
  115.4 4.6 %collective-permute-start.19 = (bf16[256,128]{1,0:T(8,128)(2,1)}, bf16[256,128]{1,0:T(8,128)(2,1)}, u32[]{:S(2)}, u32[]{:S(2)}) collective-permute-start(bf16[256,128]{1,0:T(8,128)(2,1)} %slice.65), channel_id=1, source_target_pairs={{0,4},{1,5},{2,6},{3,7},{4,0},{5,1},{6,2},{7,3},{32,36},{33,37},{3... | collective-permute-start | bytes 196616 | tf_op jit(solution)/shard_map/ppermute | solution.py:37
  120.0 4.3 %collective-permute-start.26 = (bf16[256,128]{1,0:T(8,128)(2,1)S(1)}, bf16[256,128]{1,0:T(8,128)(2,1)S(1)}, u32[]{:S(2)}, u32[]{:S(2)}) collective-permute-start(bf16[256,128]{1,0:T(8,128)(2,1)S(1)} %fusion.4.g0.va), channel_id=1, source_target_pairs={{0,24},{8,0},{16,8},{24,16},{1,25},{9,1},{17,9},{25,17},{2,26},{10... | collective-permute-start | bytes 196616 | tf_op jit(solution)/shard_map/ppermute | solution.py:433
where the time goes:
time: 129 us; the launch traced here: 128 us
  starting transfers between devices  55 us (43%)
  Pallas kernels  31.6 us (24%)
  waiting for transfers between devices  24.5 us (19%)
  local copies, waits for them, and re-layouts  10.2 us (8%)
  other arithmetic  5.91 us (5%)
    ppermute x35, starting transfers between devices, moved(): return lax.ppermute(value, ('dp', 'ctx'), pairs)  44.4 us
    pallas_call x6, Pallas kernels, call(): pl.pallas_call(kernel, out_shape=tuple((jax.ShapeDtypeStruct(s, d) for s,...  26.5 us
    ppermute x35, waiting for transfers between devices, moved(): return lax.ppermute(value, ('dp', 'ctx'), pairs)  16.6 us
    unnamed x28, local copies, waits for them, and re-layouts  7.74 us
    ppermute x3, starting transfers between devices, along_y(): return lax.ppermute(value, ('dp', 'head'), pairs)  5.88 us
    ppermute x3, waiting for transfers between devices, along_y(): return lax.ppermute(value, ('dp', 'head'), pairs)  5.44 us
    pallas_call x1, Pallas kernels, local(): pl.pallas_call(pick_kernel, grid_spec=pltpu.PrefetchScalarGridSpec(num_sc...  5.08 us
    ppermute x3, starting transfers between devices, local(): lax.ppermute(value_grads, 'head', [(s, (s + i) % 4) for s in range(4)])  4.71 us
  transfers between devices with their start and end apart: 41, of which 13 were waited for; matrix products, arithmetic and copies ran while one was open for 9% of the time, Pallas kernels for 18%

commit v1 on v0

--- a/solution.py
+++ b/solution.py
@@ -1,3 +1,5 @@
+import functools
+
 import jax
 import jax.numpy as jnp
 from jax import lax
@@ -13,6 +15,8 @@
 SPAN = WINDOW * BLOCK
 SLAB = 384
 QUARTER = 3072
+HALF = QUARTER // 2
+COST_UNIT = 3 << 20
 MASKED = -1e30
 LOG2E = 1.4426950408889634
 SCALING = float(HEAD_SIZE) ** (-0.5)
@@ -45,16 +49,20 @@
     return moved(value, lambda x, z, c: (x ^ 1, z, c))
 
 
-def z_step(value, by):
-    return moved(value, lambda x, z, c: (x, z + by, c))
-
-
-def first_step(value, by):
-    return moved(value, lambda x, z, c: (x, z + by, c) if c == 0 else (x + by, z, c))
-
-
-def second_step(value, by):
-    return moved(value, lambda x, z, c: (x + by, z, c) if c == 0 else (x, z + by, c))
+def z_with(value, bits):
+    return moved(value, lambda x, z, c: (x, z ^ bits, c))
+
+
+def first_with(value, bits):
+    return moved(value, lambda x, z, c: (x, z ^ bits, c) if c == 0 else (x ^ bits, z, c))
+
+
+def second_with(value, bits):
+    return moved(value, lambda x, z, c: (x ^ bits, z, c) if c == 0 else (x, z ^ bits, c))
+
+
+def y_with(value, bits):
+    return lax.ppermute(value, "head", [(y, y ^ bits) for y in range(4)])
 
 
 def nt(a, b):
@@ -79,8 +87,13 @@
             out_ref[at : at + 1, :] = jnp.sum(product.T, axis=0, keepdims=True)
 
 
-def pick_kernel(table_ref, in_ref, out_ref):
-    out_ref[...] = in_ref[...]
+def join_kernel(*refs):
+    join(refs[:-1], refs[-1])
+
+
+def fold_kernel(scale, own, one, two, three, out):
+    total = own[...] + one[...].astype(f32) + two[...].astype(f32) + three[...].astype(f32)
+    out[...] = (total * scale).T
 
 
 def fill_bias(place, doc_ref, bias_ref):
@@ -211,73 +224,59 @@
         out[...] = (sum_ref[512 * (i + 1) : 512 * (i + 2), :] * SCALING).astype(bf16)
 
 
-def own_half_copies(table_ref, hidden, half_ref, sems):
-    return [
-        pltpu.make_async_copy(
-            hidden.at[:, pl.ds(pl.multiple_of(table_ref[16 + p] * QUARTER, BLOCK), QUARTER)],
-            half_ref.at[:, p * QUARTER : (p + 1) * QUARTER],
-            sems.at[p],
+def project_kernel(
+    table_ref, hidden, w0, w1, w2, w3, s0, s1, s2, s3, out, own_rows, r1, r2, r3, all_ref
+):
+    for k, w in enumerate((w0, w1, w2, w3, s0, s1, s2, s3)):
+        for i in range(4):
+            at = pl.multiple_of(table_ref[k * 4 + i] * SLAB, BLOCK)
+            all_ref[pl.ds(at, SLAB), :] = w[i * SLAB : (i + 1) * SLAB, :]
+    out[...] = nn(hidden[...], all_ref[...]).astype(bf16)
+    own_rows[...] = all_ref[pl.ds(pl.multiple_of(table_ref[32] * QUARTER, BLOCK), QUARTER), :]
+    for d, r in enumerate((r1, r2, r3)):
+        r[...] = all_ref[pl.ds(pl.multiple_of(table_ref[33 + d] * HALF, BLOCK), HALF), :]
+
+
+def weight_kernel(table_ref, hidden, grads, r1, r2, r3, own, other, m1, m2, m3):
+    turned = grads[...].T
+    for k in range(16):
+        for out, at in ((other, 16 + k), (own, k)):
+            cols = pl.ds(pl.multiple_of(table_ref[at] * SLAB, BLOCK), SLAB)
+            block = nn(turned, hidden[:, cols])
+            out[k * HEAD_SIZE : (k + 1) * HEAD_SIZE, :] = block.astype(out.dtype)
+    for r, m in ((r1, m1), (r2, m2), (r3, m3)):
+        m[:HALF, :] = r[...]
+        m[HALF:, :] = grads[...]
+
+
+def input_kernel(table_ref, grads, own, a1, a2, a3, b1, b2, b3, out, rows_ref, grads_ref, sems):
+    mine = pl.multiple_of(table_ref[36] * HALF, BLOCK)
+    other = pl.multiple_of((1 - table_ref[36]) * HALF, BLOCK)
+    copies = [pltpu.make_async_copy(own, rows_ref.at[:, 0:BLOCK], sems.at[0])]
+    for d, (a, b) in enumerate(((a1, b1), (a2, b2), (a3, b3))):
+        cols = slice((d + 1) * BLOCK, (d + 2) * BLOCK)
+        pieces = (
+            (a.at[0:HALF, :], rows_ref.at[pl.ds(mine, HALF), cols]),
+            (b.at[0:HALF, :], rows_ref.at[pl.ds(other, HALF), cols]),
+            (a.at[HALF : HALF + 256, :], grads_ref.at[:, cols]),
         )
-        for p in range(2)
-    ]
-
-
-def project_kernel(table_ref, hidden, hb, w0, w1, w2, w3, oa, ob, lower, upper, ha_ref, all_ref, sems):
-    copies = own_half_copies(table_ref, hidden, ha_ref, sems)
+        for i, (source, target) in enumerate(pieces):
+            copies.append(pltpu.make_async_copy(source, target, sems.at[3 * d + 1 + i]))
     for copy in copies:
         copy.start()
-    for r, w in enumerate((w0, w1, w2, w3)):
-        for i in range(4):
-            at = pl.multiple_of(table_ref[r * 4 + i] * SLAB, BLOCK)
-            all_ref[pl.ds(at, SLAB), :] = w[i * SLAB : (i + 1) * SLAB, :]
-    lower[...] = all_ref[:QUARTER, :]
-    upper[...] = all_ref[QUARTER:, :]
-    ob[...] = nn(hb[...], all_ref[...])
+    grads_ref[:, 0:BLOCK] = grads[...]
     for copy in copies:
         copy.wait()
-    oa[...] = nn(ha_ref[...], all_ref[...])
-
-
-def weight_kernel(table_ref, hidden, hb, va, vb, o0, o1, o2, o3, ha_ref, sems):
-    copies = own_half_copies(table_ref, hidden, ha_ref, sems)
-    for copy in copies:
-        copy.start()
-    one, two = va[...].T, vb[...].T
-    for copy in copies:
-        copy.wait()
-    for r, out in enumerate((o0, o1, o2, o3)):
-        for i in range(4):
-            cols = pl.ds(pl.multiple_of(table_ref[r * 4 + i] * SLAB, BLOCK), SLAB)
-            block = nn(one, ha_ref[:, cols]) + nn(two, hb[:, cols])
-            out[:, i * SLAB : (i + 1) * SLAB] = block.astype(out.dtype)
-
-
-def input_kernel(table_ref, g0, g1, g2, g3, *refs):
-    mine, other, out, rows_ref, sems = refs[:4], refs[4:8], refs[8], refs[9], refs[10]
-    for choice, pieces in ((1, mine), (0, other)):
-
-        @pl.when(table_ref[18] == choice)
-        def _(pieces=pieces):
-            copies = [
-                pltpu.make_async_copy(p, rows_ref.at[:, d * BLOCK : (d + 1) * BLOCK], sems.at[d])
-                for d, p in enumerate(pieces)
-            ]
-            for copy in copies:
-                copy.start()
-            for copy in copies:
-                copy.wait()
-
-    grads = jnp.concatenate([g0[...], g1[...], g2[...], g3[...]], axis=1)
     for part in range(4):
         cols = slice(part * 768, (part + 1) * 768)
-        out[:, cols] = nt(grads, rows_ref[cols, :]).astype(bf16)
+        out[:, cols] = nt(grads_ref[...], rows_ref[cols, :]).astype(bf16)
 
 
 SMEM = pl.BlockSpec(memory_space=pltpu.SMEM)
 VMEM = pl.BlockSpec(memory_space=pltpu.VMEM)
 
 
-def call(kernel, outs, ins, scratch=(), flops=0, moved_bytes=0, exps=0, smem=1, anys=(), limit=40):
+def call(kernel, outs, ins, scratch=(), cost=1, smem=1, anys=(), limit=8):
     any_spec = pl.BlockSpec(memory_space=pl.ANY)
     specs = [SMEM] * smem + [any_spec if i in anys else VMEM for i in range(smem, len(ins))]
     return pl.pallas_call(
@@ -287,24 +286,22 @@
         out_specs=tuple(VMEM for _ in outs),
         scratch_shapes=[s if not isinstance(s, tuple) else pltpu.VMEM(*s) for s in scratch],
         compiler_params=pltpu.CompilerParams(vmem_limit_bytes=limit * 1024 * 1024),
-        cost_estimate=pl.CostEstimate(flops=flops, bytes_accessed=moved_bytes, transcendentals=exps),
+        cost_estimate=pl.CostEstimate(
+            flops=0, bytes_accessed=int(cost * COST_UNIT), transcendentals=0
+        ),
     )(*ins)
 
 
-def gathered(value):
-    both = jnp.concatenate([value, x_swap(value)], axis=0)
-    return (both, z_step(both, -1), z_step(both, -2), z_step(both, -3))
-
-
-def summed(own, one, two, three):
-    rows = own.shape[0] // 2
-    total = (
-        own
-        + z_step(one, 1).astype(f32)
-        + z_step(two, 2).astype(f32)
-        + z_step(three, 3).astype(f32)
-    )
-    return total[:rows] + x_swap(total[rows:].astype(bf16)).astype(f32)
+def joined(parts):
+    rows = sum(part.shape[0] for part in parts)
+    (whole,) = call(join_kernel, [((rows, HEAD_SIZE), bf16)], parts, smem=0)
+    return whole
+
+
+def summed_along_z(own, *parts):
+    for r, part in enumerate(parts):
+        own = own + z_with(part, r + 1).astype(f32)
+    return own
 
 
 def local(
@@ -326,54 +323,29 @@
     grad_scale = float(rows * 32) ** (-0.5)
     query, grad, saved = queries[0], output_gradient[0], attended[0]
     docs = doc_ids[0].reshape(16, BLOCK)
-    placing = block_place[0]
-
-    stored = jnp.arange(16, dtype=jnp.int32)
-    owner = stored // 2
-    lies = ((owner % 4 - z) % 4) * 4 + ((owner // 4 + x_lo) % 2) * 2 + stored % 2
-    at_place = jnp.sum(jnp.where(placing[None, :] == stored[:, None], lies[None, :], 0), axis=1)
-    mine = jnp.sum(jnp.where(stored[None, :] == (2 * ctx + jnp.arange(2))[:, None], placing[None, :], 0), axis=1)
-    table = jnp.concatenate([at_place, mine])
-
-    head = lax.axis_index("head")
-
-    def quarters_of(core):
-        lead = ((head + (head % 2 != core)) % 4) // 2
-        return jnp.stack([2 * lead + core, 2 * (1 - lead) + core]), lead
-
-    own_quarters, lead = quarters_of(core)
-    other_quarters, _ = quarters_of(1 - core)
-
-    outer, inner = jnp.arange(16, dtype=jnp.int32) // 4, jnp.arange(16, dtype=jnp.int32) % 4
-    slab_x = (x + jnp.where(core == 0, outer, inner)) % 4
-    slab_z = (z + jnp.where(core == 0, inner, outer)) % 4
-    slabs = ((slab_x // 2 + lead) % 2) * 8 + (slab_x % 2) * 4 + slab_z
-    has_rows = (head % 2 == core).astype(jnp.int32)
-    slabs = jnp.concatenate([slabs, own_quarters, has_rows[None]]).astype(jnp.int32)
-
-    keys = gathered(rotary_key_rows[0])
-
-    first = jnp.concatenate(
-        [value_projection] + [first_step(value_projection, -i) for i in (1, 2, 3)], axis=0
-    )
-    weights = (first,) + tuple(second_step(first, -i) for i in (1, 2, 3))
+
+    def places_of_keys(placing):
+        stored = jnp.arange(16, dtype=jnp.int32)
+        owner = stored // 2
+        lies = ((owner % 4) ^ z) * 4 + ((owner // 4) ^ x_lo) * 2 + stored % 2
+        by_place = jnp.sum(jnp.where(placing[None, :] == stored[:, None], lies[None, :], 0), axis=1)
+        mine = jnp.sum(
+            jnp.where(stored[None, :] == (2 * ctx + jnp.arange(2))[:, None], placing[None, :], 0), axis=1
+        )
+        return jnp.concatenate([by_place, mine])
+
+    def places_of_slabs(head):
+        outer, inner = jnp.arange(16, dtype=jnp.int32) // 4, jnp.arange(16, dtype=jnp.int32) % 4
+
+        def slabs_of(core):
+            at_x = x ^ jnp.where(core == 0, outer, inner)
+            at_z = z ^ jnp.where(core == 0, inner, outer)
+            return (2 * (at_x // 2) + core) * 8 + (at_x % 2) * 4 + at_z
+
+        asked = jnp.stack([head] + [2 * (head ^ d) + core for d in (1, 2, 3)] + [core])
+        return jnp.concatenate([slabs_of(core), slabs_of(1 - core), asked]).astype(jnp.int32)
 
     hidden = hidden_in[0]
-    picked = pl.pallas_call(
-        pick_kernel,
-        grid_spec=pltpu.PrefetchScalarGridSpec(
-            num_scalar_prefetch=1,
-            grid=(4,),
-            in_specs=[pl.BlockSpec((rows, QUARTER // 2), lambda i, t: (0, t[i // 2] * 2 + i % 2))],
-            out_specs=pl.BlockSpec((rows, QUARTER // 2), lambda i, t: (0, i)),
-        ),
-        out_shape=jax.ShapeDtypeStruct((rows, 2 * QUARTER), bf16),
-        cost_estimate=pl.CostEstimate(flops=0, bytes_accessed=6 << 20, transcendentals=0),
-    )(other_quarters.astype(jnp.int32), hidden)
-    hb = core_swap(picked)
-
-    (terms,) = call(row_terms_kernel, [((24, 128), f32)], [grad, saved], smem=0, moved_bytes=1 << 21)
-
     window = ((SPAN, HEAD_SIZE), bf16)
     whole = ((2048, HEAD_SIZE), bf16)
     bias = ((SPAN, BLOCK), f32)
@@ -381,73 +353,119 @@
     stack = ((1536, HEAD_SIZE), bf16)
     sums = [((SPAN, HEAD_SIZE), f32), ((2048, HEAD_SIZE), f32)]
     parts_out = [((512, HEAD_SIZE), f32)] + [((512, HEAD_SIZE), bf16)] * 3
-    dots = 2 * 12 * 256 * SPAN * HEAD_SIZE
+    together = lax.optimization_barrier
+
+    own_keys = rotary_key_rows[0]
+    near, first, placing, head = together(
+        (
+            [own_keys, x_swap(own_keys)],
+            [value_projection] + [first_with(value_projection, r) for r in (1, 2, 3)],
+            block_place[0],
+            lax.axis_index("head"),
+        )
+    )
+    near, first = joined(near), joined(first)
+
+    keys, w1, w3, first, table, slabs = together(
+        (
+            [near] + [z_with(near, r) for r in (1, 2, 3)],
+            second_with(first, 1),
+            second_with(first, 3),
+            first,
+            places_of_keys(placing),
+            places_of_slabs(head),
+        )
+    )
+
+    w2 = second_with(first, 2)
+    s0, s1, s3 = core_swap(first), core_swap(w1), core_swap(w3)
     totals, *value_parts = call(
         value_side_kernel,
         [((24, 128), f32)] + parts_out,
         [table, docs, query, grad, *keys],
         scratch=[whole, window, bias, ((SPAN, 256), f32), square, stack] + sums,
-        flops=4 * dots, moved_bytes=4 << 20, exps=12 * 256 * SPAN,
-    )
-    value_grads = summed(*value_parts).astype(bf16)
-    sibling_grads = core_swap(value_grads)
-
-    half = ((rows, 2 * QUARTER), bf16)
-    sems = pltpu.SemaphoreType.DMA((4,))
-    part_a, part_b, lower, upper = call(
+        cost=7, limit=24,
+    )
+    w2, s0, s1, s3, totals, value_parts, slabs = together((w2, s0, s1, s3, totals, value_parts, slabs))
+
+    s2 = core_swap(w2)
+    own_values, own_rows, *halves = call(
         project_kernel,
-        [((rows, HEAD_SIZE), f32)] * 2 + [((QUARTER, HEAD_SIZE), bf16)] * 2,
-        [slabs, hidden, hb, *weights],
-        scratch=[half, ((2 * QUARTER, HEAD_SIZE), bf16), sems], anys=(1,),
-        flops=2 * 512 * 6144 * 128, moved_bytes=10 << 20,
-    )
-    values = gathered((part_a + core_swap(part_b)).astype(bf16))
-
-    def along_y(value, by):
-        pairs = []
-        for s in range(4):
-            for dp_at in range(4):
-                if (s + by) % 2 == dp_at % 2:
-                    pairs.append((dp_at * 4 + s, dp_at * 4 + (s + by) % 4))
-        return lax.ppermute(value, ("dp", "head"), pairs)
-
-    own_rows = [lower, along_y(lower, 1), along_y(upper, 2), along_y(upper, 3)]
-    swapped_rows = [core_swap(r) for r in own_rows]
-
-    w_parts = call(
+        [((rows, HEAD_SIZE), bf16), ((QUARTER, HEAD_SIZE), bf16)] + [((HALF, HEAD_SIZE), bf16)] * 3,
+        [slabs, hidden, first, w1, w2, w3, s0, s1, s2, s3],
+        scratch=[((4 * QUARTER, HEAD_SIZE), bf16)],
+        cost=4, limit=24,
+    )
+    arrived = [z_with(part, r + 1) for r, part in enumerate(value_parts[1:])]
+    own_values, arrived, value_sum, saved = together((own_values, arrived, value_parts[0], saved))
+    for part in arrived:
+        value_sum = value_sum + part.astype(f32)
+
+    (terms,) = call(row_terms_kernel, [((24, 128), f32)], [grad, saved], smem=0)
+    value_rest = x_swap(value_sum[rows:].astype(bf16))
+    near_values, value_rest, value_sum, terms = together(
+        ([own_values, x_swap(own_values)], value_rest, value_sum, terms)
+    )
+    near_values = joined(near_values)
+    value_grads = (value_sum[:rows] + value_rest.astype(f32)).astype(bf16)
+
+    message = ((HALF + rows, HEAD_SIZE), bf16)
+    w_own, w_other, *messages = call(
         weight_kernel,
-        [((HEAD_SIZE, 1536), f32)] + [((HEAD_SIZE, 1536), bf16)] * 3,
-        [slabs, hidden, hb, value_grads, sibling_grads],
-        scratch=[half, sems], anys=(1,),
-        flops=2 * 512 * 6144 * 128, moved_bytes=8 << 20,
-    )
+        [((2048, SLAB), f32), ((2048, SLAB), bf16)] + [message] * 3,
+        [slabs, hidden, value_grads, *halves],
+        cost=4, limit=24,
+    )
+    w_other = core_swap(w_other)
+    w_parts = [
+        w_own[512 * r : 512 * (r + 1)] + w_other[512 * r : 512 * (r + 1)].astype(f32) for r in range(4)
+    ]
+    w_parts = [w_parts[0]] + [part.astype(bf16) for part in w_parts[1:]]
+    values, w_parts, messages = together(
+        ([near_values] + [z_with(near_values, r) for r in (1, 2, 3)], w_parts, messages)
+    )
+
+    messages[0], messages[2] = y_with(messages[0], 1), y_with(messages[2], 3)
     w_sum = w_parts[0]
-    for i in (1, 2, 3):
-        w_sum = w_sum + second_step(w_parts[i], i).astype(f32)
-    w_total = w_sum[:, :SLAB]
-    for i in (1, 2, 3):
-        w_total = w_total + first_step(w_sum[:, i * SLAB : (i + 1) * SLAB].astype(bf16), i).astype(f32)
-    weight_grad = (w_total * grad_scale).T
-
-    every = [value_grads] + [
-        lax.ppermute(value_grads, "head", [(s, (s + i) % 4) for s in range(4)]) for i in (1, 2, 3)
-    ]
-    (input_grad,) = call(
-        input_kernel,
-        [((rows, QUARTER), bf16)],
-        [slabs, *every, *own_rows, *swapped_rows],
-        scratch=[((QUARTER, 512), bf16), sems], anys=tuple(range(5, 13)),
-        flops=2 * 256 * 512 * 3072, moved_bytes=5 << 20,
-    )
-
+    for r in (1, 2, 3):
+        w_sum = w_sum + second_with(w_parts[r], r).astype(f32)
     dquery, *key_parts = call(
         key_side_kernel,
         [((rows, 1536), bf16)] + parts_out,
         [table, docs, query, grad, totals, terms, *keys, *values],
         scratch=[whole, whole, window, window, bias, square, stack] + sums,
-        flops=8 * dots, moved_bytes=6 << 20, exps=12 * 256 * SPAN,
-    )
-    key_grads = summed(*key_parts).astype(bf16)
+        cost=9, limit=28,
+    )
+    key_parts, w_sum, messages = together((key_parts, w_sum, messages))
+
+    messages[1] = y_with(messages[1], 2)
+    swapped = [core_swap(messages[0]), None, core_swap(messages[2])]
+    got = [
+        first_with(w_sum[i * HEAD_SIZE : (i + 1) * HEAD_SIZE].astype(bf16), i) for i in (1, 2, 3)
+    ]
+    arrived = [z_with(part, r + 1) for r, part in enumerate(key_parts[1:])]
+    arrived, key_sum, messages, swapped[0], swapped[2] = together(
+        (arrived, key_parts[0], messages, swapped[0], swapped[2])
+    )
+    for part in arrived:
+        key_sum = key_sum + part.astype(f32)
+
+    swapped[1] = core_swap(messages[1])
+    key_grads = (key_sum[:rows] + x_swap(key_sum[rows:].astype(bf16)).astype(f32)).astype(bf16)
+    (input_grad,) = call(
+        input_kernel,
+        [((rows, QUARTER), bf16)],
+        [slabs, value_grads, own_rows, *messages, *swapped],
+        scratch=[((QUARTER, 512), bf16), ((rows, 512), bf16), pltpu.SemaphoreType.DMA((10,))],
+        anys=tuple(range(2, 9)),
+        cost=4, limit=16,
+    )
+    (weight_grad,) = call(
+        functools.partial(fold_kernel, grad_scale),
+        [((SLAB, HEAD_SIZE), f32)],
+        [w_sum[:HEAD_SIZE], *got],
+        smem=0,
+    )
     return dquery[None], key_grads[None], input_grad[None], weight_grad
 
 

time: 129 us -> 116 us (0.90)
  waiting for transfers between devices: 24.5 us -> 34.7 us
  starting transfers between devices: 55 us -> 46.2 us
  Pallas kernels: 31.6 us -> 24.3 us
  local copies, waits for them, and re-layouts: 10.2 us -> 6.52 us
  other arithmetic: 5.91 us -> 3.07 us
    ppermute x35 -> x36, waiting for transfers between devices: 16.6 us -> 33.2 us  [moved(): return lax.ppermute(value, ('dp', 'ctx'), pairs)]
    ppermute x6 -> x3, waiting for transfers between devices: 7.92 us -> 1.46 us  [y_with(): return lax.ppermute(value, 'head', [(y, y ^ bits) for y in range(4)])]
    ppermute x6 -> x3, starting transfers between devices: 10.6 us -> 5.45 us  [y_with(): return lax.ppermute(value, 'head', [(y, y ^ bits) for y in range(4)])]
    pallas_call x1 -> x0, Pallas kernels: 5.08 us -> none  [local(): pl.pallas_call(pick_kernel, grid_spec=pltpu.PrefetchScalarGridSpec(num_sc...]
    ppermute x35 -> x36, starting transfers between devices: 44.4 us -> 40.8 us  [moved(): return lax.ppermute(value, ('dp', 'ctx'), pairs)]
    pallas_call x6 -> x10, Pallas kernels: 26.5 us -> 24.3 us  [call(): pl.pallas_call(kernel, out_shape=tuple((jax.ShapeDtypeStruct(s, d) for s,...]
    concatenate x4 -> x1, other arithmetic: 1.7 us -> 0.07 us  [places_of_keys(): return jnp.concatenate([by_place, mine])]
    slice x3 -> x4, local copies, waits for them, and re-layouts: 1.58 us -> 0.06 us  [the longest x1 0.03 us: local(): w_sum[i * HEAD_SIZE:(i + 1) * HEAD_SIZE].astype(bf16)]
  transfers between devices with their start and end apart: 41 -> 39, of which waited for: 13 -> 16; matrix products, arithmetic and copies ran while one was open for 9% -> 3% of each run, Pallas kernels for 18% -> 16%
where the time goes in v1:
time: 116 us
  starting transfers between devices  46.2 us (40%)
  waiting for transfers between devices  34.7 us (30%)
  Pallas kernels  24.3 us (21%)
  local copies, waits for them, and re-layouts  6.52 us (6%)
  other arithmetic  3.07 us (3%)
    ppermute x36, starting transfers between devices, moved(): return lax.ppermute(value, ('dp', 'ctx'), pairs)  40.8 us
    ppermute x36, waiting for transfers between devices, moved(): return lax.ppermute(value, ('dp', 'ctx'), pairs)  33.2 us
    pallas_call x10, Pallas kernels, call(): pl.pallas_call(kernel, out_shape=tuple((jax.ShapeDtypeStruct(s, d) for s,...  24.3 us
    unnamed x20, local copies, waits for them, and re-layouts  6.37 us
    ppermute x3, starting transfers between devices, y_with(): return lax.ppermute(value, 'head', [(y, y ^ bits) for y in range(4)])  5.45 us
  transfers between devices with their start and end apart: 39, of which 16 were waited for; matrix products, arithmetic and copies ran while one was open for 3% of the time, Pallas kernels for 16%

profile of v1, /device:TPU:0, one launch (start us, length us, event | category | flops | bytes accessed | tf_op | source)
XLA Modules:
  0.0 115.9 jit_solution(1066099040156082154)
XLA Ops:
  0.6 2.1 %collective-permute-start.1 = (bf16[384,128]{1,0:T(8,128)(2,1)}, bf16[384,128]{1,0:T(8,128)(2,1)S(1)}, u32[]{:S(2)}, u32[]{:S(2)}) collective-permute-start(bf16[384,128]{1,0:T(8,128)(2,1)} %refs_0_), channel_id=1, source_target_pairs={{0,1},{1,0},{2,3},{3,2},{4,5},{5,4},{6,7},{7,6},{32,36},{33,37},{3... | collective-permute-start | bytes 294920 | tf_op jit(solution)/shard_map/ppermute | solution.py:41
  2.7 3.6 %collective-permute-start.2 = (bf16[384,128]{1,0:T(8,128)(2,1)}, bf16[384,128]{1,0:T(8,128)(2,1)S(1)}, u32[]{:S(2)}, u32[]{:S(2)}) collective-permute-start(bf16[384,128]{1,0:T(8,128)(2,1)} %refs_0_), channel_id=1, source_target_pairs={{0,2},{1,3},{2,0},{3,1},{4,6},{5,7},{6,4},{7,5},{32,96},{33,97},{3... | collective-permute-start | bytes 294920 | tf_op jit(solution)/shard_map/ppermute | solution.py:41
  6.3 1.5 %collective-permute-start = (bf16[256,128]{1,0:T(8,128)(2,1)}, bf16[256,128]{1,0:T(8,128)(2,1)S(1)}, u32[]{:S(2)}, u32[]{:S(2)}) collective-permute-start(bf16[256,128]{1,0:T(8,128)(2,1)} %bitcast.24), channel_id=1, source_target_pairs={{0,4},{1,5},{2,6},{3,7},{4,0},{5,1},{6,2},{7,3},{32,36},{33,37},{3... | collective-permute-start | bytes 196616 | tf_op jit(solution)/shard_map/ppermute | solution.py:41
  7.8 2.9 %collective-permute-done.refs_1_ = bf16[256,128]{1,0:T(8,128)(2,1)S(1)} collective-permute-done((bf16[256,128]{1,0:T(8,128)(2,1)}, bf16[256,128]{1,0:T(8,128)(2,1)S(1)}, u32[]{:S(2)}, u32[]{:S(2)}) %collective-permute-start) | collective-permute-done | bytes 65568 | tf_op jit(solution)/shard_map/ppermute | solution.py:41
  10.8 1.6 %collective-permute-done.3.refs_3_ = bf16[384,128]{1,0:T(8,128)(2,1)S(1)} collective-permute-done((bf16[384,128]{1,0:T(8,128)(2,1)}, bf16[384,128]{1,0:T(8,128)(2,1)S(1)}, u32[]{:S(2)}, u32[]{:S(2)}) %collective-permute-start.3) | collective-permute-done | bytes 98336 | tf_op jit(solution)/shard_map/ppermute | solution.py:41
  12.3 0.9 copy-done.6
  13.3 1.6 %collective-permute-start.7 = (bf16[1536,128]{1,0:T(8,128)(2,1)S(1)}, bf16[1536,128]{1,0:T(8,128)(2,1)S(1)}, u32[]{:S(2)}, u32[]{:S(2)}) collective-permute-start(bf16[1536,128]{1,0:T(8,128)(2,1)S(1)} %shard_map.112.w0), channel_id=1, source_target_pairs={{0,4},{1,5},{2,6},{3,7},{4,0},{5,1},{6,2},{7,3},{32,33},{33,32},{3... | collective-permute-start | bytes 1179656 | tf_op jit(solution)/shard_map/ppermute | solution.py:41
  14.8 2.1 %collective-permute-start.8 = (bf16[1536,128]{1,0:T(8,128)(2,1)S(1)}, bf16[1536,128]{1,0:T(8,128)(2,1)S(1)}, u32[]{:S(2)}, u32[]{:S(2)}) collective-permute-start(bf16[1536,128]{1,0:T(8,128)(2,1)S(1)} %shard_map.112.w0), channel_id=1, source_target_pairs={{0,68},{1,69},{2,70},{3,71},{4,64},{5,65},{6,66},{7,67},{32,35},{3... | collective-permute-start | bytes 1179656 | tf_op jit(solution)/shard_map/ppermute | solution.py:41
  16.9 0.8 copy-done.7
  17.8 0.1 collective-permute-start.4
  17.9 3.1 %collective-permute-start.5 = (bf16[512,128]{1,0:T(8,128)(2,1)S(1)}, bf16[512,128]{1,0:T(8,128)(2,1)S(1)}, u32[]{:S(2)}, u32[]{:S(2)}) collective-permute-start(bf16[512,128]{1,0:T(8,128)(2,1)S(1)} %shard_map.111.k0), channel_id=1, source_target_pairs={{0,2},{1,3},{2,0},{3,1},{4,6},{5,7},{6,4},{7,5},{32,34},{33,35},{3... | collective-permute-start | bytes 393224 | tf_op jit(solution)/shard_map/ppermute | solution.py:41
  21.0 1.5 %collective-permute-start.6 = (bf16[512,128]{1,0:T(8,128)(2,1)S(1)}, bf16[512,128]{1,0:T(8,128)(2,1)S(1)}, u32[]{:S(2)}, u32[]{:S(2)}) collective-permute-start(bf16[512,128]{1,0:T(8,128)(2,1)S(1)} %shard_map.111.k0), channel_id=1, source_target_pairs={{0,3},{1,2},{2,1},{3,0},{4,7},{5,6},{6,5},{7,4},{32,35},{33,34},{3... | collective-permute-start | bytes 393224 | tf_op jit(solution)/shard_map/ppermute | solution.py:41
  22.6 0.8 fusion.2
  23.4 0.8 select_reduce_fusion
  24.3 1.8 %collective-permute-done.5.k2 = bf16[512,128]{1,0:T(8,128)(2,1)S(1)} collective-permute-done((bf16[512,128]{1,0:T(8,128)(2,1)S(1)}, bf16[512,128]{1,0:T(8,128)(2,1)S(1)}, u32[]{:S(2)}, u32[]{:S(2)}) %collective-permute-start.5) | collective-permute-done | bytes 131104 | tf_op jit(solution)/shard_map/ppermute | solution.py:41
  26.1 1.4 %collective-permute-done.6.k3 = bf16[512,128]{1,0:T(8,128)(2,1)S(1)} collective-permute-done((bf16[512,128]{1,0:T(8,128)(2,1)S(1)}, bf16[512,128]{1,0:T(8,128)(2,1)S(1)}, u32[]{:S(2)}, u32[]{:S(2)}) %collective-permute-start.6) | collective-permute-done | bytes 131104 | tf_op jit(solution)/shard_map/ppermute | solution.py:41
  27.5 0.5 collective-permute-start.11
  28.0 0.1 collective-permute-start.12
  28.1 1.4 %collective-permute-start.9 = (bf16[1536,128]{1,0:T(8,128)(2,1)S(1)}, bf16[1536,128]{1,0:T(8,128)(2,1)S(1)}, u32[]{:S(2)}, u32[]{:S(2)}) collective-permute-start(bf16[1536,128]{1,0:T(8,128)(2,1)S(1)} %shard_map.112.w0), channel_id=1, source_target_pairs={{0,64},{1,65},{2,66},{3,67},{4,68},{5,69},{6,70},{7,71},{32,34},{3... | collective-permute-start | bytes 1179656 | tf_op jit(solution)/shard_map/ppermute | solution.py:41
  29.5 1.1 copy-done.3
  30.7 0.7 copy-done.8
  31.4 6.6 %shard_map.113 = (f32[24,128]{1,0:T(8,128)S(1)}, f32[512,128]{1,0:T(8,128)S(1)}, bf16[512,128]{1,0:T(8,128)(2,1)S(1)}, bf16[512,128]{1,0:T(8,128)(2,1)S(1)}, bf16[512,128]{1,0:T(8,128)(2,1)S(1)}) custom-call(s32[18]{0:T(128)S(1)} %pad_add_fusion.table_ref, s32[16,128]{1,0:T(8,128)S(1)} %bitcast.26, bf16[256,1536]{1,0:T(8,128)(2,1)S(1)} %bitcast.21, ...), custom_call_target="tpu_custom_call" | custom-call | bytes 22020096 | tf_op jit(solution)/shard_map/pallas_call | solution.py:282
  38.1 0.8 collective-permute-start.14
  38.9 1.4 %collective-permute-start.15 = (bf16[512,128]{1,0:T(8,128)(2,1)S(1)}, bf16[512,128]{1,0:T(8,128)(2,1)S(1)}, u32[]{:S(2)}, u32[]{:S(2)}) collective-permute-start(bf16[512,128]{1,0:T(8,128)(2,1)S(1)} %get-tuple-element.120), channel_id=1, source_target_pairs={{0,2},{1,3},{2,0},{3,1},{4,6},{5,7},{6,4},{7,5},{32,34},{33,35},{3... | collective-permute-start | bytes 393224 | tf_op jit(solution)/shard_map/ppermute | solution.py:41
  40.4 2.5 %collective-permute-start.16 = (bf16[512,128]{1,0:T(8,128)(2,1)S(1)}, bf16[512,128]{1,0:T(8,128)(2,1)S(1)}, u32[]{:S(2)}, u32[]{:S(2)}) collective-permute-start(bf16[512,128]{1,0:T(8,128)(2,1)S(1)} %get-tuple-element.121), channel_id=1, source_target_pairs={{0,3},{1,2},{2,1},{3,0},{4,7},{5,6},{6,5},{7,4},{32,35},{33,34},{3... | collective-permute-start | bytes 393224 | tf_op jit(solution)/shard_map/ppermute | solution.py:41
  42.9 2.8 %copy-done = bf16[1,256,12288]{2,1,0:T(8,128)(2,1)S(1)} copy-done((bf16[1,256,12288]{2,1,0:T(8,128)(2,1)S(1)}, bf16[1,256,12288]{2,1,0:T(8,128)(2,1)}, u32[]{:S(2)}) %copy-start) | copy-done | bytes 6291480
  45.7 2.6 %shard_map.114 = (bf16[256,128]{1,0:T(8,128)(2,1)S(1)}, bf16[3072,128]{1,0:T(8,128)(2,1)S(1)}, bf16[1536,128]{1,0:T(8,128)(2,1)S(1)}, bf16[1536,128]{1,0:T(8,128)(2,1)S(1)}, bf16[1536,128]{1,0:T(8,128)(2,1)S(1)}) custom-call(s32[37]{0:T(128)S(1)} %concatenate.7.table_ref, bf16[256,12288]{1,0:T(8,128)(2,1)S(1)} %bitcast.16, ...), custom_call_target="tpu_custom_call" | custom-call | bytes 12582912 | tf_op jit(solution)/shard_map/pallas_call | solution.py:282
  48.4 1.1 collective-permute-done.16
  49.5 1.3 %collective-permute-start.18 = (bf16[256,128]{1,0:T(8,128)(2,1)S(1)}, bf16[256,128]{1,0:T(8,128)(2,1)S(1)}, u32[]{:S(2)}, u32[]{:S(2)}) collective-permute-start(bf16[256,128]{1,0:T(8,128)(2,1)S(1)} %slice.96), channel_id=1, source_target_pairs={{0,4},{1,5},{2,6},{3,7},{4,0},{5,1},{6,2},{7,3},{32,36},{33,37},{3... | collective-permute-start | bytes 196616 | tf_op jit(solution)/shard_map/ppermute | solution.py:41
  50.8 0.8 collective-permute-start.17
  51.6 0.5 shard_map.115.term_ref
  52.1 2.1 %collective-permute-done.18 = bf16[256,128]{1,0:T(8,128)(2,1)S(1)} collective-permute-done((bf16[256,128]{1,0:T(8,128)(2,1)S(1)}, bf16[256,128]{1,0:T(8,128)(2,1)S(1)}, u32[]{:S(2)}, u32[]{:S(2)}) %collective-permute-start.18) | collective-permute-done | bytes 65568 | tf_op jit(solution)/shard_map/ppermute | solution.py:41
  54.2 0.8 collective-permute-done.17.refs_1_
  55.1 1.9 %shard_map.117 = (f32[2048,384]{1,0:T(8,128)S(1)}, bf16[2048,384]{1,0:T(8,128)(2,1)S(1)}, bf16[1792,128]{1,0:T(8,128)(2,1)S(1)}, bf16[1792,128]{1,0:T(8,128)(2,1)S(1)}, bf16[1792,128]{1,0:T(8,128)(2,1)S(1)}) custom-call(s32[37]{0:T(128)S(1)} %concatenate.7.table_ref, bf16[256,12288]{1,0:T(8,128)(2,1)S(1)} %bitcast.17, ...), custom_call_target="tpu_custom_call" | custom-call | bytes 12582912 | tf_op jit(solution)/shard_map/pallas_call | solution.py:282
  57.1 4.0 %collective-permute-start.20 = (bf16[512,128]{1,0:T(8,128)(2,1)S(1)}, bf16[512,128]{1,0:T(8,128)(2,1)S(1)}, u32[]{:S(2)}, u32[]{:S(2)}) collective-permute-start(bf16[512,128]{1,0:T(8,128)(2,1)S(1)} %shard_map.116.v0), channel_id=1, source_target_pairs={{0,2},{1,3},{2,0},{3,1},{4,6},{5,7},{6,4},{7,5},{32,34},{33,35},{3... | collective-permute-start | bytes 393224 | tf_op jit(solution)/shard_map/ppermute | solution.py:41
  61.2 0.7 collective-permute-start.21
  61.8 0.4 add_convert_fusion
  62.2 1.2 %collective-permute-done.19.v1 = bf16[512,128]{1,0:T(8,128)(2,1)S(1)} collective-permute-done((bf16[512,128]{1,0:T(8,128)(2,1)S(1)}, bf16[512,128]{1,0:T(8,128)(2,1)S(1)}, u32[]{:S(2)}, u32[]{:S(2)}) %collective-permute-start.19) | collective-permute-done | bytes 131104 | tf_op jit(solution)/shard_map/ppermute | solution.py:41
  63.4 4.5 %collective-permute-done.20.v2 = bf16[512,128]{1,0:T(8,128)(2,1)S(1)} collective-permute-done((bf16[512,128]{1,0:T(8,128)(2,1)S(1)}, bf16[512,128]{1,0:T(8,128)(2,1)S(1)}, u32[]{:S(2)}, u32[]{:S(2)}) %collective-permute-start.20) | collective-permute-done | bytes 131104 | tf_op jit(solution)/shard_map/ppermute | solution.py:41
  67.9 2.4 %collective-permute-done.21.v3 = bf16[512,128]{1,0:T(8,128)(2,1)S(1)} collective-permute-done((bf16[512,128]{1,0:T(8,128)(2,1)S(1)}, bf16[512,128]{1,0:T(8,128)(2,1)S(1)}, u32[]{:S(2)}, u32[]{:S(2)}) %collective-permute-start.21) | collective-permute-done | bytes 131104 | tf_op jit(solution)/shard_map/ppermute | solution.py:41
  70.4 0.9 collective-permute-start.23
  71.3 2.1 %collective-permute-start.24 = (bf16[512,384]{1,0:T(8,128)(2,1)S(1)}, bf16[512,384]{1,0:T(8,128)(2,1)S(1)}, u32[]{:S(2)}, u32[]{:S(2)}) collective-permute-start(bf16[512,384]{1,0:T(8,128)(2,1)S(1)} %get-tuple-element.153), channel_id=1, source_target_pairs={{0,64},{1,65},{2,66},{3,67},{4,68},{5,69},{6,70},{7,71},{32,34},{3... | collective-permute-start | bytes 1179656 | tf_op jit(solution)/shard_map/ppermute | solution.py:41
  73.4 1.7 %collective-permute-start.25 = (bf16[512,384]{1,0:T(8,128)(2,1)S(1)}, bf16[512,384]{1,0:T(8,128)(2,1)S(1)}, u32[]{:S(2)}, u32[]{:S(2)}) collective-permute-start(bf16[512,384]{1,0:T(8,128)(2,1)S(1)} %get-tuple-element.154), channel_id=1, source_target_pairs={{0,68},{1,69},{2,70},{3,71},{4,64},{5,65},{6,66},{7,67},{32,35},{3... | collective-permute-start | bytes 1179656 | tf_op jit(solution)/shard_map/ppermute | solution.py:41
  75.1 1.6 %collective-permute-start.26 = (bf16[1792,128]{1,0:T(8,128)(2,1)S(1)}, bf16[1792,128]{1,0:T(8,128)(2,1)S(1)}, u32[]{:S(2)}, u32[]{:S(2)}) collective-permute-start(bf16[1792,128]{1,0:T(8,128)(2,1)S(1)} %get-tuple-element.155), channel_id=1, source_target_pairs={{0,8},{8,0},{16,24},{24,16},{1,9},{9,1},{17,25},{25,17},{2,10},{10... | collective-permute-start | bytes 1376264 | tf_op jit(solution)/shard_map/ppermute | solution.py:65
  76.7 2.2 %collective-permute-start.27 = (bf16[1792,128]{1,0:T(8,128)(2,1)S(1)}, bf16[1792,128]{1,0:T(8,128)(2,1)S(1)}, u32[]{:S(2)}, u32[]{:S(2)}) collective-permute-start(bf16[1792,128]{1,0:T(8,128)(2,1)S(1)} %get-tuple-element.157), channel_id=1, source_target_pairs={{0,24},{8,16},{16,8},{24,0},{1,25},{9,17},{17,9},{25,1},{2,26},{10... | collective-permute-start | bytes 1376264 | tf_op jit(solution)/shard_map/ppermute | solution.py:65
  78.8 8.4 %shard_map.118 = (bf16[256,1536]{1,0:T(8,128)(2,1)}, f32[512,128]{1,0:T(8,128)S(1)}, bf16[512,128]{1,0:T(8,128)(2,1)S(1)}, bf16[512,128]{1,0:T(8,128)(2,1)S(1)}, bf16[512,128]{1,0:T(8,128)(2,1)S(1)}) custom-call(s32[18]{0:T(128)S(1)} %pad_add_fusion.table_ref, s32[16,128]{1,0:T(8,128)S(1)} %bitcast.27, bf16[256,1536]{1,0:T(8,128)(2,1)S(1)} %bitcast.22, ...), custom_call_target="tpu_custom_call" | custom-call | bytes 28311552 | tf_op jit(solution)/shard_map/pallas_call | solution.py:282
  87.3 0.2 convert_add_fusion
  87.5 1.5 %collective-permute-done.27.a3 = bf16[1792,128]{1,0:T(8,128)(2,1)S(1)} collective-permute-done((bf16[1792,128]{1,0:T(8,128)(2,1)S(1)}, bf16[1792,128]{1,0:T(8,128)(2,1)S(1)}, u32[]{:S(2)}, u32[]{:S(2)}) %collective-permute-start.27) | collective-permute-done | bytes 458784 | tf_op jit(solution)/shard_map/ppermute | solution.py:65
  88.9 1.7 %collective-permute-start.31 = (bf16[1792,128]{1,0:T(8,128)(2,1)S(1)}, bf16[1792,128]{1,0:T(8,128)(2,1)S(1)}, u32[]{:S(2)}, u32[]{:S(2)}) collective-permute-start(bf16[1792,128]{1,0:T(8,128)(2,1)S(1)} %get-tuple-element.163), channel_id=1, source_target_pairs={{0,16},{8,24},{16,0},{24,8},{1,17},{9,25},{17,1},{25,9},{2,18},{10... | collective-permute-start | bytes 1376264 | tf_op jit(solution)/shard_map/ppermute | solution.py:65
  90.6 0.5 collective-permute-start.33
  91.2 2.2 %collective-permute-start.29 = (bf16[512,128]{1,0:T(8,128)(2,1)S(1)}, bf16[512,128]{1,0:T(8,128)(2,1)S(1)}, u32[]{:S(2)}, u32[]{:S(2)}) collective-permute-start(bf16[512,128]{1,0:T(8,128)(2,1)S(1)} %get-tuple-element.159), channel_id=1, source_target_pairs={{0,2},{1,3},{2,0},{3,1},{4,6},{5,7},{6,4},{7,5},{32,34},{33,35},{3... | collective-permute-start | bytes 393224 | tf_op jit(solution)/shard_map/ppermute | solution.py:41
  93.4 4.1 %collective-permute-done.28 = bf16[512,128]{1,0:T(8,128)(2,1)S(1)} collective-permute-done((bf16[512,128]{1,0:T(8,128)(2,1)S(1)}, bf16[512,128]{1,0:T(8,128)(2,1)S(1)}, u32[]{:S(2)}, u32[]{:S(2)}) %collective-permute-start.28) | collective-permute-done | bytes 131104 | tf_op jit(solution)/shard_map/ppermute | solution.py:41
  97.5 0.7 collective-permute-start.30
  98.2 1.3 %collective-permute-done.29 = bf16[512,128]{1,0:T(8,128)(2,1)S(1)} collective-permute-done((bf16[512,128]{1,0:T(8,128)(2,1)S(1)}, bf16[512,128]{1,0:T(8,128)(2,1)S(1)}, u32[]{:S(2)}, u32[]{:S(2)}) %collective-permute-start.29) | collective-permute-done | bytes 131104 | tf_op jit(solution)/shard_map/ppermute | solution.py:41
  99.5 0.6 collective-permute-start.36
  100.0 3.7 %collective-permute-done.30 = bf16[512,128]{1,0:T(8,128)(2,1)S(1)} collective-permute-done((bf16[512,128]{1,0:T(8,128)(2,1)S(1)}, bf16[512,128]{1,0:T(8,128)(2,1)S(1)}, u32[]{:S(2)}, u32[]{:S(2)}) %collective-permute-start.30) | collective-permute-done | bytes 131104 | tf_op jit(solution)/shard_map/ppermute | solution.py:41
  103.7 0.3 collective-permute-start.37
  103.9 1.5 %collective-permute-start.38 = (bf16[128,384]{1,0:T(8,128)(2,1)S(1)}, bf16[128,384]{1,0:T(8,128)(2,1)S(1)}, u32[]{:S(2)}, u32[]{:S(2)}) collective-permute-start(bf16[128,384]{1,0:T(8,128)(2,1)S(1)} %get-tuple-element.180), channel_id=1, source_target_pairs={{0,3},{1,2},{2,1},{3,0},{4,7},{5,6},{6,5},{7,4},{32,100},{33,101},... | collective-permute-start | bytes 294920 | tf_op jit(solution)/shard_map/ppermute | solution.py:41
  105.5 1.0 collective-permute-start.34
  106.5 3.4 %collective-permute-done.37.two = bf16[128,384]{1,0:T(8,128)(2,1)S(1)} collective-permute-done((bf16[128,384]{1,0:T(8,128)(2,1)S(1)}, bf16[128,384]{1,0:T(8,128)(2,1)S(1)}, u32[]{:S(2)}, u32[]{:S(2)}) %collective-permute-start.37) | collective-permute-done | bytes 98336 | tf_op jit(solution)/shard_map/ppermute | solution.py:41
  109.9 0.9 collective-permute-done.38.three
  110.8 0.8 shard_map.120
  111.6 0.6 fusion.1
  112.3 3.4 %shard_map.119 = bf16[256,3072]{1,0:T(8,128)(2,1)} custom-call(s32[37]{0:T(128)S(1)} %concatenate.7.table_ref, bf16[256,128]{1,0:T(8,128)(2,1)S(1)} %add_convert_fusion.3.grads, bf16[3072,128]{1,0:T(8,128)(2,1)S(1)} %get-tuple-element.169.own, bf16[1792,128]{1,0:T(8,128)(2,1)S(1)} %collective-permute-done.26.a1, ...), custom_call_target="tpu_custom_call" | custom-call | bytes 12582912 | tf_op jit(solution)/shard_map/pallas_call | solution.py:282
  (62 shorter events, 0.9 us)
Async XLA Ops:
  0.6 28.9 %copy-start.2 = (bf16[1,256,1536]{2,1,0:T(8,128)(2,1)S(1)}, bf16[1,256,1536]{2,1,0:T(8,128)(2,1)}, u32[]{:S(2)}) copy-start(bf16[1,256,1536]{2,1,0:T(8,128)(2,1)} %param.12) | copy-start | bytes 2359300
  0.6 10.1 %collective-permute-start.1 = (bf16[384,128]{1,0:T(8,128)(2,1)}, bf16[384,128]{1,0:T(8,128)(2,1)S(1)}, u32[]{:S(2)}, u32[]{:S(2)}) collective-permute-start(bf16[384,128]{1,0:T(8,128)(2,1)} %refs_0_), channel_id=1, source_target_pairs={{0,1},{1,0},{2,3},{3,2},{4,5},{5,4},{6,7},{7,6},{32,36},{33,37},{3... | collective-permute-start | bytes 294920 | tf_op jit(solution)/shard_map/ppermute | solution.py:41
  2.7 8.1 %collective-permute-start.2 = (bf16[384,128]{1,0:T(8,128)(2,1)}, bf16[384,128]{1,0:T(8,128)(2,1)S(1)}, u32[]{:S(2)}, u32[]{:S(2)}) collective-permute-start(bf16[384,128]{1,0:T(8,128)(2,1)} %refs_0_), channel_id=1, source_target_pairs={{0,2},{1,3},{2,0},{3,1},{4,6},{5,7},{6,4},{7,5},{32,96},{33,97},{3... | collective-permute-start | bytes 294920 | tf_op jit(solution)/shard_map/ppermute | solution.py:41
  6.3 6.0 %collective-permute-start.3 = (bf16[384,128]{1,0:T(8,128)(2,1)}, bf16[384,128]{1,0:T(8,128)(2,1)S(1)}, u32[]{:S(2)}, u32[]{:S(2)}) collective-permute-start(bf16[384,128]{1,0:T(8,128)(2,1)} %refs_0_), channel_id=1, source_target_pairs={{0,3},{1,2},{2,1},{3,0},{4,7},{5,6},{6,5},{7,4},{32,100},{33,101},... | collective-permute-start | bytes 294920 | tf_op jit(solution)/shard_map/ppermute | solution.py:41
  6.3 4.5 %collective-permute-start = (bf16[256,128]{1,0:T(8,128)(2,1)}, bf16[256,128]{1,0:T(8,128)(2,1)S(1)}, u32[]{:S(2)}, u32[]{:S(2)}) collective-permute-start(bf16[256,128]{1,0:T(8,128)(2,1)} %bitcast.24), channel_id=1, source_target_pairs={{0,4},{1,5},{2,6},{3,7},{4,0},{5,1},{6,2},{7,3},{32,36},{33,37},{3... | collective-permute-start | bytes 196616 | tf_op jit(solution)/shard_map/ppermute | solution.py:41
  12.3 0.9 copy-start.6
  13.3 14.2 %collective-permute-start.7 = (bf16[1536,128]{1,0:T(8,128)(2,1)S(1)}, bf16[1536,128]{1,0:T(8,128)(2,1)S(1)}, u32[]{:S(2)}, u32[]{:S(2)}) collective-permute-start(bf16[1536,128]{1,0:T(8,128)(2,1)S(1)} %shard_map.112.w0), channel_id=1, source_target_pairs={{0,4},{1,5},{2,6},{3,7},{4,0},{5,1},{6,2},{7,3},{32,33},{33,32},{3... | collective-permute-start | bytes 1179656 | tf_op jit(solution)/shard_map/ppermute | solution.py:41
  14.8 12.7 %collective-permute-start.8 = (bf16[1536,128]{1,0:T(8,128)(2,1)S(1)}, bf16[1536,128]{1,0:T(8,128)(2,1)S(1)}, u32[]{:S(2)}, u32[]{:S(2)}) collective-permute-start(bf16[1536,128]{1,0:T(8,128)(2,1)S(1)} %shard_map.112.w0), channel_id=1, source_target_pairs={{0,68},{1,69},{2,70},{3,71},{4,64},{5,65},{6,66},{7,67},{32,35},{3... | collective-permute-start | bytes 1179656 | tf_op jit(solution)/shard_map/ppermute | solution.py:41
  16.9 0.8 copy-start.7
  17.8 6.6 %collective-permute-start.4 = (bf16[512,128]{1,0:T(8,128)(2,1)S(1)}, bf16[512,128]{1,0:T(8,128)(2,1)S(1)}, u32[]{:S(2)}, u32[]{:S(2)}) collective-permute-start(bf16[512,128]{1,0:T(8,128)(2,1)S(1)} %shard_map.111.k0), channel_id=1, source_target_pairs={{0,1},{1,0},{2,3},{3,2},{4,5},{5,4},{6,7},{7,6},{32,33},{33,32},{3... | collective-permute-start | bytes 393224 | tf_op jit(solution)/shard_map/ppermute | solution.py:41
  17.9 8.2 %collective-permute-start.5 = (bf16[512,128]{1,0:T(8,128)(2,1)S(1)}, bf16[512,128]{1,0:T(8,128)(2,1)S(1)}, u32[]{:S(2)}, u32[]{:S(2)}) collective-permute-start(bf16[512,128]{1,0:T(8,128)(2,1)S(1)} %shard_map.111.k0), channel_id=1, source_target_pairs={{0,2},{1,3},{2,0},{3,1},{4,6},{5,7},{6,4},{7,5},{32,34},{33,35},{3... | collective-permute-start | bytes 393224 | tf_op jit(solution)/shard_map/ppermute | solution.py:41
  21.0 6.5 %collective-permute-start.6 = (bf16[512,128]{1,0:T(8,128)(2,1)S(1)}, bf16[512,128]{1,0:T(8,128)(2,1)S(1)}, u32[]{:S(2)}, u32[]{:S(2)}) collective-permute-start(bf16[512,128]{1,0:T(8,128)(2,1)S(1)} %shard_map.111.k0), channel_id=1, source_target_pairs={{0,3},{1,2},{2,1},{3,0},{4,7},{5,6},{6,5},{7,4},{32,35},{33,34},{3... | collective-permute-start | bytes 393224 | tf_op jit(solution)/shard_map/ppermute | solution.py:41
  27.5 10.5 %collective-permute-start.10 = (bf16[1536,128]{1,0:T(8,128)(2,1)S(1)}, bf16[1536,128]{1,0:T(8,128)(2,1)S(1)}, u32[]{:S(2)}, u32[]{:S(2)}) collective-permute-start(bf16[1536,128]{1,0:T(8,128)(2,1)S(1)} %shard_map.112.w0), channel_id=1, source_target_pairs={{0,32},{1,33},{2,34},{3,35},{4,36},{5,37},{6,38},{7,39},{32,0},{33... | collective-permute-start | bytes 1179656 | tf_op jit(solution)/shard_map/ppermute | solution.py:41
  27.5 10.5 %collective-permute-start.11 = (bf16[1536,128]{1,0:T(8,128)(2,1)S(1)}, bf16[1536,128]{1,0:T(8,128)(2,1)S(1)}, u32[]{:S(2)}, u32[]{:S(2)}) collective-permute-start(bf16[1536,128]{1,0:T(8,128)(2,1)S(1)} %collective-permute-done.7.w1), channel_id=1, source_target_pairs={{0,32},{1,33},{2,34},{3,35},{4,36},{5,37},{6,38},{7,39},{32,0},{33... | collective-permute-start | bytes 1179656 | tf_op jit(solution)/shard_map/ppermute | solution.py:41
  28.0 10.0 %collective-permute-start.12 = (bf16[1536,128]{1,0:T(8,128)(2,1)S(1)}, bf16[1536,128]{1,0:T(8,128)(2,1)S(1)}, u32[]{:S(2)}, u32[]{:S(2)}) collective-permute-start(bf16[1536,128]{1,0:T(8,128)(2,1)S(1)} %collective-permute-done.8.w3), channel_id=1, source_target_pairs={{0,32},{1,33},{2,34},{3,35},{4,36},{5,37},{6,38},{7,39},{32,0},{33... | collective-permute-start | bytes 1179656 | tf_op jit(solution)/shard_map/ppermute | solution.py:41
  28.1 9.9 %collective-permute-start.9 = (bf16[1536,128]{1,0:T(8,128)(2,1)S(1)}, bf16[1536,128]{1,0:T(8,128)(2,1)S(1)}, u32[]{:S(2)}, u32[]{:S(2)}) collective-permute-start(bf16[1536,128]{1,0:T(8,128)(2,1)S(1)} %shard_map.112.w0), channel_id=1, source_target_pairs={{0,64},{1,65},{2,66},{3,67},{4,68},{5,69},{6,70},{7,71},{32,34},{3... | collective-permute-start | bytes 1179656 | tf_op jit(solution)/shard_map/ppermute | solution.py:41
  29.5 1.1 copy-start.3
  30.7 0.7 copy-start.8
  38.0 4.9 %collective-permute-start.13 = (bf16[1536,128]{1,0:T(8,128)(2,1)S(1)}, bf16[1536,128]{1,0:T(8,128)(2,1)S(1)}, u32[]{:S(2)}, u32[]{:S(2)}) collective-permute-start(bf16[1536,128]{1,0:T(8,128)(2,1)S(1)} %collective-permute-done.9.w2), channel_id=1, source_target_pairs={{0,32},{1,33},{2,34},{3,35},{4,36},{5,37},{6,38},{7,39},{32,0},{33... | collective-permute-start | bytes 1179656 | tf_op jit(solution)/shard_map/ppermute | solution.py:41
  38.1 10.2 %collective-permute-start.14 = (bf16[512,128]{1,0:T(8,128)(2,1)S(1)}, bf16[512,128]{1,0:T(8,128)(2,1)S(1)}, u32[]{:S(2)}, u32[]{:S(2)}) collective-permute-start(bf16[512,128]{1,0:T(8,128)(2,1)S(1)} %get-tuple-element.119), channel_id=1, source_target_pairs={{0,1},{1,0},{2,3},{3,2},{4,5},{5,4},{6,7},{7,6},{32,33},{33,32},{3... | collective-permute-start | bytes 393224 | tf_op jit(solution)/shard_map/ppermute | solution.py:41
  38.9 9.4 %collective-permute-start.15 = (bf16[512,128]{1,0:T(8,128)(2,1)S(1)}, bf16[512,128]{1,0:T(8,128)(2,1)S(1)}, u32[]{:S(2)}, u32[]{:S(2)}) collective-permute-start(bf16[512,128]{1,0:T(8,128)(2,1)S(1)} %get-tuple-element.120), channel_id=1, source_target_pairs={{0,2},{1,3},{2,0},{3,1},{4,6},{5,7},{6,4},{7,5},{32,34},{33,35},{3... | collective-permute-start | bytes 393224 | tf_op jit(solution)/shard_map/ppermute | solution.py:41
  40.4 9.0 %collective-permute-start.16 = (bf16[512,128]{1,0:T(8,128)(2,1)S(1)}, bf16[512,128]{1,0:T(8,128)(2,1)S(1)}, u32[]{:S(2)}, u32[]{:S(2)}) collective-permute-start(bf16[512,128]{1,0:T(8,128)(2,1)S(1)} %get-tuple-element.121), channel_id=1, source_target_pairs={{0,3},{1,2},{2,1},{3,0},{4,7},{5,6},{6,5},{7,4},{32,35},{33,34},{3... | collective-permute-start | bytes 393224 | tf_op jit(solution)/shard_map/ppermute | solution.py:41
  42.9 2.8 %copy-start = (bf16[1,256,12288]{2,1,0:T(8,128)(2,1)S(1)}, bf16[1,256,12288]{2,1,0:T(8,128)(2,1)}, u32[]{:S(2)}) copy-start(bf16[1,256,12288]{2,1,0:T(8,128)(2,1)} %param.8) | copy-start | bytes 18874372
  45.7 9.4 %copy-start.1 = (bf16[1,256,12288]{2,1,0:T(8,128)(2,1)S(1)}, bf16[1,256,12288]{2,1,0:T(8,128)(2,1)}, u32[]{:S(2)}) copy-start(bf16[1,256,12288]{2,1,0:T(8,128)(2,1)} %param.8) | copy-start | bytes 18874372
  48.3 3.3 %copy-start.5 = (bf16[1,256,1536]{2,1,0:T(8,128)(2,1)S(1)}, bf16[1,256,1536]{2,1,0:T(8,128)(2,1)}, u32[]{:S(2)}) copy-start(bf16[1,256,1536]{2,1,0:T(8,128)(2,1)} %param.13) | copy-start | bytes 2359300
  49.5 4.7 %collective-permute-start.18 = (bf16[256,128]{1,0:T(8,128)(2,1)S(1)}, bf16[256,128]{1,0:T(8,128)(2,1)S(1)}, u32[]{:S(2)}, u32[]{:S(2)}) collective-permute-start(bf16[256,128]{1,0:T(8,128)(2,1)S(1)} %slice.96), channel_id=1, source_target_pairs={{0,4},{1,5},{2,6},{3,7},{4,0},{5,1},{6,2},{7,3},{32,36},{33,37},{3... | collective-permute-start | bytes 196616 | tf_op jit(solution)/shard_map/ppermute | solution.py:41
  50.8 4.3 %collective-permute-start.17 = (bf16[256,128]{1,0:T(8,128)(2,1)S(1)}, bf16[256,128]{1,0:T(8,128)(2,1)S(1)}, u32[]{:S(2)}, u32[]{:S(2)}) collective-permute-start(bf16[256,128]{1,0:T(8,128)(2,1)S(1)} %get-tuple-element.130.refs_0_), channel_id=1, source_target_pairs={{0,4},{1,5},{2,6},{3,7},{4,0},{5,1},{6,2},{7,3},{32,36},{33,37},{3... | collective-permute-start | bytes 196616 | tf_op jit(solution)/shard_map/ppermute | solution.py:41
  56.9 4.9 %collective-permute-start.22 = (bf16[2048,384]{1,0:T(8,128)(2,1)S(1)}, bf16[2048,384]{1,0:T(8,128)(2,1)S(1)}, u32[]{:S(2)}, u32[]{:S(2)}) collective-permute-start(bf16[2048,384]{1,0:T(8,128)(2,1)S(1)} %get-tuple-element.138), channel_id=1, source_target_pairs={{0,32},{1,33},{2,34},{3,35},{4,36},{5,37},{6,38},{7,39},{32,0},{33... | collective-permute-start | bytes 4718600 | tf_op jit(solution)/shard_map/ppermute | solution.py:41
  57.1 6.4 %collective-permute-start.19 = (bf16[512,128]{1,0:T(8,128)(2,1)S(1)}, bf16[512,128]{1,0:T(8,128)(2,1)S(1)}, u32[]{:S(2)}, u32[]{:S(2)}) collective-permute-start(bf16[512,128]{1,0:T(8,128)(2,1)S(1)} %shard_map.116.v0), channel_id=1, source_target_pairs={{0,1},{1,0},{2,3},{3,2},{4,5},{5,4},{6,7},{7,6},{32,33},{33,32},{3... | collective-permute-start | bytes 393224 | tf_op jit(solution)/shard_map/ppermute | solution.py:41
  57.1 10.8 %collective-permute-start.20 = (bf16[512,128]{1,0:T(8,128)(2,1)S(1)}, bf16[512,128]{1,0:T(8,128)(2,1)S(1)}, u32[]{:S(2)}, u32[]{:S(2)}) collective-permute-start(bf16[512,128]{1,0:T(8,128)(2,1)S(1)} %shard_map.116.v0), channel_id=1, source_target_pairs={{0,2},{1,3},{2,0},{3,1},{4,6},{5,7},{6,4},{7,5},{32,34},{33,35},{3... | collective-permute-start | bytes 393224 | tf_op jit(solution)/shard_map/ppermute | solution.py:41
  61.2 9.2 %collective-permute-start.21 = (bf16[512,128]{1,0:T(8,128)(2,1)S(1)}, bf16[512,128]{1,0:T(8,128)(2,1)S(1)}, u32[]{:S(2)}, u32[]{:S(2)}) collective-permute-start(bf16[512,128]{1,0:T(8,128)(2,1)S(1)} %shard_map.116.v0), channel_id=1, source_target_pairs={{0,3},{1,2},{2,1},{3,0},{4,7},{5,6},{6,5},{7,4},{32,35},{33,34},{3... | collective-permute-start | bytes 393224 | tf_op jit(solution)/shard_map/ppermute | solution.py:41
  61.8 17.0 %copy-start.4 = (bf16[1,256,1536]{2,1,0:T(8,128)(2,1)S(1)}, bf16[1,256,1536]{2,1,0:T(8,128)(2,1)}, u32[]{:S(2)}) copy-start(bf16[1,256,1536]{2,1,0:T(8,128)(2,1)} %param.9) | copy-start | bytes 2359300
  61.8 17.0 %copy-start.9 = (s32[1,2048]{1,0:T(1,128)S(1)}, s32[1,2048]{1,0:T(1,128)}, u32[]{:S(2)}) copy-start(s32[1,2048]{1,0:T(1,128)} %param.14) | copy-start | bytes 24580
  70.4 16.9 %collective-permute-start.23 = (bf16[512,384]{1,0:T(8,128)(2,1)S(1)}, bf16[512,384]{1,0:T(8,128)(2,1)S(1)}, u32[]{:S(2)}, u32[]{:S(2)}) collective-permute-start(bf16[512,384]{1,0:T(8,128)(2,1)S(1)} %get-tuple-element.152), channel_id=1, source_target_pairs={{0,4},{1,5},{2,6},{3,7},{4,0},{5,1},{6,2},{7,3},{32,33},{33,32},{3... | collective-permute-start | bytes 1179656 | tf_op jit(solution)/shard_map/ppermute | solution.py:41
  71.3 16.0 %collective-permute-start.24 = (bf16[512,384]{1,0:T(8,128)(2,1)S(1)}, bf16[512,384]{1,0:T(8,128)(2,1)S(1)}, u32[]{:S(2)}, u32[]{:S(2)}) collective-permute-start(bf16[512,384]{1,0:T(8,128)(2,1)S(1)} %get-tuple-element.153), channel_id=1, source_target_pairs={{0,64},{1,65},{2,66},{3,67},{4,68},{5,69},{6,70},{7,71},{32,34},{3... | collective-permute-start | bytes 1179656 | tf_op jit(solution)/shard_map/ppermute | solution.py:41
  73.4 13.9 %collective-permute-start.25 = (bf16[512,384]{1,0:T(8,128)(2,1)S(1)}, bf16[512,384]{1,0:T(8,128)(2,1)S(1)}, u32[]{:S(2)}, u32[]{:S(2)}) collective-permute-start(bf16[512,384]{1,0:T(8,128)(2,1)S(1)} %get-tuple-element.154), channel_id=1, source_target_pairs={{0,68},{1,69},{2,70},{3,71},{4,64},{5,65},{6,66},{7,67},{32,35},{3... | collective-permute-start | bytes 1179656 | tf_op jit(solution)/shard_map/ppermute | solution.py:41
  75.1 12.4 %collective-permute-start.26 = (bf16[1792,128]{1,0:T(8,128)(2,1)S(1)}, bf16[1792,128]{1,0:T(8,128)(2,1)S(1)}, u32[]{:S(2)}, u32[]{:S(2)}) collective-permute-start(bf16[1792,128]{1,0:T(8,128)(2,1)S(1)} %get-tuple-element.155), channel_id=1, source_target_pairs={{0,8},{8,0},{16,24},{24,16},{1,9},{9,1},{17,25},{25,17},{2,10},{10... | collective-permute-start | bytes 1376264 | tf_op jit(solution)/shard_map/ppermute | solution.py:65
  76.7 12.3 %collective-permute-start.27 = (bf16[1792,128]{1,0:T(8,128)(2,1)S(1)}, bf16[1792,128]{1,0:T(8,128)(2,1)S(1)}, u32[]{:S(2)}, u32[]{:S(2)}) collective-permute-start(bf16[1792,128]{1,0:T(8,128)(2,1)S(1)} %get-tuple-element.157), channel_id=1, source_target_pairs={{0,24},{8,16},{16,8},{24,0},{1,25},{9,17},{17,9},{25,1},{2,26},{10... | collective-permute-start | bytes 1376264 | tf_op jit(solution)/shard_map/ppermute | solution.py:65
  88.9 15.0 %collective-permute-start.31 = (bf16[1792,128]{1,0:T(8,128)(2,1)S(1)}, bf16[1792,128]{1,0:T(8,128)(2,1)S(1)}, u32[]{:S(2)}, u32[]{:S(2)}) collective-permute-start(bf16[1792,128]{1,0:T(8,128)(2,1)S(1)} %get-tuple-element.163), channel_id=1, source_target_pairs={{0,16},{8,24},{16,0},{24,8},{1,17},{9,25},{17,1},{25,9},{2,18},{10... | collective-permute-start | bytes 1376264 | tf_op jit(solution)/shard_map/ppermute | solution.py:65
  90.6 14.8 %collective-permute-start.32 = (bf16[1792,128]{1,0:T(8,128)(2,1)S(1)}, bf16[1792,128]{1,0:T(8,128)(2,1)S(1)}, u32[]{:S(2)}, u32[]{:S(2)}) collective-permute-start(bf16[1792,128]{1,0:T(8,128)(2,1)S(1)} %collective-permute-done.26.a1), channel_id=1, source_target_pairs={{0,32},{1,33},{2,34},{3,35},{4,36},{5,37},{6,38},{7,39},{32,0},{33... | collective-permute-start | bytes 1376264 | tf_op jit(solution)/shard_map/ppermute | solution.py:41
  90.6 14.8 %collective-permute-start.33 = (bf16[1792,128]{1,0:T(8,128)(2,1)S(1)}, bf16[1792,128]{1,0:T(8,128)(2,1)S(1)}, u32[]{:S(2)}, u32[]{:S(2)}) collective-permute-start(bf16[1792,128]{1,0:T(8,128)(2,1)S(1)} %collective-permute-done.27.a3), channel_id=1, source_target_pairs={{0,32},{1,33},{2,34},{3,35},{4,36},{5,37},{6,38},{7,39},{32,0},{33... | collective-permute-start | bytes 1376264 | tf_op jit(solution)/shard_map/ppermute | solution.py:41
  91.1 6.4 %collective-permute-start.28 = (bf16[512,128]{1,0:T(8,128)(2,1)S(1)}, bf16[512,128]{1,0:T(8,128)(2,1)S(1)}, u32[]{:S(2)}, u32[]{:S(2)}) collective-permute-start(bf16[512,128]{1,0:T(8,128)(2,1)S(1)} %get-tuple-element.158), channel_id=1, source_target_pairs={{0,1},{1,0},{2,3},{3,2},{4,5},{5,4},{6,7},{7,6},{32,33},{33,32},{3... | collective-permute-start | bytes 393224 | tf_op jit(solution)/shard_map/ppermute | solution.py:41
  91.2 8.3 %collective-permute-start.29 = (bf16[512,128]{1,0:T(8,128)(2,1)S(1)}, bf16[512,128]{1,0:T(8,128)(2,1)S(1)}, u32[]{:S(2)}, u32[]{:S(2)}) collective-permute-start(bf16[512,128]{1,0:T(8,128)(2,1)S(1)} %get-tuple-element.159), channel_id=1, source_target_pairs={{0,2},{1,3},{2,0},{3,1},{4,6},{5,7},{6,4},{7,5},{32,34},{33,35},{3... | collective-permute-start | bytes 393224 | tf_op jit(solution)/shard_map/ppermute | solution.py:41
  97.5 6.2 %collective-permute-start.30 = (bf16[512,128]{1,0:T(8,128)(2,1)S(1)}, bf16[512,128]{1,0:T(8,128)(2,1)S(1)}, u32[]{:S(2)}, u32[]{:S(2)}) collective-permute-start(bf16[512,128]{1,0:T(8,128)(2,1)S(1)} %get-tuple-element.160), channel_id=1, source_target_pairs={{0,3},{1,2},{2,1},{3,0},{4,7},{5,6},{6,5},{7,4},{32,35},{33,34},{3... | collective-permute-start | bytes 393224 | tf_op jit(solution)/shard_map/ppermute | solution.py:41
  99.5 7.0 %collective-permute-start.36 = (bf16[128,384]{1,0:T(8,128)(2,1)S(1)}, bf16[128,384]{1,0:T(8,128)(2,1)S(1)}, u32[]{:S(2)}, u32[]{:S(2)}) collective-permute-start(bf16[128,384]{1,0:T(8,128)(2,1)S(1)} %get-tuple-element.182), channel_id=1, source_target_pairs={{0,1},{1,0},{2,3},{3,2},{4,5},{5,4},{6,7},{7,6},{32,36},{33,37},{3... | collective-permute-start | bytes 294920 | tf_op jit(solution)/shard_map/ppermute | solution.py:41
  103.7 6.2 %collective-permute-start.37 = (bf16[128,384]{1,0:T(8,128)(2,1)S(1)}, bf16[128,384]{1,0:T(8,128)(2,1)S(1)}, u32[]{:S(2)}, u32[]{:S(2)}) collective-permute-start(bf16[128,384]{1,0:T(8,128)(2,1)S(1)} %get-tuple-element.181), channel_id=1, source_target_pairs={{0,2},{1,3},{2,0},{3,1},{4,6},{5,7},{6,4},{7,5},{32,96},{33,97},{3... | collective-permute-start | bytes 294920 | tf_op jit(solution)/shard_map/ppermute | solution.py:41
  103.9 6.9 %collective-permute-start.38 = (bf16[128,384]{1,0:T(8,128)(2,1)S(1)}, bf16[128,384]{1,0:T(8,128)(2,1)S(1)}, u32[]{:S(2)}, u32[]{:S(2)}) collective-permute-start(bf16[128,384]{1,0:T(8,128)(2,1)S(1)} %get-tuple-element.180), channel_id=1, source_target_pairs={{0,3},{1,2},{2,1},{3,0},{4,7},{5,6},{6,5},{7,4},{32,100},{33,101},... | collective-permute-start | bytes 294920 | tf_op jit(solution)/shard_map/ppermute | solution.py:41
  105.4 6.9 %collective-permute-start.35 = (bf16[1792,128]{1,0:T(8,128)(2,1)S(1)}, bf16[1792,128]{1,0:T(8,128)(2,1)S(1)}, u32[]{:S(2)}, u32[]{:S(2)}) collective-permute-start(bf16[1792,128]{1,0:T(8,128)(2,1)S(1)} %collective-permute-done.31.a2), channel_id=1, source_target_pairs={{0,32},{1,33},{2,34},{3,35},{4,36},{5,37},{6,38},{7,39},{32,0},{33... | collective-permute-start | bytes 1376264 | tf_op jit(solution)/shard_map/ppermute | solution.py:41
  105.5 6.1 %collective-permute-start.34 = (bf16[256,128]{1,0:T(8,128)(2,1)S(1)}, bf16[256,128]{1,0:T(8,128)(2,1)S(1)}, u32[]{:S(2)}, u32[]{:S(2)}) collective-permute-start(bf16[256,128]{1,0:T(8,128)(2,1)S(1)} %slice.95), channel_id=1, source_target_pairs={{0,4},{1,5},{2,6},{3,7},{4,0},{5,1},{6,2},{7,3},{32,36},{33,37},{3... | collective-permute-start | bytes 196616 | tf_op jit(solution)/shard_map/ppermute | solution.py:41

commit v2 on v1

--- a/solution.py
+++ b/solution.py
@@ -87,8 +87,14 @@
             out_ref[at : at + 1, :] = jnp.sum(product.T, axis=0, keepdims=True)
 
 
-def join_kernel(*refs):
-    join(refs[:-1], refs[-1])
+def join_kernel(own, *refs):
+    parts, out, sem = refs[:-2], refs[-2], refs[-1]
+    rows = parts[0].shape[0]
+    copy = pltpu.make_async_copy(own, out.at[:rows, :], sem)
+    copy.start()
+    for i, part in enumerate(parts):
+        out[(i + 1) * rows : (i + 2) * rows, :] = part[...]
+    copy.wait()
 
 
 def fold_kernel(scale, own, one, two, three, out):
@@ -294,7 +300,13 @@
 
 def joined(parts):
     rows = sum(part.shape[0] for part in parts)
-    (whole,) = call(join_kernel, [((rows, HEAD_SIZE), bf16)], parts, smem=0)
+    (whole,) = call(
+        join_kernel,
+        [((rows, HEAD_SIZE), bf16)],
+        parts,
+        scratch=[pltpu.SemaphoreType.DMA],
+        smem=0, anys=(0,),
+    )
     return whole
 
 
@@ -377,7 +389,7 @@
         )
     )
 
-    w2 = second_with(first, 2)
+    w2 = second_with(w3, 1)
     s0, s1, s3 = core_swap(first), core_swap(w1), core_swap(w3)
     totals, *value_parts = call(
         value_side_kernel,
@@ -421,11 +433,13 @@
         w_own[512 * r : 512 * (r + 1)] + w_other[512 * r : 512 * (r + 1)].astype(f32) for r in range(4)
     ]
     w_parts = [w_parts[0]] + [part.astype(bf16) for part in w_parts[1:]]
+    messages[0], messages[2] = y_with(messages[0], 1), y_with(messages[2], 3)
     values, w_parts, messages = together(
         ([near_values] + [z_with(near_values, r) for r in (1, 2, 3)], w_parts, messages)
     )
 
-    messages[0], messages[2] = y_with(messages[0], 1), y_with(messages[2], 3)
+    messages[1] = y_with(messages[1], 2)
+    swapped = [core_swap(messages[0]), None, core_swap(messages[2])]
     w_sum = w_parts[0]
     for r in (1, 2, 3):
         w_sum = w_sum + second_with(w_parts[r], r).astype(f32)
@@ -436,21 +450,19 @@
         scratch=[whole, whole, window, window, bias, square, stack] + sums,
         cost=9, limit=28,
     )
-    key_parts, w_sum, messages = together((key_parts, w_sum, messages))
-
-    messages[1] = y_with(messages[1], 2)
-    swapped = [core_swap(messages[0]), None, core_swap(messages[2])]
+    key_parts, w_sum, messages, swapped[0], swapped[2] = together(
+        (key_parts, w_sum, messages, swapped[0], swapped[2])
+    )
+
+    swapped[1] = core_swap(messages[1])
     got = [
         first_with(w_sum[i * HEAD_SIZE : (i + 1) * HEAD_SIZE].astype(bf16), i) for i in (1, 2, 3)
     ]
     arrived = [z_with(part, r + 1) for r, part in enumerate(key_parts[1:])]
-    arrived, key_sum, messages, swapped[0], swapped[2] = together(
-        (arrived, key_parts[0], messages, swapped[0], swapped[2])
-    )
+    arrived, key_sum, slabs, swapped[1] = together((arrived, key_parts[0], slabs, swapped[1]))
     for part in arrived:
         key_sum = key_sum + part.astype(f32)
 
-    swapped[1] = core_swap(messages[1])
     key_grads = (key_sum[:rows] + x_swap(key_sum[rows:].astype(bf16)).astype(f32)).astype(bf16)
     (input_grad,) = call(
         input_kernel,
@@ -460,6 +472,7 @@
         anys=tuple(range(2, 9)),
         cost=4, limit=16,
     )
+    got, input_grad = together((got, input_grad))
     (weight_grad,) = call(
         functools.partial(fold_kernel, grad_scale),
         [((SLAB, HEAD_SIZE), f32)],

time: 116 us -> 110 us (0.948)
  waiting for transfers between devices: 34.7 us -> 26.9 us
  starting transfers between devices: 46.2 us -> 47.4 us
    ppermute x36, waiting for transfers between devices: 33.2 us -> 26.3 us  [moved(): return lax.ppermute(value, ('dp', 'ctx'), pairs)]
    ppermute x36, starting transfers between devices: 40.8 us -> 42.1 us  [moved(): return lax.ppermute(value, ('dp', 'ctx'), pairs)]
  transfers between devices with their start and end apart: 39 -> 39, of which waited for: 16 -> 16; matrix products, arithmetic and copies ran while one was open for 3% -> 2% of each run, Pallas kernels for 16% -> 21%
where the time goes in v2:
time: 110 us; the launch traced here: 109 us
  starting transfers between devices  47.4 us (43%)
  waiting for transfers between devices  26.9 us (24%)
  Pallas kernels  24.5 us (22%)
  local copies, waits for them, and re-layouts  6.52 us (6%)
  other arithmetic  3.09 us (3%)
    ppermute x36, starting transfers between devices, moved(): return lax.ppermute(value, ('dp', 'ctx'), pairs)  42.1 us
    ppermute x36, waiting for transfers between devices, moved(): return lax.ppermute(value, ('dp', 'ctx'), pairs)  26.3 us
    pallas_call x10, Pallas kernels, call(): pl.pallas_call(kernel, out_shape=tuple((jax.ShapeDtypeStruct(s, d) for s,...  24.5 us
    unnamed x20, local copies, waits for them, and re-layouts  6.37 us
    ppermute x3, starting transfers between devices, y_with(): return lax.ppermute(value, 'head', [(y, y ^ bits) for y in range(4)])  5.31 us
  transfers between devices with their start and end apart: 39, of which 16 were waited for; matrix products, arithmetic and copies ran while one was open for 2% of the time, Pallas kernels for 21%

profile of v2, /device:TPU:0, one launch (start us, length us, event | category | flops | bytes accessed | tf_op | source)
XLA Modules:
  0.0 109.4 jit_solution(4473144238855458125)
XLA Ops:
  0.6 2.1 %collective-permute-start.1 = (bf16[384,128]{1,0:T(8,128)(2,1)}, bf16[384,128]{1,0:T(8,128)(2,1)S(1)}, u32[]{:S(2)}, u32[]{:S(2)}) collective-permute-start(bf16[384,128]{1,0:T(8,128)(2,1)} %own), channel_id=1, source_target_pairs={{0,1},{1,0},{2,3},{3,2},{4,5},{5,4},{6,7},{7,6},{32,36},{33,37},{3... | collective-permute-start | bytes 294920 | tf_op jit(solution)/shard_map/ppermute | solution.py:41
  2.7 3.6 %collective-permute-start.2 = (bf16[384,128]{1,0:T(8,128)(2,1)}, bf16[384,128]{1,0:T(8,128)(2,1)S(1)}, u32[]{:S(2)}, u32[]{:S(2)}) collective-permute-start(bf16[384,128]{1,0:T(8,128)(2,1)} %own), channel_id=1, source_target_pairs={{0,2},{1,3},{2,0},{3,1},{4,6},{5,7},{6,4},{7,5},{32,96},{33,97},{3... | collective-permute-start | bytes 294920 | tf_op jit(solution)/shard_map/ppermute | solution.py:41
  6.3 1.5 %collective-permute-start = (bf16[256,128]{1,0:T(8,128)(2,1)}, bf16[256,128]{1,0:T(8,128)(2,1)S(1)}, u32[]{:S(2)}, u32[]{:S(2)}) collective-permute-start(bf16[256,128]{1,0:T(8,128)(2,1)} %bitcast.24), channel_id=1, source_target_pairs={{0,4},{1,5},{2,6},{3,7},{4,0},{5,1},{6,2},{7,3},{32,36},{33,37},{3... | collective-permute-start | bytes 196616 | tf_op jit(solution)/shard_map/ppermute | solution.py:41
  7.8 2.9 %collective-permute-done.refs_0_ = bf16[256,128]{1,0:T(8,128)(2,1)S(1)} collective-permute-done((bf16[256,128]{1,0:T(8,128)(2,1)}, bf16[256,128]{1,0:T(8,128)(2,1)S(1)}, u32[]{:S(2)}, u32[]{:S(2)}) %collective-permute-start) | collective-permute-done | bytes 65568 | tf_op jit(solution)/shard_map/ppermute | solution.py:41
  10.8 1.6 %collective-permute-done.3.refs_2_ = bf16[384,128]{1,0:T(8,128)(2,1)S(1)} collective-permute-done((bf16[384,128]{1,0:T(8,128)(2,1)}, bf16[384,128]{1,0:T(8,128)(2,1)S(1)}, u32[]{:S(2)}, u32[]{:S(2)}) %collective-permute-start.3) | collective-permute-done | bytes 98336 | tf_op jit(solution)/shard_map/ppermute | solution.py:41
  12.3 0.9 copy-done.6
  13.2 0.1 shard_map.112.w0
  13.4 1.6 %collective-permute-start.7 = (bf16[1536,128]{1,0:T(8,128)(2,1)S(1)}, bf16[1536,128]{1,0:T(8,128)(2,1)S(1)}, u32[]{:S(2)}, u32[]{:S(2)}) collective-permute-start(bf16[1536,128]{1,0:T(8,128)(2,1)S(1)} %shard_map.112.w0), channel_id=1, source_target_pairs={{0,4},{1,5},{2,6},{3,7},{4,0},{5,1},{6,2},{7,3},{32,33},{33,32},{3... | collective-permute-start | bytes 1179656 | tf_op jit(solution)/shard_map/ppermute | solution.py:41
  14.9 2.1 %collective-permute-start.8 = (bf16[1536,128]{1,0:T(8,128)(2,1)S(1)}, bf16[1536,128]{1,0:T(8,128)(2,1)S(1)}, u32[]{:S(2)}, u32[]{:S(2)}) collective-permute-start(bf16[1536,128]{1,0:T(8,128)(2,1)S(1)} %shard_map.112.w0), channel_id=1, source_target_pairs={{0,68},{1,69},{2,70},{3,71},{4,64},{5,65},{6,66},{7,67},{32,35},{3... | collective-permute-start | bytes 1179656 | tf_op jit(solution)/shard_map/ppermute | solution.py:41
  17.0 0.8 copy-done.7
  17.9 0.1 collective-permute-start.4
  18.0 3.1 %collective-permute-start.5 = (bf16[512,128]{1,0:T(8,128)(2,1)S(1)}, bf16[512,128]{1,0:T(8,128)(2,1)S(1)}, u32[]{:S(2)}, u32[]{:S(2)}) collective-permute-start(bf16[512,128]{1,0:T(8,128)(2,1)S(1)} %shard_map.111.k0), channel_id=1, source_target_pairs={{0,2},{1,3},{2,0},{3,1},{4,6},{5,7},{6,4},{7,5},{32,34},{33,35},{3... | collective-permute-start | bytes 393224 | tf_op jit(solution)/shard_map/ppermute | solution.py:41
  21.2 1.5 %collective-permute-start.6 = (bf16[512,128]{1,0:T(8,128)(2,1)S(1)}, bf16[512,128]{1,0:T(8,128)(2,1)S(1)}, u32[]{:S(2)}, u32[]{:S(2)}) collective-permute-start(bf16[512,128]{1,0:T(8,128)(2,1)S(1)} %shard_map.111.k0), channel_id=1, source_target_pairs={{0,3},{1,2},{2,1},{3,0},{4,7},{5,6},{6,5},{7,4},{32,35},{33,34},{3... | collective-permute-start | bytes 393224 | tf_op jit(solution)/shard_map/ppermute | solution.py:41
  22.7 0.8 fusion.2
  23.6 0.8 select_reduce_fusion
  24.5 1.7 %collective-permute-done.5.k2 = bf16[512,128]{1,0:T(8,128)(2,1)S(1)} collective-permute-done((bf16[512,128]{1,0:T(8,128)(2,1)S(1)}, bf16[512,128]{1,0:T(8,128)(2,1)S(1)}, u32[]{:S(2)}, u32[]{:S(2)}) %collective-permute-start.5) | collective-permute-done | bytes 131104 | tf_op jit(solution)/shard_map/ppermute | solution.py:41
  26.2 1.4 %collective-permute-done.6.k3 = bf16[512,128]{1,0:T(8,128)(2,1)S(1)} collective-permute-done((bf16[512,128]{1,0:T(8,128)(2,1)S(1)}, bf16[512,128]{1,0:T(8,128)(2,1)S(1)}, u32[]{:S(2)}, u32[]{:S(2)}) %collective-permute-start.6) | collective-permute-done | bytes 131104 | tf_op jit(solution)/shard_map/ppermute | solution.py:41
  27.6 0.5 collective-permute-start.11
  28.1 0.1 collective-permute-start.12
  28.2 0.4 collective-permute-start.9
  28.6 1.1 %copy-done.3 = bf16[1,256,1536]{2,1,0:T(8,128)(2,1)S(1)} copy-done((bf16[1,256,1536]{2,1,0:T(8,128)(2,1)S(1)}, bf16[1,256,1536]{2,1,0:T(8,128)(2,1)}, u32[]{:S(2)}) %copy-start.3) | copy-done | bytes 786456
  29.7 0.7 copy-done.8
  30.4 6.6 %shard_map.113 = (f32[24,128]{1,0:T(8,128)S(1)}, f32[512,128]{1,0:T(8,128)S(1)}, bf16[512,128]{1,0:T(8,128)(2,1)S(1)}, bf16[512,128]{1,0:T(8,128)(2,1)S(1)}, bf16[512,128]{1,0:T(8,128)(2,1)S(1)}) custom-call(s32[18]{0:T(128)S(1)} %pad_add_fusion.table_ref, s32[16,128]{1,0:T(8,128)S(1)} %bitcast.26, bf16[256,1536]{1,0:T(8,128)(2,1)S(1)} %bitcast.21, ...), custom_call_target="tpu_custom_call" | custom-call | bytes 22020096 | tf_op jit(solution)/shard_map/pallas_call | solution.py:288
  37.1 0.1 collective-permute-start.13
  37.2 1.8 %collective-permute-start.14 = (bf16[512,128]{1,0:T(8,128)(2,1)S(1)}, bf16[512,128]{1,0:T(8,128)(2,1)S(1)}, u32[]{:S(2)}, u32[]{:S(2)}) collective-permute-start(bf16[512,128]{1,0:T(8,128)(2,1)S(1)} %get-tuple-element.122), channel_id=1, source_target_pairs={{0,1},{1,0},{2,3},{3,2},{4,5},{5,4},{6,7},{7,6},{32,33},{33,32},{3... | collective-permute-start | bytes 393224 | tf_op jit(solution)/shard_map/ppermute | solution.py:41
  39.0 1.3 %collective-permute-start.15 = (bf16[512,128]{1,0:T(8,128)(2,1)S(1)}, bf16[512,128]{1,0:T(8,128)(2,1)S(1)}, u32[]{:S(2)}, u32[]{:S(2)}) collective-permute-start(bf16[512,128]{1,0:T(8,128)(2,1)S(1)} %get-tuple-element.123), channel_id=1, source_target_pairs={{0,2},{1,3},{2,0},{3,1},{4,6},{5,7},{6,4},{7,5},{32,34},{33,35},{3... | collective-permute-start | bytes 393224 | tf_op jit(solution)/shard_map/ppermute | solution.py:41
  40.2 1.7 %collective-permute-start.16 = (bf16[512,128]{1,0:T(8,128)(2,1)S(1)}, bf16[512,128]{1,0:T(8,128)(2,1)S(1)}, u32[]{:S(2)}, u32[]{:S(2)}) collective-permute-start(bf16[512,128]{1,0:T(8,128)(2,1)S(1)} %get-tuple-element.124), channel_id=1, source_target_pairs={{0,3},{1,2},{2,1},{3,0},{4,7},{5,6},{6,5},{7,4},{32,35},{33,34},{3... | collective-permute-start | bytes 393224 | tf_op jit(solution)/shard_map/ppermute | solution.py:41
  41.9 2.8 %copy-done = bf16[1,256,12288]{2,1,0:T(8,128)(2,1)S(1)} copy-done((bf16[1,256,12288]{2,1,0:T(8,128)(2,1)S(1)}, bf16[1,256,12288]{2,1,0:T(8,128)(2,1)}, u32[]{:S(2)}) %copy-start) | copy-done | bytes 6291480
  44.7 2.6 %shard_map.114 = (bf16[256,128]{1,0:T(8,128)(2,1)S(1)}, bf16[3072,128]{1,0:T(8,128)(2,1)S(1)}, bf16[1536,128]{1,0:T(8,128)(2,1)S(1)}, bf16[1536,128]{1,0:T(8,128)(2,1)S(1)}, bf16[1536,128]{1,0:T(8,128)(2,1)S(1)}) custom-call(s32[37]{0:T(128)S(1)} %concatenate.7.table_ref, bf16[256,12288]{1,0:T(8,128)(2,1)S(1)} %bitcast.16, ...), custom_call_target="tpu_custom_call" | custom-call | bytes 12582912 | tf_op jit(solution)/shard_map/pallas_call | solution.py:288
  47.4 2.0 %collective-permute-done.16 = bf16[512,128]{1,0:T(8,128)(2,1)S(1)} collective-permute-done((bf16[512,128]{1,0:T(8,128)(2,1)S(1)}, bf16[512,128]{1,0:T(8,128)(2,1)S(1)}, u32[]{:S(2)}, u32[]{:S(2)}) %collective-permute-start.16) | collective-permute-done | bytes 131104 | tf_op jit(solution)/shard_map/ppermute | solution.py:41
  49.4 1.5 %collective-permute-start.18 = (bf16[256,128]{1,0:T(8,128)(2,1)S(1)}, bf16[256,128]{1,0:T(8,128)(2,1)S(1)}, u32[]{:S(2)}, u32[]{:S(2)}) collective-permute-start(bf16[256,128]{1,0:T(8,128)(2,1)S(1)} %slice.96), channel_id=1, source_target_pairs={{0,4},{1,5},{2,6},{3,7},{4,0},{5,1},{6,2},{7,3},{32,36},{33,37},{3... | collective-permute-start | bytes 196616 | tf_op jit(solution)/shard_map/ppermute | solution.py:41
  51.0 0.6 collective-permute-start.17
  51.5 0.5 shard_map.115.term_ref
  52.0 2.4 %collective-permute-done.18 = bf16[256,128]{1,0:T(8,128)(2,1)S(1)} collective-permute-done((bf16[256,128]{1,0:T(8,128)(2,1)S(1)}, bf16[256,128]{1,0:T(8,128)(2,1)S(1)}, u32[]{:S(2)}, u32[]{:S(2)}) %collective-permute-start.18) | collective-permute-done | bytes 65568 | tf_op jit(solution)/shard_map/ppermute | solution.py:41
  54.4 0.8 collective-permute-done.17.refs_0_
  55.3 1.9 %shard_map.117 = (f32[2048,384]{1,0:T(8,128)S(1)}, bf16[2048,384]{1,0:T(8,128)(2,1)S(1)}, bf16[1792,128]{1,0:T(8,128)(2,1)S(1)}, bf16[1792,128]{1,0:T(8,128)(2,1)S(1)}, bf16[1792,128]{1,0:T(8,128)(2,1)S(1)}) custom-call(s32[37]{0:T(128)S(1)} %concatenate.7.table_ref, bf16[256,12288]{1,0:T(8,128)(2,1)S(1)} %bitcast.17, ...), custom_call_target="tpu_custom_call" | custom-call | bytes 12582912 | tf_op jit(solution)/shard_map/pallas_call | solution.py:288
  57.2 1.7 %collective-permute-start.23 = (bf16[1792,128]{1,0:T(8,128)(2,1)S(1)}, bf16[1792,128]{1,0:T(8,128)(2,1)S(1)}, u32[]{:S(2)}, u32[]{:S(2)}) collective-permute-start(bf16[1792,128]{1,0:T(8,128)(2,1)S(1)} %get-tuple-element.142), channel_id=1, source_target_pairs={{0,8},{8,0},{16,24},{24,16},{1,9},{9,1},{17,25},{25,17},{2,10},{10... | collective-permute-start | bytes 1376264 | tf_op jit(solution)/shard_map/ppermute | solution.py:65
  58.9 2.2 %collective-permute-start.24 = (bf16[1792,128]{1,0:T(8,128)(2,1)S(1)}, bf16[1792,128]{1,0:T(8,128)(2,1)S(1)}, u32[]{:S(2)}, u32[]{:S(2)}) collective-permute-start(bf16[1792,128]{1,0:T(8,128)(2,1)S(1)} %get-tuple-element.144), channel_id=1, source_target_pairs={{0,24},{8,16},{16,8},{24,0},{1,25},{9,17},{17,9},{25,1},{2,26},{10... | collective-permute-start | bytes 1376264 | tf_op jit(solution)/shard_map/ppermute | solution.py:65
  61.2 3.4 %collective-permute-start.20 = (bf16[512,128]{1,0:T(8,128)(2,1)S(1)}, bf16[512,128]{1,0:T(8,128)(2,1)S(1)}, u32[]{:S(2)}, u32[]{:S(2)}) collective-permute-start(bf16[512,128]{1,0:T(8,128)(2,1)S(1)} %shard_map.116.v0), channel_id=1, source_target_pairs={{0,2},{1,3},{2,0},{3,1},{4,6},{5,7},{6,4},{7,5},{32,34},{33,35},{3... | collective-permute-start | bytes 393224 | tf_op jit(solution)/shard_map/ppermute | solution.py:41
  64.6 1.3 %collective-permute-start.21 = (bf16[512,128]{1,0:T(8,128)(2,1)S(1)}, bf16[512,128]{1,0:T(8,128)(2,1)S(1)}, u32[]{:S(2)}, u32[]{:S(2)}) collective-permute-start(bf16[512,128]{1,0:T(8,128)(2,1)S(1)} %shard_map.116.v0), channel_id=1, source_target_pairs={{0,3},{1,2},{2,1},{3,0},{4,7},{5,6},{6,5},{7,4},{32,35},{33,34},{3... | collective-permute-start | bytes 393224 | tf_op jit(solution)/shard_map/ppermute | solution.py:41
  65.9 0.4 add_convert_fusion
  66.3 1.3 %collective-permute-done.19.v1 = bf16[512,128]{1,0:T(8,128)(2,1)S(1)} collective-permute-done((bf16[512,128]{1,0:T(8,128)(2,1)S(1)}, bf16[512,128]{1,0:T(8,128)(2,1)S(1)}, u32[]{:S(2)}, u32[]{:S(2)}) %collective-permute-start.19) | collective-permute-done | bytes 131104 | tf_op jit(solution)/shard_map/ppermute | solution.py:41
  67.6 3.2 %collective-permute-done.20.v2 = bf16[512,128]{1,0:T(8,128)(2,1)S(1)} collective-permute-done((bf16[512,128]{1,0:T(8,128)(2,1)S(1)}, bf16[512,128]{1,0:T(8,128)(2,1)S(1)}, u32[]{:S(2)}, u32[]{:S(2)}) %collective-permute-start.20) | collective-permute-done | bytes 131104 | tf_op jit(solution)/shard_map/ppermute | solution.py:41
  70.8 2.1 %collective-permute-done.21.v3 = bf16[512,128]{1,0:T(8,128)(2,1)S(1)} collective-permute-done((bf16[512,128]{1,0:T(8,128)(2,1)S(1)}, bf16[512,128]{1,0:T(8,128)(2,1)S(1)}, u32[]{:S(2)}, u32[]{:S(2)}) %collective-permute-start.21) | collective-permute-done | bytes 131104 | tf_op jit(solution)/shard_map/ppermute | solution.py:41
  72.9 0.8 collective-permute-start.25
  73.7 2.3 %collective-permute-start.26 = (bf16[512,384]{1,0:T(8,128)(2,1)S(1)}, bf16[512,384]{1,0:T(8,128)(2,1)S(1)}, u32[]{:S(2)}, u32[]{:S(2)}) collective-permute-start(bf16[512,384]{1,0:T(8,128)(2,1)S(1)} %get-tuple-element.156), channel_id=1, source_target_pairs={{0,64},{1,65},{2,66},{3,67},{4,68},{5,69},{6,70},{7,71},{32,34},{3... | collective-permute-start | bytes 1179656 | tf_op jit(solution)/shard_map/ppermute | solution.py:41
  76.0 1.5 %collective-permute-start.27 = (bf16[512,384]{1,0:T(8,128)(2,1)S(1)}, bf16[512,384]{1,0:T(8,128)(2,1)S(1)}, u32[]{:S(2)}, u32[]{:S(2)}) collective-permute-start(bf16[512,384]{1,0:T(8,128)(2,1)S(1)} %get-tuple-element.157), channel_id=1, source_target_pairs={{0,68},{1,69},{2,70},{3,71},{4,64},{5,65},{6,66},{7,67},{32,35},{3... | collective-permute-start | bytes 1179656 | tf_op jit(solution)/shard_map/ppermute | solution.py:41
  77.6 1.5 %collective-permute-start.28 = (bf16[1792,128]{1,0:T(8,128)(2,1)S(1)}, bf16[1792,128]{1,0:T(8,128)(2,1)S(1)}, u32[]{:S(2)}, u32[]{:S(2)}) collective-permute-start(bf16[1792,128]{1,0:T(8,128)(2,1)S(1)} %get-tuple-element.159), channel_id=1, source_target_pairs={{0,16},{8,24},{16,0},{24,8},{1,17},{9,25},{17,1},{25,9},{2,18},{10... | collective-permute-start | bytes 1376264 | tf_op jit(solution)/shard_map/ppermute | solution.py:65
  79.1 1.6 %collective-permute-done.25 = bf16[512,384]{1,0:T(8,128)(2,1)S(1)} collective-permute-done((bf16[512,384]{1,0:T(8,128)(2,1)S(1)}, bf16[512,384]{1,0:T(8,128)(2,1)S(1)}, u32[]{:S(2)}, u32[]{:S(2)}) %collective-permute-start.25) | collective-permute-done | bytes 393248 | tf_op jit(solution)/shard_map/ppermute | solution.py:41
  80.7 8.4 %shard_map.118 = (bf16[256,1536]{1,0:T(8,128)(2,1)}, f32[512,128]{1,0:T(8,128)S(1)}, bf16[512,128]{1,0:T(8,128)(2,1)S(1)}, bf16[512,128]{1,0:T(8,128)(2,1)S(1)}, bf16[512,128]{1,0:T(8,128)(2,1)S(1)}) custom-call(s32[18]{0:T(128)S(1)} %pad_add_fusion.table_ref, s32[16,128]{1,0:T(8,128)S(1)} %bitcast.27, bf16[256,1536]{1,0:T(8,128)(2,1)S(1)} %bitcast.22, ...), custom_call_target="tpu_custom_call" | custom-call | bytes 28311552 | tf_op jit(solution)/shard_map/pallas_call | solution.py:288
  89.1 0.1 collective-permute-done.27
  89.2 0.2 convert_add_fusion
  89.4 0.6 collective-permute-done.28.a2
  90.1 3.2 %collective-permute-start.32 = (bf16[512,128]{1,0:T(8,128)(2,1)S(1)}, bf16[512,128]{1,0:T(8,128)(2,1)S(1)}, u32[]{:S(2)}, u32[]{:S(2)}) collective-permute-start(bf16[512,128]{1,0:T(8,128)(2,1)S(1)} %get-tuple-element.162), channel_id=1, source_target_pairs={{0,2},{1,3},{2,0},{3,1},{4,6},{5,7},{6,4},{7,5},{32,34},{33,35},{3... | collective-permute-start | bytes 393224 | tf_op jit(solution)/shard_map/ppermute | solution.py:41
  93.3 1.5 %collective-permute-start.33 = (bf16[512,128]{1,0:T(8,128)(2,1)S(1)}, bf16[512,128]{1,0:T(8,128)(2,1)S(1)}, u32[]{:S(2)}, u32[]{:S(2)}) collective-permute-start(bf16[512,128]{1,0:T(8,128)(2,1)S(1)} %get-tuple-element.163), channel_id=1, source_target_pairs={{0,3},{1,2},{2,1},{3,0},{4,7},{5,6},{6,5},{7,4},{32,35},{33,34},{3... | collective-permute-start | bytes 393224 | tf_op jit(solution)/shard_map/ppermute | solution.py:41
  95.0 1.4 %collective-permute-done.31 = bf16[512,128]{1,0:T(8,128)(2,1)S(1)} collective-permute-done((bf16[512,128]{1,0:T(8,128)(2,1)S(1)}, bf16[512,128]{1,0:T(8,128)(2,1)S(1)}, u32[]{:S(2)}, u32[]{:S(2)}) %collective-permute-start.31) | collective-permute-done | bytes 131104 | tf_op jit(solution)/shard_map/ppermute | solution.py:41
  96.4 1.7 %collective-permute-start.37 = (bf16[128,384]{1,0:T(8,128)(2,1)S(1)}, bf16[128,384]{1,0:T(8,128)(2,1)S(1)}, u32[]{:S(2)}, u32[]{:S(2)}) collective-permute-start(bf16[128,384]{1,0:T(8,128)(2,1)S(1)} %get-tuple-element.187), channel_id=1, source_target_pairs={{0,2},{1,3},{2,0},{3,1},{4,6},{5,7},{6,4},{7,5},{32,96},{33,97},{3... | collective-permute-start | bytes 294920 | tf_op jit(solution)/shard_map/ppermute | solution.py:41
  98.1 1.9 %collective-permute-done.32 = bf16[512,128]{1,0:T(8,128)(2,1)S(1)} collective-permute-done((bf16[512,128]{1,0:T(8,128)(2,1)S(1)}, bf16[512,128]{1,0:T(8,128)(2,1)S(1)}, u32[]{:S(2)}, u32[]{:S(2)}) %collective-permute-start.32) | collective-permute-done | bytes 131104 | tf_op jit(solution)/shard_map/ppermute | solution.py:41
  100.0 1.5 %collective-permute-start.38 = (bf16[128,384]{1,0:T(8,128)(2,1)S(1)}, bf16[128,384]{1,0:T(8,128)(2,1)S(1)}, u32[]{:S(2)}, u32[]{:S(2)}) collective-permute-start(bf16[128,384]{1,0:T(8,128)(2,1)S(1)} %get-tuple-element.186), channel_id=1, source_target_pairs={{0,3},{1,2},{2,1},{3,0},{4,7},{5,6},{6,5},{7,4},{32,100},{33,101},... | collective-permute-start | bytes 294920 | tf_op jit(solution)/shard_map/ppermute | solution.py:41
  101.5 1.9 %collective-permute-done.33 = bf16[512,128]{1,0:T(8,128)(2,1)S(1)} collective-permute-done((bf16[512,128]{1,0:T(8,128)(2,1)S(1)}, bf16[512,128]{1,0:T(8,128)(2,1)S(1)}, u32[]{:S(2)}, u32[]{:S(2)}) %collective-permute-start.33) | collective-permute-done | bytes 131104 | tf_op jit(solution)/shard_map/ppermute | solution.py:41
  103.5 0.9 collective-permute-start.35
  104.5 3.4 %shard_map.119 = bf16[256,3072]{1,0:T(8,128)(2,1)} custom-call(s32[37]{0:T(128)S(1)} %concatenate.7.table_ref, bf16[256,128]{1,0:T(8,128)(2,1)S(1)} %add_convert_fusion.3.grads, bf16[3072,128]{1,0:T(8,128)(2,1)S(1)} %get-tuple-element.172.own, bf16[1792,128]{1,0:T(8,128)(2,1)S(1)} %collective-permute-done.23.a1, ...), custom_call_target="tpu_custom_call" | custom-call | bytes 12582912 | tf_op jit(solution)/shard_map/pallas_call | solution.py:288
  107.9 0.8 shard_map.120
  108.7 0.6 fusion.1
  (62 shorter events, 1.0 us)
Async XLA Ops:
  0.6 27.9 %copy-start.2 = (bf16[1,256,1536]{2,1,0:T(8,128)(2,1)S(1)}, bf16[1,256,1536]{2,1,0:T(8,128)(2,1)}, u32[]{:S(2)}) copy-start(bf16[1,256,1536]{2,1,0:T(8,128)(2,1)} %param.12) | copy-start | bytes 2359300
  0.6 10.1 %collective-permute-start.1 = (bf16[384,128]{1,0:T(8,128)(2,1)}, bf16[384,128]{1,0:T(8,128)(2,1)S(1)}, u32[]{:S(2)}, u32[]{:S(2)}) collective-permute-start(bf16[384,128]{1,0:T(8,128)(2,1)} %own), channel_id=1, source_target_pairs={{0,1},{1,0},{2,3},{3,2},{4,5},{5,4},{6,7},{7,6},{32,36},{33,37},{3... | collective-permute-start | bytes 294920 | tf_op jit(solution)/shard_map/ppermute | solution.py:41
  2.7 8.1 %collective-permute-start.2 = (bf16[384,128]{1,0:T(8,128)(2,1)}, bf16[384,128]{1,0:T(8,128)(2,1)S(1)}, u32[]{:S(2)}, u32[]{:S(2)}) collective-permute-start(bf16[384,128]{1,0:T(8,128)(2,1)} %own), channel_id=1, source_target_pairs={{0,2},{1,3},{2,0},{3,1},{4,6},{5,7},{6,4},{7,5},{32,96},{33,97},{3... | collective-permute-start | bytes 294920 | tf_op jit(solution)/shard_map/ppermute | solution.py:41
  6.3 6.0 %collective-permute-start.3 = (bf16[384,128]{1,0:T(8,128)(2,1)}, bf16[384,128]{1,0:T(8,128)(2,1)S(1)}, u32[]{:S(2)}, u32[]{:S(2)}) collective-permute-start(bf16[384,128]{1,0:T(8,128)(2,1)} %own), channel_id=1, source_target_pairs={{0,3},{1,2},{2,1},{3,0},{4,7},{5,6},{6,5},{7,4},{32,100},{33,101},... | collective-permute-start | bytes 294920 | tf_op jit(solution)/shard_map/ppermute | solution.py:41
  6.3 4.5 %collective-permute-start = (bf16[256,128]{1,0:T(8,128)(2,1)}, bf16[256,128]{1,0:T(8,128)(2,1)S(1)}, u32[]{:S(2)}, u32[]{:S(2)}) collective-permute-start(bf16[256,128]{1,0:T(8,128)(2,1)} %bitcast.24), channel_id=1, source_target_pairs={{0,4},{1,5},{2,6},{3,7},{4,0},{5,1},{6,2},{7,3},{32,36},{33,37},{3... | collective-permute-start | bytes 196616 | tf_op jit(solution)/shard_map/ppermute | solution.py:41
  12.3 0.9 copy-start.6
  13.4 14.2 %collective-permute-start.7 = (bf16[1536,128]{1,0:T(8,128)(2,1)S(1)}, bf16[1536,128]{1,0:T(8,128)(2,1)S(1)}, u32[]{:S(2)}, u32[]{:S(2)}) collective-permute-start(bf16[1536,128]{1,0:T(8,128)(2,1)S(1)} %shard_map.112.w0), channel_id=1, source_target_pairs={{0,4},{1,5},{2,6},{3,7},{4,0},{5,1},{6,2},{7,3},{32,33},{33,32},{3... | collective-permute-start | bytes 1179656 | tf_op jit(solution)/shard_map/ppermute | solution.py:41
  14.9 12.7 %collective-permute-start.8 = (bf16[1536,128]{1,0:T(8,128)(2,1)S(1)}, bf16[1536,128]{1,0:T(8,128)(2,1)S(1)}, u32[]{:S(2)}, u32[]{:S(2)}) collective-permute-start(bf16[1536,128]{1,0:T(8,128)(2,1)S(1)} %shard_map.112.w0), channel_id=1, source_target_pairs={{0,68},{1,69},{2,70},{3,71},{4,64},{5,65},{6,66},{7,67},{32,35},{3... | collective-permute-start | bytes 1179656 | tf_op jit(solution)/shard_map/ppermute | solution.py:41
  17.0 0.8 copy-start.7
  17.9 6.6 %collective-permute-start.4 = (bf16[512,128]{1,0:T(8,128)(2,1)S(1)}, bf16[512,128]{1,0:T(8,128)(2,1)S(1)}, u32[]{:S(2)}, u32[]{:S(2)}) collective-permute-start(bf16[512,128]{1,0:T(8,128)(2,1)S(1)} %shard_map.111.k0), channel_id=1, source_target_pairs={{0,1},{1,0},{2,3},{3,2},{4,5},{5,4},{6,7},{7,6},{32,33},{33,32},{3... | collective-permute-start | bytes 393224 | tf_op jit(solution)/shard_map/ppermute | solution.py:41
  18.0 8.2 %collective-permute-start.5 = (bf16[512,128]{1,0:T(8,128)(2,1)S(1)}, bf16[512,128]{1,0:T(8,128)(2,1)S(1)}, u32[]{:S(2)}, u32[]{:S(2)}) collective-permute-start(bf16[512,128]{1,0:T(8,128)(2,1)S(1)} %shard_map.111.k0), channel_id=1, source_target_pairs={{0,2},{1,3},{2,0},{3,1},{4,6},{5,7},{6,4},{7,5},{32,34},{33,35},{3... | collective-permute-start | bytes 393224 | tf_op jit(solution)/shard_map/ppermute | solution.py:41
  21.2 6.4 %collective-permute-start.6 = (bf16[512,128]{1,0:T(8,128)(2,1)S(1)}, bf16[512,128]{1,0:T(8,128)(2,1)S(1)}, u32[]{:S(2)}, u32[]{:S(2)}) collective-permute-start(bf16[512,128]{1,0:T(8,128)(2,1)S(1)} %shard_map.111.k0), channel_id=1, source_target_pairs={{0,3},{1,2},{2,1},{3,0},{4,7},{5,6},{6,5},{7,4},{32,35},{33,34},{3... | collective-permute-start | bytes 393224 | tf_op jit(solution)/shard_map/ppermute | solution.py:41
  27.6 9.4 %collective-permute-start.10 = (bf16[1536,128]{1,0:T(8,128)(2,1)S(1)}, bf16[1536,128]{1,0:T(8,128)(2,1)S(1)}, u32[]{:S(2)}, u32[]{:S(2)}) collective-permute-start(bf16[1536,128]{1,0:T(8,128)(2,1)S(1)} %shard_map.112.w0), channel_id=1, source_target_pairs={{0,32},{1,33},{2,34},{3,35},{4,36},{5,37},{6,38},{7,39},{32,0},{33... | collective-permute-start | bytes 1179656 | tf_op jit(solution)/shard_map/ppermute | solution.py:41
  27.6 9.4 %collective-permute-start.11 = (bf16[1536,128]{1,0:T(8,128)(2,1)S(1)}, bf16[1536,128]{1,0:T(8,128)(2,1)S(1)}, u32[]{:S(2)}, u32[]{:S(2)}) collective-permute-start(bf16[1536,128]{1,0:T(8,128)(2,1)S(1)} %collective-permute-done.7.w1), channel_id=1, source_target_pairs={{0,32},{1,33},{2,34},{3,35},{4,36},{5,37},{6,38},{7,39},{32,0},{33... | collective-permute-start | bytes 1179656 | tf_op jit(solution)/shard_map/ppermute | solution.py:41
  28.1 8.9 %collective-permute-start.12 = (bf16[1536,128]{1,0:T(8,128)(2,1)S(1)}, bf16[1536,128]{1,0:T(8,128)(2,1)S(1)}, u32[]{:S(2)}, u32[]{:S(2)}) collective-permute-start(bf16[1536,128]{1,0:T(8,128)(2,1)S(1)} %collective-permute-done.8.w3), channel_id=1, source_target_pairs={{0,32},{1,33},{2,34},{3,35},{4,36},{5,37},{6,38},{7,39},{32,0},{33... | collective-permute-start | bytes 1179656 | tf_op jit(solution)/shard_map/ppermute | solution.py:41
  28.2 8.9 %collective-permute-start.9 = (bf16[1536,128]{1,0:T(8,128)(2,1)S(1)}, bf16[1536,128]{1,0:T(8,128)(2,1)S(1)}, u32[]{:S(2)}, u32[]{:S(2)}) collective-permute-start(bf16[1536,128]{1,0:T(8,128)(2,1)S(1)} %collective-permute-done.8.w3), channel_id=1, source_target_pairs={{0,4},{1,5},{2,6},{3,7},{4,0},{5,1},{6,2},{7,3},{32,33},{33,32},{3... | collective-permute-start | bytes 1179656 | tf_op jit(solution)/shard_map/ppermute | solution.py:41
  28.6 1.1 %copy-start.3 = (bf16[1,256,1536]{2,1,0:T(8,128)(2,1)S(1)}, bf16[1,256,1536]{2,1,0:T(8,128)(2,1)}, u32[]{:S(2)}) copy-start(bf16[1,256,1536]{2,1,0:T(8,128)(2,1)} %param.9) | copy-start | bytes 2359300
  29.7 0.7 copy-start.8
  37.1 4.9 %collective-permute-start.13 = (bf16[1536,128]{1,0:T(8,128)(2,1)S(1)}, bf16[1536,128]{1,0:T(8,128)(2,1)S(1)}, u32[]{:S(2)}, u32[]{:S(2)}) collective-permute-start(bf16[1536,128]{1,0:T(8,128)(2,1)S(1)} %collective-permute-done.9.w2), channel_id=1, source_target_pairs={{0,32},{1,33},{2,34},{3,35},{4,36},{5,37},{6,38},{7,39},{32,0},{33... | collective-permute-start | bytes 1179656 | tf_op jit(solution)/shard_map/ppermute | solution.py:41
  37.2 10.2 %collective-permute-start.14 = (bf16[512,128]{1,0:T(8,128)(2,1)S(1)}, bf16[512,128]{1,0:T(8,128)(2,1)S(1)}, u32[]{:S(2)}, u32[]{:S(2)}) collective-permute-start(bf16[512,128]{1,0:T(8,128)(2,1)S(1)} %get-tuple-element.122), channel_id=1, source_target_pairs={{0,1},{1,0},{2,3},{3,2},{4,5},{5,4},{6,7},{7,6},{32,33},{33,32},{3... | collective-permute-start | bytes 393224 | tf_op jit(solution)/shard_map/ppermute | solution.py:41
  39.0 8.4 %collective-permute-start.15 = (bf16[512,128]{1,0:T(8,128)(2,1)S(1)}, bf16[512,128]{1,0:T(8,128)(2,1)S(1)}, u32[]{:S(2)}, u32[]{:S(2)}) collective-permute-start(bf16[512,128]{1,0:T(8,128)(2,1)S(1)} %get-tuple-element.123), channel_id=1, source_target_pairs={{0,2},{1,3},{2,0},{3,1},{4,6},{5,7},{6,4},{7,5},{32,34},{33,35},{3... | collective-permute-start | bytes 393224 | tf_op jit(solution)/shard_map/ppermute | solution.py:41
  40.2 9.1 %collective-permute-start.16 = (bf16[512,128]{1,0:T(8,128)(2,1)S(1)}, bf16[512,128]{1,0:T(8,128)(2,1)S(1)}, u32[]{:S(2)}, u32[]{:S(2)}) collective-permute-start(bf16[512,128]{1,0:T(8,128)(2,1)S(1)} %get-tuple-element.124), channel_id=1, source_target_pairs={{0,3},{1,2},{2,1},{3,0},{4,7},{5,6},{6,5},{7,4},{32,35},{33,34},{3... | collective-permute-start | bytes 393224 | tf_op jit(solution)/shard_map/ppermute | solution.py:41
  41.9 2.8 %copy-start = (bf16[1,256,12288]{2,1,0:T(8,128)(2,1)S(1)}, bf16[1,256,12288]{2,1,0:T(8,128)(2,1)}, u32[]{:S(2)}) copy-start(bf16[1,256,12288]{2,1,0:T(8,128)(2,1)} %param.8) | copy-start | bytes 18874372
  44.7 10.5 %copy-start.1 = (bf16[1,256,12288]{2,1,0:T(8,128)(2,1)S(1)}, bf16[1,256,12288]{2,1,0:T(8,128)(2,1)}, u32[]{:S(2)}) copy-start(bf16[1,256,12288]{2,1,0:T(8,128)(2,1)} %param.8) | copy-start | bytes 18874372
  47.4 4.2 %copy-start.5 = (bf16[1,256,1536]{2,1,0:T(8,128)(2,1)S(1)}, bf16[1,256,1536]{2,1,0:T(8,128)(2,1)}, u32[]{:S(2)}) copy-start(bf16[1,256,1536]{2,1,0:T(8,128)(2,1)} %param.13) | copy-start | bytes 2359300
  49.4 4.9 %collective-permute-start.18 = (bf16[256,128]{1,0:T(8,128)(2,1)S(1)}, bf16[256,128]{1,0:T(8,128)(2,1)S(1)}, u32[]{:S(2)}, u32[]{:S(2)}) collective-permute-start(bf16[256,128]{1,0:T(8,128)(2,1)S(1)} %slice.96), channel_id=1, source_target_pairs={{0,4},{1,5},{2,6},{3,7},{4,0},{5,1},{6,2},{7,3},{32,36},{33,37},{3... | collective-permute-start | bytes 196616 | tf_op jit(solution)/shard_map/ppermute | solution.py:41
  51.0 4.3 %collective-permute-start.17 = (bf16[256,128]{1,0:T(8,128)(2,1)S(1)}, bf16[256,128]{1,0:T(8,128)(2,1)S(1)}, u32[]{:S(2)}, u32[]{:S(2)}) collective-permute-start(bf16[256,128]{1,0:T(8,128)(2,1)S(1)} %get-tuple-element.133.own), channel_id=1, source_target_pairs={{0,4},{1,5},{2,6},{3,7},{4,0},{5,1},{6,2},{7,3},{32,36},{33,37},{3... | collective-permute-start | bytes 196616 | tf_op jit(solution)/shard_map/ppermute | solution.py:41
  57.1 7.5 %collective-permute-start.22 = (bf16[2048,384]{1,0:T(8,128)(2,1)S(1)}, bf16[2048,384]{1,0:T(8,128)(2,1)S(1)}, u32[]{:S(2)}, u32[]{:S(2)}) collective-permute-start(bf16[2048,384]{1,0:T(8,128)(2,1)S(1)} %get-tuple-element.141), channel_id=1, source_target_pairs={{0,32},{1,33},{2,34},{3,35},{4,36},{5,37},{6,38},{7,39},{32,0},{33... | collective-permute-start | bytes 4718600 | tf_op jit(solution)/shard_map/ppermute | solution.py:41
  57.2 15.6 %collective-permute-start.23 = (bf16[1792,128]{1,0:T(8,128)(2,1)S(1)}, bf16[1792,128]{1,0:T(8,128)(2,1)S(1)}, u32[]{:S(2)}, u32[]{:S(2)}) collective-permute-start(bf16[1792,128]{1,0:T(8,128)(2,1)S(1)} %get-tuple-element.142), channel_id=1, source_target_pairs={{0,8},{8,0},{16,24},{24,16},{1,9},{9,1},{17,25},{25,17},{2,10},{10... | collective-permute-start | bytes 1376264 | tf_op jit(solution)/shard_map/ppermute | solution.py:65
  58.9 14.0 %collective-permute-start.24 = (bf16[1792,128]{1,0:T(8,128)(2,1)S(1)}, bf16[1792,128]{1,0:T(8,128)(2,1)S(1)}, u32[]{:S(2)}, u32[]{:S(2)}) collective-permute-start(bf16[1792,128]{1,0:T(8,128)(2,1)S(1)} %get-tuple-element.144), channel_id=1, source_target_pairs={{0,24},{8,16},{16,8},{24,0},{1,25},{9,17},{17,9},{25,1},{2,26},{10... | collective-permute-start | bytes 1376264 | tf_op jit(solution)/shard_map/ppermute | solution.py:65
  61.1 6.5 %collective-permute-start.19 = (bf16[512,128]{1,0:T(8,128)(2,1)S(1)}, bf16[512,128]{1,0:T(8,128)(2,1)S(1)}, u32[]{:S(2)}, u32[]{:S(2)}) collective-permute-start(bf16[512,128]{1,0:T(8,128)(2,1)S(1)} %shard_map.116.v0), channel_id=1, source_target_pairs={{0,1},{1,0},{2,3},{3,2},{4,5},{5,4},{6,7},{7,6},{32,33},{33,32},{3... | collective-permute-start | bytes 393224 | tf_op jit(solution)/shard_map/ppermute | solution.py:41
  61.2 9.6 %collective-permute-start.20 = (bf16[512,128]{1,0:T(8,128)(2,1)S(1)}, bf16[512,128]{1,0:T(8,128)(2,1)S(1)}, u32[]{:S(2)}, u32[]{:S(2)}) collective-permute-start(bf16[512,128]{1,0:T(8,128)(2,1)S(1)} %shard_map.116.v0), channel_id=1, source_target_pairs={{0,2},{1,3},{2,0},{3,1},{4,6},{5,7},{6,4},{7,5},{32,34},{33,35},{3... | collective-permute-start | bytes 393224 | tf_op jit(solution)/shard_map/ppermute | solution.py:41
  64.6 8.2 %collective-permute-start.21 = (bf16[512,128]{1,0:T(8,128)(2,1)S(1)}, bf16[512,128]{1,0:T(8,128)(2,1)S(1)}, u32[]{:S(2)}, u32[]{:S(2)}) collective-permute-start(bf16[512,128]{1,0:T(8,128)(2,1)S(1)} %shard_map.116.v0), channel_id=1, source_target_pairs={{0,3},{1,2},{2,1},{3,0},{4,7},{5,6},{6,5},{7,4},{32,35},{33,34},{3... | collective-permute-start | bytes 393224 | tf_op jit(solution)/shard_map/ppermute | solution.py:41
  65.9 14.7 %copy-start.4 = (bf16[1,256,1536]{2,1,0:T(8,128)(2,1)S(1)}, bf16[1,256,1536]{2,1,0:T(8,128)(2,1)}, u32[]{:S(2)}) copy-start(bf16[1,256,1536]{2,1,0:T(8,128)(2,1)} %param.9) | copy-start | bytes 2359300
  65.9 14.7 %copy-start.9 = (s32[1,2048]{1,0:T(1,128)S(1)}, s32[1,2048]{1,0:T(1,128)}, u32[]{:S(2)}) copy-start(s32[1,2048]{1,0:T(1,128)} %param.14) | copy-start | bytes 24580
  72.9 7.8 %collective-permute-start.25 = (bf16[512,384]{1,0:T(8,128)(2,1)S(1)}, bf16[512,384]{1,0:T(8,128)(2,1)S(1)}, u32[]{:S(2)}, u32[]{:S(2)}) collective-permute-start(bf16[512,384]{1,0:T(8,128)(2,1)S(1)} %get-tuple-element.155), channel_id=1, source_target_pairs={{0,4},{1,5},{2,6},{3,7},{4,0},{5,1},{6,2},{7,3},{32,33},{33,32},{3... | collective-permute-start | bytes 1179656 | tf_op jit(solution)/shard_map/ppermute | solution.py:41
  73.7 15.4 %collective-permute-start.26 = (bf16[512,384]{1,0:T(8,128)(2,1)S(1)}, bf16[512,384]{1,0:T(8,128)(2,1)S(1)}, u32[]{:S(2)}, u32[]{:S(2)}) collective-permute-start(bf16[512,384]{1,0:T(8,128)(2,1)S(1)} %get-tuple-element.156), channel_id=1, source_target_pairs={{0,64},{1,65},{2,66},{3,67},{4,68},{5,69},{6,70},{7,71},{32,34},{3... | collective-permute-start | bytes 1179656 | tf_op jit(solution)/shard_map/ppermute | solution.py:41
  76.0 13.2 %collective-permute-start.27 = (bf16[512,384]{1,0:T(8,128)(2,1)S(1)}, bf16[512,384]{1,0:T(8,128)(2,1)S(1)}, u32[]{:S(2)}, u32[]{:S(2)}) collective-permute-start(bf16[512,384]{1,0:T(8,128)(2,1)S(1)} %get-tuple-element.157), channel_id=1, source_target_pairs={{0,68},{1,69},{2,70},{3,71},{4,64},{5,65},{6,66},{7,67},{32,35},{3... | collective-permute-start | bytes 1179656 | tf_op jit(solution)/shard_map/ppermute | solution.py:41
  77.6 12.4 %collective-permute-start.28 = (bf16[1792,128]{1,0:T(8,128)(2,1)S(1)}, bf16[1792,128]{1,0:T(8,128)(2,1)S(1)}, u32[]{:S(2)}, u32[]{:S(2)}) collective-permute-start(bf16[1792,128]{1,0:T(8,128)(2,1)S(1)} %get-tuple-element.159), channel_id=1, source_target_pairs={{0,16},{8,24},{16,0},{24,8},{1,17},{9,25},{17,1},{25,9},{2,18},{10... | collective-permute-start | bytes 1376264 | tf_op jit(solution)/shard_map/ppermute | solution.py:65
  79.1 10.9 %collective-permute-start.29 = (bf16[1792,128]{1,0:T(8,128)(2,1)S(1)}, bf16[1792,128]{1,0:T(8,128)(2,1)S(1)}, u32[]{:S(2)}, u32[]{:S(2)}) collective-permute-start(bf16[1792,128]{1,0:T(8,128)(2,1)S(1)} %collective-permute-done.23.a1), channel_id=1, source_target_pairs={{0,32},{1,33},{2,34},{3,35},{4,36},{5,37},{6,38},{7,39},{32,0},{33... | collective-permute-start | bytes 1376264 | tf_op jit(solution)/shard_map/ppermute | solution.py:41
  80.7 9.3 %collective-permute-start.30 = (bf16[1792,128]{1,0:T(8,128)(2,1)S(1)}, bf16[1792,128]{1,0:T(8,128)(2,1)S(1)}, u32[]{:S(2)}, u32[]{:S(2)}) collective-permute-start(bf16[1792,128]{1,0:T(8,128)(2,1)S(1)} %collective-permute-done.24.a3), channel_id=1, source_target_pairs={{0,32},{1,33},{2,34},{3,35},{4,36},{5,37},{6,38},{7,39},{32,0},{33... | collective-permute-start | bytes 1376264 | tf_op jit(solution)/shard_map/ppermute | solution.py:41
  90.0 13.5 %collective-permute-start.34 = (bf16[1792,128]{1,0:T(8,128)(2,1)S(1)}, bf16[1792,128]{1,0:T(8,128)(2,1)S(1)}, u32[]{:S(2)}, u32[]{:S(2)}) collective-permute-start(bf16[1792,128]{1,0:T(8,128)(2,1)S(1)} %collective-permute-done.28.a2), channel_id=1, source_target_pairs={{0,32},{1,33},{2,34},{3,35},{4,36},{5,37},{6,38},{7,39},{32,0},{33... | collective-permute-start | bytes 1376264 | tf_op jit(solution)/shard_map/ppermute | solution.py:41
  90.0 6.4 %collective-permute-start.31 = (bf16[512,128]{1,0:T(8,128)(2,1)S(1)}, bf16[512,128]{1,0:T(8,128)(2,1)S(1)}, u32[]{:S(2)}, u32[]{:S(2)}) collective-permute-start(bf16[512,128]{1,0:T(8,128)(2,1)S(1)} %get-tuple-element.161), channel_id=1, source_target_pairs={{0,1},{1,0},{2,3},{3,2},{4,5},{5,4},{6,7},{7,6},{32,33},{33,32},{3... | collective-permute-start | bytes 393224 | tf_op jit(solution)/shard_map/ppermute | solution.py:41
  90.1 9.9 %collective-permute-start.32 = (bf16[512,128]{1,0:T(8,128)(2,1)S(1)}, bf16[512,128]{1,0:T(8,128)(2,1)S(1)}, u32[]{:S(2)}, u32[]{:S(2)}) collective-permute-start(bf16[512,128]{1,0:T(8,128)(2,1)S(1)} %get-tuple-element.162), channel_id=1, source_target_pairs={{0,2},{1,3},{2,0},{3,1},{4,6},{5,7},{6,4},{7,5},{32,34},{33,35},{3... | collective-permute-start | bytes 393224 | tf_op jit(solution)/shard_map/ppermute | solution.py:41
  93.3 10.2 %collective-permute-start.33 = (bf16[512,128]{1,0:T(8,128)(2,1)S(1)}, bf16[512,128]{1,0:T(8,128)(2,1)S(1)}, u32[]{:S(2)}, u32[]{:S(2)}) collective-permute-start(bf16[512,128]{1,0:T(8,128)(2,1)S(1)} %get-tuple-element.163), channel_id=1, source_target_pairs={{0,3},{1,2},{2,1},{3,0},{4,7},{5,6},{6,5},{7,4},{32,35},{33,34},{3... | collective-permute-start | bytes 393224 | tf_op jit(solution)/shard_map/ppermute | solution.py:41
  94.9 13.0 %collective-permute-start.36 = (bf16[128,384]{1,0:T(8,128)(2,1)S(1)}, bf16[128,384]{1,0:T(8,128)(2,1)S(1)}, u32[]{:S(2)}, u32[]{:S(2)}) collective-permute-start(bf16[128,384]{1,0:T(8,128)(2,1)S(1)} %get-tuple-element.188), channel_id=1, source_target_pairs={{0,1},{1,0},{2,3},{3,2},{4,5},{5,4},{6,7},{7,6},{32,36},{33,37},{3... | collective-permute-start | bytes 294920 | tf_op jit(solution)/shard_map/ppermute | solution.py:41
  96.4 11.5 %collective-permute-start.37 = (bf16[128,384]{1,0:T(8,128)(2,1)S(1)}, bf16[128,384]{1,0:T(8,128)(2,1)S(1)}, u32[]{:S(2)}, u32[]{:S(2)}) collective-permute-start(bf16[128,384]{1,0:T(8,128)(2,1)S(1)} %get-tuple-element.187), channel_id=1, source_target_pairs={{0,2},{1,3},{2,0},{3,1},{4,6},{5,7},{6,4},{7,5},{32,96},{33,97},{3... | collective-permute-start | bytes 294920 | tf_op jit(solution)/shard_map/ppermute | solution.py:41
  100.0 7.9 %collective-permute-start.38 = (bf16[128,384]{1,0:T(8,128)(2,1)S(1)}, bf16[128,384]{1,0:T(8,128)(2,1)S(1)}, u32[]{:S(2)}, u32[]{:S(2)}) collective-permute-start(bf16[128,384]{1,0:T(8,128)(2,1)S(1)} %get-tuple-element.186), channel_id=1, source_target_pairs={{0,3},{1,2},{2,1},{3,0},{4,7},{5,6},{6,5},{7,4},{32,100},{33,101},... | collective-permute-start | bytes 294920 | tf_op jit(solution)/shard_map/ppermute | solution.py:41
  103.5 5.2 %collective-permute-start.35 = (bf16[256,128]{1,0:T(8,128)(2,1)S(1)}, bf16[256,128]{1,0:T(8,128)(2,1)S(1)}, u32[]{:S(2)}, u32[]{:S(2)}) collective-permute-start(bf16[256,128]{1,0:T(8,128)(2,1)S(1)} %slice.95), channel_id=1, source_target_pairs={{0,4},{1,5},{2,6},{3,7},{4,0},{5,1},{6,2},{7,3},{32,36},{33,37},{3... | collective-permute-start | bytes 196616 | tf_op jit(solution)/shard_map/ppermute | solution.py:41

commit v3 on v2

--- a/solution.py
+++ b/solution.py
@@ -147,16 +147,25 @@
 
 
 def value_side_kernel(
-    table_ref, doc_ref, q_ref, g_ref, k0, k1, k2, k3,
+    table_ref, doc_ref, q_any, g_any, k0, k1, k2, k3,
     total_ref, o0, o1, o2, o3,
-    all_ref, win_ref, bias_ref, score_ref, raised_ref, scaled_ref, acc_ref, sum_ref,
+    q_ref, g_ref, all_ref, win_ref, bias_ref, score_ref, raised_ref, scaled_ref, acc_ref, sum_ref, sems,
 ):
+    copies = [
+        pltpu.make_async_copy(q_any, q_ref, sems.at[0]),
+        pltpu.make_async_copy(g_any, g_ref, sems.at[1]),
+    ]
+    for copy in copies:
+        copy.start()
     join((k0, k1, k2, k3), all_ref)
     sum_ref[...] = jnp.zeros_like(sum_ref)
     for a in range(2):
         place = table_ref[16 + a]
         fill_bias(place, doc_ref, bias_ref)
         fill_window(table_ref, place, all_ref, win_ref)
+        if a == 0:
+            for copy in copies:
+                copy.wait()
         for pair in range(PAIRS):
             cols = slice(pair * 256, (pair + 1) * 256)
             products = nt(win_ref[...], stacked(q_ref, a, pair))
@@ -231,16 +240,32 @@
 
 
 def project_kernel(
-    table_ref, hidden, w0, w1, w2, w3, s0, s1, s2, s3, out, own_rows, r1, r2, r3, all_ref
+    table_ref, hidden, w0, w1, w2, w3, s0, s1, s2, s3,
+    out, own_rows, r1, r2, r3, hidden_ref, all_ref, sems,
 ):
+    copies = [
+        pltpu.make_async_copy(
+            hidden.at[:, i * QUARTER : (i + 1) * QUARTER],
+            hidden_ref.at[:, i * QUARTER : (i + 1) * QUARTER],
+            sems.at[i],
+        )
+        for i in range(4)
+    ]
+    for copy in copies:
+        copy.start()
     for k, w in enumerate((w0, w1, w2, w3, s0, s1, s2, s3)):
         for i in range(4):
             at = pl.multiple_of(table_ref[k * 4 + i] * SLAB, BLOCK)
             all_ref[pl.ds(at, SLAB), :] = w[i * SLAB : (i + 1) * SLAB, :]
-    out[...] = nn(hidden[...], all_ref[...]).astype(bf16)
     own_rows[...] = all_ref[pl.ds(pl.multiple_of(table_ref[32] * QUARTER, BLOCK), QUARTER), :]
     for d, r in enumerate((r1, r2, r3)):
         r[...] = all_ref[pl.ds(pl.multiple_of(table_ref[33 + d] * HALF, BLOCK), HALF), :]
+    total = jnp.zeros(out.shape, f32)
+    for i, copy in enumerate(copies):
+        copy.wait()
+        part = slice(i * QUARTER, (i + 1) * QUARTER)
+        total = total + nn(hidden_ref[:, part], all_ref[part, :])
+    out[...] = total.astype(bf16)
 
 
 def weight_kernel(table_ref, hidden, grads, r1, r2, r3, own, other, m1, m2, m3):
@@ -334,7 +359,6 @@
     rows = queries.shape[1]
     grad_scale = float(rows * 32) ** (-0.5)
     query, grad, saved = queries[0], output_gradient[0], attended[0]
-    docs = doc_ids[0].reshape(16, BLOCK)
 
     def places_of_keys(placing):
         stored = jnp.arange(16, dtype=jnp.int32)
@@ -368,12 +392,13 @@
     together = lax.optimization_barrier
 
     own_keys = rotary_key_rows[0]
-    near, first, placing, head = together(
+    near, first, placing, head, docs = together(
         (
             [own_keys, x_swap(own_keys)],
             [value_projection] + [first_with(value_projection, r) for r in (1, 2, 3)],
             block_place[0],
             lax.axis_index("head"),
+            jnp.maximum(doc_ids[0], 0).reshape(16, BLOCK),
         )
     )
     near, first = joined(near), joined(first)
@@ -395,8 +420,11 @@
         value_side_kernel,
         [((24, 128), f32)] + parts_out,
         [table, docs, query, grad, *keys],
-        scratch=[whole, window, bias, ((SPAN, 256), f32), square, stack] + sums,
-        cost=7, limit=24,
+        scratch=[((rows, 1536), bf16)] * 2
+        + [whole, window, bias, ((SPAN, 256), f32), square, stack]
+        + sums
+        + [pltpu.SemaphoreType.DMA((2,))],
+        anys=(2, 3), cost=7, limit=48,
     )
     w2, s0, s1, s3, totals, value_parts, slabs = together((w2, s0, s1, s3, totals, value_parts, slabs))
 
@@ -405,20 +433,25 @@
         project_kernel,
         [((rows, HEAD_SIZE), bf16), ((QUARTER, HEAD_SIZE), bf16)] + [((HALF, HEAD_SIZE), bf16)] * 3,
         [slabs, hidden, first, w1, w2, w3, s0, s1, s2, s3],
-        scratch=[((4 * QUARTER, HEAD_SIZE), bf16)],
-        cost=4, limit=24,
+        scratch=[
+            ((rows, 4 * QUARTER), bf16),
+            ((4 * QUARTER, HEAD_SIZE), bf16),
+            pltpu.SemaphoreType.DMA((4,)),
+        ],
+        anys=(1,), cost=4, limit=48,
     )
     arrived = [z_with(part, r + 1) for r, part in enumerate(value_parts[1:])]
-    own_values, arrived, value_sum, saved = together((own_values, arrived, value_parts[0], saved))
+    own_values, halves = together((own_values, halves))
+
+    near_values, value_sum = together(([own_values, x_swap(own_values)], value_parts[0]))
+    near_values = joined(near_values)
     for part in arrived:
         value_sum = value_sum + part.astype(f32)
-
+    value_rest = x_swap(value_sum[rows:].astype(bf16))
+
+    values = [near_values] + [z_with(near_values, r) for r in (1, 2, 3)]
     (terms,) = call(row_terms_kernel, [((24, 128), f32)], [grad, saved], smem=0)
-    value_rest = x_swap(value_sum[rows:].astype(bf16))
-    near_values, value_rest, value_sum, terms = together(
-        ([own_values, x_swap(own_values)], value_rest, value_sum, terms)
-    )
-    near_values = joined(near_values)
+    values, value_sum, value_rest, terms = together((values, value_sum, value_rest, terms))
     value_grads = (value_sum[:rows] + value_rest.astype(f32)).astype(bf16)
 
     message = ((HALF + rows, HEAD_SIZE), bf16)
@@ -434,15 +467,7 @@
     ]
     w_parts = [w_parts[0]] + [part.astype(bf16) for part in w_parts[1:]]
     messages[0], messages[2] = y_with(messages[0], 1), y_with(messages[2], 3)
-    values, w_parts, messages = together(
-        ([near_values] + [z_with(near_values, r) for r in (1, 2, 3)], w_parts, messages)
-    )
-
-    messages[1] = y_with(messages[1], 2)
-    swapped = [core_swap(messages[0]), None, core_swap(messages[2])]
-    w_sum = w_parts[0]
-    for r in (1, 2, 3):
-        w_sum = w_sum + second_with(w_parts[r], r).astype(f32)
+    w_got = [w_parts[0]] + [second_with(w_parts[r], r) for r in (1, 2, 3)]
     dquery, *key_parts = call(
         key_side_kernel,
         [((rows, 1536), bf16)] + parts_out,
@@ -450,20 +475,27 @@
         scratch=[whole, whole, window, window, bias, square, stack] + sums,
         cost=9, limit=28,
     )
-    key_parts, w_sum, messages, swapped[0], swapped[2] = together(
-        (key_parts, w_sum, messages, swapped[0], swapped[2])
-    )
-
-    swapped[1] = core_swap(messages[1])
+    key_parts, w_got, messages = together((key_parts, w_got, messages))
+
+    messages[1] = y_with(messages[1], 2)
+    swapped = [core_swap(messages[0]), None, core_swap(messages[2])]
+    key_parts[3], swapped = together((key_parts[3], swapped))
+    arrived = [z_with(part, r + 1) for r, part in enumerate(key_parts[1:])]
+    arrived[0], w_got = together((arrived[0], w_got))
+    w_sum = w_got[0]
+    for part in w_got[1:]:
+        w_sum = w_sum + part.astype(f32)
     got = [
         first_with(w_sum[i * HEAD_SIZE : (i + 1) * HEAD_SIZE].astype(bf16), i) for i in (1, 2, 3)
     ]
-    arrived = [z_with(part, r + 1) for r, part in enumerate(key_parts[1:])]
-    arrived, key_sum, slabs, swapped[1] = together((arrived, key_parts[0], slabs, swapped[1]))
+    arrived, key_sum, slabs, messages, got[:2] = together(
+        (arrived, key_parts[0], slabs, messages, got[:2])
+    )
     for part in arrived:
         key_sum = key_sum + part.astype(f32)
 
-    key_grads = (key_sum[:rows] + x_swap(key_sum[rows:].astype(bf16)).astype(f32)).astype(bf16)
+    swapped[1] = core_swap(messages[1])
+    key_rest = x_swap(key_sum[rows:].astype(bf16))
     (input_grad,) = call(
         input_kernel,
         [((rows, QUARTER), bf16)],
@@ -472,7 +504,8 @@
         anys=tuple(range(2, 9)),
         cost=4, limit=16,
     )
-    got, input_grad = together((got, input_grad))
+    got, input_grad, key_rest = together((got, input_grad, key_rest))
+    key_grads = (key_sum[:rows] + key_rest.astype(f32)).astype(bf16)
     (weight_grad,) = call(
         functools.partial(fold_kernel, grad_scale),
         [((SLAB, HEAD_SIZE), f32)],

time: 110 us -> 106 us (0.964)
  waiting for transfers between devices: 26.9 us -> 19.3 us
  starting transfers between devices: 47.4 us -> 51.3 us
  local copies, waits for them, and re-layouts: 6.52 us -> 3.04 us
  Pallas kernels: 24.5 us -> 26.9 us
    ppermute x36, waiting for transfers between devices: 26.3 us -> 19.3 us  [moved(): return lax.ppermute(value, ('dp', 'ctx'), pairs)]
    unnamed x20 -> x16, local copies, waits for them, and re-layouts: 6.37 us -> 2.89 us
    ppermute x36, starting transfers between devices: 42.1 us -> 44.8 us  [moved(): return lax.ppermute(value, ('dp', 'ctx'), pairs)]
    pallas_call x10, Pallas kernels: 24.5 us -> 26.9 us  [call(): pl.pallas_call(kernel, out_shape=tuple((jax.ShapeDtypeStruct(s, d) for s,...]
    ppermute x3, starting transfers between devices: 5.31 us -> 6.57 us  [y_with(): return lax.ppermute(value, 'head', [(y, y ^ bits) for y in range(4)])]
  transfers between devices with their start and end apart: 39 -> 39, of which waited for: 16 -> 12; matrix products, arithmetic and copies ran while one was open for 2% -> 3% of each run, Pallas kernels for 21% -> 23%
where the time goes in v3:
time: 106 us; the launch traced here: 105 us
  starting transfers between devices  51.3 us (48%)
  Pallas kernels  26.9 us (25%)
  waiting for transfers between devices  19.3 us (18%)
  other arithmetic  3.79 us (4%)
  local copies, waits for them, and re-layouts  3.04 us (3%)
    ppermute x36, starting transfers between devices, moved(): return lax.ppermute(value, ('dp', 'ctx'), pairs)  44.8 us
    pallas_call x10, Pallas kernels, call(): pl.pallas_call(kernel, out_shape=tuple((jax.ShapeDtypeStruct(s, d) for s,...  26.9 us
    ppermute x36, waiting for transfers between devices, moved(): return lax.ppermute(value, ('dp', 'ctx'), pairs)  19.3 us
    ppermute x3, starting transfers between devices, y_with(): return lax.ppermute(value, 'head', [(y, y ^ bits) for y in range(4)])  6.57 us
    unnamed x16, local copies, waits for them, and re-layouts  2.89 us
  transfers between devices with their start and end apart: 39, of which 12 were waited for; matrix products, arithmetic and copies ran while one was open for 3% of the time, Pallas kernels for 23%

profile of v3, /device:TPU:0, one launch (start us, length us, event | category | flops | bytes accessed | tf_op | source)
XLA Modules:
  0.0 105.4 jit_solution(8984160066332082794)
XLA Ops:
  0.6 2.1 %collective-permute-start.1 = (bf16[384,128]{1,0:T(8,128)(2,1)}, bf16[384,128]{1,0:T(8,128)(2,1)S(1)}, u32[]{:S(2)}, u32[]{:S(2)}) collective-permute-start(bf16[384,128]{1,0:T(8,128)(2,1)} %own), channel_id=1, source_target_pairs={{0,1},{1,0},{2,3},{3,2},{4,5},{5,4},{6,7},{7,6},{32,36},{33,37},{3... | collective-permute-start | bytes 294920 | tf_op jit(solution)/shard_map/ppermute | solution.py:41
  2.7 3.6 %collective-permute-start.2 = (bf16[384,128]{1,0:T(8,128)(2,1)}, bf16[384,128]{1,0:T(8,128)(2,1)S(1)}, u32[]{:S(2)}, u32[]{:S(2)}) collective-permute-start(bf16[384,128]{1,0:T(8,128)(2,1)} %own), channel_id=1, source_target_pairs={{0,2},{1,3},{2,0},{3,1},{4,6},{5,7},{6,4},{7,5},{32,96},{33,97},{3... | collective-permute-start | bytes 294920 | tf_op jit(solution)/shard_map/ppermute | solution.py:41
  6.3 1.5 %collective-permute-start = (bf16[256,128]{1,0:T(8,128)(2,1)}, bf16[256,128]{1,0:T(8,128)(2,1)S(1)}, u32[]{:S(2)}, u32[]{:S(2)}) collective-permute-start(bf16[256,128]{1,0:T(8,128)(2,1)} %bitcast.28), channel_id=1, source_target_pairs={{0,4},{1,5},{2,6},{3,7},{4,0},{5,1},{6,2},{7,3},{32,36},{33,37},{3... | collective-permute-start | bytes 196616 | tf_op jit(solution)/shard_map/ppermute | solution.py:41
  7.8 0.7 broadcast_maximum_fusion
  8.6 2.2 %collective-permute-done.refs_0_ = bf16[256,128]{1,0:T(8,128)(2,1)S(1)} collective-permute-done((bf16[256,128]{1,0:T(8,128)(2,1)}, bf16[256,128]{1,0:T(8,128)(2,1)S(1)}, u32[]{:S(2)}, u32[]{:S(2)}) %collective-permute-start) | collective-permute-done | bytes 65568 | tf_op jit(solution)/shard_map/ppermute | solution.py:41
  10.8 1.6 %collective-permute-done.3.refs_2_ = bf16[384,128]{1,0:T(8,128)(2,1)S(1)} collective-permute-done((bf16[384,128]{1,0:T(8,128)(2,1)}, bf16[384,128]{1,0:T(8,128)(2,1)S(1)}, u32[]{:S(2)}, u32[]{:S(2)}) %collective-permute-start.3) | collective-permute-done | bytes 98336 | tf_op jit(solution)/shard_map/ppermute | solution.py:41
  12.3 0.9 copy-done.4
  13.2 0.1 shard_map.112.w0
  13.4 1.6 %collective-permute-start.7 = (bf16[1536,128]{1,0:T(8,128)(2,1)S(1)}, bf16[1536,128]{1,0:T(8,128)(2,1)S(1)}, u32[]{:S(2)}, u32[]{:S(2)}) collective-permute-start(bf16[1536,128]{1,0:T(8,128)(2,1)S(1)} %shard_map.112.w0), channel_id=1, source_target_pairs={{0,4},{1,5},{2,6},{3,7},{4,0},{5,1},{6,2},{7,3},{32,33},{33,32},{3... | collective-permute-start | bytes 1179656 | tf_op jit(solution)/shard_map/ppermute | solution.py:41
  14.9 2.1 %collective-permute-start.8 = (bf16[1536,128]{1,0:T(8,128)(2,1)S(1)}, bf16[1536,128]{1,0:T(8,128)(2,1)S(1)}, u32[]{:S(2)}, u32[]{:S(2)}) collective-permute-start(bf16[1536,128]{1,0:T(8,128)(2,1)S(1)} %shard_map.112.w0), channel_id=1, source_target_pairs={{0,68},{1,69},{2,70},{3,71},{4,64},{5,65},{6,66},{7,67},{32,35},{3... | collective-permute-start | bytes 1179656 | tf_op jit(solution)/shard_map/ppermute | solution.py:41
  17.0 0.8 copy-done.5
  17.9 0.1 collective-permute-start.4
  18.0 3.1 %collective-permute-start.5 = (bf16[512,128]{1,0:T(8,128)(2,1)S(1)}, bf16[512,128]{1,0:T(8,128)(2,1)S(1)}, u32[]{:S(2)}, u32[]{:S(2)}) collective-permute-start(bf16[512,128]{1,0:T(8,128)(2,1)S(1)} %shard_map.111.k0), channel_id=1, source_target_pairs={{0,2},{1,3},{2,0},{3,1},{4,6},{5,7},{6,4},{7,5},{32,34},{33,35},{3... | collective-permute-start | bytes 393224 | tf_op jit(solution)/shard_map/ppermute | solution.py:41
  21.2 1.5 %collective-permute-start.6 = (bf16[512,128]{1,0:T(8,128)(2,1)S(1)}, bf16[512,128]{1,0:T(8,128)(2,1)S(1)}, u32[]{:S(2)}, u32[]{:S(2)}) collective-permute-start(bf16[512,128]{1,0:T(8,128)(2,1)S(1)} %shard_map.111.k0), channel_id=1, source_target_pairs={{0,3},{1,2},{2,1},{3,0},{4,7},{5,6},{6,5},{7,4},{32,35},{33,34},{3... | collective-permute-start | bytes 393224 | tf_op jit(solution)/shard_map/ppermute | solution.py:41
  22.7 0.8 fusion.2
  23.6 0.8 select_reduce_fusion
  24.3 0.1 concatenate.7.table_ref
  24.4 0.1 pad_add_fusion.table_ref
  24.5 1.7 %collective-permute-done.5.k2 = bf16[512,128]{1,0:T(8,128)(2,1)S(1)} collective-permute-done((bf16[512,128]{1,0:T(8,128)(2,1)S(1)}, bf16[512,128]{1,0:T(8,128)(2,1)S(1)}, u32[]{:S(2)}, u32[]{:S(2)}) %collective-permute-start.5) | collective-permute-done | bytes 131104 | tf_op jit(solution)/shard_map/ppermute | solution.py:41
  26.2 1.4 %collective-permute-done.6.k3 = bf16[512,128]{1,0:T(8,128)(2,1)S(1)} collective-permute-done((bf16[512,128]{1,0:T(8,128)(2,1)S(1)}, bf16[512,128]{1,0:T(8,128)(2,1)S(1)}, u32[]{:S(2)}, u32[]{:S(2)}) %collective-permute-start.6) | collective-permute-done | bytes 131104 | tf_op jit(solution)/shard_map/ppermute | solution.py:41
  27.6 0.5 collective-permute-start.11
  28.1 0.1 collective-permute-start.12
  28.2 0.4 collective-permute-start.9
  28.6 1.1 %copy-done.1 = bf16[1,256,1536]{2,1,0:T(8,128)(2,1)S(1)} copy-done((bf16[1,256,1536]{2,1,0:T(8,128)(2,1)S(1)}, bf16[1,256,1536]{2,1,0:T(8,128)(2,1)}, u32[]{:S(2)}) %copy-start.1) | copy-done | bytes 786456
  29.7 6.9 %shard_map.113 = (f32[24,128]{1,0:T(8,128)S(1)}, f32[512,128]{1,0:T(8,128)S(1)}, bf16[512,128]{1,0:T(8,128)(2,1)S(1)}, bf16[512,128]{1,0:T(8,128)(2,1)S(1)}, bf16[512,128]{1,0:T(8,128)(2,1)S(1)}) custom-call(s32[18]{0:T(128)S(1)} %pad_add_fusion.table_ref, s32[16,128]{1,0:T(8,128)S(1)} %bitcast.26, bf16[256,1536]{1,0:T(8,128)(2,1)S(1)} %bitcast.23, ...), custom_call_target="tpu_custom_call" | custom-call | bytes 22020096 | tf_op jit(solution)/shard_map/pallas_call | solution.py:313
  36.6 0.2 collective-permute-start.13
  36.8 1.7 %collective-permute-start.18 = (bf16[512,128]{1,0:T(8,128)(2,1)S(1)}, bf16[512,128]{1,0:T(8,128)(2,1)S(1)}, u32[]{:S(2)}, u32[]{:S(2)}) collective-permute-start(bf16[512,128]{1,0:T(8,128)(2,1)S(1)} %get-tuple-element.138), channel_id=1, source_target_pairs={{0,1},{1,0},{2,3},{3,2},{4,5},{5,4},{6,7},{7,6},{32,33},{33,32},{3... | collective-permute-start | bytes 393224 | tf_op jit(solution)/shard_map/ppermute | solution.py:41
  38.5 1.3 %collective-permute-start.19 = (bf16[512,128]{1,0:T(8,128)(2,1)S(1)}, bf16[512,128]{1,0:T(8,128)(2,1)S(1)}, u32[]{:S(2)}, u32[]{:S(2)}) collective-permute-start(bf16[512,128]{1,0:T(8,128)(2,1)S(1)} %get-tuple-element.139), channel_id=1, source_target_pairs={{0,2},{1,3},{2,0},{3,1},{4,6},{5,7},{6,4},{7,5},{32,34},{33,35},{3... | collective-permute-start | bytes 393224 | tf_op jit(solution)/shard_map/ppermute | solution.py:41
  39.8 1.7 %collective-permute-start.20 = (bf16[512,128]{1,0:T(8,128)(2,1)S(1)}, bf16[512,128]{1,0:T(8,128)(2,1)S(1)}, u32[]{:S(2)}, u32[]{:S(2)}) collective-permute-start(bf16[512,128]{1,0:T(8,128)(2,1)S(1)} %get-tuple-element.140), channel_id=1, source_target_pairs={{0,3},{1,2},{2,1},{3,0},{4,7},{5,6},{6,5},{7,4},{32,35},{33,34},{3... | collective-permute-start | bytes 393224 | tf_op jit(solution)/shard_map/ppermute | solution.py:41
  41.5 4.8 %shard_map.114 = (bf16[256,128]{1,0:T(8,128)(2,1)S(1)}, bf16[3072,128]{1,0:T(8,128)(2,1)S(1)}, bf16[1536,128]{1,0:T(8,128)(2,1)S(1)}, bf16[1536,128]{1,0:T(8,128)(2,1)S(1)}, bf16[1536,128]{1,0:T(8,128)(2,1)S(1)}) custom-call(s32[37]{0:T(128)S(1)} %concatenate.7.table_ref, bf16[256,12288]{1,0:T(8,128)(2,1)} %bitcast.16, bf16[1536,128]{1,0:T(8,128)(2,1)S(1)} %shard_map.112.w0, ...), custom_call_target="tpu_custom_call" | custom-call | bytes 12582912 | tf_op jit(solution)/shard_map/pallas_call | solution.py:313
  46.3 1.7 %collective-permute-start.14 = (bf16[256,128]{1,0:T(8,128)(2,1)S(1)}, bf16[256,128]{1,0:T(8,128)(2,1)S(1)}, u32[]{:S(2)}, u32[]{:S(2)}) collective-permute-start(bf16[256,128]{1,0:T(8,128)(2,1)S(1)} %get-tuple-element.135.own), channel_id=1, source_target_pairs={{0,4},{1,5},{2,6},{3,7},{4,0},{5,1},{6,2},{7,3},{32,36},{33,37},{3... | collective-permute-start | bytes 196616 | tf_op jit(solution)/shard_map/ppermute | solution.py:41
  48.1 2.6 %collective-permute-done.14.refs_0_ = bf16[256,128]{1,0:T(8,128)(2,1)S(1)} collective-permute-done((bf16[256,128]{1,0:T(8,128)(2,1)S(1)}, bf16[256,128]{1,0:T(8,128)(2,1)S(1)}, u32[]{:S(2)}, u32[]{:S(2)}) %collective-permute-start.14) | collective-permute-done | bytes 65568 | tf_op jit(solution)/shard_map/ppermute | solution.py:41
  50.8 0.6 collective-permute-start.15
  51.3 2.5 %collective-permute-start.16 = (bf16[512,128]{1,0:T(8,128)(2,1)S(1)}, bf16[512,128]{1,0:T(8,128)(2,1)S(1)}, u32[]{:S(2)}, u32[]{:S(2)}) collective-permute-start(bf16[512,128]{1,0:T(8,128)(2,1)S(1)} %shard_map.115.v0), channel_id=1, source_target_pairs={{0,2},{1,3},{2,0},{3,1},{4,6},{5,7},{6,4},{7,5},{32,34},{33,35},{3... | collective-permute-start | bytes 393224 | tf_op jit(solution)/shard_map/ppermute | solution.py:41
  53.9 1.7 %collective-permute-start.17 = (bf16[512,128]{1,0:T(8,128)(2,1)S(1)}, bf16[512,128]{1,0:T(8,128)(2,1)S(1)}, u32[]{:S(2)}, u32[]{:S(2)}) collective-permute-start(bf16[512,128]{1,0:T(8,128)(2,1)S(1)} %shard_map.115.v0), channel_id=1, source_target_pairs={{0,3},{1,2},{2,1},{3,0},{4,7},{5,6},{6,5},{7,4},{32,35},{33,34},{3... | collective-permute-start | bytes 393224 | tf_op jit(solution)/shard_map/ppermute | solution.py:41
  55.6 1.7 %collective-permute-start.21 = (bf16[256,128]{1,0:T(8,128)(2,1)S(1)}, bf16[256,128]{1,0:T(8,128)(2,1)S(1)}, u32[]{:S(2)}, u32[]{:S(2)}) collective-permute-start(bf16[256,128]{1,0:T(8,128)(2,1)S(1)} %slice.97), channel_id=1, source_target_pairs={{0,4},{1,5},{2,6},{3,7},{4,0},{5,1},{6,2},{7,3},{32,36},{33,37},{3... | collective-permute-start | bytes 196616 | tf_op jit(solution)/shard_map/ppermute | solution.py:41
  57.4 0.5 shard_map.116.term_ref
  57.9 2.1 %collective-permute-done.21 = bf16[256,128]{1,0:T(8,128)(2,1)S(1)} collective-permute-done((bf16[256,128]{1,0:T(8,128)(2,1)S(1)}, bf16[256,128]{1,0:T(8,128)(2,1)S(1)}, u32[]{:S(2)}, u32[]{:S(2)}) %collective-permute-start.21) | collective-permute-done | bytes 65568 | tf_op jit(solution)/shard_map/ppermute | solution.py:41
  60.1 1.9 %shard_map.118 = (f32[2048,384]{1,0:T(8,128)S(1)}, bf16[2048,384]{1,0:T(8,128)(2,1)S(1)}, bf16[1792,128]{1,0:T(8,128)(2,1)S(1)}, bf16[1792,128]{1,0:T(8,128)(2,1)S(1)}, bf16[1792,128]{1,0:T(8,128)(2,1)S(1)}) custom-call(s32[37]{0:T(128)S(1)} %concatenate.7.table_ref, bf16[256,12288]{1,0:T(8,128)(2,1)S(1)} %bitcast.19, ...), custom_call_target="tpu_custom_call" | custom-call | bytes 12582912 | tf_op jit(solution)/shard_map/pallas_call | solution.py:313
  62.0 0.1 collective-permute-start.22
  62.1 1.6 %collective-permute-start.26 = (bf16[1792,128]{1,0:T(8,128)(2,1)S(1)}, bf16[1792,128]{1,0:T(8,128)(2,1)S(1)}, u32[]{:S(2)}, u32[]{:S(2)}) collective-permute-start(bf16[1792,128]{1,0:T(8,128)(2,1)S(1)} %get-tuple-element.158), channel_id=1, source_target_pairs={{0,8},{8,0},{16,24},{24,16},{1,9},{9,1},{17,25},{25,17},{2,10},{10... | collective-permute-start | bytes 1376264 | tf_op jit(solution)/shard_map/ppermute | solution.py:65
  63.7 2.2 %collective-permute-start.27 = (bf16[1792,128]{1,0:T(8,128)(2,1)S(1)}, bf16[1792,128]{1,0:T(8,128)(2,1)S(1)}, u32[]{:S(2)}, u32[]{:S(2)}) collective-permute-start(bf16[1792,128]{1,0:T(8,128)(2,1)S(1)} %get-tuple-element.160), channel_id=1, source_target_pairs={{0,24},{8,16},{16,8},{24,0},{1,25},{9,17},{17,9},{25,1},{2,26},{10... | collective-permute-start | bytes 1376264 | tf_op jit(solution)/shard_map/ppermute | solution.py:65
  65.9 0.4 add_convert_fusion
  66.3 1.8 %collective-permute-start.23 = (bf16[512,384]{1,0:T(8,128)(2,1)S(1)}, bf16[512,384]{1,0:T(8,128)(2,1)S(1)}, u32[]{:S(2)}, u32[]{:S(2)}) collective-permute-start(bf16[512,384]{1,0:T(8,128)(2,1)S(1)} %get-tuple-element.200), channel_id=1, source_target_pairs={{0,4},{1,5},{2,6},{3,7},{4,0},{5,1},{6,2},{7,3},{32,33},{33,32},{3... | collective-permute-start | bytes 1179656 | tf_op jit(solution)/shard_map/ppermute | solution.py:41
  68.1 1.4 %collective-permute-start.24 = (bf16[512,384]{1,0:T(8,128)(2,1)S(1)}, bf16[512,384]{1,0:T(8,128)(2,1)S(1)}, u32[]{:S(2)}, u32[]{:S(2)}) collective-permute-start(bf16[512,384]{1,0:T(8,128)(2,1)S(1)} %get-tuple-element.199), channel_id=1, source_target_pairs={{0,64},{1,65},{2,66},{3,67},{4,68},{5,69},{6,70},{7,71},{32,34},{3... | collective-permute-start | bytes 1179656 | tf_op jit(solution)/shard_map/ppermute | solution.py:41
  69.5 1.6 %collective-permute-start.25 = (bf16[512,384]{1,0:T(8,128)(2,1)S(1)}, bf16[512,384]{1,0:T(8,128)(2,1)S(1)}, u32[]{:S(2)}, u32[]{:S(2)}) collective-permute-start(bf16[512,384]{1,0:T(8,128)(2,1)S(1)} %get-tuple-element.198), channel_id=1, source_target_pairs={{0,68},{1,69},{2,70},{3,71},{4,64},{5,65},{6,66},{7,67},{32,35},{3... | collective-permute-start | bytes 1179656 | tf_op jit(solution)/shard_map/ppermute | solution.py:41
  71.1 8.4 %shard_map.117 = (bf16[256,1536]{1,0:T(8,128)(2,1)}, f32[512,128]{1,0:T(8,128)S(1)}, bf16[512,128]{1,0:T(8,128)(2,1)S(1)}, bf16[512,128]{1,0:T(8,128)(2,1)S(1)}, bf16[512,128]{1,0:T(8,128)(2,1)S(1)}) custom-call(s32[18]{0:T(128)S(1)} %pad_add_fusion.table_ref, s32[16,128]{1,0:T(8,128)S(1)} %bitcast.27, bf16[256,1536]{1,0:T(8,128)(2,1)S(1)} %bitcast.24, ...), custom_call_target="tpu_custom_call" | custom-call | bytes 28311552 | tf_op jit(solution)/shard_map/pallas_call | solution.py:313
  79.5 3.1 %collective-permute-done.25 = bf16[512,384]{1,0:T(8,128)(2,1)S(1)} collective-permute-done((bf16[512,384]{1,0:T(8,128)(2,1)S(1)}, bf16[512,384]{1,0:T(8,128)(2,1)S(1)}, u32[]{:S(2)}, u32[]{:S(2)}) %collective-permute-start.25) | collective-permute-done | bytes 393248 | tf_op jit(solution)/shard_map/ppermute | solution.py:41
  82.7 0.5 collective-permute-start.31
  83.2 2.8 %collective-permute-start.33 = (bf16[1792,128]{1,0:T(8,128)(2,1)S(1)}, bf16[1792,128]{1,0:T(8,128)(2,1)S(1)}, u32[]{:S(2)}, u32[]{:S(2)}) collective-permute-start(bf16[1792,128]{1,0:T(8,128)(2,1)S(1)} %get-tuple-element.173), channel_id=1, source_target_pairs={{0,16},{8,24},{16,0},{24,8},{1,17},{9,25},{17,1},{25,9},{2,18},{10... | collective-permute-start | bytes 1376264 | tf_op jit(solution)/shard_map/ppermute | solution.py:65
  85.9 3.2 %collective-permute-start.29 = (bf16[512,128]{1,0:T(8,128)(2,1)S(1)}, bf16[512,128]{1,0:T(8,128)(2,1)S(1)}, u32[]{:S(2)}, u32[]{:S(2)}) collective-permute-start(bf16[512,128]{1,0:T(8,128)(2,1)S(1)} %get-tuple-element.167), channel_id=1, source_target_pairs={{0,2},{1,3},{2,0},{3,1},{4,6},{5,7},{6,4},{7,5},{32,34},{33,35},{3... | collective-permute-start | bytes 393224 | tf_op jit(solution)/shard_map/ppermute | solution.py:41
  89.1 0.2 fusion.17
  89.4 1.6 %collective-permute-start.32 = (bf16[512,128]{1,0:T(8,128)(2,1)S(1)}, bf16[512,128]{1,0:T(8,128)(2,1)S(1)}, u32[]{:S(2)}, u32[]{:S(2)}) collective-permute-start(bf16[512,128]{1,0:T(8,128)(2,1)S(1)} %get-tuple-element.171), channel_id=1, source_target_pairs={{0,3},{1,2},{2,1},{3,0},{4,7},{5,6},{6,5},{7,4},{32,35},{33,34},{3... | collective-permute-start | bytes 393224 | tf_op jit(solution)/shard_map/ppermute | solution.py:41
  91.0 0.1 collective-permute-start.34
  91.1 3.2 %collective-permute-start.35 = (bf16[128,384]{1,0:T(8,128)(2,1)S(1)}, bf16[128,384]{1,0:T(8,128)(2,1)S(1)}, u32[]{:S(2)}, u32[]{:S(2)}) collective-permute-start(bf16[128,384]{1,0:T(8,128)(2,1)S(1)} %get-tuple-element.203), channel_id=1, source_target_pairs={{0,2},{1,3},{2,0},{3,1},{4,6},{5,7},{6,4},{7,5},{32,96},{33,97},{3... | collective-permute-start | bytes 294920 | tf_op jit(solution)/shard_map/ppermute | solution.py:41
  94.3 1.4 %collective-permute-done.34.one = bf16[128,384]{1,0:T(8,128)(2,1)S(1)} collective-permute-done((bf16[128,384]{1,0:T(8,128)(2,1)S(1)}, bf16[128,384]{1,0:T(8,128)(2,1)S(1)}, u32[]{:S(2)}, u32[]{:S(2)}) %collective-permute-start.34) | collective-permute-done | bytes 98336 | tf_op jit(solution)/shard_map/ppermute | solution.py:41
  95.7 2.2 %collective-permute-done.35.two = bf16[128,384]{1,0:T(8,128)(2,1)S(1)} collective-permute-done((bf16[128,384]{1,0:T(8,128)(2,1)S(1)}, bf16[128,384]{1,0:T(8,128)(2,1)S(1)}, u32[]{:S(2)}, u32[]{:S(2)}) %collective-permute-start.35) | collective-permute-done | bytes 98336 | tf_op jit(solution)/shard_map/ppermute | solution.py:41
  97.9 1.6 %collective-permute-start.36 = (bf16[128,384]{1,0:T(8,128)(2,1)S(1)}, bf16[128,384]{1,0:T(8,128)(2,1)S(1)}, u32[]{:S(2)}, u32[]{:S(2)}) collective-permute-start(bf16[128,384]{1,0:T(8,128)(2,1)S(1)} %get-tuple-element.202), channel_id=1, source_target_pairs={{0,3},{1,2},{2,1},{3,0},{4,7},{5,6},{6,5},{7,4},{32,100},{33,101},... | collective-permute-start | bytes 294920 | tf_op jit(solution)/shard_map/ppermute | solution.py:41
  99.6 0.1 collective-permute-start.38
  99.7 3.4 %shard_map.119 = bf16[256,3072]{1,0:T(8,128)(2,1)} custom-call(s32[37]{0:T(128)S(1)} %concatenate.7.table_ref, bf16[256,128]{1,0:T(8,128)(2,1)S(1)} %add_convert_fusion.3.grads, bf16[3072,128]{1,0:T(8,128)(2,1)S(1)} %get-tuple-element.185.own, bf16[1792,128]{1,0:T(8,128)(2,1)S(1)} %collective-permute-done.26.a1, ...), custom_call_target="tpu_custom_call" | custom-call | bytes 12582912 | tf_op jit(solution)/shard_map/pallas_call | solution.py:313
  103.1 0.7 collective-permute-done.36.three
  103.8 0.1 collective-permute-done.38
  103.9 0.6 fusion.1
  104.6 0.8 shard_map.120
  (59 shorter events, 0.6 us)
Async XLA Ops:
  0.6 27.9 %copy-start = (bf16[1,256,1536]{2,1,0:T(8,128)(2,1)S(1)}, bf16[1,256,1536]{2,1,0:T(8,128)(2,1)}, u32[]{:S(2)}) copy-start(bf16[1,256,1536]{2,1,0:T(8,128)(2,1)} %param.12) | copy-start | bytes 2359300
  0.6 10.1 %collective-permute-start.1 = (bf16[384,128]{1,0:T(8,128)(2,1)}, bf16[384,128]{1,0:T(8,128)(2,1)S(1)}, u32[]{:S(2)}, u32[]{:S(2)}) collective-permute-start(bf16[384,128]{1,0:T(8,128)(2,1)} %own), channel_id=1, source_target_pairs={{0,1},{1,0},{2,3},{3,2},{4,5},{5,4},{6,7},{7,6},{32,36},{33,37},{3... | collective-permute-start | bytes 294920 | tf_op jit(solution)/shard_map/ppermute | solution.py:41
  2.7 8.1 %collective-permute-start.2 = (bf16[384,128]{1,0:T(8,128)(2,1)}, bf16[384,128]{1,0:T(8,128)(2,1)S(1)}, u32[]{:S(2)}, u32[]{:S(2)}) collective-permute-start(bf16[384,128]{1,0:T(8,128)(2,1)} %own), channel_id=1, source_target_pairs={{0,2},{1,3},{2,0},{3,1},{4,6},{5,7},{6,4},{7,5},{32,96},{33,97},{3... | collective-permute-start | bytes 294920 | tf_op jit(solution)/shard_map/ppermute | solution.py:41
  6.3 6.0 %collective-permute-start.3 = (bf16[384,128]{1,0:T(8,128)(2,1)}, bf16[384,128]{1,0:T(8,128)(2,1)S(1)}, u32[]{:S(2)}, u32[]{:S(2)}) collective-permute-start(bf16[384,128]{1,0:T(8,128)(2,1)} %own), channel_id=1, source_target_pairs={{0,3},{1,2},{2,1},{3,0},{4,7},{5,6},{6,5},{7,4},{32,100},{33,101},... | collective-permute-start | bytes 294920 | tf_op jit(solution)/shard_map/ppermute | solution.py:41
  6.3 4.5 %collective-permute-start = (bf16[256,128]{1,0:T(8,128)(2,1)}, bf16[256,128]{1,0:T(8,128)(2,1)S(1)}, u32[]{:S(2)}, u32[]{:S(2)}) collective-permute-start(bf16[256,128]{1,0:T(8,128)(2,1)} %bitcast.28), channel_id=1, source_target_pairs={{0,4},{1,5},{2,6},{3,7},{4,0},{5,1},{6,2},{7,3},{32,36},{33,37},{3... | collective-permute-start | bytes 196616 | tf_op jit(solution)/shard_map/ppermute | solution.py:41
  12.3 0.9 copy-start.4
  13.4 14.2 %collective-permute-start.7 = (bf16[1536,128]{1,0:T(8,128)(2,1)S(1)}, bf16[1536,128]{1,0:T(8,128)(2,1)S(1)}, u32[]{:S(2)}, u32[]{:S(2)}) collective-permute-start(bf16[1536,128]{1,0:T(8,128)(2,1)S(1)} %shard_map.112.w0), channel_id=1, source_target_pairs={{0,4},{1,5},{2,6},{3,7},{4,0},{5,1},{6,2},{7,3},{32,33},{33,32},{3... | collective-permute-start | bytes 1179656 | tf_op jit(solution)/shard_map/ppermute | solution.py:41
  14.9 12.7 %collective-permute-start.8 = (bf16[1536,128]{1,0:T(8,128)(2,1)S(1)}, bf16[1536,128]{1,0:T(8,128)(2,1)S(1)}, u32[]{:S(2)}, u32[]{:S(2)}) collective-permute-start(bf16[1536,128]{1,0:T(8,128)(2,1)S(1)} %shard_map.112.w0), channel_id=1, source_target_pairs={{0,68},{1,69},{2,70},{3,71},{4,64},{5,65},{6,66},{7,67},{32,35},{3... | collective-permute-start | bytes 1179656 | tf_op jit(solution)/shard_map/ppermute | solution.py:41
  17.0 0.8 copy-start.5
  17.9 6.6 %collective-permute-start.4 = (bf16[512,128]{1,0:T(8,128)(2,1)S(1)}, bf16[512,128]{1,0:T(8,128)(2,1)S(1)}, u32[]{:S(2)}, u32[]{:S(2)}) collective-permute-start(bf16[512,128]{1,0:T(8,128)(2,1)S(1)} %shard_map.111.k0), channel_id=1, source_target_pairs={{0,1},{1,0},{2,3},{3,2},{4,5},{5,4},{6,7},{7,6},{32,33},{33,32},{3... | collective-permute-start | bytes 393224 | tf_op jit(solution)/shard_map/ppermute | solution.py:41
  18.0 8.2 %collective-permute-start.5 = (bf16[512,128]{1,0:T(8,128)(2,1)S(1)}, bf16[512,128]{1,0:T(8,128)(2,1)S(1)}, u32[]{:S(2)}, u32[]{:S(2)}) collective-permute-start(bf16[512,128]{1,0:T(8,128)(2,1)S(1)} %shard_map.111.k0), channel_id=1, source_target_pairs={{0,2},{1,3},{2,0},{3,1},{4,6},{5,7},{6,4},{7,5},{32,34},{33,35},{3... | collective-permute-start | bytes 393224 | tf_op jit(solution)/shard_map/ppermute | solution.py:41
  21.2 6.4 %collective-permute-start.6 = (bf16[512,128]{1,0:T(8,128)(2,1)S(1)}, bf16[512,128]{1,0:T(8,128)(2,1)S(1)}, u32[]{:S(2)}, u32[]{:S(2)}) collective-permute-start(bf16[512,128]{1,0:T(8,128)(2,1)S(1)} %shard_map.111.k0), channel_id=1, source_target_pairs={{0,3},{1,2},{2,1},{3,0},{4,7},{5,6},{6,5},{7,4},{32,35},{33,34},{3... | collective-permute-start | bytes 393224 | tf_op jit(solution)/shard_map/ppermute | solution.py:41
  27.6 9.0 %collective-permute-start.10 = (bf16[1536,128]{1,0:T(8,128)(2,1)S(1)}, bf16[1536,128]{1,0:T(8,128)(2,1)S(1)}, u32[]{:S(2)}, u32[]{:S(2)}) collective-permute-start(bf16[1536,128]{1,0:T(8,128)(2,1)S(1)} %shard_map.112.w0), channel_id=1, source_target_pairs={{0,32},{1,33},{2,34},{3,35},{4,36},{5,37},{6,38},{7,39},{32,0},{33... | collective-permute-start | bytes 1179656 | tf_op jit(solution)/shard_map/ppermute | solution.py:41
  27.6 9.0 %collective-permute-start.11 = (bf16[1536,128]{1,0:T(8,128)(2,1)S(1)}, bf16[1536,128]{1,0:T(8,128)(2,1)S(1)}, u32[]{:S(2)}, u32[]{:S(2)}) collective-permute-start(bf16[1536,128]{1,0:T(8,128)(2,1)S(1)} %collective-permute-done.7.w1), channel_id=1, source_target_pairs={{0,32},{1,33},{2,34},{3,35},{4,36},{5,37},{6,38},{7,39},{32,0},{33... | collective-permute-start | bytes 1179656 | tf_op jit(solution)/shard_map/ppermute | solution.py:41
  28.1 8.5 %collective-permute-start.12 = (bf16[1536,128]{1,0:T(8,128)(2,1)S(1)}, bf16[1536,128]{1,0:T(8,128)(2,1)S(1)}, u32[]{:S(2)}, u32[]{:S(2)}) collective-permute-start(bf16[1536,128]{1,0:T(8,128)(2,1)S(1)} %collective-permute-done.8.w3), channel_id=1, source_target_pairs={{0,32},{1,33},{2,34},{3,35},{4,36},{5,37},{6,38},{7,39},{32,0},{33... | collective-permute-start | bytes 1179656 | tf_op jit(solution)/shard_map/ppermute | solution.py:41
  28.2 8.4 %collective-permute-start.9 = (bf16[1536,128]{1,0:T(8,128)(2,1)S(1)}, bf16[1536,128]{1,0:T(8,128)(2,1)S(1)}, u32[]{:S(2)}, u32[]{:S(2)}) collective-permute-start(bf16[1536,128]{1,0:T(8,128)(2,1)S(1)} %collective-permute-done.8.w3), channel_id=1, source_target_pairs={{0,4},{1,5},{2,6},{3,7},{4,0},{5,1},{6,2},{7,3},{32,33},{33,32},{3... | collective-permute-start | bytes 1179656 | tf_op jit(solution)/shard_map/ppermute | solution.py:41
  28.6 1.1 %copy-start.1 = (bf16[1,256,1536]{2,1,0:T(8,128)(2,1)S(1)}, bf16[1,256,1536]{2,1,0:T(8,128)(2,1)}, u32[]{:S(2)}) copy-start(bf16[1,256,1536]{2,1,0:T(8,128)(2,1)} %param.9) | copy-start | bytes 2359300
  36.6 4.9 %collective-permute-start.13 = (bf16[1536,128]{1,0:T(8,128)(2,1)S(1)}, bf16[1536,128]{1,0:T(8,128)(2,1)S(1)}, u32[]{:S(2)}, u32[]{:S(2)}) collective-permute-start(bf16[1536,128]{1,0:T(8,128)(2,1)S(1)} %collective-permute-done.9.w2), channel_id=1, source_target_pairs={{0,32},{1,33},{2,34},{3,35},{4,36},{5,37},{6,38},{7,39},{32,0},{33... | collective-permute-start | bytes 1179656 | tf_op jit(solution)/shard_map/ppermute | solution.py:41
  36.8 17.1 %collective-permute-start.18 = (bf16[512,128]{1,0:T(8,128)(2,1)S(1)}, bf16[512,128]{1,0:T(8,128)(2,1)S(1)}, u32[]{:S(2)}, u32[]{:S(2)}) collective-permute-start(bf16[512,128]{1,0:T(8,128)(2,1)S(1)} %get-tuple-element.138), channel_id=1, source_target_pairs={{0,1},{1,0},{2,3},{3,2},{4,5},{5,4},{6,7},{7,6},{32,33},{33,32},{3... | collective-permute-start | bytes 393224 | tf_op jit(solution)/shard_map/ppermute | solution.py:41
  38.5 17.0 %collective-permute-start.19 = (bf16[512,128]{1,0:T(8,128)(2,1)S(1)}, bf16[512,128]{1,0:T(8,128)(2,1)S(1)}, u32[]{:S(2)}, u32[]{:S(2)}) collective-permute-start(bf16[512,128]{1,0:T(8,128)(2,1)S(1)} %get-tuple-element.139), channel_id=1, source_target_pairs={{0,2},{1,3},{2,0},{3,1},{4,6},{5,7},{6,4},{7,5},{32,34},{33,35},{3... | collective-permute-start | bytes 393224 | tf_op jit(solution)/shard_map/ppermute | solution.py:41
  39.8 15.7 %collective-permute-start.20 = (bf16[512,128]{1,0:T(8,128)(2,1)S(1)}, bf16[512,128]{1,0:T(8,128)(2,1)S(1)}, u32[]{:S(2)}, u32[]{:S(2)}) collective-permute-start(bf16[512,128]{1,0:T(8,128)(2,1)S(1)} %get-tuple-element.140), channel_id=1, source_target_pairs={{0,3},{1,2},{2,1},{3,0},{4,7},{5,6},{6,5},{7,4},{32,35},{33,34},{3... | collective-permute-start | bytes 393224 | tf_op jit(solution)/shard_map/ppermute | solution.py:41
  41.5 18.6 %slice-start = ((s8[6291456]{0:T(1024)(128)(4,1)}), s8[4194304]{0:T(1024)(128)(4,1)S(1)}, s32[]{:S(2)}) async-start(s8[6291456]{0:T(1024)(128)(4,1)} %bitcast.17), calls=%async_computation | async-start | bytes 8388608
  41.5 18.6 %slice-start.1 = ((s8[6291456]{0:T(1024)(128)(4,1)}), s8[2097152]{0:T(1024)(128)(4,1)S(1)}, s32[]{:S(2)}) async-start(s8[6291456]{0:T(1024)(128)(4,1)} %bitcast.17), calls=%async_computation.1 | async-start | bytes 4194304
  46.3 11.1 %copy-start.3 = (bf16[1,256,1536]{2,1,0:T(8,128)(2,1)S(1)}, bf16[1,256,1536]{2,1,0:T(8,128)(2,1)}, u32[]{:S(2)}) copy-start(bf16[1,256,1536]{2,1,0:T(8,128)(2,1)} %param.13) | copy-start | bytes 2359300
  46.3 4.3 %collective-permute-start.14 = (bf16[256,128]{1,0:T(8,128)(2,1)S(1)}, bf16[256,128]{1,0:T(8,128)(2,1)S(1)}, u32[]{:S(2)}, u32[]{:S(2)}) collective-permute-start(bf16[256,128]{1,0:T(8,128)(2,1)S(1)} %get-tuple-element.135.own), channel_id=1, source_target_pairs={{0,4},{1,5},{2,6},{3,7},{4,0},{5,1},{6,2},{7,3},{32,36},{33,37},{3... | collective-permute-start | bytes 196616 | tf_op jit(solution)/shard_map/ppermute | solution.py:41
  50.8 9.2 %collective-permute-start.15 = (bf16[512,128]{1,0:T(8,128)(2,1)S(1)}, bf16[512,128]{1,0:T(8,128)(2,1)S(1)}, u32[]{:S(2)}, u32[]{:S(2)}) collective-permute-start(bf16[512,128]{1,0:T(8,128)(2,1)S(1)} %shard_map.115.v0), channel_id=1, source_target_pairs={{0,1},{1,0},{2,3},{3,2},{4,5},{5,4},{6,7},{7,6},{32,33},{33,32},{3... | collective-permute-start | bytes 393224 | tf_op jit(solution)/shard_map/ppermute | solution.py:41
  51.3 8.7 %collective-permute-start.16 = (bf16[512,128]{1,0:T(8,128)(2,1)S(1)}, bf16[512,128]{1,0:T(8,128)(2,1)S(1)}, u32[]{:S(2)}, u32[]{:S(2)}) collective-permute-start(bf16[512,128]{1,0:T(8,128)(2,1)S(1)} %shard_map.115.v0), channel_id=1, source_target_pairs={{0,2},{1,3},{2,0},{3,1},{4,6},{5,7},{6,4},{7,5},{32,34},{33,35},{3... | collective-permute-start | bytes 393224 | tf_op jit(solution)/shard_map/ppermute | solution.py:41
  53.9 6.2 %collective-permute-start.17 = (bf16[512,128]{1,0:T(8,128)(2,1)S(1)}, bf16[512,128]{1,0:T(8,128)(2,1)S(1)}, u32[]{:S(2)}, u32[]{:S(2)}) collective-permute-start(bf16[512,128]{1,0:T(8,128)(2,1)S(1)} %shard_map.115.v0), channel_id=1, source_target_pairs={{0,3},{1,2},{2,1},{3,0},{4,7},{5,6},{6,5},{7,4},{32,35},{33,34},{3... | collective-permute-start | bytes 393224 | tf_op jit(solution)/shard_map/ppermute | solution.py:41
  55.6 4.3 %collective-permute-start.21 = (bf16[256,128]{1,0:T(8,128)(2,1)S(1)}, bf16[256,128]{1,0:T(8,128)(2,1)S(1)}, u32[]{:S(2)}, u32[]{:S(2)}) collective-permute-start(bf16[256,128]{1,0:T(8,128)(2,1)S(1)} %slice.97), channel_id=1, source_target_pairs={{0,4},{1,5},{2,6},{3,7},{4,0},{5,1},{6,2},{7,3},{32,36},{33,37},{3... | collective-permute-start | bytes 196616 | tf_op jit(solution)/shard_map/ppermute | solution.py:41
  62.0 3.9 %collective-permute-start.22 = (bf16[2048,384]{1,0:T(8,128)(2,1)S(1)}, bf16[2048,384]{1,0:T(8,128)(2,1)S(1)}, u32[]{:S(2)}, u32[]{:S(2)}) collective-permute-start(bf16[2048,384]{1,0:T(8,128)(2,1)S(1)} %get-tuple-element.157), channel_id=1, source_target_pairs={{0,32},{1,33},{2,34},{3,35},{4,36},{5,37},{6,38},{7,39},{32,0},{33... | collective-permute-start | bytes 4718600 | tf_op jit(solution)/shard_map/ppermute | solution.py:41
  62.1 17.4 %collective-permute-start.26 = (bf16[1792,128]{1,0:T(8,128)(2,1)S(1)}, bf16[1792,128]{1,0:T(8,128)(2,1)S(1)}, u32[]{:S(2)}, u32[]{:S(2)}) collective-permute-start(bf16[1792,128]{1,0:T(8,128)(2,1)S(1)} %get-tuple-element.158), channel_id=1, source_target_pairs={{0,8},{8,0},{16,24},{24,16},{1,9},{9,1},{17,25},{25,17},{2,10},{10... | collective-permute-start | bytes 1376264 | tf_op jit(solution)/shard_map/ppermute | solution.py:65
  63.7 15.8 %collective-permute-start.27 = (bf16[1792,128]{1,0:T(8,128)(2,1)S(1)}, bf16[1792,128]{1,0:T(8,128)(2,1)S(1)}, u32[]{:S(2)}, u32[]{:S(2)}) collective-permute-start(bf16[1792,128]{1,0:T(8,128)(2,1)S(1)} %get-tuple-element.160), channel_id=1, source_target_pairs={{0,24},{8,16},{16,8},{24,0},{1,25},{9,17},{17,9},{25,1},{2,26},{10... | collective-permute-start | bytes 1376264 | tf_op jit(solution)/shard_map/ppermute | solution.py:65
  65.9 5.2 %copy-start.2 = (bf16[1,256,1536]{2,1,0:T(8,128)(2,1)S(1)}, bf16[1,256,1536]{2,1,0:T(8,128)(2,1)}, u32[]{:S(2)}) copy-start(bf16[1,256,1536]{2,1,0:T(8,128)(2,1)} %param.9) | copy-start | bytes 2359300
  66.3 13.2 %collective-permute-start.23 = (bf16[512,384]{1,0:T(8,128)(2,1)S(1)}, bf16[512,384]{1,0:T(8,128)(2,1)S(1)}, u32[]{:S(2)}, u32[]{:S(2)}) collective-permute-start(bf16[512,384]{1,0:T(8,128)(2,1)S(1)} %get-tuple-element.200), channel_id=1, source_target_pairs={{0,4},{1,5},{2,6},{3,7},{4,0},{5,1},{6,2},{7,3},{32,33},{33,32},{3... | collective-permute-start | bytes 1179656 | tf_op jit(solution)/shard_map/ppermute | solution.py:41
  68.1 11.4 %collective-permute-start.24 = (bf16[512,384]{1,0:T(8,128)(2,1)S(1)}, bf16[512,384]{1,0:T(8,128)(2,1)S(1)}, u32[]{:S(2)}, u32[]{:S(2)}) collective-permute-start(bf16[512,384]{1,0:T(8,128)(2,1)S(1)} %get-tuple-element.199), channel_id=1, source_target_pairs={{0,64},{1,65},{2,66},{3,67},{4,68},{5,69},{6,70},{7,71},{32,34},{3... | collective-permute-start | bytes 1179656 | tf_op jit(solution)/shard_map/ppermute | solution.py:41
  69.5 13.2 %collective-permute-start.25 = (bf16[512,384]{1,0:T(8,128)(2,1)S(1)}, bf16[512,384]{1,0:T(8,128)(2,1)S(1)}, u32[]{:S(2)}, u32[]{:S(2)}) collective-permute-start(bf16[512,384]{1,0:T(8,128)(2,1)S(1)} %get-tuple-element.198), channel_id=1, source_target_pairs={{0,68},{1,69},{2,70},{3,71},{4,64},{5,65},{6,66},{7,67},{32,35},{3... | collective-permute-start | bytes 1179656 | tf_op jit(solution)/shard_map/ppermute | solution.py:41
  82.7 6.7 %collective-permute-start.30 = (bf16[1792,128]{1,0:T(8,128)(2,1)S(1)}, bf16[1792,128]{1,0:T(8,128)(2,1)S(1)}, u32[]{:S(2)}, u32[]{:S(2)}) collective-permute-start(bf16[1792,128]{1,0:T(8,128)(2,1)S(1)} %collective-permute-done.26.a1), channel_id=1, source_target_pairs={{0,32},{1,33},{2,34},{3,35},{4,36},{5,37},{6,38},{7,39},{32,0},{33... | collective-permute-start | bytes 1376264 | tf_op jit(solution)/shard_map/ppermute | solution.py:41
  82.7 6.7 %collective-permute-start.31 = (bf16[1792,128]{1,0:T(8,128)(2,1)S(1)}, bf16[1792,128]{1,0:T(8,128)(2,1)S(1)}, u32[]{:S(2)}, u32[]{:S(2)}) collective-permute-start(bf16[1792,128]{1,0:T(8,128)(2,1)S(1)} %collective-permute-done.27.a3), channel_id=1, source_target_pairs={{0,32},{1,33},{2,34},{3,35},{4,36},{5,37},{6,38},{7,39},{32,0},{33... | collective-permute-start | bytes 1376264 | tf_op jit(solution)/shard_map/ppermute | solution.py:41
  83.2 5.9 %collective-permute-start.28 = (bf16[512,128]{1,0:T(8,128)(2,1)S(1)}, bf16[512,128]{1,0:T(8,128)(2,1)S(1)}, u32[]{:S(2)}, u32[]{:S(2)}) collective-permute-start(bf16[512,128]{1,0:T(8,128)(2,1)S(1)} %get-tuple-element.161), channel_id=1, source_target_pairs={{0,1},{1,0},{2,3},{3,2},{4,5},{5,4},{6,7},{7,6},{32,33},{33,32},{3... | collective-permute-start | bytes 393224 | tf_op jit(solution)/shard_map/ppermute | solution.py:41
  83.2 14.7 %collective-permute-start.33 = (bf16[1792,128]{1,0:T(8,128)(2,1)S(1)}, bf16[1792,128]{1,0:T(8,128)(2,1)S(1)}, u32[]{:S(2)}, u32[]{:S(2)}) collective-permute-start(bf16[1792,128]{1,0:T(8,128)(2,1)S(1)} %get-tuple-element.173), channel_id=1, source_target_pairs={{0,16},{8,24},{16,0},{24,8},{1,17},{9,25},{17,1},{25,9},{2,18},{10... | collective-permute-start | bytes 1376264 | tf_op jit(solution)/shard_map/ppermute | solution.py:65
  85.9 8.3 %collective-permute-start.29 = (bf16[512,128]{1,0:T(8,128)(2,1)S(1)}, bf16[512,128]{1,0:T(8,128)(2,1)S(1)}, u32[]{:S(2)}, u32[]{:S(2)}) collective-permute-start(bf16[512,128]{1,0:T(8,128)(2,1)S(1)} %get-tuple-element.167), channel_id=1, source_target_pairs={{0,2},{1,3},{2,0},{3,1},{4,6},{5,7},{6,4},{7,5},{32,34},{33,35},{3... | collective-permute-start | bytes 393224 | tf_op jit(solution)/shard_map/ppermute | solution.py:41
  89.4 8.5 %collective-permute-start.32 = (bf16[512,128]{1,0:T(8,128)(2,1)S(1)}, bf16[512,128]{1,0:T(8,128)(2,1)S(1)}, u32[]{:S(2)}, u32[]{:S(2)}) collective-permute-start(bf16[512,128]{1,0:T(8,128)(2,1)S(1)} %get-tuple-element.171), channel_id=1, source_target_pairs={{0,3},{1,2},{2,1},{3,0},{4,7},{5,6},{6,5},{7,4},{32,35},{33,34},{3... | collective-permute-start | bytes 393224 | tf_op jit(solution)/shard_map/ppermute | solution.py:41
  91.0 4.7 %collective-permute-start.34 = (bf16[128,384]{1,0:T(8,128)(2,1)S(1)}, bf16[128,384]{1,0:T(8,128)(2,1)S(1)}, u32[]{:S(2)}, u32[]{:S(2)}) collective-permute-start(bf16[128,384]{1,0:T(8,128)(2,1)S(1)} %get-tuple-element.204), channel_id=1, source_target_pairs={{0,1},{1,0},{2,3},{3,2},{4,5},{5,4},{6,7},{7,6},{32,36},{33,37},{3... | collective-permute-start | bytes 294920 | tf_op jit(solution)/shard_map/ppermute | solution.py:41
  91.1 6.8 %collective-permute-start.35 = (bf16[128,384]{1,0:T(8,128)(2,1)S(1)}, bf16[128,384]{1,0:T(8,128)(2,1)S(1)}, u32[]{:S(2)}, u32[]{:S(2)}) collective-permute-start(bf16[128,384]{1,0:T(8,128)(2,1)S(1)} %get-tuple-element.203), channel_id=1, source_target_pairs={{0,2},{1,3},{2,0},{3,1},{4,6},{5,7},{6,4},{7,5},{32,96},{33,97},{3... | collective-permute-start | bytes 294920 | tf_op jit(solution)/shard_map/ppermute | solution.py:41
  97.9 1.8 %collective-permute-start.37 = (bf16[1792,128]{1,0:T(8,128)(2,1)S(1)}, bf16[1792,128]{1,0:T(8,128)(2,1)S(1)}, u32[]{:S(2)}, u32[]{:S(2)}) collective-permute-start(bf16[1792,128]{1,0:T(8,128)(2,1)S(1)} %collective-permute-done.33.a2), channel_id=1, source_target_pairs={{0,32},{1,33},{2,34},{3,35},{4,36},{5,37},{6,38},{7,39},{32,0},{33... | collective-permute-start | bytes 1376264 | tf_op jit(solution)/shard_map/ppermute | solution.py:41
  97.9 5.9 %collective-permute-start.36 = (bf16[128,384]{1,0:T(8,128)(2,1)S(1)}, bf16[128,384]{1,0:T(8,128)(2,1)S(1)}, u32[]{:S(2)}, u32[]{:S(2)}) collective-permute-start(bf16[128,384]{1,0:T(8,128)(2,1)S(1)} %get-tuple-element.202), channel_id=1, source_target_pairs={{0,3},{1,2},{2,1},{3,0},{4,7},{5,6},{6,5},{7,4},{32,100},{33,101},... | collective-permute-start | bytes 294920 | tf_op jit(solution)/shard_map/ppermute | solution.py:41
  99.6 4.3 %collective-permute-start.38 = (bf16[256,128]{1,0:T(8,128)(2,1)S(1)}, bf16[256,128]{1,0:T(8,128)(2,1)S(1)}, u32[]{:S(2)}, u32[]{:S(2)}) collective-permute-start(bf16[256,128]{1,0:T(8,128)(2,1)S(1)} %slice.96), channel_id=1, source_target_pairs={{0,4},{1,5},{2,6},{3,7},{4,0},{5,1},{6,2},{7,3},{32,36},{33,37},{3... | collective-permute-start | bytes 196616 | tf_op jit(solution)/shard_map/ppermute | solution.py:41

commit v4 on v3

--- a/solution.py
+++ b/solution.py
@@ -392,10 +392,11 @@
     together = lax.optimization_barrier
 
     own_keys = rotary_key_rows[0]
+    lowest = jnp.finfo(bf16).min
     near, first, placing, head, docs = together(
         (
-            [own_keys, x_swap(own_keys)],
-            [value_projection] + [first_with(value_projection, r) for r in (1, 2, 3)],
+            [jnp.maximum(own_keys, lowest), x_swap(own_keys)],
+            [jnp.maximum(value_projection, lowest)] + [first_with(value_projection, r) for r in (1, 2, 3)],
             block_place[0],
             lax.axis_index("head"),
             jnp.maximum(doc_ids[0], 0).reshape(16, BLOCK),
@@ -403,7 +404,7 @@
     )
     near, first = joined(near), joined(first)
 
-    keys, w1, w3, first, table, slabs = together(
+    keys, w1, w3, first, table, slabs, first_query = together(
         (
             [near] + [z_with(near, r) for r in (1, 2, 3)],
             second_with(first, 1),
@@ -411,6 +412,7 @@
             first,
             places_of_keys(placing),
             places_of_slabs(head),
+            jnp.maximum(query, lowest),
         )
     )
 
@@ -419,7 +421,7 @@
     totals, *value_parts = call(
         value_side_kernel,
         [((24, 128), f32)] + parts_out,
-        [table, docs, query, grad, *keys],
+        [table, docs, first_query, grad, *keys],
         scratch=[((rows, 1536), bf16)] * 2
         + [whole, window, bias, ((SPAN, 256), f32), square, stack]
         + sums
@@ -475,7 +477,7 @@
         scratch=[whole, whole, window, window, bias, square, stack] + sums,
         cost=9, limit=28,
     )
-    key_parts, w_got, messages = together((key_parts, w_got, messages))
+    key_parts, w_got[:3], messages = together((key_parts, w_got[:3], messages))
 
     messages[1] = y_with(messages[1], 2)
     swapped = [core_swap(messages[0]), None, core_swap(messages[2])]

time: 106 us -> 102 us (0.962)
  local copies, waits for them, and re-layouts: 3.04 us -> 0.17 us
  waiting for transfers between devices: 19.3 us -> 17.3 us
  other arithmetic: 3.79 us -> 5.41 us
    max x0 -> x3, other arithmetic: none -> 2.96 us  [the longest x1 1.2 us: local(): jnp.maximum(query, lowest)]
    unnamed x16 -> x12, local copies, waits for them, and re-layouts: 2.89 us -> 0.03 us
    ppermute x36, waiting for transfers between devices: 19.3 us -> 17.2 us  [moved(): return lax.ppermute(value, ('dp', 'ctx'), pairs)]
  transfers between devices with their start and end apart: 39 -> 39, of which waited for: 12 -> 10; matrix products, arithmetic and copies ran while one was open for 3% -> 5% of each run, Pallas kernels for 23% -> 24%
where the time goes in v4:
time: 102 us
  starting transfers between devices  50.9 us (50%)
  Pallas kernels  26.9 us (26%)
  waiting for transfers between devices  17.3 us (17%)
  other arithmetic  5.41 us (5%)
    ppermute x36, starting transfers between devices, moved(): return lax.ppermute(value, ('dp', 'ctx'), pairs)  44.3 us
    pallas_call x10, Pallas kernels, call(): pl.pallas_call(kernel, out_shape=tuple((jax.ShapeDtypeStruct(s, d) for s,...  26.9 us
    ppermute x36, waiting for transfers between devices, moved(): return lax.ppermute(value, ('dp', 'ctx'), pairs)  17.2 us
    ppermute x3, starting transfers between devices, y_with(): return lax.ppermute(value, 'head', [(y, y ^ bits) for y in range(4)])  6.58 us
  transfers between devices with their start and end apart: 39, of which 10 were waited for; matrix products, arithmetic and copies ran while one was open for 5% of the time, Pallas kernels for 24%

profile of v4, /device:TPU:0, one launch (start us, length us, event | category | flops | bytes accessed | tf_op | source)
XLA Modules:
  0.0 101.7 jit_solution(801540490987205154)
XLA Ops:
  0.7 2.1 %collective-permute-start.1 = (bf16[384,128]{1,0:T(8,128)(2,1)}, bf16[384,128]{1,0:T(8,128)(2,1)S(1)}, u32[]{:S(2)}, u32[]{:S(2)}) collective-permute-start(bf16[384,128]{1,0:T(8,128)(2,1)} %param.11), channel_id=1, source_target_pairs={{0,1},{1,0},{2,3},{3,2},{4,5},{5,4},{6,7},{7,6},{32,36},{33,37},{3... | collective-permute-start | bytes 294920 | tf_op jit(solution)/shard_map/ppermute | solution.py:41
  2.7 3.6 %collective-permute-start.2 = (bf16[384,128]{1,0:T(8,128)(2,1)}, bf16[384,128]{1,0:T(8,128)(2,1)S(1)}, u32[]{:S(2)}, u32[]{:S(2)}) collective-permute-start(bf16[384,128]{1,0:T(8,128)(2,1)} %param.11), channel_id=1, source_target_pairs={{0,2},{1,3},{2,0},{3,1},{4,6},{5,7},{6,4},{7,5},{32,96},{33,97},{3... | collective-permute-start | bytes 294920 | tf_op jit(solution)/shard_map/ppermute | solution.py:41
  6.3 1.5 %collective-permute-start = (bf16[256,128]{1,0:T(8,128)(2,1)}, bf16[256,128]{1,0:T(8,128)(2,1)S(1)}, u32[]{:S(2)}, u32[]{:S(2)}) collective-permute-start(bf16[256,128]{1,0:T(8,128)(2,1)} %bitcast.30), channel_id=1, source_target_pairs={{0,4},{1,5},{2,6},{3,7},{4,0},{5,1},{6,2},{7,3},{32,36},{33,37},{3... | collective-permute-start | bytes 196616 | tf_op jit(solution)/shard_map/ppermute | solution.py:41
  7.8 0.9 broadcast_maximum_fusion.1.own
  8.7 0.8 broadcast_maximum_fusion.2.own
  9.6 0.7 broadcast_maximum_fusion.3
  10.3 1.2 %broadcast_maximum_fusion.q_any = bf16[256,1536]{1,0:T(8,128)(2,1)S(1)} fusion(bf16[1,256,1536]{2,1,0:T(8,128)(2,1)} %param.9), kind=kLoop, calls=%fused_computation.5 | loop fusion | flops 393216 | bytes 1572864 | tf_op jit(solution)/shard_map/max | solution.py:415
  11.6 0.8 collective-permute-done.3.refs_2_
  12.4 0.1 shard_map.112.w0
  12.5 1.6 %collective-permute-start.7 = (bf16[1536,128]{1,0:T(8,128)(2,1)S(1)}, bf16[1536,128]{1,0:T(8,128)(2,1)S(1)}, u32[]{:S(2)}, u32[]{:S(2)}) collective-permute-start(bf16[1536,128]{1,0:T(8,128)(2,1)S(1)} %shard_map.112.w0), channel_id=1, source_target_pairs={{0,4},{1,5},{2,6},{3,7},{4,0},{5,1},{6,2},{7,3},{32,33},{33,32},{3... | collective-permute-start | bytes 1179656 | tf_op jit(solution)/shard_map/ppermute | solution.py:41
  14.1 2.1 %collective-permute-start.8 = (bf16[1536,128]{1,0:T(8,128)(2,1)S(1)}, bf16[1536,128]{1,0:T(8,128)(2,1)S(1)}, u32[]{:S(2)}, u32[]{:S(2)}) collective-permute-start(bf16[1536,128]{1,0:T(8,128)(2,1)S(1)} %shard_map.112.w0), channel_id=1, source_target_pairs={{0,68},{1,69},{2,70},{3,71},{4,64},{5,65},{6,66},{7,67},{32,35},{3... | collective-permute-start | bytes 1179656 | tf_op jit(solution)/shard_map/ppermute | solution.py:41
  16.2 0.1 shard_map.111.k0
  16.2 0.1 collective-permute-start.4
  16.3 3.7 %collective-permute-start.5 = (bf16[512,128]{1,0:T(8,128)(2,1)S(1)}, bf16[512,128]{1,0:T(8,128)(2,1)S(1)}, u32[]{:S(2)}, u32[]{:S(2)}) collective-permute-start(bf16[512,128]{1,0:T(8,128)(2,1)S(1)} %shard_map.111.k0), channel_id=1, source_target_pairs={{0,2},{1,3},{2,0},{3,1},{4,6},{5,7},{6,4},{7,5},{32,34},{33,35},{3... | collective-permute-start | bytes 393224 | tf_op jit(solution)/shard_map/ppermute | solution.py:41
  20.0 1.0 %collective-permute-start.6 = (bf16[512,128]{1,0:T(8,128)(2,1)S(1)}, bf16[512,128]{1,0:T(8,128)(2,1)S(1)}, u32[]{:S(2)}, u32[]{:S(2)}) collective-permute-start(bf16[512,128]{1,0:T(8,128)(2,1)S(1)} %shard_map.111.k0), channel_id=1, source_target_pairs={{0,3},{1,2},{2,1},{3,0},{4,7},{5,6},{6,5},{7,4},{32,35},{33,34},{3... | collective-permute-start | bytes 393224 | tf_op jit(solution)/shard_map/ppermute | solution.py:41
  21.0 0.2 fusion.2
  21.2 0.1 select_reduce_fusion
  21.3 0.1 concatenate.7.table_ref
  21.5 3.9 %collective-permute-done.5.k2 = bf16[512,128]{1,0:T(8,128)(2,1)S(1)} collective-permute-done((bf16[512,128]{1,0:T(8,128)(2,1)S(1)}, bf16[512,128]{1,0:T(8,128)(2,1)S(1)}, u32[]{:S(2)}, u32[]{:S(2)}) %collective-permute-start.5) | collective-permute-done | bytes 131104 | tf_op jit(solution)/shard_map/ppermute | solution.py:41
  25.4 1.3 %collective-permute-done.6.k3 = bf16[512,128]{1,0:T(8,128)(2,1)S(1)} collective-permute-done((bf16[512,128]{1,0:T(8,128)(2,1)S(1)}, bf16[512,128]{1,0:T(8,128)(2,1)S(1)}, u32[]{:S(2)}, u32[]{:S(2)}) %collective-permute-start.6) | collective-permute-done | bytes 131104 | tf_op jit(solution)/shard_map/ppermute | solution.py:41
  26.7 0.5 collective-permute-start.11
  27.2 0.1 collective-permute-start.12
  27.3 0.9 collective-permute-start.9
  28.2 6.9 %shard_map.113 = (f32[24,128]{1,0:T(8,128)S(1)}, f32[512,128]{1,0:T(8,128)S(1)}, bf16[512,128]{1,0:T(8,128)(2,1)S(1)}, bf16[512,128]{1,0:T(8,128)(2,1)S(1)}, bf16[512,128]{1,0:T(8,128)(2,1)S(1)}) custom-call(s32[18]{0:T(128)S(1)} %pad_add_fusion.table_ref, s32[16,128]{1,0:T(8,128)S(1)} %bitcast.27, bf16[256,1536]{1,0:T(8,128)(2,1)S(1)} %broadcast_maximum_fusion.q_any, ...), custom_call_target="tpu_custom_call" | custom-call | bytes 22020096 | tf_op jit(solution)/shard_map/pallas_call | solution.py:313
  35.1 0.1 collective-permute-start.13
  35.2 1.3 %collective-permute-start.18 = (bf16[512,128]{1,0:T(8,128)(2,1)S(1)}, bf16[512,128]{1,0:T(8,128)(2,1)S(1)}, u32[]{:S(2)}, u32[]{:S(2)}) collective-permute-start(bf16[512,128]{1,0:T(8,128)(2,1)S(1)} %get-tuple-element.139), channel_id=1, source_target_pairs={{0,1},{1,0},{2,3},{3,2},{4,5},{5,4},{6,7},{7,6},{32,33},{33,32},{3... | collective-permute-start | bytes 393224 | tf_op jit(solution)/shard_map/ppermute | solution.py:41
  36.5 0.7 collective-permute-start.19
  37.2 2.7 %collective-permute-start.20 = (bf16[512,128]{1,0:T(8,128)(2,1)S(1)}, bf16[512,128]{1,0:T(8,128)(2,1)S(1)}, u32[]{:S(2)}, u32[]{:S(2)}) collective-permute-start(bf16[512,128]{1,0:T(8,128)(2,1)S(1)} %get-tuple-element.141), channel_id=1, source_target_pairs={{0,3},{1,2},{2,1},{3,0},{4,7},{5,6},{6,5},{7,4},{32,35},{33,34},{3... | collective-permute-start | bytes 393224 | tf_op jit(solution)/shard_map/ppermute | solution.py:41
  40.0 4.8 %shard_map.114 = (bf16[256,128]{1,0:T(8,128)(2,1)S(1)}, bf16[3072,128]{1,0:T(8,128)(2,1)S(1)}, bf16[1536,128]{1,0:T(8,128)(2,1)S(1)}, bf16[1536,128]{1,0:T(8,128)(2,1)S(1)}, bf16[1536,128]{1,0:T(8,128)(2,1)S(1)}) custom-call(s32[37]{0:T(128)S(1)} %concatenate.7.table_ref, bf16[256,12288]{1,0:T(8,128)(2,1)} %bitcast.18, bf16[1536,128]{1,0:T(8,128)(2,1)S(1)} %shard_map.112.w0, ...), custom_call_target="tpu_custom_call" | custom-call | bytes 12582912 | tf_op jit(solution)/shard_map/pallas_call | solution.py:313
  44.8 1.2 %collective-permute-start.14 = (bf16[256,128]{1,0:T(8,128)(2,1)S(1)}, bf16[256,128]{1,0:T(8,128)(2,1)S(1)}, u32[]{:S(2)}, u32[]{:S(2)}) collective-permute-start(bf16[256,128]{1,0:T(8,128)(2,1)S(1)} %get-tuple-element.136.own), channel_id=1, source_target_pairs={{0,4},{1,5},{2,6},{3,7},{4,0},{5,1},{6,2},{7,3},{32,36},{33,37},{3... | collective-permute-start | bytes 196616 | tf_op jit(solution)/shard_map/ppermute | solution.py:41
  46.1 3.1 %collective-permute-done.14.refs_0_ = bf16[256,128]{1,0:T(8,128)(2,1)S(1)} collective-permute-done((bf16[256,128]{1,0:T(8,128)(2,1)S(1)}, bf16[256,128]{1,0:T(8,128)(2,1)S(1)}, u32[]{:S(2)}, u32[]{:S(2)}) %collective-permute-start.14) | collective-permute-done | bytes 65568 | tf_op jit(solution)/shard_map/ppermute | solution.py:41
  49.3 0.1 collective-permute-start.15
  49.4 1.9 %collective-permute-start.16 = (bf16[512,128]{1,0:T(8,128)(2,1)S(1)}, bf16[512,128]{1,0:T(8,128)(2,1)S(1)}, u32[]{:S(2)}, u32[]{:S(2)}) collective-permute-start(bf16[512,128]{1,0:T(8,128)(2,1)S(1)} %shard_map.115.v0), channel_id=1, source_target_pairs={{0,2},{1,3},{2,0},{3,1},{4,6},{5,7},{6,4},{7,5},{32,34},{33,35},{3... | collective-permute-start | bytes 393224 | tf_op jit(solution)/shard_map/ppermute | solution.py:41
  51.3 2.7 %collective-permute-start.17 = (bf16[512,128]{1,0:T(8,128)(2,1)S(1)}, bf16[512,128]{1,0:T(8,128)(2,1)S(1)}, u32[]{:S(2)}, u32[]{:S(2)}) collective-permute-start(bf16[512,128]{1,0:T(8,128)(2,1)S(1)} %shard_map.115.v0), channel_id=1, source_target_pairs={{0,3},{1,2},{2,1},{3,0},{4,7},{5,6},{6,5},{7,4},{32,35},{33,34},{3... | collective-permute-start | bytes 393224 | tf_op jit(solution)/shard_map/ppermute | solution.py:41
  54.1 1.2 %collective-permute-start.21 = (bf16[256,128]{1,0:T(8,128)(2,1)S(1)}, bf16[256,128]{1,0:T(8,128)(2,1)S(1)}, u32[]{:S(2)}, u32[]{:S(2)}) collective-permute-start(bf16[256,128]{1,0:T(8,128)(2,1)S(1)} %slice.97), channel_id=1, source_target_pairs={{0,4},{1,5},{2,6},{3,7},{4,0},{5,1},{6,2},{7,3},{32,36},{33,37},{3... | collective-permute-start | bytes 196616 | tf_op jit(solution)/shard_map/ppermute | solution.py:41
  55.4 0.5 shard_map.116.term_ref
  55.8 2.6 %collective-permute-done.21 = bf16[256,128]{1,0:T(8,128)(2,1)S(1)} collective-permute-done((bf16[256,128]{1,0:T(8,128)(2,1)S(1)}, bf16[256,128]{1,0:T(8,128)(2,1)S(1)}, u32[]{:S(2)}, u32[]{:S(2)}) %collective-permute-start.21) | collective-permute-done | bytes 65568 | tf_op jit(solution)/shard_map/ppermute | solution.py:41
  58.5 1.9 %shard_map.118 = (f32[2048,384]{1,0:T(8,128)S(1)}, bf16[2048,384]{1,0:T(8,128)(2,1)S(1)}, bf16[1792,128]{1,0:T(8,128)(2,1)S(1)}, bf16[1792,128]{1,0:T(8,128)(2,1)S(1)}, bf16[1792,128]{1,0:T(8,128)(2,1)S(1)}) custom-call(s32[37]{0:T(128)S(1)} %concatenate.7.table_ref, bf16[256,12288]{1,0:T(8,128)(2,1)S(1)} %bitcast.21, ...), custom_call_target="tpu_custom_call" | custom-call | bytes 12582912 | tf_op jit(solution)/shard_map/pallas_call | solution.py:313
  60.4 0.1 collective-permute-start.22
  60.5 1.7 %collective-permute-start.25 = (bf16[1792,128]{1,0:T(8,128)(2,1)S(1)}, bf16[1792,128]{1,0:T(8,128)(2,1)S(1)}, u32[]{:S(2)}, u32[]{:S(2)}) collective-permute-start(bf16[1792,128]{1,0:T(8,128)(2,1)S(1)} %get-tuple-element.159), channel_id=1, source_target_pairs={{0,8},{8,0},{16,24},{24,16},{1,9},{9,1},{17,25},{25,17},{2,10},{10... | collective-permute-start | bytes 1376264 | tf_op jit(solution)/shard_map/ppermute | solution.py:65
  62.2 2.2 %collective-permute-start.26 = (bf16[1792,128]{1,0:T(8,128)(2,1)S(1)}, bf16[1792,128]{1,0:T(8,128)(2,1)S(1)}, u32[]{:S(2)}, u32[]{:S(2)}) collective-permute-start(bf16[1792,128]{1,0:T(8,128)(2,1)S(1)} %get-tuple-element.161), channel_id=1, source_target_pairs={{0,24},{8,16},{16,8},{24,0},{1,25},{9,17},{17,9},{25,1},{2,26},{10... | collective-permute-start | bytes 1376264 | tf_op jit(solution)/shard_map/ppermute | solution.py:65
  64.4 0.4 add_convert_fusion
  64.7 1.2 %collective-permute-start.23 = (bf16[512,384]{1,0:T(8,128)(2,1)S(1)}, bf16[512,384]{1,0:T(8,128)(2,1)S(1)}, u32[]{:S(2)}, u32[]{:S(2)}) collective-permute-start(bf16[512,384]{1,0:T(8,128)(2,1)S(1)} %get-tuple-element.200), channel_id=1, source_target_pairs={{0,4},{1,5},{2,6},{3,7},{4,0},{5,1},{6,2},{7,3},{32,33},{33,32},{3... | collective-permute-start | bytes 1179656 | tf_op jit(solution)/shard_map/ppermute | solution.py:41
  66.0 2.9 %collective-permute-start.24 = (bf16[512,384]{1,0:T(8,128)(2,1)S(1)}, bf16[512,384]{1,0:T(8,128)(2,1)S(1)}, u32[]{:S(2)}, u32[]{:S(2)}) collective-permute-start(bf16[512,384]{1,0:T(8,128)(2,1)S(1)} %get-tuple-element.199), channel_id=1, source_target_pairs={{0,64},{1,65},{2,66},{3,67},{4,68},{5,69},{6,70},{7,71},{32,34},{3... | collective-permute-start | bytes 1179656 | tf_op jit(solution)/shard_map/ppermute | solution.py:41
  68.8 0.7 collective-permute-start.28
  69.5 8.4 %shard_map.117 = (bf16[256,1536]{1,0:T(8,128)(2,1)}, f32[512,128]{1,0:T(8,128)S(1)}, bf16[512,128]{1,0:T(8,128)(2,1)S(1)}, bf16[512,128]{1,0:T(8,128)(2,1)S(1)}, bf16[512,128]{1,0:T(8,128)(2,1)S(1)}) custom-call(s32[18]{0:T(128)S(1)} %pad_add_fusion.table_ref, s32[16,128]{1,0:T(8,128)S(1)} %bitcast.28, bf16[256,1536]{1,0:T(8,128)(2,1)S(1)} %bitcast.25, ...), custom_call_target="tpu_custom_call" | custom-call | bytes 28311552 | tf_op jit(solution)/shard_map/pallas_call | solution.py:313
  77.9 1.0 collective-permute-done.24
  78.9 0.5 collective-permute-start.31
  79.4 2.8 %collective-permute-start.33 = (bf16[1792,128]{1,0:T(8,128)(2,1)S(1)}, bf16[1792,128]{1,0:T(8,128)(2,1)S(1)}, u32[]{:S(2)}, u32[]{:S(2)}) collective-permute-start(bf16[1792,128]{1,0:T(8,128)(2,1)S(1)} %get-tuple-element.173), channel_id=1, source_target_pairs={{0,16},{8,24},{16,0},{24,8},{1,17},{9,25},{17,1},{25,9},{2,18},{10... | collective-permute-start | bytes 1376264 | tf_op jit(solution)/shard_map/ppermute | solution.py:65
  82.2 3.2 %collective-permute-start.29 = (bf16[512,128]{1,0:T(8,128)(2,1)S(1)}, bf16[512,128]{1,0:T(8,128)(2,1)S(1)}, u32[]{:S(2)}, u32[]{:S(2)}) collective-permute-start(bf16[512,128]{1,0:T(8,128)(2,1)S(1)} %get-tuple-element.167), channel_id=1, source_target_pairs={{0,2},{1,3},{2,0},{3,1},{4,6},{5,7},{6,4},{7,5},{32,34},{33,35},{3... | collective-permute-start | bytes 393224 | tf_op jit(solution)/shard_map/ppermute | solution.py:41
  85.4 0.2 fusion.17
  85.6 1.6 %collective-permute-start.32 = (bf16[512,128]{1,0:T(8,128)(2,1)S(1)}, bf16[512,128]{1,0:T(8,128)(2,1)S(1)}, u32[]{:S(2)}, u32[]{:S(2)}) collective-permute-start(bf16[512,128]{1,0:T(8,128)(2,1)S(1)} %get-tuple-element.171), channel_id=1, source_target_pairs={{0,3},{1,2},{2,1},{3,0},{4,7},{5,6},{6,5},{7,4},{32,35},{33,34},{3... | collective-permute-start | bytes 393224 | tf_op jit(solution)/shard_map/ppermute | solution.py:41
  87.2 0.1 collective-permute-start.34
  87.3 3.2 %collective-permute-start.35 = (bf16[128,384]{1,0:T(8,128)(2,1)S(1)}, bf16[128,384]{1,0:T(8,128)(2,1)S(1)}, u32[]{:S(2)}, u32[]{:S(2)}) collective-permute-start(bf16[128,384]{1,0:T(8,128)(2,1)S(1)} %get-tuple-element.203), channel_id=1, source_target_pairs={{0,2},{1,3},{2,0},{3,1},{4,6},{5,7},{6,4},{7,5},{32,96},{33,97},{3... | collective-permute-start | bytes 294920 | tf_op jit(solution)/shard_map/ppermute | solution.py:41
  90.5 1.4 %collective-permute-done.34.one = bf16[128,384]{1,0:T(8,128)(2,1)S(1)} collective-permute-done((bf16[128,384]{1,0:T(8,128)(2,1)S(1)}, bf16[128,384]{1,0:T(8,128)(2,1)S(1)}, u32[]{:S(2)}, u32[]{:S(2)}) %collective-permute-start.34) | collective-permute-done | bytes 98336 | tf_op jit(solution)/shard_map/ppermute | solution.py:41
  91.9 2.2 %collective-permute-done.35.two = bf16[128,384]{1,0:T(8,128)(2,1)S(1)} collective-permute-done((bf16[128,384]{1,0:T(8,128)(2,1)S(1)}, bf16[128,384]{1,0:T(8,128)(2,1)S(1)}, u32[]{:S(2)}, u32[]{:S(2)}) %collective-permute-start.35) | collective-permute-done | bytes 98336 | tf_op jit(solution)/shard_map/ppermute | solution.py:41
  94.1 1.6 %collective-permute-start.36 = (bf16[128,384]{1,0:T(8,128)(2,1)S(1)}, bf16[128,384]{1,0:T(8,128)(2,1)S(1)}, u32[]{:S(2)}, u32[]{:S(2)}) collective-permute-start(bf16[128,384]{1,0:T(8,128)(2,1)S(1)} %get-tuple-element.202), channel_id=1, source_target_pairs={{0,3},{1,2},{2,1},{3,0},{4,7},{5,6},{6,5},{7,4},{32,100},{33,101},... | collective-permute-start | bytes 294920 | tf_op jit(solution)/shard_map/ppermute | solution.py:41
  95.7 0.1 convert_add_fusion.2
  95.8 0.2 collective-permute-start.38
  96.0 3.4 %shard_map.119 = bf16[256,3072]{1,0:T(8,128)(2,1)} custom-call(s32[37]{0:T(128)S(1)} %concatenate.7.table_ref, bf16[256,128]{1,0:T(8,128)(2,1)S(1)} %add_convert_fusion.3.grads, bf16[3072,128]{1,0:T(8,128)(2,1)S(1)} %get-tuple-element.185.own, bf16[1792,128]{1,0:T(8,128)(2,1)S(1)} %collective-permute-done.25.a1, ...), custom_call_target="tpu_custom_call" | custom-call | bytes 12582912 | tf_op jit(solution)/shard_map/pallas_call | solution.py:313
  99.4 0.6 collective-permute-done.36.three
  100.0 0.2 collective-permute-done.38
  100.2 0.6 fusion.1
  100.9 0.8 shard_map.120
  (58 shorter events, 0.4 us)
Async XLA Ops:
  0.6 20.4 %copy-start.3 = (s32[1,16]{1,0:T(1,128)S(1)}, s32[1,16]{1,0:T(1,128)}, u32[]{:S(2)}) copy-start(s32[1,16]{1,0:T(1,128)} %param.15) | copy-start | bytes 196
  0.6 27.6 %copy-start = (bf16[1,256,1536]{2,1,0:T(8,128)(2,1)S(1)}, bf16[1,256,1536]{2,1,0:T(8,128)(2,1)}, u32[]{:S(2)}) copy-start(bf16[1,256,1536]{2,1,0:T(8,128)(2,1)} %param.12) | copy-start | bytes 2359300
  0.7 10.9 %collective-permute-start.1 = (bf16[384,128]{1,0:T(8,128)(2,1)}, bf16[384,128]{1,0:T(8,128)(2,1)S(1)}, u32[]{:S(2)}, u32[]{:S(2)}) collective-permute-start(bf16[384,128]{1,0:T(8,128)(2,1)} %param.11), channel_id=1, source_target_pairs={{0,1},{1,0},{2,3},{3,2},{4,5},{5,4},{6,7},{7,6},{32,36},{33,37},{3... | collective-permute-start | bytes 294920 | tf_op jit(solution)/shard_map/ppermute | solution.py:41
  2.7 8.8 %collective-permute-start.2 = (bf16[384,128]{1,0:T(8,128)(2,1)}, bf16[384,128]{1,0:T(8,128)(2,1)S(1)}, u32[]{:S(2)}, u32[]{:S(2)}) collective-permute-start(bf16[384,128]{1,0:T(8,128)(2,1)} %param.11), channel_id=1, source_target_pairs={{0,2},{1,3},{2,0},{3,1},{4,6},{5,7},{6,4},{7,5},{32,96},{33,97},{3... | collective-permute-start | bytes 294920 | tf_op jit(solution)/shard_map/ppermute | solution.py:41
  6.3 6.0 %collective-permute-start.3 = (bf16[384,128]{1,0:T(8,128)(2,1)}, bf16[384,128]{1,0:T(8,128)(2,1)S(1)}, u32[]{:S(2)}, u32[]{:S(2)}) collective-permute-start(bf16[384,128]{1,0:T(8,128)(2,1)} %param.11), channel_id=1, source_target_pairs={{0,3},{1,2},{2,1},{3,0},{4,7},{5,6},{6,5},{7,4},{32,100},{33,101},... | collective-permute-start | bytes 294920 | tf_op jit(solution)/shard_map/ppermute | solution.py:41
  6.3 5.2 %collective-permute-start = (bf16[256,128]{1,0:T(8,128)(2,1)}, bf16[256,128]{1,0:T(8,128)(2,1)S(1)}, u32[]{:S(2)}, u32[]{:S(2)}) collective-permute-start(bf16[256,128]{1,0:T(8,128)(2,1)} %bitcast.30), channel_id=1, source_target_pairs={{0,4},{1,5},{2,6},{3,7},{4,0},{5,1},{6,2},{7,3},{32,36},{33,37},{3... | collective-permute-start | bytes 196616 | tf_op jit(solution)/shard_map/ppermute | solution.py:41
  12.5 14.2 %collective-permute-start.7 = (bf16[1536,128]{1,0:T(8,128)(2,1)S(1)}, bf16[1536,128]{1,0:T(8,128)(2,1)S(1)}, u32[]{:S(2)}, u32[]{:S(2)}) collective-permute-start(bf16[1536,128]{1,0:T(8,128)(2,1)S(1)} %shard_map.112.w0), channel_id=1, source_target_pairs={{0,4},{1,5},{2,6},{3,7},{4,0},{5,1},{6,2},{7,3},{32,33},{33,32},{3... | collective-permute-start | bytes 1179656 | tf_op jit(solution)/shard_map/ppermute | solution.py:41
  14.1 12.7 %collective-permute-start.8 = (bf16[1536,128]{1,0:T(8,128)(2,1)S(1)}, bf16[1536,128]{1,0:T(8,128)(2,1)S(1)}, u32[]{:S(2)}, u32[]{:S(2)}) collective-permute-start(bf16[1536,128]{1,0:T(8,128)(2,1)S(1)} %shard_map.112.w0), channel_id=1, source_target_pairs={{0,68},{1,69},{2,70},{3,71},{4,64},{5,65},{6,66},{7,67},{32,35},{3... | collective-permute-start | bytes 1179656 | tf_op jit(solution)/shard_map/ppermute | solution.py:41
  16.2 5.2 %collective-permute-start.4 = (bf16[512,128]{1,0:T(8,128)(2,1)S(1)}, bf16[512,128]{1,0:T(8,128)(2,1)S(1)}, u32[]{:S(2)}, u32[]{:S(2)}) collective-permute-start(bf16[512,128]{1,0:T(8,128)(2,1)S(1)} %shard_map.111.k0), channel_id=1, source_target_pairs={{0,1},{1,0},{2,3},{3,2},{4,5},{5,4},{6,7},{7,6},{32,33},{33,32},{3... | collective-permute-start | bytes 393224 | tf_op jit(solution)/shard_map/ppermute | solution.py:41
  16.3 9.0 %collective-permute-start.5 = (bf16[512,128]{1,0:T(8,128)(2,1)S(1)}, bf16[512,128]{1,0:T(8,128)(2,1)S(1)}, u32[]{:S(2)}, u32[]{:S(2)}) collective-permute-start(bf16[512,128]{1,0:T(8,128)(2,1)S(1)} %shard_map.111.k0), channel_id=1, source_target_pairs={{0,2},{1,3},{2,0},{3,1},{4,6},{5,7},{6,4},{7,5},{32,34},{33,35},{3... | collective-permute-start | bytes 393224 | tf_op jit(solution)/shard_map/ppermute | solution.py:41
  20.0 6.7 %collective-permute-start.6 = (bf16[512,128]{1,0:T(8,128)(2,1)S(1)}, bf16[512,128]{1,0:T(8,128)(2,1)S(1)}, u32[]{:S(2)}, u32[]{:S(2)}) collective-permute-start(bf16[512,128]{1,0:T(8,128)(2,1)S(1)} %shard_map.111.k0), channel_id=1, source_target_pairs={{0,3},{1,2},{2,1},{3,0},{4,7},{5,6},{6,5},{7,4},{32,35},{33,34},{3... | collective-permute-start | bytes 393224 | tf_op jit(solution)/shard_map/ppermute | solution.py:41
  26.7 8.4 %collective-permute-start.10 = (bf16[1536,128]{1,0:T(8,128)(2,1)S(1)}, bf16[1536,128]{1,0:T(8,128)(2,1)S(1)}, u32[]{:S(2)}, u32[]{:S(2)}) collective-permute-start(bf16[1536,128]{1,0:T(8,128)(2,1)S(1)} %shard_map.112.w0), channel_id=1, source_target_pairs={{0,32},{1,33},{2,34},{3,35},{4,36},{5,37},{6,38},{7,39},{32,0},{33... | collective-permute-start | bytes 1179656 | tf_op jit(solution)/shard_map/ppermute | solution.py:41
  26.7 8.4 %collective-permute-start.11 = (bf16[1536,128]{1,0:T(8,128)(2,1)S(1)}, bf16[1536,128]{1,0:T(8,128)(2,1)S(1)}, u32[]{:S(2)}, u32[]{:S(2)}) collective-permute-start(bf16[1536,128]{1,0:T(8,128)(2,1)S(1)} %collective-permute-done.7.w1), channel_id=1, source_target_pairs={{0,32},{1,33},{2,34},{3,35},{4,36},{5,37},{6,38},{7,39},{32,0},{33... | collective-permute-start | bytes 1179656 | tf_op jit(solution)/shard_map/ppermute | solution.py:41
  27.2 7.9 %collective-permute-start.12 = (bf16[1536,128]{1,0:T(8,128)(2,1)S(1)}, bf16[1536,128]{1,0:T(8,128)(2,1)S(1)}, u32[]{:S(2)}, u32[]{:S(2)}) collective-permute-start(bf16[1536,128]{1,0:T(8,128)(2,1)S(1)} %collective-permute-done.8.w3), channel_id=1, source_target_pairs={{0,32},{1,33},{2,34},{3,35},{4,36},{5,37},{6,38},{7,39},{32,0},{33... | collective-permute-start | bytes 1179656 | tf_op jit(solution)/shard_map/ppermute | solution.py:41
  27.3 7.8 %collective-permute-start.9 = (bf16[1536,128]{1,0:T(8,128)(2,1)S(1)}, bf16[1536,128]{1,0:T(8,128)(2,1)S(1)}, u32[]{:S(2)}, u32[]{:S(2)}) collective-permute-start(bf16[1536,128]{1,0:T(8,128)(2,1)S(1)} %collective-permute-done.8.w3), channel_id=1, source_target_pairs={{0,4},{1,5},{2,6},{3,7},{4,0},{5,1},{6,2},{7,3},{32,33},{33,32},{3... | collective-permute-start | bytes 1179656 | tf_op jit(solution)/shard_map/ppermute | solution.py:41
  35.1 4.9 %collective-permute-start.13 = (bf16[1536,128]{1,0:T(8,128)(2,1)S(1)}, bf16[1536,128]{1,0:T(8,128)(2,1)S(1)}, u32[]{:S(2)}, u32[]{:S(2)}) collective-permute-start(bf16[1536,128]{1,0:T(8,128)(2,1)S(1)} %collective-permute-done.9.w2), channel_id=1, source_target_pairs={{0,32},{1,33},{2,34},{3,35},{4,36},{5,37},{6,38},{7,39},{32,0},{33... | collective-permute-start | bytes 1179656 | tf_op jit(solution)/shard_map/ppermute | solution.py:41
  35.2 16.1 %collective-permute-start.18 = (bf16[512,128]{1,0:T(8,128)(2,1)S(1)}, bf16[512,128]{1,0:T(8,128)(2,1)S(1)}, u32[]{:S(2)}, u32[]{:S(2)}) collective-permute-start(bf16[512,128]{1,0:T(8,128)(2,1)S(1)} %get-tuple-element.139), channel_id=1, source_target_pairs={{0,1},{1,0},{2,3},{3,2},{4,5},{5,4},{6,7},{7,6},{32,33},{33,32},{3... | collective-permute-start | bytes 393224 | tf_op jit(solution)/shard_map/ppermute | solution.py:41
  36.5 17.6 %collective-permute-start.19 = (bf16[512,128]{1,0:T(8,128)(2,1)S(1)}, bf16[512,128]{1,0:T(8,128)(2,1)S(1)}, u32[]{:S(2)}, u32[]{:S(2)}) collective-permute-start(bf16[512,128]{1,0:T(8,128)(2,1)S(1)} %get-tuple-element.140), channel_id=1, source_target_pairs={{0,2},{1,3},{2,0},{3,1},{4,6},{5,7},{6,4},{7,5},{32,34},{33,35},{3... | collective-permute-start | bytes 393224 | tf_op jit(solution)/shard_map/ppermute | solution.py:41
  37.2 16.8 %collective-permute-start.20 = (bf16[512,128]{1,0:T(8,128)(2,1)S(1)}, bf16[512,128]{1,0:T(8,128)(2,1)S(1)}, u32[]{:S(2)}, u32[]{:S(2)}) collective-permute-start(bf16[512,128]{1,0:T(8,128)(2,1)S(1)} %get-tuple-element.141), channel_id=1, source_target_pairs={{0,3},{1,2},{2,1},{3,0},{4,7},{5,6},{6,5},{7,4},{32,35},{33,34},{3... | collective-permute-start | bytes 393224 | tf_op jit(solution)/shard_map/ppermute | solution.py:41
  40.0 18.5 %slice-start = ((s8[6291456]{0:T(1024)(128)(4,1)}), s8[4194304]{0:T(1024)(128)(4,1)S(1)}, s32[]{:S(2)}) async-start(s8[6291456]{0:T(1024)(128)(4,1)} %bitcast.19), calls=%async_computation | async-start | bytes 8388608
  40.0 18.5 %slice-start.1 = ((s8[6291456]{0:T(1024)(128)(4,1)}), s8[2097152]{0:T(1024)(128)(4,1)S(1)}, s32[]{:S(2)}) async-start(s8[6291456]{0:T(1024)(128)(4,1)} %bitcast.19), calls=%async_computation.1 | async-start | bytes 4194304
  44.8 10.5 %copy-start.2 = (bf16[1,256,1536]{2,1,0:T(8,128)(2,1)S(1)}, bf16[1,256,1536]{2,1,0:T(8,128)(2,1)}, u32[]{:S(2)}) copy-start(bf16[1,256,1536]{2,1,0:T(8,128)(2,1)} %param.13) | copy-start | bytes 2359300
  44.8 4.3 %collective-permute-start.14 = (bf16[256,128]{1,0:T(8,128)(2,1)S(1)}, bf16[256,128]{1,0:T(8,128)(2,1)S(1)}, u32[]{:S(2)}, u32[]{:S(2)}) collective-permute-start(bf16[256,128]{1,0:T(8,128)(2,1)S(1)} %get-tuple-element.136.own), channel_id=1, source_target_pairs={{0,4},{1,5},{2,6},{3,7},{4,0},{5,1},{6,2},{7,3},{32,36},{33,37},{3... | collective-permute-start | bytes 196616 | tf_op jit(solution)/shard_map/ppermute | solution.py:41
  49.3 9.2 %collective-permute-start.15 = (bf16[512,128]{1,0:T(8,128)(2,1)S(1)}, bf16[512,128]{1,0:T(8,128)(2,1)S(1)}, u32[]{:S(2)}, u32[]{:S(2)}) collective-permute-start(bf16[512,128]{1,0:T(8,128)(2,1)S(1)} %shard_map.115.v0), channel_id=1, source_target_pairs={{0,1},{1,0},{2,3},{3,2},{4,5},{5,4},{6,7},{7,6},{32,33},{33,32},{3... | collective-permute-start | bytes 393224 | tf_op jit(solution)/shard_map/ppermute | solution.py:41
  49.4 9.1 %collective-permute-start.16 = (bf16[512,128]{1,0:T(8,128)(2,1)S(1)}, bf16[512,128]{1,0:T(8,128)(2,1)S(1)}, u32[]{:S(2)}, u32[]{:S(2)}) collective-permute-start(bf16[512,128]{1,0:T(8,128)(2,1)S(1)} %shard_map.115.v0), channel_id=1, source_target_pairs={{0,2},{1,3},{2,0},{3,1},{4,6},{5,7},{6,4},{7,5},{32,34},{33,35},{3... | collective-permute-start | bytes 393224 | tf_op jit(solution)/shard_map/ppermute | solution.py:41
  51.3 7.2 %collective-permute-start.17 = (bf16[512,128]{1,0:T(8,128)(2,1)S(1)}, bf16[512,128]{1,0:T(8,128)(2,1)S(1)}, u32[]{:S(2)}, u32[]{:S(2)}) collective-permute-start(bf16[512,128]{1,0:T(8,128)(2,1)S(1)} %shard_map.115.v0), channel_id=1, source_target_pairs={{0,3},{1,2},{2,1},{3,0},{4,7},{5,6},{6,5},{7,4},{32,35},{33,34},{3... | collective-permute-start | bytes 393224 | tf_op jit(solution)/shard_map/ppermute | solution.py:41
  54.1 4.3 %collective-permute-start.21 = (bf16[256,128]{1,0:T(8,128)(2,1)S(1)}, bf16[256,128]{1,0:T(8,128)(2,1)S(1)}, u32[]{:S(2)}, u32[]{:S(2)}) collective-permute-start(bf16[256,128]{1,0:T(8,128)(2,1)S(1)} %slice.97), channel_id=1, source_target_pairs={{0,4},{1,5},{2,6},{3,7},{4,0},{5,1},{6,2},{7,3},{32,36},{33,37},{3... | collective-permute-start | bytes 196616 | tf_op jit(solution)/shard_map/ppermute | solution.py:41
  60.4 3.9 %collective-permute-start.22 = (bf16[2048,384]{1,0:T(8,128)(2,1)S(1)}, bf16[2048,384]{1,0:T(8,128)(2,1)S(1)}, u32[]{:S(2)}, u32[]{:S(2)}) collective-permute-start(bf16[2048,384]{1,0:T(8,128)(2,1)S(1)} %get-tuple-element.158), channel_id=1, source_target_pairs={{0,32},{1,33},{2,34},{3,35},{4,36},{5,37},{6,38},{7,39},{32,0},{33... | collective-permute-start | bytes 4718600 | tf_op jit(solution)/shard_map/ppermute | solution.py:41
  60.5 17.4 %collective-permute-start.25 = (bf16[1792,128]{1,0:T(8,128)(2,1)S(1)}, bf16[1792,128]{1,0:T(8,128)(2,1)S(1)}, u32[]{:S(2)}, u32[]{:S(2)}) collective-permute-start(bf16[1792,128]{1,0:T(8,128)(2,1)S(1)} %get-tuple-element.159), channel_id=1, source_target_pairs={{0,8},{8,0},{16,24},{24,16},{1,9},{9,1},{17,25},{25,17},{2,10},{10... | collective-permute-start | bytes 1376264 | tf_op jit(solution)/shard_map/ppermute | solution.py:65
  62.2 15.8 %collective-permute-start.26 = (bf16[1792,128]{1,0:T(8,128)(2,1)S(1)}, bf16[1792,128]{1,0:T(8,128)(2,1)S(1)}, u32[]{:S(2)}, u32[]{:S(2)}) collective-permute-start(bf16[1792,128]{1,0:T(8,128)(2,1)S(1)} %get-tuple-element.161), channel_id=1, source_target_pairs={{0,24},{8,16},{16,8},{24,0},{1,25},{9,17},{17,9},{25,1},{2,26},{10... | collective-permute-start | bytes 1376264 | tf_op jit(solution)/shard_map/ppermute | solution.py:65
  64.3 5.2 %copy-start.1 = (bf16[1,256,1536]{2,1,0:T(8,128)(2,1)S(1)}, bf16[1,256,1536]{2,1,0:T(8,128)(2,1)}, u32[]{:S(2)}) copy-start(bf16[1,256,1536]{2,1,0:T(8,128)(2,1)} %param.9) | copy-start | bytes 2359300
  64.7 13.2 %collective-permute-start.23 = (bf16[512,384]{1,0:T(8,128)(2,1)S(1)}, bf16[512,384]{1,0:T(8,128)(2,1)S(1)}, u32[]{:S(2)}, u32[]{:S(2)}) collective-permute-start(bf16[512,384]{1,0:T(8,128)(2,1)S(1)} %get-tuple-element.200), channel_id=1, source_target_pairs={{0,4},{1,5},{2,6},{3,7},{4,0},{5,1},{6,2},{7,3},{32,33},{33,32},{3... | collective-permute-start | bytes 1179656 | tf_op jit(solution)/shard_map/ppermute | solution.py:41
  66.0 13.0 %collective-permute-start.24 = (bf16[512,384]{1,0:T(8,128)(2,1)S(1)}, bf16[512,384]{1,0:T(8,128)(2,1)S(1)}, u32[]{:S(2)}, u32[]{:S(2)}) collective-permute-start(bf16[512,384]{1,0:T(8,128)(2,1)S(1)} %get-tuple-element.199), channel_id=1, source_target_pairs={{0,64},{1,65},{2,66},{3,67},{4,68},{5,69},{6,70},{7,71},{32,34},{3... | collective-permute-start | bytes 1179656 | tf_op jit(solution)/shard_map/ppermute | solution.py:41
  68.8 13.3 %collective-permute-start.28 = (bf16[512,384]{1,0:T(8,128)(2,1)S(1)}, bf16[512,384]{1,0:T(8,128)(2,1)S(1)}, u32[]{:S(2)}, u32[]{:S(2)}) collective-permute-start(bf16[512,384]{1,0:T(8,128)(2,1)S(1)} %get-tuple-element.198), channel_id=1, source_target_pairs={{0,68},{1,69},{2,70},{3,71},{4,64},{5,65},{6,66},{7,67},{32,35},{3... | collective-permute-start | bytes 1179656 | tf_op jit(solution)/shard_map/ppermute | solution.py:41
  78.9 6.7 %collective-permute-start.30 = (bf16[1792,128]{1,0:T(8,128)(2,1)S(1)}, bf16[1792,128]{1,0:T(8,128)(2,1)S(1)}, u32[]{:S(2)}, u32[]{:S(2)}) collective-permute-start(bf16[1792,128]{1,0:T(8,128)(2,1)S(1)} %collective-permute-done.25.a1), channel_id=1, source_target_pairs={{0,32},{1,33},{2,34},{3,35},{4,36},{5,37},{6,38},{7,39},{32,0},{33... | collective-permute-start | bytes 1376264 | tf_op jit(solution)/shard_map/ppermute | solution.py:41
  78.9 6.7 %collective-permute-start.31 = (bf16[1792,128]{1,0:T(8,128)(2,1)S(1)}, bf16[1792,128]{1,0:T(8,128)(2,1)S(1)}, u32[]{:S(2)}, u32[]{:S(2)}) collective-permute-start(bf16[1792,128]{1,0:T(8,128)(2,1)S(1)} %collective-permute-done.26.a3), channel_id=1, source_target_pairs={{0,32},{1,33},{2,34},{3,35},{4,36},{5,37},{6,38},{7,39},{32,0},{33... | collective-permute-start | bytes 1376264 | tf_op jit(solution)/shard_map/ppermute | solution.py:41
  79.4 6.0 %collective-permute-start.27 = (bf16[512,128]{1,0:T(8,128)(2,1)S(1)}, bf16[512,128]{1,0:T(8,128)(2,1)S(1)}, u32[]{:S(2)}, u32[]{:S(2)}) collective-permute-start(bf16[512,128]{1,0:T(8,128)(2,1)S(1)} %get-tuple-element.162), channel_id=1, source_target_pairs={{0,1},{1,0},{2,3},{3,2},{4,5},{5,4},{6,7},{7,6},{32,33},{33,32},{3... | collective-permute-start | bytes 393224 | tf_op jit(solution)/shard_map/ppermute | solution.py:41
  79.4 14.7 %collective-permute-start.33 = (bf16[1792,128]{1,0:T(8,128)(2,1)S(1)}, bf16[1792,128]{1,0:T(8,128)(2,1)S(1)}, u32[]{:S(2)}, u32[]{:S(2)}) collective-permute-start(bf16[1792,128]{1,0:T(8,128)(2,1)S(1)} %get-tuple-element.173), channel_id=1, source_target_pairs={{0,16},{8,24},{16,0},{24,8},{1,17},{9,25},{17,1},{25,9},{2,18},{10... | collective-permute-start | bytes 1376264 | tf_op jit(solution)/shard_map/ppermute | solution.py:65
  82.2 8.3 %collective-permute-start.29 = (bf16[512,128]{1,0:T(8,128)(2,1)S(1)}, bf16[512,128]{1,0:T(8,128)(2,1)S(1)}, u32[]{:S(2)}, u32[]{:S(2)}) collective-permute-start(bf16[512,128]{1,0:T(8,128)(2,1)S(1)} %get-tuple-element.167), channel_id=1, source_target_pairs={{0,2},{1,3},{2,0},{3,1},{4,6},{5,7},{6,4},{7,5},{32,34},{33,35},{3... | collective-permute-start | bytes 393224 | tf_op jit(solution)/shard_map/ppermute | solution.py:41
  85.6 8.5 %collective-permute-start.32 = (bf16[512,128]{1,0:T(8,128)(2,1)S(1)}, bf16[512,128]{1,0:T(8,128)(2,1)S(1)}, u32[]{:S(2)}, u32[]{:S(2)}) collective-permute-start(bf16[512,128]{1,0:T(8,128)(2,1)S(1)} %get-tuple-element.171), channel_id=1, source_target_pairs={{0,3},{1,2},{2,1},{3,0},{4,7},{5,6},{6,5},{7,4},{32,35},{33,34},{3... | collective-permute-start | bytes 393224 | tf_op jit(solution)/shard_map/ppermute | solution.py:41
  87.2 4.7 %collective-permute-start.34 = (bf16[128,384]{1,0:T(8,128)(2,1)S(1)}, bf16[128,384]{1,0:T(8,128)(2,1)S(1)}, u32[]{:S(2)}, u32[]{:S(2)}) collective-permute-start(bf16[128,384]{1,0:T(8,128)(2,1)S(1)} %get-tuple-element.204), channel_id=1, source_target_pairs={{0,1},{1,0},{2,3},{3,2},{4,5},{5,4},{6,7},{7,6},{32,36},{33,37},{3... | collective-permute-start | bytes 294920 | tf_op jit(solution)/shard_map/ppermute | solution.py:41
  87.3 6.8 %collective-permute-start.35 = (bf16[128,384]{1,0:T(8,128)(2,1)S(1)}, bf16[128,384]{1,0:T(8,128)(2,1)S(1)}, u32[]{:S(2)}, u32[]{:S(2)}) collective-permute-start(bf16[128,384]{1,0:T(8,128)(2,1)S(1)} %get-tuple-element.203), channel_id=1, source_target_pairs={{0,2},{1,3},{2,0},{3,1},{4,6},{5,7},{6,4},{7,5},{32,96},{33,97},{3... | collective-permute-start | bytes 294920 | tf_op jit(solution)/shard_map/ppermute | solution.py:41
  94.1 1.9 %collective-permute-start.37 = (bf16[1792,128]{1,0:T(8,128)(2,1)S(1)}, bf16[1792,128]{1,0:T(8,128)(2,1)S(1)}, u32[]{:S(2)}, u32[]{:S(2)}) collective-permute-start(bf16[1792,128]{1,0:T(8,128)(2,1)S(1)} %collective-permute-done.33.a2), channel_id=1, source_target_pairs={{0,32},{1,33},{2,34},{3,35},{4,36},{5,37},{6,38},{7,39},{32,0},{33... | collective-permute-start | bytes 1376264 | tf_op jit(solution)/shard_map/ppermute | solution.py:41
  94.1 5.9 %collective-permute-start.36 = (bf16[128,384]{1,0:T(8,128)(2,1)S(1)}, bf16[128,384]{1,0:T(8,128)(2,1)S(1)}, u32[]{:S(2)}, u32[]{:S(2)}) collective-permute-start(bf16[128,384]{1,0:T(8,128)(2,1)S(1)} %get-tuple-element.202), channel_id=1, source_target_pairs={{0,3},{1,2},{2,1},{3,0},{4,7},{5,6},{6,5},{7,4},{32,100},{33,101},... | collective-permute-start | bytes 294920 | tf_op jit(solution)/shard_map/ppermute | solution.py:41
  95.8 4.4 %collective-permute-start.38 = (bf16[256,128]{1,0:T(8,128)(2,1)S(1)}, bf16[256,128]{1,0:T(8,128)(2,1)S(1)}, u32[]{:S(2)}, u32[]{:S(2)}) collective-permute-start(bf16[256,128]{1,0:T(8,128)(2,1)S(1)} %slice.96), channel_id=1, source_target_pairs={{0,4},{1,5},{2,6},{3,7},{4,0},{5,1},{6,2},{7,3},{32,36},{33,37},{3... | collective-permute-start | bytes 196616 | tf_op jit(solution)/shard_map/ppermute | solution.py:41

commit v5 on v4

--- a/solution.py
+++ b/solution.py
@@ -449,11 +449,10 @@
     near_values = joined(near_values)
     for part in arrived:
         value_sum = value_sum + part.astype(f32)
-    value_rest = x_swap(value_sum[rows:].astype(bf16))
+    value_rest = x_swap(value_sum.astype(bf16))[rows:]
 
     values = [near_values] + [z_with(near_values, r) for r in (1, 2, 3)]
     (terms,) = call(row_terms_kernel, [((24, 128), f32)], [grad, saved], smem=0)
-    values, value_sum, value_rest, terms = together((values, value_sum, value_rest, terms))
     value_grads = (value_sum[:rows] + value_rest.astype(f32)).astype(bf16)
 
     message = ((HALF + rows, HEAD_SIZE), bf16)
@@ -463,6 +462,10 @@
         [slabs, hidden, value_grads, *halves],
         cost=4, limit=24,
     )
+    values, terms, w_own, w_other, messages, value_grads = together(
+        (values, terms, w_own, w_other, messages, value_grads)
+    )
+
     w_other = core_swap(w_other)
     w_parts = [
         w_own[512 * r : 512 * (r + 1)] + w_other[512 * r : 512 * (r + 1)].astype(f32) for r in range(4)

time: 102 us -> 102 us (level)
  waiting for transfers between devices: 17.3 us -> 15.8 us
    ppermute x36, waiting for transfers between devices: 17.2 us -> 15.8 us  [moved(): return lax.ppermute(value, ('dp', 'ctx'), pairs)]
  transfers between devices with their start and end apart: 39 -> 39, of which waited for: 10 -> 11; matrix products, arithmetic and copies ran while one was open for 5% -> 5% of each run, Pallas kernels for 24% -> 26%
where the time goes in v5:
time: 102 us; the launch traced here: 101 us
  starting transfers between devices  51.6 us (51%)
  Pallas kernels  27 us (26%)
  waiting for transfers between devices  15.8 us (15%)
  other arithmetic  5.42 us (5%)
    ppermute x36, starting transfers between devices, moved(): return lax.ppermute(value, ('dp', 'ctx'), pairs)  45 us
    pallas_call x10, Pallas kernels, call(): pl.pallas_call(kernel, out_shape=tuple((jax.ShapeDtypeStruct(s, d) for s,...  27 us
    ppermute x36, waiting for transfers between devices, moved(): return lax.ppermute(value, ('dp', 'ctx'), pairs)  15.8 us
    ppermute x3, starting transfers between devices, y_with(): return lax.ppermute(value, 'head', [(y, y ^ bits) for y in range(4)])  6.59 us
  transfers between devices with their start and end apart: 39, of which 11 were waited for; matrix products, arithmetic and copies ran while one was open for 5% of the time, Pallas kernels for 26%

profile of v5, /device:TPU:0, one launch (start us, length us, event | category | flops | bytes accessed | tf_op | source)
XLA Modules:
  0.0 101.0 jit_solution(3912198259634619095)
XLA Ops:
  0.7 2.1 %collective-permute-start.1 = (bf16[384,128]{1,0:T(8,128)(2,1)}, bf16[384,128]{1,0:T(8,128)(2,1)S(1)}, u32[]{:S(2)}, u32[]{:S(2)}) collective-permute-start(bf16[384,128]{1,0:T(8,128)(2,1)} %param.11), channel_id=1, source_target_pairs={{0,1},{1,0},{2,3},{3,2},{4,5},{5,4},{6,7},{7,6},{32,36},{33,37},{3... | collective-permute-start | bytes 294920 | tf_op jit(solution)/shard_map/ppermute | solution.py:41
  2.7 3.6 %collective-permute-start.2 = (bf16[384,128]{1,0:T(8,128)(2,1)}, bf16[384,128]{1,0:T(8,128)(2,1)S(1)}, u32[]{:S(2)}, u32[]{:S(2)}) collective-permute-start(bf16[384,128]{1,0:T(8,128)(2,1)} %param.11), channel_id=1, source_target_pairs={{0,2},{1,3},{2,0},{3,1},{4,6},{5,7},{6,4},{7,5},{32,96},{33,97},{3... | collective-permute-start | bytes 294920 | tf_op jit(solution)/shard_map/ppermute | solution.py:41
  6.3 1.5 %collective-permute-start = (bf16[256,128]{1,0:T(8,128)(2,1)}, bf16[256,128]{1,0:T(8,128)(2,1)S(1)}, u32[]{:S(2)}, u32[]{:S(2)}) collective-permute-start(bf16[256,128]{1,0:T(8,128)(2,1)} %bitcast.30), channel_id=1, source_target_pairs={{0,4},{1,5},{2,6},{3,7},{4,0},{5,1},{6,2},{7,3},{32,36},{33,37},{3... | collective-permute-start | bytes 196616 | tf_op jit(solution)/shard_map/ppermute | solution.py:41
  7.8 0.9 broadcast_maximum_fusion.1.own
  8.7 0.8 broadcast_maximum_fusion.2.own
  9.6 0.7 broadcast_maximum_fusion.3
  10.3 1.2 %broadcast_maximum_fusion.q_any = bf16[256,1536]{1,0:T(8,128)(2,1)S(1)} fusion(bf16[1,256,1536]{2,1,0:T(8,128)(2,1)} %param.9), kind=kLoop, calls=%fused_computation.5 | loop fusion | flops 393216 | bytes 1572864 | tf_op jit(solution)/shard_map/max | solution.py:415
  11.6 0.8 collective-permute-done.3.refs_2_
  12.4 0.1 shard_map.112.w0
  12.5 1.6 %collective-permute-start.7 = (bf16[1536,128]{1,0:T(8,128)(2,1)S(1)}, bf16[1536,128]{1,0:T(8,128)(2,1)S(1)}, u32[]{:S(2)}, u32[]{:S(2)}) collective-permute-start(bf16[1536,128]{1,0:T(8,128)(2,1)S(1)} %shard_map.112.w0), channel_id=1, source_target_pairs={{0,4},{1,5},{2,6},{3,7},{4,0},{5,1},{6,2},{7,3},{32,33},{33,32},{3... | collective-permute-start | bytes 1179656 | tf_op jit(solution)/shard_map/ppermute | solution.py:41
  14.1 2.1 %collective-permute-start.8 = (bf16[1536,128]{1,0:T(8,128)(2,1)S(1)}, bf16[1536,128]{1,0:T(8,128)(2,1)S(1)}, u32[]{:S(2)}, u32[]{:S(2)}) collective-permute-start(bf16[1536,128]{1,0:T(8,128)(2,1)S(1)} %shard_map.112.w0), channel_id=1, source_target_pairs={{0,68},{1,69},{2,70},{3,71},{4,64},{5,65},{6,66},{7,67},{32,35},{3... | collective-permute-start | bytes 1179656 | tf_op jit(solution)/shard_map/ppermute | solution.py:41
  16.2 0.1 collective-permute-start.4
  16.3 3.7 %collective-permute-start.5 = (bf16[512,128]{1,0:T(8,128)(2,1)S(1)}, bf16[512,128]{1,0:T(8,128)(2,1)S(1)}, u32[]{:S(2)}, u32[]{:S(2)}) collective-permute-start(bf16[512,128]{1,0:T(8,128)(2,1)S(1)} %shard_map.111.k0), channel_id=1, source_target_pairs={{0,2},{1,3},{2,0},{3,1},{4,6},{5,7},{6,4},{7,5},{32,34},{33,35},{3... | collective-permute-start | bytes 393224 | tf_op jit(solution)/shard_map/ppermute | solution.py:41
  20.0 1.0 %collective-permute-start.6 = (bf16[512,128]{1,0:T(8,128)(2,1)S(1)}, bf16[512,128]{1,0:T(8,128)(2,1)S(1)}, u32[]{:S(2)}, u32[]{:S(2)}) collective-permute-start(bf16[512,128]{1,0:T(8,128)(2,1)S(1)} %shard_map.111.k0), channel_id=1, source_target_pairs={{0,3},{1,2},{2,1},{3,0},{4,7},{5,6},{6,5},{7,4},{32,35},{33,34},{3... | collective-permute-start | bytes 393224 | tf_op jit(solution)/shard_map/ppermute | solution.py:41
  21.0 0.2 fusion.3
  21.2 0.1 select_reduce_fusion
  21.3 0.1 concatenate.7.table_ref
  21.5 3.9 %collective-permute-done.5.k2 = bf16[512,128]{1,0:T(8,128)(2,1)S(1)} collective-permute-done((bf16[512,128]{1,0:T(8,128)(2,1)S(1)}, bf16[512,128]{1,0:T(8,128)(2,1)S(1)}, u32[]{:S(2)}, u32[]{:S(2)}) %collective-permute-start.5) | collective-permute-done | bytes 131104 | tf_op jit(solution)/shard_map/ppermute | solution.py:41
  25.4 1.3 %collective-permute-done.6.k3 = bf16[512,128]{1,0:T(8,128)(2,1)S(1)} collective-permute-done((bf16[512,128]{1,0:T(8,128)(2,1)S(1)}, bf16[512,128]{1,0:T(8,128)(2,1)S(1)}, u32[]{:S(2)}, u32[]{:S(2)}) %collective-permute-start.6) | collective-permute-done | bytes 131104 | tf_op jit(solution)/shard_map/ppermute | solution.py:41
  26.7 0.5 collective-permute-start.11
  27.2 0.1 collective-permute-start.12
  27.3 0.9 collective-permute-start.9
  28.2 6.9 %shard_map.113 = (f32[24,128]{1,0:T(8,128)S(1)}, f32[512,128]{1,0:T(8,128)S(1)}, bf16[512,128]{1,0:T(8,128)(2,1)S(1)}, bf16[512,128]{1,0:T(8,128)(2,1)S(1)}, bf16[512,128]{1,0:T(8,128)(2,1)S(1)}) custom-call(s32[18]{0:T(128)S(1)} %pad_add_fusion.table_ref, s32[16,128]{1,0:T(8,128)S(1)} %bitcast.27, bf16[256,1536]{1,0:T(8,128)(2,1)S(1)} %broadcast_maximum_fusion.q_any, ...), custom_call_target="tpu_custom_call" | custom-call | bytes 22020096 | tf_op jit(solution)/shard_map/pallas_call | solution.py:313
  35.1 0.1 collective-permute-start.13
  35.2 1.3 %collective-permute-start.18 = (bf16[512,128]{1,0:T(8,128)(2,1)S(1)}, bf16[512,128]{1,0:T(8,128)(2,1)S(1)}, u32[]{:S(2)}, u32[]{:S(2)}) collective-permute-start(bf16[512,128]{1,0:T(8,128)(2,1)S(1)} %get-tuple-element.143), channel_id=1, source_target_pairs={{0,1},{1,0},{2,3},{3,2},{4,5},{5,4},{6,7},{7,6},{32,33},{33,32},{3... | collective-permute-start | bytes 393224 | tf_op jit(solution)/shard_map/ppermute | solution.py:41
  36.5 0.7 collective-permute-start.19
  37.2 2.7 %collective-permute-start.20 = (bf16[512,128]{1,0:T(8,128)(2,1)S(1)}, bf16[512,128]{1,0:T(8,128)(2,1)S(1)}, u32[]{:S(2)}, u32[]{:S(2)}) collective-permute-start(bf16[512,128]{1,0:T(8,128)(2,1)S(1)} %get-tuple-element.145), channel_id=1, source_target_pairs={{0,3},{1,2},{2,1},{3,0},{4,7},{5,6},{6,5},{7,4},{32,35},{33,34},{3... | collective-permute-start | bytes 393224 | tf_op jit(solution)/shard_map/ppermute | solution.py:41
  40.0 4.8 %shard_map.114 = (bf16[256,128]{1,0:T(8,128)(2,1)S(1)}, bf16[3072,128]{1,0:T(8,128)(2,1)S(1)}, bf16[1536,128]{1,0:T(8,128)(2,1)S(1)}, bf16[1536,128]{1,0:T(8,128)(2,1)S(1)}, bf16[1536,128]{1,0:T(8,128)(2,1)S(1)}) custom-call(s32[37]{0:T(128)S(1)} %concatenate.7.table_ref, bf16[256,12288]{1,0:T(8,128)(2,1)} %bitcast.18, bf16[1536,128]{1,0:T(8,128)(2,1)S(1)} %shard_map.112.w0, ...), custom_call_target="tpu_custom_call" | custom-call | bytes 12582912 | tf_op jit(solution)/shard_map/pallas_call | solution.py:313
  44.8 1.2 %collective-permute-start.14 = (bf16[256,128]{1,0:T(8,128)(2,1)S(1)}, bf16[256,128]{1,0:T(8,128)(2,1)S(1)}, u32[]{:S(2)}, u32[]{:S(2)}) collective-permute-start(bf16[256,128]{1,0:T(8,128)(2,1)S(1)} %get-tuple-element.140.own), channel_id=1, source_target_pairs={{0,4},{1,5},{2,6},{3,7},{4,0},{5,1},{6,2},{7,3},{32,36},{33,37},{3... | collective-permute-start | bytes 196616 | tf_op jit(solution)/shard_map/ppermute | solution.py:41
  46.1 3.1 %collective-permute-done.14.refs_0_ = bf16[256,128]{1,0:T(8,128)(2,1)S(1)} collective-permute-done((bf16[256,128]{1,0:T(8,128)(2,1)S(1)}, bf16[256,128]{1,0:T(8,128)(2,1)S(1)}, u32[]{:S(2)}, u32[]{:S(2)}) %collective-permute-start.14) | collective-permute-done | bytes 65568 | tf_op jit(solution)/shard_map/ppermute | solution.py:41
  49.3 1.2 %collective-permute-start.21 = (bf16[512,128]{1,0:T(8,128)(2,1)S(1)}, bf16[512,128]{1,0:T(8,128)(2,1)S(1)}, u32[]{:S(2)}, u32[]{:S(2)}) collective-permute-start(bf16[512,128]{1,0:T(8,128)(2,1)S(1)} %get-tuple-element.206), channel_id=1, source_target_pairs={{0,4},{1,5},{2,6},{3,7},{4,0},{5,1},{6,2},{7,3},{32,36},{33,37},{3... | collective-permute-start | bytes 393224 | tf_op jit(solution)/shard_map/ppermute | solution.py:41
  50.5 0.5 shard_map.116.term_ref
  51.0 0.1 shard_map.115.v0
  51.1 0.1 collective-permute-start.15
  51.2 1.9 %collective-permute-start.16 = (bf16[512,128]{1,0:T(8,128)(2,1)S(1)}, bf16[512,128]{1,0:T(8,128)(2,1)S(1)}, u32[]{:S(2)}, u32[]{:S(2)}) collective-permute-start(bf16[512,128]{1,0:T(8,128)(2,1)S(1)} %shard_map.115.v0), channel_id=1, source_target_pairs={{0,2},{1,3},{2,0},{3,1},{4,6},{5,7},{6,4},{7,5},{32,34},{33,35},{3... | collective-permute-start | bytes 393224 | tf_op jit(solution)/shard_map/ppermute | solution.py:41
  53.1 2.7 %collective-permute-start.17 = (bf16[512,128]{1,0:T(8,128)(2,1)S(1)}, bf16[512,128]{1,0:T(8,128)(2,1)S(1)}, u32[]{:S(2)}, u32[]{:S(2)}) collective-permute-start(bf16[512,128]{1,0:T(8,128)(2,1)S(1)} %shard_map.115.v0), channel_id=1, source_target_pairs={{0,3},{1,2},{2,1},{3,0},{4,7},{5,6},{6,5},{7,4},{32,35},{33,34},{3... | collective-permute-start | bytes 393224 | tf_op jit(solution)/shard_map/ppermute | solution.py:41
  55.9 1.9 %shard_map.117 = (f32[2048,384]{1,0:T(8,128)S(1)}, bf16[2048,384]{1,0:T(8,128)(2,1)S(1)}, bf16[1792,128]{1,0:T(8,128)(2,1)S(1)}, bf16[1792,128]{1,0:T(8,128)(2,1)S(1)}, bf16[1792,128]{1,0:T(8,128)(2,1)S(1)}) custom-call(s32[37]{0:T(128)S(1)} %concatenate.7.table_ref, bf16[256,12288]{1,0:T(8,128)(2,1)S(1)} %bitcast.21, bf16[256,128]{1,0:T(8,128)(2,1)S(1)} %fusion.1.grads, ...), custom_call_target="tpu_custom_call" | custom-call | bytes 12582912 | tf_op jit(solution)/shard_map/pallas_call | solution.py:313
  57.8 0.4 collective-permute-done.16.v2
  58.3 1.5 %collective-permute-done.17.v3 = bf16[512,128]{1,0:T(8,128)(2,1)S(1)} collective-permute-done((bf16[512,128]{1,0:T(8,128)(2,1)S(1)}, bf16[512,128]{1,0:T(8,128)(2,1)S(1)}, u32[]{:S(2)}, u32[]{:S(2)}) %collective-permute-start.17) | collective-permute-done | bytes 131104 | tf_op jit(solution)/shard_map/ppermute | solution.py:41
  59.8 1.6 %collective-permute-start.25 = (bf16[1792,128]{1,0:T(8,128)(2,1)S(1)}, bf16[1792,128]{1,0:T(8,128)(2,1)S(1)}, u32[]{:S(2)}, u32[]{:S(2)}) collective-permute-start(bf16[1792,128]{1,0:T(8,128)(2,1)S(1)} %get-tuple-element.166), channel_id=1, source_target_pairs={{0,8},{8,0},{16,24},{24,16},{1,9},{9,1},{17,25},{25,17},{2,10},{10... | collective-permute-start | bytes 1376264 | tf_op jit(solution)/shard_map/ppermute | solution.py:65
  61.4 2.2 %collective-permute-start.26 = (bf16[1792,128]{1,0:T(8,128)(2,1)S(1)}, bf16[1792,128]{1,0:T(8,128)(2,1)S(1)}, u32[]{:S(2)}, u32[]{:S(2)}) collective-permute-start(bf16[1792,128]{1,0:T(8,128)(2,1)S(1)} %get-tuple-element.168), channel_id=1, source_target_pairs={{0,24},{8,16},{16,8},{24,0},{1,25},{9,17},{17,9},{25,1},{2,26},{10... | collective-permute-start | bytes 1376264 | tf_op jit(solution)/shard_map/ppermute | solution.py:65
  63.6 0.4 add_convert_fusion
  63.9 0.9 collective-permute-start.23
  64.9 2.9 %collective-permute-start.24 = (bf16[512,384]{1,0:T(8,128)(2,1)S(1)}, bf16[512,384]{1,0:T(8,128)(2,1)S(1)}, u32[]{:S(2)}, u32[]{:S(2)}) collective-permute-start(bf16[512,384]{1,0:T(8,128)(2,1)S(1)} %get-tuple-element.209), channel_id=1, source_target_pairs={{0,64},{1,65},{2,66},{3,67},{4,68},{5,69},{6,70},{7,71},{32,34},{3... | collective-permute-start | bytes 1179656 | tf_op jit(solution)/shard_map/ppermute | solution.py:41
  67.8 1.0 collective-permute-start.28
  68.7 8.4 %shard_map.118 = (bf16[256,1536]{1,0:T(8,128)(2,1)}, f32[512,128]{1,0:T(8,128)S(1)}, bf16[512,128]{1,0:T(8,128)(2,1)S(1)}, bf16[512,128]{1,0:T(8,128)(2,1)S(1)}, bf16[512,128]{1,0:T(8,128)(2,1)S(1)}) custom-call(s32[18]{0:T(128)S(1)} %pad_add_fusion.table_ref, s32[16,128]{1,0:T(8,128)S(1)} %bitcast.28, bf16[256,1536]{1,0:T(8,128)(2,1)S(1)} %bitcast.25, ...), custom_call_target="tpu_custom_call" | custom-call | bytes 28311552 | tf_op jit(solution)/shard_map/pallas_call | solution.py:313
  77.1 0.7 collective-permute-done.24
  77.8 0.5 collective-permute-start.31
  78.4 2.8 %collective-permute-start.33 = (bf16[1792,128]{1,0:T(8,128)(2,1)S(1)}, bf16[1792,128]{1,0:T(8,128)(2,1)S(1)}, u32[]{:S(2)}, u32[]{:S(2)}) collective-permute-start(bf16[1792,128]{1,0:T(8,128)(2,1)S(1)} %get-tuple-element.180), channel_id=1, source_target_pairs={{0,16},{8,24},{16,0},{24,8},{1,17},{9,25},{17,1},{25,9},{2,18},{10... | collective-permute-start | bytes 1376264 | tf_op jit(solution)/shard_map/ppermute | solution.py:65
  81.2 3.5 %collective-permute-start.29 = (bf16[512,128]{1,0:T(8,128)(2,1)S(1)}, bf16[512,128]{1,0:T(8,128)(2,1)S(1)}, u32[]{:S(2)}, u32[]{:S(2)}) collective-permute-start(bf16[512,128]{1,0:T(8,128)(2,1)S(1)} %get-tuple-element.174), channel_id=1, source_target_pairs={{0,2},{1,3},{2,0},{3,1},{4,6},{5,7},{6,4},{7,5},{32,34},{33,35},{3... | collective-permute-start | bytes 393224 | tf_op jit(solution)/shard_map/ppermute | solution.py:41
  84.7 0.2 fusion.18
  84.9 1.4 %collective-permute-start.32 = (bf16[512,128]{1,0:T(8,128)(2,1)S(1)}, bf16[512,128]{1,0:T(8,128)(2,1)S(1)}, u32[]{:S(2)}, u32[]{:S(2)}) collective-permute-start(bf16[512,128]{1,0:T(8,128)(2,1)S(1)} %get-tuple-element.178), channel_id=1, source_target_pairs={{0,3},{1,2},{2,1},{3,0},{4,7},{5,6},{6,5},{7,4},{32,35},{33,34},{3... | collective-permute-start | bytes 393224 | tf_op jit(solution)/shard_map/ppermute | solution.py:41
  86.3 0.1 collective-permute-start.34
  86.4 3.4 %collective-permute-start.35 = (bf16[128,384]{1,0:T(8,128)(2,1)S(1)}, bf16[128,384]{1,0:T(8,128)(2,1)S(1)}, u32[]{:S(2)}, u32[]{:S(2)}) collective-permute-start(bf16[128,384]{1,0:T(8,128)(2,1)S(1)} %get-tuple-element.213), channel_id=1, source_target_pairs={{0,2},{1,3},{2,0},{3,1},{4,6},{5,7},{6,4},{7,5},{32,96},{33,97},{3... | collective-permute-start | bytes 294920 | tf_op jit(solution)/shard_map/ppermute | solution.py:41
  89.8 1.2 %collective-permute-done.34.one = bf16[128,384]{1,0:T(8,128)(2,1)S(1)} collective-permute-done((bf16[128,384]{1,0:T(8,128)(2,1)S(1)}, bf16[128,384]{1,0:T(8,128)(2,1)S(1)}, u32[]{:S(2)}, u32[]{:S(2)}) %collective-permute-start.34) | collective-permute-done | bytes 98336 | tf_op jit(solution)/shard_map/ppermute | solution.py:41
  91.0 2.5 %collective-permute-done.35.two = bf16[128,384]{1,0:T(8,128)(2,1)S(1)} collective-permute-done((bf16[128,384]{1,0:T(8,128)(2,1)S(1)}, bf16[128,384]{1,0:T(8,128)(2,1)S(1)}, u32[]{:S(2)}, u32[]{:S(2)}) %collective-permute-start.35) | collective-permute-done | bytes 98336 | tf_op jit(solution)/shard_map/ppermute | solution.py:41
  93.5 1.3 %collective-permute-start.36 = (bf16[128,384]{1,0:T(8,128)(2,1)S(1)}, bf16[128,384]{1,0:T(8,128)(2,1)S(1)}, u32[]{:S(2)}, u32[]{:S(2)}) collective-permute-start(bf16[128,384]{1,0:T(8,128)(2,1)S(1)} %get-tuple-element.212), channel_id=1, source_target_pairs={{0,3},{1,2},{2,1},{3,0},{4,7},{5,6},{6,5},{7,4},{32,100},{33,101},... | collective-permute-start | bytes 294920 | tf_op jit(solution)/shard_map/ppermute | solution.py:41
  94.8 0.1 convert_add_fusion.2
  94.9 0.8 collective-permute-start.38
  95.8 3.4 %shard_map.119 = bf16[256,3072]{1,0:T(8,128)(2,1)} custom-call(s32[37]{0:T(128)S(1)} %concatenate.7.table_ref, bf16[256,128]{1,0:T(8,128)(2,1)S(1)} %fusion.1.grads, bf16[3072,128]{1,0:T(8,128)(2,1)S(1)} %get-tuple-element.193.own, bf16[1792,128]{1,0:T(8,128)(2,1)S(1)} %collective-permute-done.25.a1, bf16[1792,128]{1,0:T(8,128)(2,1)S(1)} %collective-permute-done.33.a2, ...), custom_call_target="tpu_custom_call" | custom-call | bytes 12582912 | tf_op jit(solution)/shard_map/pallas_call | solution.py:313
  99.2 0.2 collective-permute-done.36.three
  99.4 0.2 collective-permute-done.38
  99.6 0.6 fusion.2
  100.2 0.8 shard_map.120
  (57 shorter events, 0.5 us)
Async XLA Ops:
  0.6 20.4 %copy-start.3 = (s32[1,16]{1,0:T(1,128)S(1)}, s32[1,16]{1,0:T(1,128)}, u32[]{:S(2)}) copy-start(s32[1,16]{1,0:T(1,128)} %param.15) | copy-start | bytes 196
  0.6 27.6 %copy-start = (bf16[1,256,1536]{2,1,0:T(8,128)(2,1)S(1)}, bf16[1,256,1536]{2,1,0:T(8,128)(2,1)}, u32[]{:S(2)}) copy-start(bf16[1,256,1536]{2,1,0:T(8,128)(2,1)} %param.12) | copy-start | bytes 2359300
  0.7 10.9 %collective-permute-start.1 = (bf16[384,128]{1,0:T(8,128)(2,1)}, bf16[384,128]{1,0:T(8,128)(2,1)S(1)}, u32[]{:S(2)}, u32[]{:S(2)}) collective-permute-start(bf16[384,128]{1,0:T(8,128)(2,1)} %param.11), channel_id=1, source_target_pairs={{0,1},{1,0},{2,3},{3,2},{4,5},{5,4},{6,7},{7,6},{32,36},{33,37},{3... | collective-permute-start | bytes 294920 | tf_op jit(solution)/shard_map/ppermute | solution.py:41
  2.7 8.8 %collective-permute-start.2 = (bf16[384,128]{1,0:T(8,128)(2,1)}, bf16[384,128]{1,0:T(8,128)(2,1)S(1)}, u32[]{:S(2)}, u32[]{:S(2)}) collective-permute-start(bf16[384,128]{1,0:T(8,128)(2,1)} %param.11), channel_id=1, source_target_pairs={{0,2},{1,3},{2,0},{3,1},{4,6},{5,7},{6,4},{7,5},{32,96},{33,97},{3... | collective-permute-start | bytes 294920 | tf_op jit(solution)/shard_map/ppermute | solution.py:41
  6.3 6.0 %collective-permute-start.3 = (bf16[384,128]{1,0:T(8,128)(2,1)}, bf16[384,128]{1,0:T(8,128)(2,1)S(1)}, u32[]{:S(2)}, u32[]{:S(2)}) collective-permute-start(bf16[384,128]{1,0:T(8,128)(2,1)} %param.11), channel_id=1, source_target_pairs={{0,3},{1,2},{2,1},{3,0},{4,7},{5,6},{6,5},{7,4},{32,100},{33,101},... | collective-permute-start | bytes 294920 | tf_op jit(solution)/shard_map/ppermute | solution.py:41
  6.3 5.2 %collective-permute-start = (bf16[256,128]{1,0:T(8,128)(2,1)}, bf16[256,128]{1,0:T(8,128)(2,1)S(1)}, u32[]{:S(2)}, u32[]{:S(2)}) collective-permute-start(bf16[256,128]{1,0:T(8,128)(2,1)} %bitcast.30), channel_id=1, source_target_pairs={{0,4},{1,5},{2,6},{3,7},{4,0},{5,1},{6,2},{7,3},{32,36},{33,37},{3... | collective-permute-start | bytes 196616 | tf_op jit(solution)/shard_map/ppermute | solution.py:41
  12.5 14.2 %collective-permute-start.7 = (bf16[1536,128]{1,0:T(8,128)(2,1)S(1)}, bf16[1536,128]{1,0:T(8,128)(2,1)S(1)}, u32[]{:S(2)}, u32[]{:S(2)}) collective-permute-start(bf16[1536,128]{1,0:T(8,128)(2,1)S(1)} %shard_map.112.w0), channel_id=1, source_target_pairs={{0,4},{1,5},{2,6},{3,7},{4,0},{5,1},{6,2},{7,3},{32,33},{33,32},{3... | collective-permute-start | bytes 1179656 | tf_op jit(solution)/shard_map/ppermute | solution.py:41
  14.1 12.7 %collective-permute-start.8 = (bf16[1536,128]{1,0:T(8,128)(2,1)S(1)}, bf16[1536,128]{1,0:T(8,128)(2,1)S(1)}, u32[]{:S(2)}, u32[]{:S(2)}) collective-permute-start(bf16[1536,128]{1,0:T(8,128)(2,1)S(1)} %shard_map.112.w0), channel_id=1, source_target_pairs={{0,68},{1,69},{2,70},{3,71},{4,64},{5,65},{6,66},{7,67},{32,35},{3... | collective-permute-start | bytes 1179656 | tf_op jit(solution)/shard_map/ppermute | solution.py:41
  16.2 5.2 %collective-permute-start.4 = (bf16[512,128]{1,0:T(8,128)(2,1)S(1)}, bf16[512,128]{1,0:T(8,128)(2,1)S(1)}, u32[]{:S(2)}, u32[]{:S(2)}) collective-permute-start(bf16[512,128]{1,0:T(8,128)(2,1)S(1)} %shard_map.111.k0), channel_id=1, source_target_pairs={{0,1},{1,0},{2,3},{3,2},{4,5},{5,4},{6,7},{7,6},{32,33},{33,32},{3... | collective-permute-start | bytes 393224 | tf_op jit(solution)/shard_map/ppermute | solution.py:41
  16.3 9.0 %collective-permute-start.5 = (bf16[512,128]{1,0:T(8,128)(2,1)S(1)}, bf16[512,128]{1,0:T(8,128)(2,1)S(1)}, u32[]{:S(2)}, u32[]{:S(2)}) collective-permute-start(bf16[512,128]{1,0:T(8,128)(2,1)S(1)} %shard_map.111.k0), channel_id=1, source_target_pairs={{0,2},{1,3},{2,0},{3,1},{4,6},{5,7},{6,4},{7,5},{32,34},{33,35},{3... | collective-permute-start | bytes 393224 | tf_op jit(solution)/shard_map/ppermute | solution.py:41
  20.0 6.7 %collective-permute-start.6 = (bf16[512,128]{1,0:T(8,128)(2,1)S(1)}, bf16[512,128]{1,0:T(8,128)(2,1)S(1)}, u32[]{:S(2)}, u32[]{:S(2)}) collective-permute-start(bf16[512,128]{1,0:T(8,128)(2,1)S(1)} %shard_map.111.k0), channel_id=1, source_target_pairs={{0,3},{1,2},{2,1},{3,0},{4,7},{5,6},{6,5},{7,4},{32,35},{33,34},{3... | collective-permute-start | bytes 393224 | tf_op jit(solution)/shard_map/ppermute | solution.py:41
  26.7 8.4 %collective-permute-start.10 = (bf16[1536,128]{1,0:T(8,128)(2,1)S(1)}, bf16[1536,128]{1,0:T(8,128)(2,1)S(1)}, u32[]{:S(2)}, u32[]{:S(2)}) collective-permute-start(bf16[1536,128]{1,0:T(8,128)(2,1)S(1)} %shard_map.112.w0), channel_id=1, source_target_pairs={{0,32},{1,33},{2,34},{3,35},{4,36},{5,37},{6,38},{7,39},{32,0},{33... | collective-permute-start | bytes 1179656 | tf_op jit(solution)/shard_map/ppermute | solution.py:41
  26.7 8.4 %collective-permute-start.11 = (bf16[1536,128]{1,0:T(8,128)(2,1)S(1)}, bf16[1536,128]{1,0:T(8,128)(2,1)S(1)}, u32[]{:S(2)}, u32[]{:S(2)}) collective-permute-start(bf16[1536,128]{1,0:T(8,128)(2,1)S(1)} %collective-permute-done.7.w1), channel_id=1, source_target_pairs={{0,32},{1,33},{2,34},{3,35},{4,36},{5,37},{6,38},{7,39},{32,0},{33... | collective-permute-start | bytes 1179656 | tf_op jit(solution)/shard_map/ppermute | solution.py:41
  27.2 7.9 %collective-permute-start.12 = (bf16[1536,128]{1,0:T(8,128)(2,1)S(1)}, bf16[1536,128]{1,0:T(8,128)(2,1)S(1)}, u32[]{:S(2)}, u32[]{:S(2)}) collective-permute-start(bf16[1536,128]{1,0:T(8,128)(2,1)S(1)} %collective-permute-done.8.w3), channel_id=1, source_target_pairs={{0,32},{1,33},{2,34},{3,35},{4,36},{5,37},{6,38},{7,39},{32,0},{33... | collective-permute-start | bytes 1179656 | tf_op jit(solution)/shard_map/ppermute | solution.py:41
  27.3 7.8 %collective-permute-start.9 = (bf16[1536,128]{1,0:T(8,128)(2,1)S(1)}, bf16[1536,128]{1,0:T(8,128)(2,1)S(1)}, u32[]{:S(2)}, u32[]{:S(2)}) collective-permute-start(bf16[1536,128]{1,0:T(8,128)(2,1)S(1)} %collective-permute-done.8.w3), channel_id=1, source_target_pairs={{0,4},{1,5},{2,6},{3,7},{4,0},{5,1},{6,2},{7,3},{32,33},{33,32},{3... | collective-permute-start | bytes 1179656 | tf_op jit(solution)/shard_map/ppermute | solution.py:41
  35.1 4.9 %collective-permute-start.13 = (bf16[1536,128]{1,0:T(8,128)(2,1)S(1)}, bf16[1536,128]{1,0:T(8,128)(2,1)S(1)}, u32[]{:S(2)}, u32[]{:S(2)}) collective-permute-start(bf16[1536,128]{1,0:T(8,128)(2,1)S(1)} %collective-permute-done.9.w2), channel_id=1, source_target_pairs={{0,32},{1,33},{2,34},{3,35},{4,36},{5,37},{6,38},{7,39},{32,0},{33... | collective-permute-start | bytes 1179656 | tf_op jit(solution)/shard_map/ppermute | solution.py:41
  35.2 14.0 %collective-permute-start.18 = (bf16[512,128]{1,0:T(8,128)(2,1)S(1)}, bf16[512,128]{1,0:T(8,128)(2,1)S(1)}, u32[]{:S(2)}, u32[]{:S(2)}) collective-permute-start(bf16[512,128]{1,0:T(8,128)(2,1)S(1)} %get-tuple-element.143), channel_id=1, source_target_pairs={{0,1},{1,0},{2,3},{3,2},{4,5},{5,4},{6,7},{7,6},{32,33},{33,32},{3... | collective-permute-start | bytes 393224 | tf_op jit(solution)/shard_map/ppermute | solution.py:41
  36.5 12.7 %collective-permute-start.19 = (bf16[512,128]{1,0:T(8,128)(2,1)S(1)}, bf16[512,128]{1,0:T(8,128)(2,1)S(1)}, u32[]{:S(2)}, u32[]{:S(2)}) collective-permute-start(bf16[512,128]{1,0:T(8,128)(2,1)S(1)} %get-tuple-element.144), channel_id=1, source_target_pairs={{0,2},{1,3},{2,0},{3,1},{4,6},{5,7},{6,4},{7,5},{32,34},{33,35},{3... | collective-permute-start | bytes 393224 | tf_op jit(solution)/shard_map/ppermute | solution.py:41
  37.2 11.9 %collective-permute-start.20 = (bf16[512,128]{1,0:T(8,128)(2,1)S(1)}, bf16[512,128]{1,0:T(8,128)(2,1)S(1)}, u32[]{:S(2)}, u32[]{:S(2)}) collective-permute-start(bf16[512,128]{1,0:T(8,128)(2,1)S(1)} %get-tuple-element.145), channel_id=1, source_target_pairs={{0,3},{1,2},{2,1},{3,0},{4,7},{5,6},{6,5},{7,4},{32,35},{33,34},{3... | collective-permute-start | bytes 393224 | tf_op jit(solution)/shard_map/ppermute | solution.py:41
  40.0 15.9 %slice-start = ((s8[6291456]{0:T(1024)(128)(4,1)}), s8[4194304]{0:T(1024)(128)(4,1)S(1)}, s32[]{:S(2)}) async-start(s8[6291456]{0:T(1024)(128)(4,1)} %bitcast.19), calls=%async_computation | async-start | bytes 8388608
  40.0 15.9 %slice-start.1 = ((s8[6291456]{0:T(1024)(128)(4,1)}), s8[2097152]{0:T(1024)(128)(4,1)S(1)}, s32[]{:S(2)}) async-start(s8[6291456]{0:T(1024)(128)(4,1)} %bitcast.19), calls=%async_computation.1 | async-start | bytes 4194304
  44.8 5.7 %copy-start.2 = (bf16[1,256,1536]{2,1,0:T(8,128)(2,1)S(1)}, bf16[1,256,1536]{2,1,0:T(8,128)(2,1)}, u32[]{:S(2)}) copy-start(bf16[1,256,1536]{2,1,0:T(8,128)(2,1)} %param.13) | copy-start | bytes 2359300
  44.8 4.3 %collective-permute-start.14 = (bf16[256,128]{1,0:T(8,128)(2,1)S(1)}, bf16[256,128]{1,0:T(8,128)(2,1)S(1)}, u32[]{:S(2)}, u32[]{:S(2)}) collective-permute-start(bf16[256,128]{1,0:T(8,128)(2,1)S(1)} %get-tuple-element.140.own), channel_id=1, source_target_pairs={{0,4},{1,5},{2,6},{3,7},{4,0},{5,1},{6,2},{7,3},{32,36},{33,37},{3... | collective-permute-start | bytes 196616 | tf_op jit(solution)/shard_map/ppermute | solution.py:41
  49.3 6.6 %collective-permute-start.21 = (bf16[512,128]{1,0:T(8,128)(2,1)S(1)}, bf16[512,128]{1,0:T(8,128)(2,1)S(1)}, u32[]{:S(2)}, u32[]{:S(2)}) collective-permute-start(bf16[512,128]{1,0:T(8,128)(2,1)S(1)} %get-tuple-element.206), channel_id=1, source_target_pairs={{0,4},{1,5},{2,6},{3,7},{4,0},{5,1},{6,2},{7,3},{32,36},{33,37},{3... | collective-permute-start | bytes 393224 | tf_op jit(solution)/shard_map/ppermute | solution.py:41
  51.1 6.7 %collective-permute-start.15 = (bf16[512,128]{1,0:T(8,128)(2,1)S(1)}, bf16[512,128]{1,0:T(8,128)(2,1)S(1)}, u32[]{:S(2)}, u32[]{:S(2)}) collective-permute-start(bf16[512,128]{1,0:T(8,128)(2,1)S(1)} %shard_map.115.v0), channel_id=1, source_target_pairs={{0,1},{1,0},{2,3},{3,2},{4,5},{5,4},{6,7},{7,6},{32,33},{33,32},{3... | collective-permute-start | bytes 393224 | tf_op jit(solution)/shard_map/ppermute | solution.py:41
  51.2 7.1 %collective-permute-start.16 = (bf16[512,128]{1,0:T(8,128)(2,1)S(1)}, bf16[512,128]{1,0:T(8,128)(2,1)S(1)}, u32[]{:S(2)}, u32[]{:S(2)}) collective-permute-start(bf16[512,128]{1,0:T(8,128)(2,1)S(1)} %shard_map.115.v0), channel_id=1, source_target_pairs={{0,2},{1,3},{2,0},{3,1},{4,6},{5,7},{6,4},{7,5},{32,34},{33,35},{3... | collective-permute-start | bytes 393224 | tf_op jit(solution)/shard_map/ppermute | solution.py:41
  53.1 6.7 %collective-permute-start.17 = (bf16[512,128]{1,0:T(8,128)(2,1)S(1)}, bf16[512,128]{1,0:T(8,128)(2,1)S(1)}, u32[]{:S(2)}, u32[]{:S(2)}) collective-permute-start(bf16[512,128]{1,0:T(8,128)(2,1)S(1)} %shard_map.115.v0), channel_id=1, source_target_pairs={{0,3},{1,2},{2,1},{3,0},{4,7},{5,6},{6,5},{7,4},{32,35},{33,34},{3... | collective-permute-start | bytes 393224 | tf_op jit(solution)/shard_map/ppermute | solution.py:41
  59.8 8.9 %copy-start.1 = (bf16[1,256,1536]{2,1,0:T(8,128)(2,1)S(1)}, bf16[1,256,1536]{2,1,0:T(8,128)(2,1)}, u32[]{:S(2)}) copy-start(bf16[1,256,1536]{2,1,0:T(8,128)(2,1)} %param.9) | copy-start | bytes 2359300
  59.8 3.8 %collective-permute-start.22 = (bf16[2048,384]{1,0:T(8,128)(2,1)S(1)}, bf16[2048,384]{1,0:T(8,128)(2,1)S(1)}, u32[]{:S(2)}, u32[]{:S(2)}) collective-permute-start(bf16[2048,384]{1,0:T(8,128)(2,1)S(1)} %get-tuple-element.165), channel_id=1, source_target_pairs={{0,32},{1,33},{2,34},{3,35},{4,36},{5,37},{6,38},{7,39},{32,0},{33... | collective-permute-start | bytes 4718600 | tf_op jit(solution)/shard_map/ppermute | solution.py:41
  59.8 17.3 %collective-permute-start.25 = (bf16[1792,128]{1,0:T(8,128)(2,1)S(1)}, bf16[1792,128]{1,0:T(8,128)(2,1)S(1)}, u32[]{:S(2)}, u32[]{:S(2)}) collective-permute-start(bf16[1792,128]{1,0:T(8,128)(2,1)S(1)} %get-tuple-element.166), channel_id=1, source_target_pairs={{0,8},{8,0},{16,24},{24,16},{1,9},{9,1},{17,25},{25,17},{2,10},{10... | collective-permute-start | bytes 1376264 | tf_op jit(solution)/shard_map/ppermute | solution.py:65
  61.4 15.8 %collective-permute-start.26 = (bf16[1792,128]{1,0:T(8,128)(2,1)S(1)}, bf16[1792,128]{1,0:T(8,128)(2,1)S(1)}, u32[]{:S(2)}, u32[]{:S(2)}) collective-permute-start(bf16[1792,128]{1,0:T(8,128)(2,1)S(1)} %get-tuple-element.168), channel_id=1, source_target_pairs={{0,24},{8,16},{16,8},{24,0},{1,25},{9,17},{17,9},{25,1},{2,26},{10... | collective-permute-start | bytes 1376264 | tf_op jit(solution)/shard_map/ppermute | solution.py:65
  63.9 13.2 %collective-permute-start.23 = (bf16[512,384]{1,0:T(8,128)(2,1)S(1)}, bf16[512,384]{1,0:T(8,128)(2,1)S(1)}, u32[]{:S(2)}, u32[]{:S(2)}) collective-permute-start(bf16[512,384]{1,0:T(8,128)(2,1)S(1)} %get-tuple-element.210), channel_id=1, source_target_pairs={{0,4},{1,5},{2,6},{3,7},{4,0},{5,1},{6,2},{7,3},{32,33},{33,32},{3... | collective-permute-start | bytes 1179656 | tf_op jit(solution)/shard_map/ppermute | solution.py:41
  64.9 12.9 %collective-permute-start.24 = (bf16[512,384]{1,0:T(8,128)(2,1)S(1)}, bf16[512,384]{1,0:T(8,128)(2,1)S(1)}, u32[]{:S(2)}, u32[]{:S(2)}) collective-permute-start(bf16[512,384]{1,0:T(8,128)(2,1)S(1)} %get-tuple-element.209), channel_id=1, source_target_pairs={{0,64},{1,65},{2,66},{3,67},{4,68},{5,69},{6,70},{7,71},{32,34},{3... | collective-permute-start | bytes 1179656 | tf_op jit(solution)/shard_map/ppermute | solution.py:41
  67.8 13.5 %collective-permute-start.28 = (bf16[512,384]{1,0:T(8,128)(2,1)S(1)}, bf16[512,384]{1,0:T(8,128)(2,1)S(1)}, u32[]{:S(2)}, u32[]{:S(2)}) collective-permute-start(bf16[512,384]{1,0:T(8,128)(2,1)S(1)} %get-tuple-element.208), channel_id=1, source_target_pairs={{0,68},{1,69},{2,70},{3,71},{4,64},{5,65},{6,66},{7,67},{32,35},{3... | collective-permute-start | bytes 1179656 | tf_op jit(solution)/shard_map/ppermute | solution.py:41
  77.8 7.1 %collective-permute-start.30 = (bf16[1792,128]{1,0:T(8,128)(2,1)S(1)}, bf16[1792,128]{1,0:T(8,128)(2,1)S(1)}, u32[]{:S(2)}, u32[]{:S(2)}) collective-permute-start(bf16[1792,128]{1,0:T(8,128)(2,1)S(1)} %collective-permute-done.25.a1), channel_id=1, source_target_pairs={{0,32},{1,33},{2,34},{3,35},{4,36},{5,37},{6,38},{7,39},{32,0},{33... | collective-permute-start | bytes 1376264 | tf_op jit(solution)/shard_map/ppermute | solution.py:41
  77.8 7.1 %collective-permute-start.31 = (bf16[1792,128]{1,0:T(8,128)(2,1)S(1)}, bf16[1792,128]{1,0:T(8,128)(2,1)S(1)}, u32[]{:S(2)}, u32[]{:S(2)}) collective-permute-start(bf16[1792,128]{1,0:T(8,128)(2,1)S(1)} %collective-permute-done.26.a3), channel_id=1, source_target_pairs={{0,32},{1,33},{2,34},{3,35},{4,36},{5,37},{6,38},{7,39},{32,0},{33... | collective-permute-start | bytes 1376264 | tf_op jit(solution)/shard_map/ppermute | solution.py:41
  78.3 6.4 %collective-permute-start.27 = (bf16[512,128]{1,0:T(8,128)(2,1)S(1)}, bf16[512,128]{1,0:T(8,128)(2,1)S(1)}, u32[]{:S(2)}, u32[]{:S(2)}) collective-permute-start(bf16[512,128]{1,0:T(8,128)(2,1)S(1)} %get-tuple-element.169), channel_id=1, source_target_pairs={{0,1},{1,0},{2,3},{3,2},{4,5},{5,4},{6,7},{7,6},{32,33},{33,32},{3... | collective-permute-start | bytes 393224 | tf_op jit(solution)/shard_map/ppermute | solution.py:41
  78.4 15.1 %collective-permute-start.33 = (bf16[1792,128]{1,0:T(8,128)(2,1)S(1)}, bf16[1792,128]{1,0:T(8,128)(2,1)S(1)}, u32[]{:S(2)}, u32[]{:S(2)}) collective-permute-start(bf16[1792,128]{1,0:T(8,128)(2,1)S(1)} %get-tuple-element.180), channel_id=1, source_target_pairs={{0,16},{8,24},{16,0},{24,8},{1,17},{9,25},{17,1},{25,9},{2,18},{10... | collective-permute-start | bytes 1376264 | tf_op jit(solution)/shard_map/ppermute | solution.py:65
  81.2 8.6 %collective-permute-start.29 = (bf16[512,128]{1,0:T(8,128)(2,1)S(1)}, bf16[512,128]{1,0:T(8,128)(2,1)S(1)}, u32[]{:S(2)}, u32[]{:S(2)}) collective-permute-start(bf16[512,128]{1,0:T(8,128)(2,1)S(1)} %get-tuple-element.174), channel_id=1, source_target_pairs={{0,2},{1,3},{2,0},{3,1},{4,6},{5,7},{6,4},{7,5},{32,34},{33,35},{3... | collective-permute-start | bytes 393224 | tf_op jit(solution)/shard_map/ppermute | solution.py:41
  84.9 8.5 %collective-permute-start.32 = (bf16[512,128]{1,0:T(8,128)(2,1)S(1)}, bf16[512,128]{1,0:T(8,128)(2,1)S(1)}, u32[]{:S(2)}, u32[]{:S(2)}) collective-permute-start(bf16[512,128]{1,0:T(8,128)(2,1)S(1)} %get-tuple-element.178), channel_id=1, source_target_pairs={{0,3},{1,2},{2,1},{3,0},{4,7},{5,6},{6,5},{7,4},{32,35},{33,34},{3... | collective-permute-start | bytes 393224 | tf_op jit(solution)/shard_map/ppermute | solution.py:41
  86.3 4.7 %collective-permute-start.34 = (bf16[128,384]{1,0:T(8,128)(2,1)S(1)}, bf16[128,384]{1,0:T(8,128)(2,1)S(1)}, u32[]{:S(2)}, u32[]{:S(2)}) collective-permute-start(bf16[128,384]{1,0:T(8,128)(2,1)S(1)} %get-tuple-element.214), channel_id=1, source_target_pairs={{0,1},{1,0},{2,3},{3,2},{4,5},{5,4},{6,7},{7,6},{32,36},{33,37},{3... | collective-permute-start | bytes 294920 | tf_op jit(solution)/shard_map/ppermute | solution.py:41
  86.4 7.1 %collective-permute-start.35 = (bf16[128,384]{1,0:T(8,128)(2,1)S(1)}, bf16[128,384]{1,0:T(8,128)(2,1)S(1)}, u32[]{:S(2)}, u32[]{:S(2)}) collective-permute-start(bf16[128,384]{1,0:T(8,128)(2,1)S(1)} %get-tuple-element.213), channel_id=1, source_target_pairs={{0,2},{1,3},{2,0},{3,1},{4,6},{5,7},{6,4},{7,5},{32,96},{33,97},{3... | collective-permute-start | bytes 294920 | tf_op jit(solution)/shard_map/ppermute | solution.py:41
  93.5 2.3 %collective-permute-start.37 = (bf16[1792,128]{1,0:T(8,128)(2,1)S(1)}, bf16[1792,128]{1,0:T(8,128)(2,1)S(1)}, u32[]{:S(2)}, u32[]{:S(2)}) collective-permute-start(bf16[1792,128]{1,0:T(8,128)(2,1)S(1)} %collective-permute-done.33.a2), channel_id=1, source_target_pairs={{0,32},{1,33},{2,34},{3,35},{4,36},{5,37},{6,38},{7,39},{32,0},{33... | collective-permute-start | bytes 1376264 | tf_op jit(solution)/shard_map/ppermute | solution.py:41
  93.5 5.9 %collective-permute-start.36 = (bf16[128,384]{1,0:T(8,128)(2,1)S(1)}, bf16[128,384]{1,0:T(8,128)(2,1)S(1)}, u32[]{:S(2)}, u32[]{:S(2)}) collective-permute-start(bf16[128,384]{1,0:T(8,128)(2,1)S(1)} %get-tuple-element.212), channel_id=1, source_target_pairs={{0,3},{1,2},{2,1},{3,0},{4,7},{5,6},{6,5},{7,4},{32,100},{33,101},... | collective-permute-start | bytes 294920 | tf_op jit(solution)/shard_map/ppermute | solution.py:41
  94.9 4.6 %collective-permute-start.38 = (bf16[256,128]{1,0:T(8,128)(2,1)S(1)}, bf16[256,128]{1,0:T(8,128)(2,1)S(1)}, u32[]{:S(2)}, u32[]{:S(2)}) collective-permute-start(bf16[256,128]{1,0:T(8,128)(2,1)S(1)} %slice.98), channel_id=1, source_target_pairs={{0,4},{1,5},{2,6},{3,7},{4,0},{5,1},{6,2},{7,3},{32,36},{33,37},{3... | collective-permute-start | bytes 196616 | tf_op jit(solution)/shard_map/ppermute | solution.py:41

commit v6 on v5

--- a/solution.py
+++ b/solution.py
@@ -493,13 +493,13 @@
     got = [
         first_with(w_sum[i * HEAD_SIZE : (i + 1) * HEAD_SIZE].astype(bf16), i) for i in (1, 2, 3)
     ]
-    arrived, key_sum, slabs, messages, got[:2] = together(
-        (arrived, key_parts[0], slabs, messages, got[:2])
+    swapped[1] = core_swap(messages[1])
+    arrived, key_sum, slabs, messages, swapped, got[:2] = together(
+        (arrived, key_parts[0], slabs, messages, swapped, got[:2])
     )
     for part in arrived:
         key_sum = key_sum + part.astype(f32)
 
-    swapped[1] = core_swap(messages[1])
     key_rest = x_swap(key_sum[rows:].astype(bf16))
     (input_grad,) = call(
         input_kernel,

time: 102 us -> 106 us (1.039)
  waiting for transfers between devices: 15.8 us -> 22.7 us
  starting transfers between devices: 51.6 us -> 49.5 us
    ppermute x36, waiting for transfers between devices: 15.8 us -> 22.7 us  [moved(): return lax.ppermute(value, ('dp', 'ctx'), pairs)]
    ppermute x36, starting transfers between devices: 45 us -> 42.9 us  [moved(): return lax.ppermute(value, ('dp', 'ctx'), pairs)]
  transfers between devices with their start and end apart: 39 -> 39, of which waited for: 11 -> 12; matrix products, arithmetic and copies ran while one was open for 5% -> 5% of each run, Pallas kernels for 26% -> 25%
where the time goes in v6:
time: 106 us
  starting transfers between devices  49.5 us (47%)
  Pallas kernels  27 us (25%)
  waiting for transfers between devices  22.7 us (21%)
  other arithmetic  5.41 us (5%)
    ppermute x36, starting transfers between devices, moved(): return lax.ppermute(value, ('dp', 'ctx'), pairs)  42.9 us
    pallas_call x10, Pallas kernels, call(): pl.pallas_call(kernel, out_shape=tuple((jax.ShapeDtypeStruct(s, d) for s,...  27 us
    ppermute x36, waiting for transfers between devices, moved(): return lax.ppermute(value, ('dp', 'ctx'), pairs)  22.7 us
    ppermute x3, starting transfers between devices, y_with(): return lax.ppermute(value, 'head', [(y, y ^ bits) for y in range(4)])  6.59 us
  transfers between devices with their start and end apart: 39, of which 12 were waited for; matrix products, arithmetic and copies ran while one was open for 5% of the time, Pallas kernels for 25%

profile of v6, /device:TPU:0, one launch (start us, length us, event | category | flops | bytes accessed | tf_op | source)
XLA Modules:
  0.0 105.8 jit_solution(644680390429443782)
XLA Ops:
  0.7 2.1 %collective-permute-start.1 = (bf16[384,128]{1,0:T(8,128)(2,1)}, bf16[384,128]{1,0:T(8,128)(2,1)S(1)}, u32[]{:S(2)}, u32[]{:S(2)}) collective-permute-start(bf16[384,128]{1,0:T(8,128)(2,1)} %param.11), channel_id=1, source_target_pairs={{0,1},{1,0},{2,3},{3,2},{4,5},{5,4},{6,7},{7,6},{32,36},{33,37},{3... | collective-permute-start | bytes 294920 | tf_op jit(solution)/shard_map/ppermute | solution.py:41
  2.7 3.6 %collective-permute-start.2 = (bf16[384,128]{1,0:T(8,128)(2,1)}, bf16[384,128]{1,0:T(8,128)(2,1)S(1)}, u32[]{:S(2)}, u32[]{:S(2)}) collective-permute-start(bf16[384,128]{1,0:T(8,128)(2,1)} %param.11), channel_id=1, source_target_pairs={{0,2},{1,3},{2,0},{3,1},{4,6},{5,7},{6,4},{7,5},{32,96},{33,97},{3... | collective-permute-start | bytes 294920 | tf_op jit(solution)/shard_map/ppermute | solution.py:41
  6.3 1.5 %collective-permute-start = (bf16[256,128]{1,0:T(8,128)(2,1)}, bf16[256,128]{1,0:T(8,128)(2,1)S(1)}, u32[]{:S(2)}, u32[]{:S(2)}) collective-permute-start(bf16[256,128]{1,0:T(8,128)(2,1)} %bitcast.30), channel_id=1, source_target_pairs={{0,4},{1,5},{2,6},{3,7},{4,0},{5,1},{6,2},{7,3},{32,36},{33,37},{3... | collective-permute-start | bytes 196616 | tf_op jit(solution)/shard_map/ppermute | solution.py:41
  7.8 0.9 broadcast_maximum_fusion.1.own
  8.7 0.8 broadcast_maximum_fusion.2.own
  9.6 0.7 broadcast_maximum_fusion.3
  10.3 1.2 %broadcast_maximum_fusion.q_any = bf16[256,1536]{1,0:T(8,128)(2,1)S(1)} fusion(bf16[1,256,1536]{2,1,0:T(8,128)(2,1)} %param.9), kind=kLoop, calls=%fused_computation.5 | loop fusion | flops 393216 | bytes 1572864 | tf_op jit(solution)/shard_map/max | solution.py:415
  11.6 0.8 collective-permute-done.3.refs_2_
  12.4 0.1 shard_map.112.w0
  12.5 1.6 %collective-permute-start.7 = (bf16[1536,128]{1,0:T(8,128)(2,1)S(1)}, bf16[1536,128]{1,0:T(8,128)(2,1)S(1)}, u32[]{:S(2)}, u32[]{:S(2)}) collective-permute-start(bf16[1536,128]{1,0:T(8,128)(2,1)S(1)} %shard_map.112.w0), channel_id=1, source_target_pairs={{0,4},{1,5},{2,6},{3,7},{4,0},{5,1},{6,2},{7,3},{32,33},{33,32},{3... | collective-permute-start | bytes 1179656 | tf_op jit(solution)/shard_map/ppermute | solution.py:41
  14.1 2.1 %collective-permute-start.8 = (bf16[1536,128]{1,0:T(8,128)(2,1)S(1)}, bf16[1536,128]{1,0:T(8,128)(2,1)S(1)}, u32[]{:S(2)}, u32[]{:S(2)}) collective-permute-start(bf16[1536,128]{1,0:T(8,128)(2,1)S(1)} %shard_map.112.w0), channel_id=1, source_target_pairs={{0,68},{1,69},{2,70},{3,71},{4,64},{5,65},{6,66},{7,67},{32,35},{3... | collective-permute-start | bytes 1179656 | tf_op jit(solution)/shard_map/ppermute | solution.py:41
  16.2 0.1 collective-permute-start.4
  16.3 3.7 %collective-permute-start.5 = (bf16[512,128]{1,0:T(8,128)(2,1)S(1)}, bf16[512,128]{1,0:T(8,128)(2,1)S(1)}, u32[]{:S(2)}, u32[]{:S(2)}) collective-permute-start(bf16[512,128]{1,0:T(8,128)(2,1)S(1)} %shard_map.111.k0), channel_id=1, source_target_pairs={{0,2},{1,3},{2,0},{3,1},{4,6},{5,7},{6,4},{7,5},{32,34},{33,35},{3... | collective-permute-start | bytes 393224 | tf_op jit(solution)/shard_map/ppermute | solution.py:41
  20.0 1.0 collective-permute-start.6
  21.0 0.2 fusion.3
  21.2 0.1 select_reduce_fusion
  21.3 0.1 concatenate.7.table_ref
  21.5 3.9 %collective-permute-done.5.k2 = bf16[512,128]{1,0:T(8,128)(2,1)S(1)} collective-permute-done((bf16[512,128]{1,0:T(8,128)(2,1)S(1)}, bf16[512,128]{1,0:T(8,128)(2,1)S(1)}, u32[]{:S(2)}, u32[]{:S(2)}) %collective-permute-start.5) | collective-permute-done | bytes 131104 | tf_op jit(solution)/shard_map/ppermute | solution.py:41
  25.4 1.3 %collective-permute-done.6.k3 = bf16[512,128]{1,0:T(8,128)(2,1)S(1)} collective-permute-done((bf16[512,128]{1,0:T(8,128)(2,1)S(1)}, bf16[512,128]{1,0:T(8,128)(2,1)S(1)}, u32[]{:S(2)}, u32[]{:S(2)}) %collective-permute-start.6) | collective-permute-done | bytes 131104 | tf_op jit(solution)/shard_map/ppermute | solution.py:41
  26.7 0.5 collective-permute-start.11
  27.2 0.1 collective-permute-start.12
  27.3 0.9 collective-permute-start.9
  28.2 6.9 %shard_map.113 = (f32[24,128]{1,0:T(8,128)S(1)}, f32[512,128]{1,0:T(8,128)S(1)}, bf16[512,128]{1,0:T(8,128)(2,1)S(1)}, bf16[512,128]{1,0:T(8,128)(2,1)S(1)}, bf16[512,128]{1,0:T(8,128)(2,1)S(1)}) custom-call(s32[18]{0:T(128)S(1)} %pad_add_fusion.table_ref, s32[16,128]{1,0:T(8,128)S(1)} %bitcast.27, bf16[256,1536]{1,0:T(8,128)(2,1)S(1)} %broadcast_maximum_fusion.q_any, ...), custom_call_target="tpu_custom_call" | custom-call | bytes 22020096 | tf_op jit(solution)/shard_map/pallas_call | solution.py:313
  35.1 0.1 collective-permute-start.13
  35.2 1.3 %collective-permute-start.18 = (bf16[512,128]{1,0:T(8,128)(2,1)S(1)}, bf16[512,128]{1,0:T(8,128)(2,1)S(1)}, u32[]{:S(2)}, u32[]{:S(2)}) collective-permute-start(bf16[512,128]{1,0:T(8,128)(2,1)S(1)} %get-tuple-element.146), channel_id=1, source_target_pairs={{0,1},{1,0},{2,3},{3,2},{4,5},{5,4},{6,7},{7,6},{32,33},{33,32},{3... | collective-permute-start | bytes 393224 | tf_op jit(solution)/shard_map/ppermute | solution.py:41
  36.5 0.7 collective-permute-start.19
  37.2 2.7 %collective-permute-start.20 = (bf16[512,128]{1,0:T(8,128)(2,1)S(1)}, bf16[512,128]{1,0:T(8,128)(2,1)S(1)}, u32[]{:S(2)}, u32[]{:S(2)}) collective-permute-start(bf16[512,128]{1,0:T(8,128)(2,1)S(1)} %get-tuple-element.148), channel_id=1, source_target_pairs={{0,3},{1,2},{2,1},{3,0},{4,7},{5,6},{6,5},{7,4},{32,35},{33,34},{3... | collective-permute-start | bytes 393224 | tf_op jit(solution)/shard_map/ppermute | solution.py:41
  40.0 4.8 %shard_map.114 = (bf16[256,128]{1,0:T(8,128)(2,1)S(1)}, bf16[3072,128]{1,0:T(8,128)(2,1)S(1)}, bf16[1536,128]{1,0:T(8,128)(2,1)S(1)}, bf16[1536,128]{1,0:T(8,128)(2,1)S(1)}, bf16[1536,128]{1,0:T(8,128)(2,1)S(1)}) custom-call(s32[37]{0:T(128)S(1)} %concatenate.7.table_ref, bf16[256,12288]{1,0:T(8,128)(2,1)} %bitcast.18, bf16[1536,128]{1,0:T(8,128)(2,1)S(1)} %shard_map.112.w0, ...), custom_call_target="tpu_custom_call" | custom-call | bytes 12582912 | tf_op jit(solution)/shard_map/pallas_call | solution.py:313
  44.8 1.2 %collective-permute-start.14 = (bf16[256,128]{1,0:T(8,128)(2,1)S(1)}, bf16[256,128]{1,0:T(8,128)(2,1)S(1)}, u32[]{:S(2)}, u32[]{:S(2)}) collective-permute-start(bf16[256,128]{1,0:T(8,128)(2,1)S(1)} %get-tuple-element.143.own), channel_id=1, source_target_pairs={{0,4},{1,5},{2,6},{3,7},{4,0},{5,1},{6,2},{7,3},{32,36},{33,37},{3... | collective-permute-start | bytes 196616 | tf_op jit(solution)/shard_map/ppermute | solution.py:41
  46.1 3.1 %collective-permute-done.14.refs_0_ = bf16[256,128]{1,0:T(8,128)(2,1)S(1)} collective-permute-done((bf16[256,128]{1,0:T(8,128)(2,1)S(1)}, bf16[256,128]{1,0:T(8,128)(2,1)S(1)}, u32[]{:S(2)}, u32[]{:S(2)}) %collective-permute-start.14) | collective-permute-done | bytes 65568 | tf_op jit(solution)/shard_map/ppermute | solution.py:41
  49.3 1.2 %collective-permute-start.21 = (bf16[512,128]{1,0:T(8,128)(2,1)S(1)}, bf16[512,128]{1,0:T(8,128)(2,1)S(1)}, u32[]{:S(2)}, u32[]{:S(2)}) collective-permute-start(bf16[512,128]{1,0:T(8,128)(2,1)S(1)} %get-tuple-element.212), channel_id=1, source_target_pairs={{0,4},{1,5},{2,6},{3,7},{4,0},{5,1},{6,2},{7,3},{32,36},{33,37},{3... | collective-permute-start | bytes 393224 | tf_op jit(solution)/shard_map/ppermute | solution.py:41
  50.5 0.5 shard_map.116.term_ref
  51.0 0.1 shard_map.115.v0
  51.1 0.1 collective-permute-start.15
  51.2 1.9 %collective-permute-start.16 = (bf16[512,128]{1,0:T(8,128)(2,1)S(1)}, bf16[512,128]{1,0:T(8,128)(2,1)S(1)}, u32[]{:S(2)}, u32[]{:S(2)}) collective-permute-start(bf16[512,128]{1,0:T(8,128)(2,1)S(1)} %shard_map.115.v0), channel_id=1, source_target_pairs={{0,2},{1,3},{2,0},{3,1},{4,6},{5,7},{6,4},{7,5},{32,34},{33,35},{3... | collective-permute-start | bytes 393224 | tf_op jit(solution)/shard_map/ppermute | solution.py:41
  53.1 2.7 %collective-permute-start.17 = (bf16[512,128]{1,0:T(8,128)(2,1)S(1)}, bf16[512,128]{1,0:T(8,128)(2,1)S(1)}, u32[]{:S(2)}, u32[]{:S(2)}) collective-permute-start(bf16[512,128]{1,0:T(8,128)(2,1)S(1)} %shard_map.115.v0), channel_id=1, source_target_pairs={{0,3},{1,2},{2,1},{3,0},{4,7},{5,6},{6,5},{7,4},{32,35},{33,34},{3... | collective-permute-start | bytes 393224 | tf_op jit(solution)/shard_map/ppermute | solution.py:41
  55.9 1.9 %shard_map.117 = (f32[2048,384]{1,0:T(8,128)S(1)}, bf16[2048,384]{1,0:T(8,128)(2,1)S(1)}, bf16[1792,128]{1,0:T(8,128)(2,1)S(1)}, bf16[1792,128]{1,0:T(8,128)(2,1)S(1)}, bf16[1792,128]{1,0:T(8,128)(2,1)S(1)}) custom-call(s32[37]{0:T(128)S(1)} %concatenate.7.table_ref, bf16[256,12288]{1,0:T(8,128)(2,1)S(1)} %bitcast.21, bf16[256,128]{1,0:T(8,128)(2,1)S(1)} %fusion.1.grads, ...), custom_call_target="tpu_custom_call" | custom-call | bytes 12582912 | tf_op jit(solution)/shard_map/pallas_call | solution.py:313
  57.8 0.4 collective-permute-done.16.v2
  58.3 1.5 %collective-permute-done.17.v3 = bf16[512,128]{1,0:T(8,128)(2,1)S(1)} collective-permute-done((bf16[512,128]{1,0:T(8,128)(2,1)S(1)}, bf16[512,128]{1,0:T(8,128)(2,1)S(1)}, u32[]{:S(2)}, u32[]{:S(2)}) %collective-permute-start.17) | collective-permute-done | bytes 131104 | tf_op jit(solution)/shard_map/ppermute | solution.py:41
  59.8 1.6 %collective-permute-start.25 = (bf16[1792,128]{1,0:T(8,128)(2,1)S(1)}, bf16[1792,128]{1,0:T(8,128)(2,1)S(1)}, u32[]{:S(2)}, u32[]{:S(2)}) collective-permute-start(bf16[1792,128]{1,0:T(8,128)(2,1)S(1)} %get-tuple-element.169), channel_id=1, source_target_pairs={{0,8},{8,0},{16,24},{24,16},{1,9},{9,1},{17,25},{25,17},{2,10},{10... | collective-permute-start | bytes 1376264 | tf_op jit(solution)/shard_map/ppermute | solution.py:65
  61.4 2.2 %collective-permute-start.26 = (bf16[1792,128]{1,0:T(8,128)(2,1)S(1)}, bf16[1792,128]{1,0:T(8,128)(2,1)S(1)}, u32[]{:S(2)}, u32[]{:S(2)}) collective-permute-start(bf16[1792,128]{1,0:T(8,128)(2,1)S(1)} %get-tuple-element.171), channel_id=1, source_target_pairs={{0,24},{8,16},{16,8},{24,0},{1,25},{9,17},{17,9},{25,1},{2,26},{10... | collective-permute-start | bytes 1376264 | tf_op jit(solution)/shard_map/ppermute | solution.py:65
  63.6 0.4 add_convert_fusion
  63.9 0.9 collective-permute-start.23
  64.9 2.9 %collective-permute-start.24 = (bf16[512,384]{1,0:T(8,128)(2,1)S(1)}, bf16[512,384]{1,0:T(8,128)(2,1)S(1)}, u32[]{:S(2)}, u32[]{:S(2)}) collective-permute-start(bf16[512,384]{1,0:T(8,128)(2,1)S(1)} %get-tuple-element.215), channel_id=1, source_target_pairs={{0,64},{1,65},{2,66},{3,67},{4,68},{5,69},{6,70},{7,71},{32,34},{3... | collective-permute-start | bytes 1179656 | tf_op jit(solution)/shard_map/ppermute | solution.py:41
  67.8 8.4 %shard_map.118 = (bf16[256,1536]{1,0:T(8,128)(2,1)}, f32[512,128]{1,0:T(8,128)S(1)}, bf16[512,128]{1,0:T(8,128)(2,1)S(1)}, bf16[512,128]{1,0:T(8,128)(2,1)S(1)}, bf16[512,128]{1,0:T(8,128)(2,1)S(1)}) custom-call(s32[18]{0:T(128)S(1)} %pad_add_fusion.table_ref, s32[16,128]{1,0:T(8,128)S(1)} %bitcast.28, bf16[256,1536]{1,0:T(8,128)(2,1)S(1)} %bitcast.25, ...), custom_call_target="tpu_custom_call" | custom-call | bytes 28311552 | tf_op jit(solution)/shard_map/pallas_call | solution.py:313
  76.2 1.5 %collective-permute-done.24 = bf16[512,384]{1,0:T(8,128)(2,1)S(1)} collective-permute-done((bf16[512,384]{1,0:T(8,128)(2,1)S(1)}, bf16[512,384]{1,0:T(8,128)(2,1)S(1)}, u32[]{:S(2)}, u32[]{:S(2)}) %collective-permute-start.24) | collective-permute-done | bytes 393248 | tf_op jit(solution)/shard_map/ppermute | solution.py:41
  77.7 2.8 %collective-permute-start.33 = (bf16[1792,128]{1,0:T(8,128)(2,1)S(1)}, bf16[1792,128]{1,0:T(8,128)(2,1)S(1)}, u32[]{:S(2)}, u32[]{:S(2)}) collective-permute-start(bf16[1792,128]{1,0:T(8,128)(2,1)S(1)} %get-tuple-element.183), channel_id=1, source_target_pairs={{0,16},{8,24},{16,0},{24,8},{1,17},{9,25},{17,1},{25,9},{2,18},{10... | collective-permute-start | bytes 1376264 | tf_op jit(solution)/shard_map/ppermute | solution.py:65
  80.6 1.0 collective-permute-start.28
  81.5 0.5 collective-permute-start.31
  82.0 7.5 %collective-permute-done.28 = bf16[512,384]{1,0:T(8,128)(2,1)S(1)} collective-permute-done((bf16[512,384]{1,0:T(8,128)(2,1)S(1)}, bf16[512,384]{1,0:T(8,128)(2,1)S(1)}, u32[]{:S(2)}, u32[]{:S(2)}) %collective-permute-start.28) | collective-permute-done | bytes 393248 | tf_op jit(solution)/shard_map/ppermute | solution.py:41
  89.5 1.3 %collective-permute-start.29 = (bf16[512,128]{1,0:T(8,128)(2,1)S(1)}, bf16[512,128]{1,0:T(8,128)(2,1)S(1)}, u32[]{:S(2)}, u32[]{:S(2)}) collective-permute-start(bf16[512,128]{1,0:T(8,128)(2,1)S(1)} %get-tuple-element.177), channel_id=1, source_target_pairs={{0,2},{1,3},{2,0},{3,1},{4,6},{5,7},{6,4},{7,5},{32,34},{33,35},{3... | collective-permute-start | bytes 393224 | tf_op jit(solution)/shard_map/ppermute | solution.py:41
  90.9 0.2 fusion.18
  91.1 1.5 %collective-permute-start.32 = (bf16[512,128]{1,0:T(8,128)(2,1)S(1)}, bf16[512,128]{1,0:T(8,128)(2,1)S(1)}, u32[]{:S(2)}, u32[]{:S(2)}) collective-permute-start(bf16[512,128]{1,0:T(8,128)(2,1)S(1)} %get-tuple-element.181), channel_id=1, source_target_pairs={{0,3},{1,2},{2,1},{3,0},{4,7},{5,6},{6,5},{7,4},{32,35},{33,34},{3... | collective-permute-start | bytes 393224 | tf_op jit(solution)/shard_map/ppermute | solution.py:41
  92.6 0.8 collective-permute-start.35
  93.5 2.5 %collective-permute-start.36 = (bf16[128,384]{1,0:T(8,128)(2,1)S(1)}, bf16[128,384]{1,0:T(8,128)(2,1)S(1)}, u32[]{:S(2)}, u32[]{:S(2)}) collective-permute-start(bf16[128,384]{1,0:T(8,128)(2,1)S(1)} %get-tuple-element.219), channel_id=1, source_target_pairs={{0,2},{1,3},{2,0},{3,1},{4,6},{5,7},{6,4},{7,5},{32,96},{33,97},{3... | collective-permute-start | bytes 294920 | tf_op jit(solution)/shard_map/ppermute | solution.py:41
  95.9 0.1 collective-permute-done.29
  96.1 2.1 %collective-permute-start.37 = (bf16[128,384]{1,0:T(8,128)(2,1)S(1)}, bf16[128,384]{1,0:T(8,128)(2,1)S(1)}, u32[]{:S(2)}, u32[]{:S(2)}) collective-permute-start(bf16[128,384]{1,0:T(8,128)(2,1)S(1)} %get-tuple-element.218), channel_id=1, source_target_pairs={{0,3},{1,2},{2,1},{3,0},{4,7},{5,6},{6,5},{7,4},{32,100},{33,101},... | collective-permute-start | bytes 294920 | tf_op jit(solution)/shard_map/ppermute | solution.py:41
  98.2 1.5 %collective-permute-done.36.two = bf16[128,384]{1,0:T(8,128)(2,1)S(1)} collective-permute-done((bf16[128,384]{1,0:T(8,128)(2,1)S(1)}, bf16[128,384]{1,0:T(8,128)(2,1)S(1)}, u32[]{:S(2)}, u32[]{:S(2)}) %collective-permute-start.36) | collective-permute-done | bytes 98336 | tf_op jit(solution)/shard_map/ppermute | solution.py:41
  99.7 0.2 collective-permute-done.32
  100.0 0.2 collective-permute-start.38
  100.2 3.4 %shard_map.119 = bf16[256,3072]{1,0:T(8,128)(2,1)} custom-call(s32[37]{0:T(128)S(1)} %concatenate.7.table_ref, bf16[256,128]{1,0:T(8,128)(2,1)S(1)} %fusion.1.grads, bf16[3072,128]{1,0:T(8,128)(2,1)S(1)} %get-tuple-element.198.own, bf16[1792,128]{1,0:T(8,128)(2,1)S(1)} %collective-permute-done.25.a1, bf16[1792,128]{1,0:T(8,128)(2,1)S(1)} %collective-permute-done.33.a2, ...), custom_call_target="tpu_custom_call" | custom-call | bytes 12582912 | tf_op jit(solution)/shard_map/pallas_call | solution.py:313
  103.6 0.7 collective-permute-done.38
  104.3 0.6 fusion.2
  105.0 0.8 shard_map.120
  (57 shorter events, 0.5 us)
Async XLA Ops:
  0.6 20.4 %copy-start.3 = (s32[1,16]{1,0:T(1,128)S(1)}, s32[1,16]{1,0:T(1,128)}, u32[]{:S(2)}) copy-start(s32[1,16]{1,0:T(1,128)} %param.15) | copy-start | bytes 196
  0.6 27.6 %copy-start = (bf16[1,256,1536]{2,1,0:T(8,128)(2,1)S(1)}, bf16[1,256,1536]{2,1,0:T(8,128)(2,1)}, u32[]{:S(2)}) copy-start(bf16[1,256,1536]{2,1,0:T(8,128)(2,1)} %param.12) | copy-start | bytes 2359300
  0.7 10.9 %collective-permute-start.1 = (bf16[384,128]{1,0:T(8,128)(2,1)}, bf16[384,128]{1,0:T(8,128)(2,1)S(1)}, u32[]{:S(2)}, u32[]{:S(2)}) collective-permute-start(bf16[384,128]{1,0:T(8,128)(2,1)} %param.11), channel_id=1, source_target_pairs={{0,1},{1,0},{2,3},{3,2},{4,5},{5,4},{6,7},{7,6},{32,36},{33,37},{3... | collective-permute-start | bytes 294920 | tf_op jit(solution)/shard_map/ppermute | solution.py:41
  2.7 8.8 %collective-permute-start.2 = (bf16[384,128]{1,0:T(8,128)(2,1)}, bf16[384,128]{1,0:T(8,128)(2,1)S(1)}, u32[]{:S(2)}, u32[]{:S(2)}) collective-permute-start(bf16[384,128]{1,0:T(8,128)(2,1)} %param.11), channel_id=1, source_target_pairs={{0,2},{1,3},{2,0},{3,1},{4,6},{5,7},{6,4},{7,5},{32,96},{33,97},{3... | collective-permute-start | bytes 294920 | tf_op jit(solution)/shard_map/ppermute | solution.py:41
  6.3 6.0 %collective-permute-start.3 = (bf16[384,128]{1,0:T(8,128)(2,1)}, bf16[384,128]{1,0:T(8,128)(2,1)S(1)}, u32[]{:S(2)}, u32[]{:S(2)}) collective-permute-start(bf16[384,128]{1,0:T(8,128)(2,1)} %param.11), channel_id=1, source_target_pairs={{0,3},{1,2},{2,1},{3,0},{4,7},{5,6},{6,5},{7,4},{32,100},{33,101},... | collective-permute-start | bytes 294920 | tf_op jit(solution)/shard_map/ppermute | solution.py:41
  6.3 5.2 %collective-permute-start = (bf16[256,128]{1,0:T(8,128)(2,1)}, bf16[256,128]{1,0:T(8,128)(2,1)S(1)}, u32[]{:S(2)}, u32[]{:S(2)}) collective-permute-start(bf16[256,128]{1,0:T(8,128)(2,1)} %bitcast.30), channel_id=1, source_target_pairs={{0,4},{1,5},{2,6},{3,7},{4,0},{5,1},{6,2},{7,3},{32,36},{33,37},{3... | collective-permute-start | bytes 196616 | tf_op jit(solution)/shard_map/ppermute | solution.py:41
  12.5 14.2 %collective-permute-start.7 = (bf16[1536,128]{1,0:T(8,128)(2,1)S(1)}, bf16[1536,128]{1,0:T(8,128)(2,1)S(1)}, u32[]{:S(2)}, u32[]{:S(2)}) collective-permute-start(bf16[1536,128]{1,0:T(8,128)(2,1)S(1)} %shard_map.112.w0), channel_id=1, source_target_pairs={{0,4},{1,5},{2,6},{3,7},{4,0},{5,1},{6,2},{7,3},{32,33},{33,32},{3... | collective-permute-start | bytes 1179656 | tf_op jit(solution)/shard_map/ppermute | solution.py:41
  14.1 12.7 %collective-permute-start.8 = (bf16[1536,128]{1,0:T(8,128)(2,1)S(1)}, bf16[1536,128]{1,0:T(8,128)(2,1)S(1)}, u32[]{:S(2)}, u32[]{:S(2)}) collective-permute-start(bf16[1536,128]{1,0:T(8,128)(2,1)S(1)} %shard_map.112.w0), channel_id=1, source_target_pairs={{0,68},{1,69},{2,70},{3,71},{4,64},{5,65},{6,66},{7,67},{32,35},{3... | collective-permute-start | bytes 1179656 | tf_op jit(solution)/shard_map/ppermute | solution.py:41
  16.2 5.2 %collective-permute-start.4 = (bf16[512,128]{1,0:T(8,128)(2,1)S(1)}, bf16[512,128]{1,0:T(8,128)(2,1)S(1)}, u32[]{:S(2)}, u32[]{:S(2)}) collective-permute-start(bf16[512,128]{1,0:T(8,128)(2,1)S(1)} %shard_map.111.k0), channel_id=1, source_target_pairs={{0,1},{1,0},{2,3},{3,2},{4,5},{5,4},{6,7},{7,6},{32,33},{33,32},{3... | collective-permute-start | bytes 393224 | tf_op jit(solution)/shard_map/ppermute | solution.py:41
  16.3 9.0 %collective-permute-start.5 = (bf16[512,128]{1,0:T(8,128)(2,1)S(1)}, bf16[512,128]{1,0:T(8,128)(2,1)S(1)}, u32[]{:S(2)}, u32[]{:S(2)}) collective-permute-start(bf16[512,128]{1,0:T(8,128)(2,1)S(1)} %shard_map.111.k0), channel_id=1, source_target_pairs={{0,2},{1,3},{2,0},{3,1},{4,6},{5,7},{6,4},{7,5},{32,34},{33,35},{3... | collective-permute-start | bytes 393224 | tf_op jit(solution)/shard_map/ppermute | solution.py:41
  20.0 6.7 %collective-permute-start.6 = (bf16[512,128]{1,0:T(8,128)(2,1)S(1)}, bf16[512,128]{1,0:T(8,128)(2,1)S(1)}, u32[]{:S(2)}, u32[]{:S(2)}) collective-permute-start(bf16[512,128]{1,0:T(8,128)(2,1)S(1)} %shard_map.111.k0), channel_id=1, source_target_pairs={{0,3},{1,2},{2,1},{3,0},{4,7},{5,6},{6,5},{7,4},{32,35},{33,34},{3... | collective-permute-start | bytes 393224 | tf_op jit(solution)/shard_map/ppermute | solution.py:41
  26.7 8.4 %collective-permute-start.10 = (bf16[1536,128]{1,0:T(8,128)(2,1)S(1)}, bf16[1536,128]{1,0:T(8,128)(2,1)S(1)}, u32[]{:S(2)}, u32[]{:S(2)}) collective-permute-start(bf16[1536,128]{1,0:T(8,128)(2,1)S(1)} %shard_map.112.w0), channel_id=1, source_target_pairs={{0,32},{1,33},{2,34},{3,35},{4,36},{5,37},{6,38},{7,39},{32,0},{33... | collective-permute-start | bytes 1179656 | tf_op jit(solution)/shard_map/ppermute | solution.py:41
  26.7 8.4 %collective-permute-start.11 = (bf16[1536,128]{1,0:T(8,128)(2,1)S(1)}, bf16[1536,128]{1,0:T(8,128)(2,1)S(1)}, u32[]{:S(2)}, u32[]{:S(2)}) collective-permute-start(bf16[1536,128]{1,0:T(8,128)(2,1)S(1)} %collective-permute-done.7.w1), channel_id=1, source_target_pairs={{0,32},{1,33},{2,34},{3,35},{4,36},{5,37},{6,38},{7,39},{32,0},{33... | collective-permute-start | bytes 1179656 | tf_op jit(solution)/shard_map/ppermute | solution.py:41
  27.2 7.9 %collective-permute-start.12 = (bf16[1536,128]{1,0:T(8,128)(2,1)S(1)}, bf16[1536,128]{1,0:T(8,128)(2,1)S(1)}, u32[]{:S(2)}, u32[]{:S(2)}) collective-permute-start(bf16[1536,128]{1,0:T(8,128)(2,1)S(1)} %collective-permute-done.8.w3), channel_id=1, source_target_pairs={{0,32},{1,33},{2,34},{3,35},{4,36},{5,37},{6,38},{7,39},{32,0},{33... | collective-permute-start | bytes 1179656 | tf_op jit(solution)/shard_map/ppermute | solution.py:41
  27.3 7.8 %collective-permute-start.9 = (bf16[1536,128]{1,0:T(8,128)(2,1)S(1)}, bf16[1536,128]{1,0:T(8,128)(2,1)S(1)}, u32[]{:S(2)}, u32[]{:S(2)}) collective-permute-start(bf16[1536,128]{1,0:T(8,128)(2,1)S(1)} %collective-permute-done.8.w3), channel_id=1, source_target_pairs={{0,4},{1,5},{2,6},{3,7},{4,0},{5,1},{6,2},{7,3},{32,33},{33,32},{3... | collective-permute-start | bytes 1179656 | tf_op jit(solution)/shard_map/ppermute | solution.py:41
  35.1 4.9 %collective-permute-start.13 = (bf16[1536,128]{1,0:T(8,128)(2,1)S(1)}, bf16[1536,128]{1,0:T(8,128)(2,1)S(1)}, u32[]{:S(2)}, u32[]{:S(2)}) collective-permute-start(bf16[1536,128]{1,0:T(8,128)(2,1)S(1)} %collective-permute-done.9.w2), channel_id=1, source_target_pairs={{0,32},{1,33},{2,34},{3,35},{4,36},{5,37},{6,38},{7,39},{32,0},{33... | collective-permute-start | bytes 1179656 | tf_op jit(solution)/shard_map/ppermute | solution.py:41
  35.2 14.0 %collective-permute-start.18 = (bf16[512,128]{1,0:T(8,128)(2,1)S(1)}, bf16[512,128]{1,0:T(8,128)(2,1)S(1)}, u32[]{:S(2)}, u32[]{:S(2)}) collective-permute-start(bf16[512,128]{1,0:T(8,128)(2,1)S(1)} %get-tuple-element.146), channel_id=1, source_target_pairs={{0,1},{1,0},{2,3},{3,2},{4,5},{5,4},{6,7},{7,6},{32,33},{33,32},{3... | collective-permute-start | bytes 393224 | tf_op jit(solution)/shard_map/ppermute | solution.py:41
  36.5 12.7 %collective-permute-start.19 = (bf16[512,128]{1,0:T(8,128)(2,1)S(1)}, bf16[512,128]{1,0:T(8,128)(2,1)S(1)}, u32[]{:S(2)}, u32[]{:S(2)}) collective-permute-start(bf16[512,128]{1,0:T(8,128)(2,1)S(1)} %get-tuple-element.147), channel_id=1, source_target_pairs={{0,2},{1,3},{2,0},{3,1},{4,6},{5,7},{6,4},{7,5},{32,34},{33,35},{3... | collective-permute-start | bytes 393224 | tf_op jit(solution)/shard_map/ppermute | solution.py:41
  37.2 11.9 %collective-permute-start.20 = (bf16[512,128]{1,0:T(8,128)(2,1)S(1)}, bf16[512,128]{1,0:T(8,128)(2,1)S(1)}, u32[]{:S(2)}, u32[]{:S(2)}) collective-permute-start(bf16[512,128]{1,0:T(8,128)(2,1)S(1)} %get-tuple-element.148), channel_id=1, source_target_pairs={{0,3},{1,2},{2,1},{3,0},{4,7},{5,6},{6,5},{7,4},{32,35},{33,34},{3... | collective-permute-start | bytes 393224 | tf_op jit(solution)/shard_map/ppermute | solution.py:41
  40.0 15.9 %slice-start = ((s8[6291456]{0:T(1024)(128)(4,1)}), s8[4194304]{0:T(1024)(128)(4,1)S(1)}, s32[]{:S(2)}) async-start(s8[6291456]{0:T(1024)(128)(4,1)} %bitcast.19), calls=%async_computation | async-start | bytes 8388608
  40.0 15.9 %slice-start.1 = ((s8[6291456]{0:T(1024)(128)(4,1)}), s8[2097152]{0:T(1024)(128)(4,1)S(1)}, s32[]{:S(2)}) async-start(s8[6291456]{0:T(1024)(128)(4,1)} %bitcast.19), calls=%async_computation.1 | async-start | bytes 4194304
  44.8 5.7 %copy-start.2 = (bf16[1,256,1536]{2,1,0:T(8,128)(2,1)S(1)}, bf16[1,256,1536]{2,1,0:T(8,128)(2,1)}, u32[]{:S(2)}) copy-start(bf16[1,256,1536]{2,1,0:T(8,128)(2,1)} %param.13) | copy-start | bytes 2359300
  44.8 4.3 %collective-permute-start.14 = (bf16[256,128]{1,0:T(8,128)(2,1)S(1)}, bf16[256,128]{1,0:T(8,128)(2,1)S(1)}, u32[]{:S(2)}, u32[]{:S(2)}) collective-permute-start(bf16[256,128]{1,0:T(8,128)(2,1)S(1)} %get-tuple-element.143.own), channel_id=1, source_target_pairs={{0,4},{1,5},{2,6},{3,7},{4,0},{5,1},{6,2},{7,3},{32,36},{33,37},{3... | collective-permute-start | bytes 196616 | tf_op jit(solution)/shard_map/ppermute | solution.py:41
  49.3 6.6 %collective-permute-start.21 = (bf16[512,128]{1,0:T(8,128)(2,1)S(1)}, bf16[512,128]{1,0:T(8,128)(2,1)S(1)}, u32[]{:S(2)}, u32[]{:S(2)}) collective-permute-start(bf16[512,128]{1,0:T(8,128)(2,1)S(1)} %get-tuple-element.212), channel_id=1, source_target_pairs={{0,4},{1,5},{2,6},{3,7},{4,0},{5,1},{6,2},{7,3},{32,36},{33,37},{3... | collective-permute-start | bytes 393224 | tf_op jit(solution)/shard_map/ppermute | solution.py:41
  51.1 6.7 %collective-permute-start.15 = (bf16[512,128]{1,0:T(8,128)(2,1)S(1)}, bf16[512,128]{1,0:T(8,128)(2,1)S(1)}, u32[]{:S(2)}, u32[]{:S(2)}) collective-permute-start(bf16[512,128]{1,0:T(8,128)(2,1)S(1)} %shard_map.115.v0), channel_id=1, source_target_pairs={{0,1},{1,0},{2,3},{3,2},{4,5},{5,4},{6,7},{7,6},{32,33},{33,32},{3... | collective-permute-start | bytes 393224 | tf_op jit(solution)/shard_map/ppermute | solution.py:41
  51.2 7.1 %collective-permute-start.16 = (bf16[512,128]{1,0:T(8,128)(2,1)S(1)}, bf16[512,128]{1,0:T(8,128)(2,1)S(1)}, u32[]{:S(2)}, u32[]{:S(2)}) collective-permute-start(bf16[512,128]{1,0:T(8,128)(2,1)S(1)} %shard_map.115.v0), channel_id=1, source_target_pairs={{0,2},{1,3},{2,0},{3,1},{4,6},{5,7},{6,4},{7,5},{32,34},{33,35},{3... | collective-permute-start | bytes 393224 | tf_op jit(solution)/shard_map/ppermute | solution.py:41
  53.1 6.7 %collective-permute-start.17 = (bf16[512,128]{1,0:T(8,128)(2,1)S(1)}, bf16[512,128]{1,0:T(8,128)(2,1)S(1)}, u32[]{:S(2)}, u32[]{:S(2)}) collective-permute-start(bf16[512,128]{1,0:T(8,128)(2,1)S(1)} %shard_map.115.v0), channel_id=1, source_target_pairs={{0,3},{1,2},{2,1},{3,0},{4,7},{5,6},{6,5},{7,4},{32,35},{33,34},{3... | collective-permute-start | bytes 393224 | tf_op jit(solution)/shard_map/ppermute | solution.py:41
  59.8 8.0 %copy-start.1 = (bf16[1,256,1536]{2,1,0:T(8,128)(2,1)S(1)}, bf16[1,256,1536]{2,1,0:T(8,128)(2,1)}, u32[]{:S(2)}) copy-start(bf16[1,256,1536]{2,1,0:T(8,128)(2,1)} %param.9) | copy-start | bytes 2359300
  59.8 3.8 %collective-permute-start.22 = (bf16[2048,384]{1,0:T(8,128)(2,1)S(1)}, bf16[2048,384]{1,0:T(8,128)(2,1)S(1)}, u32[]{:S(2)}, u32[]{:S(2)}) collective-permute-start(bf16[2048,384]{1,0:T(8,128)(2,1)S(1)} %get-tuple-element.168), channel_id=1, source_target_pairs={{0,32},{1,33},{2,34},{3,35},{4,36},{5,37},{6,38},{7,39},{32,0},{33... | collective-permute-start | bytes 4718600 | tf_op jit(solution)/shard_map/ppermute | solution.py:41
  59.8 16.4 %collective-permute-start.25 = (bf16[1792,128]{1,0:T(8,128)(2,1)S(1)}, bf16[1792,128]{1,0:T(8,128)(2,1)S(1)}, u32[]{:S(2)}, u32[]{:S(2)}) collective-permute-start(bf16[1792,128]{1,0:T(8,128)(2,1)S(1)} %get-tuple-element.169), channel_id=1, source_target_pairs={{0,8},{8,0},{16,24},{24,16},{1,9},{9,1},{17,25},{25,17},{2,10},{10... | collective-permute-start | bytes 1376264 | tf_op jit(solution)/shard_map/ppermute | solution.py:65
  61.4 14.8 %collective-permute-start.26 = (bf16[1792,128]{1,0:T(8,128)(2,1)S(1)}, bf16[1792,128]{1,0:T(8,128)(2,1)S(1)}, u32[]{:S(2)}, u32[]{:S(2)}) collective-permute-start(bf16[1792,128]{1,0:T(8,128)(2,1)S(1)} %get-tuple-element.171), channel_id=1, source_target_pairs={{0,24},{8,16},{16,8},{24,0},{1,25},{9,17},{17,9},{25,1},{2,26},{10... | collective-permute-start | bytes 1376264 | tf_op jit(solution)/shard_map/ppermute | solution.py:65
  63.9 12.2 %collective-permute-start.23 = (bf16[512,384]{1,0:T(8,128)(2,1)S(1)}, bf16[512,384]{1,0:T(8,128)(2,1)S(1)}, u32[]{:S(2)}, u32[]{:S(2)}) collective-permute-start(bf16[512,384]{1,0:T(8,128)(2,1)S(1)} %get-tuple-element.216), channel_id=1, source_target_pairs={{0,4},{1,5},{2,6},{3,7},{4,0},{5,1},{6,2},{7,3},{32,33},{33,32},{3... | collective-permute-start | bytes 1179656 | tf_op jit(solution)/shard_map/ppermute | solution.py:41
  64.9 12.8 %collective-permute-start.24 = (bf16[512,384]{1,0:T(8,128)(2,1)S(1)}, bf16[512,384]{1,0:T(8,128)(2,1)S(1)}, u32[]{:S(2)}, u32[]{:S(2)}) collective-permute-start(bf16[512,384]{1,0:T(8,128)(2,1)S(1)} %get-tuple-element.215), channel_id=1, source_target_pairs={{0,64},{1,65},{2,66},{3,67},{4,68},{5,69},{6,70},{7,71},{32,34},{3... | collective-permute-start | bytes 1179656 | tf_op jit(solution)/shard_map/ppermute | solution.py:41
  77.7 13.1 %collective-permute-start.33 = (bf16[1792,128]{1,0:T(8,128)(2,1)S(1)}, bf16[1792,128]{1,0:T(8,128)(2,1)S(1)}, u32[]{:S(2)}, u32[]{:S(2)}) collective-permute-start(bf16[1792,128]{1,0:T(8,128)(2,1)S(1)} %get-tuple-element.183), channel_id=1, source_target_pairs={{0,16},{8,24},{16,0},{24,8},{1,17},{9,25},{17,1},{25,9},{2,18},{10... | collective-permute-start | bytes 1376264 | tf_op jit(solution)/shard_map/ppermute | solution.py:65
  80.6 9.0 %collective-permute-start.28 = (bf16[512,384]{1,0:T(8,128)(2,1)S(1)}, bf16[512,384]{1,0:T(8,128)(2,1)S(1)}, u32[]{:S(2)}, u32[]{:S(2)}) collective-permute-start(bf16[512,384]{1,0:T(8,128)(2,1)S(1)} %get-tuple-element.214), channel_id=1, source_target_pairs={{0,68},{1,69},{2,70},{3,71},{4,64},{5,65},{6,66},{7,67},{32,35},{3... | collective-permute-start | bytes 1179656 | tf_op jit(solution)/shard_map/ppermute | solution.py:41
  81.5 9.5 %collective-permute-start.30 = (bf16[1792,128]{1,0:T(8,128)(2,1)S(1)}, bf16[1792,128]{1,0:T(8,128)(2,1)S(1)}, u32[]{:S(2)}, u32[]{:S(2)}) collective-permute-start(bf16[1792,128]{1,0:T(8,128)(2,1)S(1)} %collective-permute-done.25.a1), channel_id=1, source_target_pairs={{0,32},{1,33},{2,34},{3,35},{4,36},{5,37},{6,38},{7,39},{32,0},{33... | collective-permute-start | bytes 1376264 | tf_op jit(solution)/shard_map/ppermute | solution.py:41
  81.5 9.5 %collective-permute-start.31 = (bf16[1792,128]{1,0:T(8,128)(2,1)S(1)}, bf16[1792,128]{1,0:T(8,128)(2,1)S(1)}, u32[]{:S(2)}, u32[]{:S(2)}) collective-permute-start(bf16[1792,128]{1,0:T(8,128)(2,1)S(1)} %collective-permute-done.26.a3), channel_id=1, source_target_pairs={{0,32},{1,33},{2,34},{3,35},{4,36},{5,37},{6,38},{7,39},{32,0},{33... | collective-permute-start | bytes 1376264 | tf_op jit(solution)/shard_map/ppermute | solution.py:41
  82.0 8.8 %collective-permute-start.27 = (bf16[512,128]{1,0:T(8,128)(2,1)S(1)}, bf16[512,128]{1,0:T(8,128)(2,1)S(1)}, u32[]{:S(2)}, u32[]{:S(2)}) collective-permute-start(bf16[512,128]{1,0:T(8,128)(2,1)S(1)} %get-tuple-element.172), channel_id=1, source_target_pairs={{0,1},{1,0},{2,3},{3,2},{4,5},{5,4},{6,7},{7,6},{32,33},{33,32},{3... | collective-permute-start | bytes 393224 | tf_op jit(solution)/shard_map/ppermute | solution.py:41
  89.5 6.5 %collective-permute-start.29 = (bf16[512,128]{1,0:T(8,128)(2,1)S(1)}, bf16[512,128]{1,0:T(8,128)(2,1)S(1)}, u32[]{:S(2)}, u32[]{:S(2)}) collective-permute-start(bf16[512,128]{1,0:T(8,128)(2,1)S(1)} %get-tuple-element.177), channel_id=1, source_target_pairs={{0,2},{1,3},{2,0},{3,1},{4,6},{5,7},{6,4},{7,5},{32,34},{33,35},{3... | collective-permute-start | bytes 393224 | tf_op jit(solution)/shard_map/ppermute | solution.py:41
  90.8 9.0 %collective-permute-start.34 = (bf16[1792,128]{1,0:T(8,128)(2,1)S(1)}, bf16[1792,128]{1,0:T(8,128)(2,1)S(1)}, u32[]{:S(2)}, u32[]{:S(2)}) collective-permute-start(bf16[1792,128]{1,0:T(8,128)(2,1)S(1)} %collective-permute-done.33.a2), channel_id=1, source_target_pairs={{0,32},{1,33},{2,34},{3,35},{4,36},{5,37},{6,38},{7,39},{32,0},{33... | collective-permute-start | bytes 1376264 | tf_op jit(solution)/shard_map/ppermute | solution.py:41
  91.1 8.8 %collective-permute-start.32 = (bf16[512,128]{1,0:T(8,128)(2,1)S(1)}, bf16[512,128]{1,0:T(8,128)(2,1)S(1)}, u32[]{:S(2)}, u32[]{:S(2)}) collective-permute-start(bf16[512,128]{1,0:T(8,128)(2,1)S(1)} %get-tuple-element.181), channel_id=1, source_target_pairs={{0,3},{1,2},{2,1},{3,0},{4,7},{5,6},{6,5},{7,4},{32,35},{33,34},{3... | collective-permute-start | bytes 393224 | tf_op jit(solution)/shard_map/ppermute | solution.py:41
  92.6 5.6 %collective-permute-start.35 = (bf16[128,384]{1,0:T(8,128)(2,1)S(1)}, bf16[128,384]{1,0:T(8,128)(2,1)S(1)}, u32[]{:S(2)}, u32[]{:S(2)}) collective-permute-start(bf16[128,384]{1,0:T(8,128)(2,1)S(1)} %get-tuple-element.220), channel_id=1, source_target_pairs={{0,1},{1,0},{2,3},{3,2},{4,5},{5,4},{6,7},{7,6},{32,36},{33,37},{3... | collective-permute-start | bytes 294920 | tf_op jit(solution)/shard_map/ppermute | solution.py:41
  93.5 6.3 %collective-permute-start.36 = (bf16[128,384]{1,0:T(8,128)(2,1)S(1)}, bf16[128,384]{1,0:T(8,128)(2,1)S(1)}, u32[]{:S(2)}, u32[]{:S(2)}) collective-permute-start(bf16[128,384]{1,0:T(8,128)(2,1)S(1)} %get-tuple-element.219), channel_id=1, source_target_pairs={{0,2},{1,3},{2,0},{3,1},{4,6},{5,7},{6,4},{7,5},{32,96},{33,97},{3... | collective-permute-start | bytes 294920 | tf_op jit(solution)/shard_map/ppermute | solution.py:41
  96.1 7.5 %collective-permute-start.37 = (bf16[128,384]{1,0:T(8,128)(2,1)S(1)}, bf16[128,384]{1,0:T(8,128)(2,1)S(1)}, u32[]{:S(2)}, u32[]{:S(2)}) collective-permute-start(bf16[128,384]{1,0:T(8,128)(2,1)S(1)} %get-tuple-element.218), channel_id=1, source_target_pairs={{0,3},{1,2},{2,1},{3,0},{4,7},{5,6},{6,5},{7,4},{32,100},{33,101},... | collective-permute-start | bytes 294920 | tf_op jit(solution)/shard_map/ppermute | solution.py:41
  100.0 4.3 %collective-permute-start.38 = (bf16[256,128]{1,0:T(8,128)(2,1)S(1)}, bf16[256,128]{1,0:T(8,128)(2,1)S(1)}, u32[]{:S(2)}, u32[]{:S(2)}) collective-permute-start(bf16[256,128]{1,0:T(8,128)(2,1)S(1)} %slice.98), channel_id=1, source_target_pairs={{0,4},{1,5},{2,6},{3,7},{4,0},{5,1},{6,2},{7,3},{32,36},{33,37},{3... | collective-permute-start | bytes 196616 | tf_op jit(solution)/shard_map/ppermute | solution.py:41
